TPU v7x, 32 devices: a whole 2x2x4 slice. The times are simulated.
32 devices in a mesh: rows: 4 (over x, core), tract: 8 (over z, y).
Axes of the slice: x: 2, y: 2, z: 4, core: 2. Of those that a mesh axis runs over, the one named last changes fastest.
Arguments:
- byte_values: int32 [64, 2048], P('rows', 'tract'), may hold values from 0 to 255
- segment_ids: int32 [64, 2048], P('rows', 'tract'), may hold values from 0 to 15, as said below
- valid: int32 [64, 2048], P('rows', 'tract'), may hold values from 0 to 1, as said below
- table: float32 [256, 768], P('rows'), may hold values from -6 to 6
- conv_weight: float32 [3072, 768], P('rows'), may hold values from -0.109375 to 0.109375
- conv_bias: float32 [768], P('rows'), may hold values from -3 to 3
- score_weight: float32 [768], P('rows'), may hold values from -0.4375 to 0.4375
- cotangent: bfloat16 [64, 1024, 768], P('rows', 'tract'), may hold values from -6 to 6
Outputs:
- output: bfloat16 [64, 1024, 768], P('rows', 'tract')
- table_grad: float32 [256, 768], P('rows')
- conv_weight_grad: float32 [3072, 768], P('rows')
- conv_bias_grad: float32 [768], P('rows')
- score_weight_grad: float32 [768], P('rows')
Inputs may be any that keep to these rules, and one draw needn't show every extreme that they name: `segment_ids`: segment numbers start at 0 in each row and never fall along it; in each group of 16 consecutive rows one row is a single segment. `valid`: in each row the ones come first and cover at least half of it; in each group of 16 consecutive rows the row that is a single segment is all ones.
All inputs are finite; a program needn't handle non-finite values.
Results may differ from a plain program's by a relative error of at most 0.008.
Values may be sent and summed in bfloat16 or wider, within the bound.
No kernel may reach another device: no remote copies, remote signals or barrier semaphores. Data moves between devices by JAX's collectives and lax.ppermute only.
A program may use at most 384 MiB of HBM per device.

v0:
```python
import jax
import jax.numpy as jnp
from jax import lax
from jax.sharding import PartitionSpec as P

PRECISE = lax.Precision.HIGHEST


def passed_along(value, axis, steps):
    count = lax.axis_size(axis)
    first, last = (max(0, -steps), min(count, count - steps))
    return lax.ppermute(value, axis, [(source, source + steps) for source in range(first, last)])


def embed_codes(byte_rows, valid_rows, byte_codes, table_all):
    one_hot = (byte_rows[..., None] == byte_codes).astype(jnp.bfloat16) * valid_rows[
        ..., None
    ].astype(jnp.bfloat16)
    embedded = jnp.einsum(
        "rtv,vd->rtd", one_hot, table_all, preferred_element_type=jnp.float32
    ).astype(jnp.bfloat16)
    return (one_hot, embedded)


def placed(term, left, right):
    return jnp.pad(term, ((0, 0), (left, right), (0, 0)))


def body(byte_values, segment_ids, valid, table, conv_weight, conv_bias, score_weight, cotangent):
    table_all, weight_all, bias_all, score_all = (
        lax.all_gather(table.astype(jnp.bfloat16), "rows", axis=0, tiled=True),
        lax.all_gather(conv_weight.astype(jnp.bfloat16), "rows", axis=0, tiled=True),
        lax.all_gather(conv_bias.astype(jnp.bfloat16), "rows", axis=0, tiled=True),
        lax.all_gather(score_weight.astype(jnp.bfloat16), "rows", axis=0, tiled=True),
    )
    rows_here, run_len = byte_values.shape
    model_width = table_all.shape[1]
    weight_blocks = [
        weight_all[offset * model_width : (offset + 1) * model_width] for offset in range(4)
    ]
    byte_codes = jnp.arange(table_all.shape[0], dtype=jnp.int32)
    one_hot, embedded = embed_codes(byte_values, valid, byte_codes, table_all)
    embed_prev, seg_prev, valid_prev = passed_along(
        (embedded[:, -6:], segment_ids[:, -6:], valid[:, -6:]), "tract", 1
    )
    ext_embed = jnp.concatenate([embed_prev, embedded], 1)
    ext_seg = jnp.concatenate([seg_prev, segment_ids], 1)
    ext_valid = jnp.concatenate([valid_prev, valid], 1).astype(jnp.float32)
    conv_span = run_len + 3
    seg_conv = ext_seg[:, 3:]
    masked_list = [
        ext_embed[:, 3 - offset : 3 - offset + conv_span]
        * (ext_seg[:, 3 - offset : 3 - offset + conv_span] == seg_conv)[..., None].astype(
            jnp.bfloat16
        )
        for offset in range(4)
    ]
    conv_out = bias_all.astype(jnp.float32)
    for offset in range(4):
        conv_out = conv_out + jnp.einsum(
            "rtd,de->rte",
            masked_list[offset],
            weight_blocks[offset],
            preferred_element_type=jnp.float32,
        )
    seg_own = ext_seg[:, 6:]
    same_own = [
        (ext_seg[:, 6 - offset : 6 - offset + run_len] == seg_own).astype(jnp.float32)
        for offset in range(4)
    ]
    keep_list = [
        same_own[offset] * ext_valid[:, 6 - offset : 6 - offset + run_len] for offset in range(4)
    ]
    running = jnp.zeros((rows_here, run_len, model_width), jnp.float32)
    counts = jnp.zeros((rows_here, run_len), jnp.float32)
    pooled = []
    divisors = []
    for offset in range(4):
        running = (
            running + keep_list[offset][..., None] * conv_out[:, 3 - offset : 3 - offset + run_len]
        )
        counts = counts + keep_list[offset]
        divisor = jnp.maximum(counts, 1.0)
        pooled.append(running / divisor[..., None])
        divisors.append(divisor)
    stacked = jnp.stack(pooled, 0)
    score_float = score_all.astype(jnp.float32)
    scores = jnp.einsum("brtd,d->brt", stacked, score_float, precision=PRECISE)
    block_probs = jax.nn.softmax(scores, axis=0)
    mixed_rows = jnp.sum(block_probs[..., None] * stacked, 0)
    output = jnp.mean(mixed_rows.reshape(rows_here, run_len // 2, 2, model_width), 2).astype(
        jnp.bfloat16
    )
    upstream = jnp.repeat(cotangent.astype(jnp.float32), 2, axis=1) * 0.5
    inner_prod = jnp.sum(stacked * upstream[None], -1)
    score_rows = block_probs * (inner_prod - jnp.sum(block_probs * inner_prod, 0))
    pool_grads = block_probs[..., None] * upstream[None] + score_rows[..., None] * score_float
    score_grad = jnp.einsum("brt,brtd->d", score_rows, stacked, precision=PRECISE)
    carried = jnp.zeros((rows_here, run_len, model_width), jnp.float32)
    conv_terms = []
    for offset in (3, 2, 1, 0):
        carried = carried + pool_grads[offset] / divisors[offset][..., None]
        conv_terms.append(placed(keep_list[offset][..., None] * carried, 3 - offset, offset))
    conv_grad = conv_terms[0] + conv_terms[1] + conv_terms[2] + conv_terms[3]
    returned = passed_along(conv_grad[:, :3].astype(jnp.bfloat16), "tract", -1).astype(jnp.float32)
    conv_own = jnp.concatenate([conv_grad[:, 3:-3], conv_grad[:, -3:] + returned], 1)
    conv_low = conv_own.astype(jnp.bfloat16)
    bias_grad = jnp.sum(conv_low.astype(jnp.float32), (0, 1))
    weight_grad = jnp.concatenate(
        [
            jnp.einsum(
                "rtd,rte->de",
                masked_list[offset][:, 3:],
                conv_low,
                preferred_element_type=jnp.float32,
            )
            for offset in range(4)
        ],
        0,
    )
    embed_terms = []
    for offset in range(4):
        block_grad = jnp.einsum(
            "rte,de->rtd", conv_low, weight_blocks[offset], preferred_element_type=jnp.float32
        )
        embed_terms.append(placed(block_grad * same_own[offset][..., None], 6 - offset, offset))
    embed_grad = embed_terms[0] + embed_terms[1] + embed_terms[2] + embed_terms[3]
    hot_float = one_hot.astype(jnp.float32)
    returned_embed = passed_along(embed_grad[:, 3:6].astype(jnp.bfloat16), "tract", -1).astype(
        jnp.float32
    )
    own_grad = jnp.concatenate([embed_grad[:, 6:-3], embed_grad[:, -3:] + returned_embed], 1)
    table_grad = jnp.einsum("rtv,rtd->vd", hot_float, own_grad, precision=PRECISE)
    grad_terms = (table_grad, weight_grad, bias_grad, score_grad)
    summed = lax.psum((grad_terms[0], grad_terms[1], grad_terms[2], grad_terms[3]), "tract")
    shards = (
        lax.psum_scatter(summed[0], "rows", scatter_dimension=0, tiled=True),
        lax.psum_scatter(summed[1], "rows", scatter_dimension=0, tiled=True),
        lax.psum_scatter(summed[2], "rows", scatter_dimension=0, tiled=True),
        lax.psum_scatter(summed[3], "rows", scatter_dimension=0, tiled=True),
    )
    return (output, shards[0], shards[1], shards[2], shards[3])


def solution(mesh):
    return jax.shard_map(
        body,
        mesh=mesh,
        in_specs=(
            P("rows", "tract"),
            P("rows", "tract"),
            P("rows", "tract"),
            P("rows", None),
            P("rows", None),
            P("rows"),
            P("rows"),
            P("rows", "tract", None),
        ),
        out_specs=(
            P("rows", "tract", None),
            P("rows", None),
            P("rows", None),
            P("rows"),
            P("rows"),
        ),
        check_vma=False,
    )
```

profile of v0, /device:TPU:0, one launch (start us, length us, event | category | flops | bytes accessed | tf_op | source)
XLA Modules:
  0.0 671.2 jit_solution(363923085334741195)
XLA Ops:
  7.2 2.9 convert_element_type.95
  10.3 1.4 slice.123
  11.6 5.5 collective-permute-start
  17.1 1.4 slice.129
  18.5 2.8 collective-permute-start.2
  21.3 0.7 convert_element_type.92
  22.0 1.0 convert_element_type.93
  23.0 9.0 %all_gather.13 = bf16[256,768]{1,0:T(8,128)(2,1)S(1)} all-gather(bf16[64,768]{1,0:T(8,128)(2,1)S(1)} %convert_element_type.93), channel_id=1, replica_groups=mesh['rows'=4,'tract'=8] {'rows'}, dimensions={0}, use_global_device_ids=true | all-gather | bytes 491520 | tf_op jit(solution)/shard_map/all_gather | solution.py:31
  32.1 2.6 convolution_convert_fusion
  34.7 2.7 copy-done.2
  37.4 3.5 collective-permute-start.1
  41.4 1.2 convert_element_type.99
  43.8 0.8 dynamic-update-slice
  45.2 0.8 dynamic-update-slice.1
  46.1 7.3 %all-reduce.15 = (bf16[768]{0:T(1024)(128)(2,1)}, bf16[768]{0:T(1024)(128)(2,1)S(1)}) all-reduce(bf16[768]{0:T(1024)(128)(2,1)} %copy-done.20, bf16[768]{0:T(1024)(128)(2,1)S(1)} %dynamic-update-slice.1), channel_id=1, replica_groups=mesh['rows'=4,'tract'=8] {'rows'}, use_global_device_ids=true, to_apply=%add.8 | all-reduce | flops 1536 | bytes 6144
  54.6 0.7 convert_element_type.91
  55.3 6.5 broadcast_in_dim.2
  61.7 15.8 %mul.203 = f32[16,256,768]{2,1,0:T(8,128)} reshape(f32[16,128,2,768]{3,2,1,0:T(2,128)} %broadcast_in_dim.2) | data formatting | bytes 25165824 | tf_op jit(solution)/shard_map/mul | solution.py:94
  77.5 0.8 add_convert_fusion
  78.3 0.7 fusion.95
  79.4 19.3 %fusion.24 = (bf16[16,259,768]{2,1,0:T(8,128)(2,1)}, bf16[16,259,768]{2,1,0:T(8,128)(2,1)}, bf16[16,259,768]{2,1,0:T(8,128)(2,1)}) fusion(bf16[16,256,768]{2,1,0:T(8,128)(2,1)} %copy-done.2, bf16[16,6,768]{2,1,0:T(8,128)(2,1)S(1)} %collective-permute-done.1, bf16[16,259]{1,0:T(8,128)(2,1)S(1)} %get-tuple-element.48, ...), kind=kLoop, calls=%fused_computation.48 | loop fusion | flops 57286656 | bytes 25559328 | tf_op jit(solution)/shard_map/mul | solution.py:52
  98.7 10.7 %fusion.20 = f32[16,259,768]{2,1,0:T(8,128)} fusion(bf16[16,6,768]{2,1,0:T(8,128)(2,1)S(1)} %collective-permute-done.1, bf16[16,256,768]{2,1,0:T(8,128)(2,1)} %copy-done.2, bf16[3072,768]{1,0:T(8,128)(2,1)} %all-gather.2.cloned.1.call-done), kind=kOutput, calls=%fused_computation.44 | convolution fusion | flops 4901191680 | bytes 20348928 | tf_op jit(solution)/shard_map/rtd,de->rte/dot_general | solution.py:60
  109.3 8.4 %fusion.59 = f32[16,259,768]{2,1,0:T(8,128)} fusion(bf16[16,259,768]{2,1,0:T(8,128)(2,1)S(1)} %copy-done.4, bf16[3072,768]{1,0:T(8,128)(2,1)S(1)} %copy-done.9), kind=kOutput, calls=%fused_computation.88 | convolution fusion | flops 4888461312 | bytes 20398080 | tf_op jit(solution)/shard_map/rtd,de->rte/dot_general | solution.py:60
  117.8 8.8 %fusion.60 = f32[16,259,768]{2,1,0:T(8,128)} fusion(bf16[16,259,768]{2,1,0:T(8,128)(2,1)S(1)} %copy-done.3, bf16[3072,768]{1,0:T(8,128)(2,1)S(1)} %copy-done.9), kind=kOutput, calls=%fused_computation.89 | convolution fusion | flops 4888461312 | bytes 20398080 | tf_op jit(solution)/shard_map/rtd,de->rte/dot_general | solution.py:60
  126.5 21.3 %add_add_fusion = f32[16,259,768]{2,1,0:T(8,128)} fusion(f32[16,259,768]{2,1,0:T(8,128)} %fusion.60, f32[16,259,768]{2,1,0:T(8,128)} %fusion.59, f32[16,259,768]{2,1,0:T(8,128)} %fusion.20, bf16[16,259,768]{2,1,0:T(8,128)(2,1)} %get-tuple-element.39, f32[768]{0:T(1024)S(1)} %convert_element_type.91, bf16[3072,768]{1,0:T(8,128)(2,1)} %all-gather.2.cloned.1.call-done), kind=kOutput, calls=%fused_computation.6 | convolution fusion | flops 4901191680 | bytes 59329536 | tf_op jit(solution)/shard_map/rtd,de->rte/dot_general | solution.py:60
  147.9 23.6 %divide_bitcast_fusion.1 = (f32[1,16,256,768]{3,2,1,0:T(8,128)}, f32[16,256,768]{2,1,0:T(8,128)}, f32[1,16,256,768]{3,2,1,0:T(8,128)}) fusion(f32[16,256]{1,0:T(8,128)S(1)} %get-tuple-element.27, f32[16,259,768]{2,1,0:T(8,128)} %add_add_fusion, f32[16,256]{1,0:T(8,128)S(1)} %get-tuple-element.28, f32[16,256]{1,0:T(8,128)S(1)} %get-tuple-element.43, ...), kind=kLoop, calls=%fused_computation.35 | loop fusion | flops 15728640 | bytes 62980096 | tf_op jit(solution)/shard_map/stack | solution.py:86
  171.6 14.2 %divide_bitcast_fusion = (f32[1,16,256,768]{3,2,1,0:T(8,128)}, f32[1,16,256,768]{3,2,1,0:T(8,128)}) fusion(f32[16,256]{1,0:T(8,128)S(1)} %get-tuple-element.29, f32[16,256,768]{2,1,0:T(8,128)} %get-tuple-element.26, f32[16,259,768]{2,1,0:T(8,128)S(1)} %bitcast.103, f32[16,256]{1,0:T(8,128)S(1)} %get-tuple-element.30, f32[16,256]{1,0:T(8,128)S(1)} %get-tuple-element.31, ...), kind=kLoop, calls=%fused_computation.34 | loop fusion | flops 18874368 | bytes 62980096 | tf_op jit(solution)/shard_map/stack | solution.py:86
  185.8 26.8 %fusion.83 = f32[1,4,16,256]{3,0,2,1:T(1,128)S(1)} fusion(bf16[768,1,1,1]{0,1,2,3:T(2,128)(2,1)S(1)} %reshape.65, f32[1,16,256,768]{3,2,1,0:T(8,128)} %get-tuple-element.37, f32[1,16,256,768]{3,2,1,0:T(8,128)} %get-tuple-element.36, f32[1,16,256,768]{3,2,1,0:T(8,128)} %get-tuple-element.25, f32[1,16,256,768]{3,2,1,0:T(8,128)} %get-tuple-element.38), kind=kOutput, calls=%fused_computation.140 | convolution fusion | flops 188743680 | bytes 50398720 | tf_op jit(solution)/shard_map/brtd,d->brt/dot_general | solution.py:88
  212.6 25.2 %multiply_reduce_fusion = (f32[4,16,256]{2,1,0:T(8,128)S(1)}, f32[16,256,768]{2,1,0:T(8,128)}) fusion(f32[16,256,768]{2,1,0:T(8,128)} %mul.203, f32[1,16,256,768]{3,2,1,0:T(8,128)} %get-tuple-element.37, f32[1,16,256,768]{3,2,1,0:T(8,128)} %get-tuple-element.36, f32[1,16,256,768]{3,2,1,0:T(8,128)} %get-tuple-element.25, ...), kind=kLoop, calls=%fused_computation.2 | loop fusion | flops 84918272 | bytes 75628544 | tf_op jit(solution)/shard_map/reduce_sum | solution.py:95
  237.9 0.6 copy-done.10
  238.5 21.3 %multiply_add_fusion = f32[4,16,256,768]{3,2,1,0:T(8,128)} fusion(f32[768]{0:T(1024)S(1)} %copy-done.14, f32[4,16,256]{2,1,0:T(8,128)S(1)} %subtract_multiply_fusion, f32[16,256,768]{2,1,0:T(8,128)} %mul.203, f32[4,16,256]{2,1,0:T(8,128)S(1)} %fusion.66), kind=kLoop, calls=%fused_computation.1 | loop fusion | flops 37748736 | bytes 63048704 | tf_op jit(solution)/shard_map/add | solution.py:97
  259.8 16.4 %broadcast_multiply_fusion.4 = (f32[16,256,768]{2,1,0:T(8,128)}, f32[16,256,768]{2,1,0:T(8,128)S(1)}, f32[16,256,768]{2,1,0:T(8,128)}) fusion(f32[16,256]{1,0:T(8,128)S(1)} %get-tuple-element.30, f32[16,256]{1,0:T(8,128)S(1)} %get-tuple-element.29, f32[4,16,256,768]{3,2,1,0:T(8,128)} %multiply_add_fusion, f32[16,256]{1,0:T(8,128)S(1)} %get-tuple-element.31, ...), kind=kLoop, calls=%fused_computation.64 | loop fusion | flops 15728640 | bytes 62980096 | tf_op jit(solution)/shard_map/mul | solution.py:103
  276.2 16.6 %broadcast_multiply_fusion.5 = (f32[16,256,768]{2,1,0:T(8,128)}, f32[16,256,768]{2,1,0:T(8,128)}) fusion(f32[16,256]{1,0:T(8,128)S(1)} %get-tuple-element.28, f32[16,256,768]{2,1,0:T(8,128)S(1)} %get-tuple-element.22, f32[16,256]{1,0:T(8,128)S(1)} %get-tuple-element.27, f32[4,16,256,768]{3,2,1,0:T(8,128)} %multiply_add_fusion, ...), kind=kLoop, calls=%fused_computation.65 | loop fusion | flops 18874368 | bytes 62980096 | tf_op jit(solution)/shard_map/mul | solution.py:103
  292.8 22.5 %fusion.93 = (bf16[16,259,768]{2,1,0:T(8,128)(2,1)S(1)}, f32[16,259,768]{2,1,0:T(8,128)}) fusion(f32[16,256,768]{2,1,0:T(8,128)} %get-tuple-element.34, f32[16,256,768]{2,1,0:T(8,128)} %get-tuple-element.33, f32[16,256,768]{2,1,0:T(8,128)} %get-tuple-element.21, f32[16,256,768]{2,1,0:T(8,128)} %get-tuple-element.35), kind=kLoop, calls=%fused_computation.149 | loop fusion | flops 12730368 | bytes 69427200 | tf_op jit(solution)/shard_map/convert.3
  315.3 1.5 collective-permute-start.3
  316.8 2.8 slice.197
  319.7 2.2 collective-permute-done.3
  321.8 1.1 fusion.63
  322.9 9.7 %fusion.39 = f32[768,768]{1,0:T(8,128)} fusion(bf16[16,259,768]{2,1,0:T(8,128)(2,1)} %get-tuple-element.40, bf16[16,3,768]{2,1,0:T(4,128)(2,1)S(1)} %fusion.63, bf16[16,253,768]{2,1,0:T(8,128)(2,1)S(1)} %slice.197), kind=kOutput, calls=%fused_computation.72 | convolution fusion | flops 4844421120 | bytes 14942208 | tf_op jit(solution)/shard_map/rtd,rte->de/dot_general | solution.py:111
  332.6 7.2 %fusion.42 = f32[768,768]{1,0:T(8,128)} fusion(bf16[16,259,768]{2,1,0:T(8,128)(2,1)S(1)} %bitcast.107, bf16[16,3,768]{2,1,0:T(4,128)(2,1)S(1)} %fusion.63, bf16[16,253,768]{2,1,0:T(8,128)(2,1)S(1)} %slice.197), kind=kOutput, calls=%fused_computation.73 | convolution fusion | flops 4844421120 | bytes 15040512 | tf_op jit(solution)/shard_map/rtd,rte->de/dot_general | solution.py:111
  339.8 10.5 %fusion.58 = f32[16,256,768]{2,1,0:T(8,128)} fusion(bf16[3072,768]{1,0:T(8,128)(2,1)S(1)} %bitcast.109, bf16[16,3,768]{2,1,0:T(4,128)(2,1)S(1)} %fusion.63, bf16[16,253,768]{2,1,0:T(8,128)(2,1)S(1)} %slice.197), kind=kOutput, calls=%fused_computation.87 | convolution fusion | flops 4844421120 | bytes 20152320 | tf_op jit(solution)/shard_map/rte,de->rtd/dot_general | solution.py:123
  350.3 8.0 %broadcast_multiply_fusion.2 = f32[16,256,768]{2,1,0:T(8,128)} fusion(f32[16,256]{1,0:T(8,128)S(1)} %copy-done.17, bf16[3072,768]{1,0:T(8,128)(2,1)S(1)} %bitcast.109, bf16[16,3,768]{2,1,0:T(4,128)(2,1)S(1)} %fusion.63, bf16[16,253,768]{2,1,0:T(8,128)(2,1)S(1)} %slice.197), kind=kOutput, calls=%fused_computation.61 | convolution fusion | flops 4847566848 | bytes 20168704 | tf_op jit(solution)/shard_map/rte,de->rtd/dot_general | solution.py:123
  358.3 8.0 %broadcast_multiply_fusion.1 = f32[16,256,768]{2,1,0:T(8,128)} fusion(f32[16,256]{1,0:T(8,128)S(1)} %copy-done.16, bf16[3072,768]{1,0:T(8,128)(2,1)S(1)} %bitcast.109, bf16[16,3,768]{2,1,0:T(4,128)(2,1)S(1)} %fusion.63, bf16[16,253,768]{2,1,0:T(8,128)(2,1)S(1)} %slice.197), kind=kOutput, calls=%fused_computation.60 | convolution fusion | flops 4847566848 | bytes 20168704 | tf_op jit(solution)/shard_map/rte,de->rtd/dot_general | solution.py:123
  366.4 8.1 %broadcast_multiply_fusion = f32[16,256,768]{2,1,0:T(8,128)} fusion(f32[16,256]{1,0:T(8,128)S(1)} %copy-done.15, bf16[3072,768]{1,0:T(8,128)(2,1)S(1)} %bitcast.109, bf16[16,3,768]{2,1,0:T(4,128)(2,1)S(1)} %fusion.63, bf16[16,253,768]{2,1,0:T(8,128)(2,1)S(1)} %slice.197), kind=kOutput, calls=%fused_computation.59 | convolution fusion | flops 4847566848 | bytes 20168704 | tf_op jit(solution)/shard_map/rte,de->rtd/dot_general | solution.py:123
  374.5 17.8 %pad_add_fusion = f32[16,262,768]{2,1,0:T(8,128)S(1)} fusion(f32[16,256,768]{2,1,0:T(8,128)} %broadcast_multiply_fusion, f32[16,256,768]{2,1,0:T(8,128)} %broadcast_multiply_fusion.1, f32[16,256,768]{2,1,0:T(8,128)} %broadcast_multiply_fusion.2, f32[16,256,768]{2,1,0:T(8,128)} %fusion.58), kind=kLoop, calls=%fused_computation.4 | loop fusion | flops 9658368 | bytes 63209472 | tf_op jit(solution)/shard_map/add | solution.py:127
  392.3 4.7 copy-done
  396.9 0.7 slice.388
  397.6 1.3 collective-permute-start.4
  398.9 11.2 %fusion.45 = f32[768,768]{1,0:T(8,128)} fusion(bf16[16,259,768]{2,1,0:T(8,128)(2,1)} %get-tuple-element.39, bf16[16,3,768]{2,1,0:T(4,128)(2,1)S(1)} %fusion.63, bf16[16,253,768]{2,1,0:T(8,128)(2,1)} %copy-done.1), kind=kOutput, calls=%fused_computation.74 | convolution fusion | flops 4844421120 | bytes 15015936 | tf_op jit(solution)/shard_map/rtd,rte->de/dot_general | solution.py:111
  410.1 10.7 %slice.200 = f32[16,253,768]{2,1,0:T(8,128)} slice(f32[16,262,768]{2,1,0:T(8,128)} %copy-done), slice={[0:16], [6:259], [0:768]} | slice | bytes 24870912 | tf_op jit(solution)/shard_map/slice | solution.py:132
  420.8 1.1 slice_add_fusion
  421.9 12.5 %fusion.48 = f32[256,768]{1,0:T(8,128)} fusion(f32[16,3,768]{2,1,0:T(4,128)S(1)} %slice_add_fusion, f32[16,253,768]{2,1,0:T(8,128)} %slice.200, s32[16,256]{1,0:T(8,128)S(1)} %copy-done.22, bf16[16,256]{1,0:T(8,128)(2,1)S(1)} %copy-done.19), kind=kOutput, calls=%fused_computation.76 | convolution fusion | flops 9668919296 | bytes 13393920 | tf_op jit(solution)/shard_map/rtv,rtd->vd/dot_general | solution.py:133
  434.5 9.2 %convolution_bitcast_fusion = f32[768,768]{1,0:T(8,128)S(1)} fusion(bf16[16,256,768]{2,1,0:T(8,128)(2,1)} %copy-done.2, bf16[16,3,768]{2,1,0:T(4,128)(2,1)S(1)} %fusion.63, bf16[16,253,768]{2,1,0:T(8,128)(2,1)} %copy-done.1), kind=kOutput, calls=%fused_computation.75 | convolution fusion | flops 4844421120 | bytes 14942208 | tf_op jit(solution)/shard_map/rtd,rte->de/dot_general | solution.py:111
  443.7 4.0 pad_maximum_fusion.1
  448.7 15.8 %bitcast_reduce_fusion = f32[16,128,768]{2,0,1:T(8,128)} fusion(f32[16,256,768]{2,1,0:T(8,128)} %get-tuple-element.6), kind=kLoop, calls=%fused_computation.32 | loop fusion | flops 1572864 | bytes 18874368 | tf_op jit(solution)/shard_map/reduce_sum | solution.py:91
  464.5 76.6 %reduce-scatter.5.cloned.1.call-done = f32[768,768]{1,0:T(8,128)} async-done(((f32[3072,768]{1,0:T(8,128)}), f32[768,768]{1,0:T(8,128)}) %reduce-scatter.5.cloned.1.call-update) | async-done | bytes 2359312 | tf_op jit(solution)/shard_map/reduce_scatter | solution.py:138
  541.2 8.3 %fusion.32 = bf16[16,128,768]{2,1,0:T(8,128)(2,1)} fusion(f32[16,128,768]{2,0,1:T(8,128)} %bitcast_reduce_fusion), kind=kLoop, calls=%fused_computation.58 | loop fusion | flops 3145728 | bytes 9437184 | tf_op jit(solution)/shard_map/convert_element_type | solution.py:91
  549.5 27.9 %fusion.53 = f32[768]{0:T(1024)S(1)} fusion(f32[4,16,256,1]{2,1,0,3:T(8,128)S(1)} %bitcast.110, f32[1,16,256,768]{3,2,1,0:T(8,128)} %get-tuple-element.37, f32[1,16,256,768]{3,2,1,0:T(8,128)} %get-tuple-element.36, f32[1,16,256,768]{3,2,1,0:T(8,128)} %get-tuple-element.25, f32[1,16,256,768]{3,2,1,0:T(8,128)} %get-tuple-element.38), kind=kOutput, calls=%fused_computation.82 | convolution fusion | flops 188743680 | bytes 50400256 | tf_op jit(solution)/shard_map/brt,brtd->d/dot_general | solution.py:98
  577.5 1.4 convert_reduce_fusion
  578.8 5.9 all-reduce.14
  584.9 22.0 %all-reduce.12 = (f32[192]{0:T(256)}, f32[192]{0:T(256)}) all-reduce(f32[192]{0:T(256)S(1)} %dynamic-slice.3, f32[192]{0:T(256)S(1)} %dynamic-slice.5), channel_id=1, replica_groups=mesh['rows'=4,'tract'=8] {'tract'}, use_global_device_ids=true, to_apply=%region_11.12 | all-reduce | flops 384 | bytes 3072 | tf_op jit(solution)/shard_map/psum | solution.py:135
  606.9 52.6 %all-reduce.18.cloned.1.call-done = (f32[64,768]{1,0:T(8,128)}, f32[768,768]{1,0:T(8,128)}) async-done(((f32[64,768]{1,0:T(8,128)}, f32[768,768]{1,0:T(8,128)}), (f32[64,768]{1,0:T(8,128)}, f32[768,768]{1,0:T(8,128)})) %all-reduce.18.cloned.1.call-update) | async-done | bytes 2555920 | tf_op jit(solution)/shard_map/psum | solution.py:135
  659.4 1.6 copy.71
  661.0 3.2 copy.72
  (103 shorter events, 4.2 us)
Async XLA Ops:
  7.2 35.5 %copy-start.21 = (u32[32]{0:T(128)S(1)}, u32[32]{0:T(128)}, u32[]{:S(2)}) copy-start(u32[32]{0:T(128)} %constant.38) | copy-start | bytes 388
  7.2 33.7 %copy-start.23 = (f32[192]{0:T(256)S(1)}, f32[192]{0:T(256)}, u32[]{:S(2)}) copy-start(f32[192]{0:T(256)} %param.13) | copy-start | bytes 2308
  7.2 46.2 %copy-start.5 = (bf16[16,128,768]{2,1,0:T(8,128)(2,1)S(1)}, bf16[16,128,768]{2,1,0:T(8,128)(2,1)}, u32[]{:S(2)}) copy-start(bf16[16,128,768]{2,1,0:T(8,128)(2,1)} %param.15) | copy-start | bytes 9437188
  7.2 91.5 %all-gather.2.cloned.1.call-start = ((), (), s32[]{:S(2)}) async-start(), calls=%async_computation.2 | async-start | bytes 5898240 | tf_op jit(solution)/shard_map/all_gather | solution.py:32
  10.2 454.3 %reduce-scatter.3.cloned.1.call-start = ((), (), s32[]{:S(2)}) async-start(), calls=%async_computation.3 | async-start | bytes 983040 | tf_op jit(solution)/shard_map/reduce_scatter | solution.py:137
  11.6 65.9 %collective-permute-start = (s32[16,6]{1,0:T(8,128)}, s32[16,6]{1,0:T(8,128)}, u32[]{:S(2)}, u32[]{:S(2)}) collective-permute-start(s32[16,6]{1,0:T(8,128)} %slice.123), channel_id=1, source_target_pairs={{0,1},{1,2},{2,3},{3,4},{4,5},{5,6},{6,7},{8,9},{9,10},{10,11},{11... | collective-permute-start | bytes 1160 | tf_op jit(solution)/shard_map/ppermute | solution.py:12
  18.5 59.9 %collective-permute-start.2 = (s32[16,6]{1,0:T(8,128)}, s32[16,6]{1,0:T(8,128)S(1)}, u32[]{:S(2)}, u32[]{:S(2)}) collective-permute-start(s32[16,6]{1,0:T(8,128)} %slice.129), channel_id=1, source_target_pairs={{0,1},{1,2},{2,3},{3,4},{4,5},{5,6},{6,7},{8,9},{9,10},{10,11},{11... | collective-permute-start | bytes 1160 | tf_op jit(solution)/shard_map/ppermute | solution.py:12
  22.0 12.6 %copy-start.18 = (bf16[16,256]{1,0:T(8,128)(2,1)}, bf16[16,256]{1,0:T(8,128)(2,1)S(1)}, u32[]{:S(2)}) copy-start(bf16[16,256]{1,0:T(8,128)(2,1)S(1)} %convert_element_type.92) | copy-start | bytes 24580
  34.6 2.7 copy-start.2
  37.4 42.0 %collective-permute-start.1 = (bf16[16,6,768]{2,1,0:T(8,128)(2,1)S(1)}, bf16[16,6,768]{2,1,0:T(8,128)(2,1)S(1)}, u32[]{:S(2)}, u32[]{:S(2)}) collective-permute-start(bf16[16,6,768]{2,1,0:T(8,128)(2,1)S(1)} %slice.163), channel_id=1, source_target_pairs={{0,1},{1,2},{2,3},{3,4},{4,5},{5,6},{6,7},{8,9},{9,10},{10,11},{11... | collective-permute-start | bytes 442376 | tf_op jit(solution)/shard_map/ppermute | solution.py:12
  44.7 0.6 copy-start.20
  61.7 15.8 %copy-start.12 = (s32[16,256]{1,0:T(8,128)S(1)}, s32[16,256]{1,0:T(8,128)}, u32[]{:S(2)}) copy-start(s32[16,256]{1,0:T(8,128)} %param.10) | copy-start | bytes 49156
  61.7 16.6 %copy-start.13 = (s32[16,256]{1,0:T(8,128)S(1)}, s32[16,256]{1,0:T(8,128)}, u32[]{:S(2)}) copy-start(s32[16,256]{1,0:T(8,128)} %param.9) | copy-start | bytes 49156
  98.7 10.7 %copy-start.4 = (bf16[16,259,768]{2,1,0:T(8,128)(2,1)S(1)}, bf16[16,259,768]{2,1,0:T(8,128)(2,1)}, u32[]{:S(2)}) copy-start(bf16[16,259,768]{2,1,0:T(8,128)(2,1)} %get-tuple-element.40) | copy-start | bytes 19095556
  98.7 10.7 %copy-start.9 = (bf16[3072,768]{1,0:T(8,128)(2,1)S(1)}, bf16[3072,768]{1,0:T(8,128)(2,1)}, u32[]{:S(2)}) copy-start(bf16[3072,768]{1,0:T(8,128)(2,1)} %all-gather.2.cloned.1.call-done) | copy-start | bytes 14155780
  109.3 8.4 %copy-start.3 = (bf16[16,259,768]{2,1,0:T(8,128)(2,1)S(1)}, bf16[16,259,768]{2,1,0:T(8,128)(2,1)}, u32[]{:S(2)}) copy-start(bf16[16,259,768]{2,1,0:T(8,128)(2,1)} %get-tuple-element.41) | copy-start | bytes 19095556
  147.9 23.7 %slice-start = ((s8[12976128]{0:T(1024)(128)(4,1)}), s8[4194304]{0:T(1024)(128)(4,1)S(1)}, s32[]{:S(2)}) async-start(s8[12976128]{0:T(1024)(128)(4,1)} %bitcast.102), calls=%async_computation.6 | async-start | bytes 8388608
  147.9 23.7 %slice-start.1 = ((s8[12976128]{0:T(1024)(128)(4,1)}), s8[4194304]{0:T(1024)(128)(4,1)S(1)}, s32[]{:S(2)}) async-start(s8[12976128]{0:T(1024)(128)(4,1)} %bitcast.102), calls=%async_computation.7 | async-start | bytes 8388608
  147.9 23.7 %slice-start.2 = ((s8[12976128]{0:T(1024)(128)(4,1)}), s8[4194304]{0:T(1024)(128)(4,1)S(1)}, s32[]{:S(2)}) async-start(s8[12976128]{0:T(1024)(128)(4,1)} %bitcast.102), calls=%async_computation.8 | async-start | bytes 8388608
  147.9 23.7 %slice-start.3 = ((s8[12976128]{0:T(1024)(128)(4,1)}), s8[393216]{0:T(1024)(128)(4,1)S(1)}, s32[]{:S(2)}) async-start(s8[12976128]{0:T(1024)(128)(4,1)} %bitcast.102), calls=%async_computation.9 | async-start | bytes 786432
  212.6 25.9 %copy-start.14 = (f32[768]{0:T(1024)S(1)}, f32[768]{0:T(1024)}, u32[]{:S(2)}) copy-start(f32[768]{0:T(1024)} %convert_element_type.102) | copy-start | bytes 9220
  237.9 0.6 copy-start.10
  315.3 6.5 collective-permute-start.3
  316.8 15.8 %slice-start.6 = ((s8[6488064]{0:T(1024)(128)(4,1)}), s8[2293760]{0:T(1024)(128)(4,1)S(1)}, s32[]{:S(2)}) async-start(s8[6488064]{0:T(1024)(128)(4,1)} %bitcast.106), calls=%async_computation.12 | async-start | bytes 4587520
  319.7 46.7 %copy-start.1 = (bf16[16,253,768]{2,1,0:T(8,128)(2,1)}, bf16[16,253,768]{2,1,0:T(8,128)(2,1)S(1)}, u32[]{:S(2)}) copy-start(bf16[16,253,768]{2,1,0:T(8,128)(2,1)S(1)} %slice.197) | copy-start | bytes 18653188
  322.9 9.7 %slice-start.7 = ((s8[6488064]{0:T(1024)(128)(4,1)}), s8[4194304]{0:T(1024)(128)(4,1)S(1)}, s32[]{:S(2)}) async-start(s8[6488064]{0:T(1024)(128)(4,1)} %bitcast.106), calls=%async_computation.13 | async-start | bytes 8388608
  322.9 16.9 %slice-start.8 = ((s8[4718592]{0:T(1024)(128)(4,1)}), s8[4194304]{0:T(1024)(128)(4,1)S(1)}, s32[]{:S(2)}) async-start(s8[4718592]{0:T(1024)(128)(4,1)} %bitcast.108), calls=%async_computation.14 | async-start | bytes 8388608
  332.6 7.2 %slice-start.9 = ((s8[4718592]{0:T(1024)(128)(4,1)}), s8[524288]{0:T(1024)(128)(4,1)S(1)}, s32[]{:S(2)}) async-start(s8[4718592]{0:T(1024)(128)(4,1)} %bitcast.108), calls=%async_computation.15 | async-start | bytes 1048576
  339.8 10.5 %copy-start.17 = (f32[16,256]{1,0:T(8,128)S(1)}, f32[16,256]{1,0:T(8,128)}, u32[]{:S(2)}) copy-start(f32[16,256]{1,0:T(8,128)} %get-tuple-element.44) | copy-start | bytes 49156
  350.3 8.1 %copy-start.16 = (f32[16,256]{1,0:T(8,128)S(1)}, f32[16,256]{1,0:T(8,128)}, u32[]{:S(2)}) copy-start(f32[16,256]{1,0:T(8,128)} %get-tuple-element.46) | copy-start | bytes 49156
  358.3 8.0 %copy-start.15 = (f32[16,256]{1,0:T(8,128)S(1)}, f32[16,256]{1,0:T(8,128)}, u32[]{:S(2)}) copy-start(f32[16,256]{1,0:T(8,128)} %get-tuple-element.23) | copy-start | bytes 49156
  392.3 4.7 copy-start
  397.6 23.2 %collective-permute-start.4 = (bf16[16,3,768]{2,1,0:T(4,128)(2,1)}, bf16[16,3,768]{2,1,0:T(4,128)(2,1)S(1)}, u32[]{:S(2)}, u32[]{:S(2)}) collective-permute-start(bf16[16,3,768]{2,1,0:T(4,128)(2,1)} %slice.388), channel_id=1, source_target_pairs={{1,0},{2,1},{3,2},{4,3},{5,4},{6,5},{7,6},{9,8},{10,9},{11,10},{12... | collective-permute-start | bytes 221192 | tf_op jit(solution)/shard_map/ppermute | solution.py:12
  410.1 11.8 %copy-start.19 = (bf16[16,256]{1,0:T(8,128)(2,1)S(1)}, bf16[16,256]{1,0:T(8,128)(2,1)}, u32[]{:S(2)}) copy-start(bf16[16,256]{1,0:T(8,128)(2,1)} %copy-done.18) | copy-start | bytes 24580
  410.1 11.8 %copy-start.22 = (s32[16,256]{1,0:T(8,128)S(1)}, s32[16,256]{1,0:T(8,128)}, u32[]{:S(2)}) copy-start(s32[16,256]{1,0:T(8,128)} %param.8) | copy-start | bytes 49156
  434.4 9.3 %copy-start.6 = (f32[768,768]{1,0:T(8,128)S(1)}, f32[768,768]{1,0:T(8,128)}, u32[]{:S(2)}) copy-start(f32[768,768]{1,0:T(8,128)} %fusion.39) | copy-start | bytes 7077892
  434.4 106.7 %reduce-scatter.5.cloned.1.call-start = ((), (), s32[]{:S(2)}) async-start(), calls=%async_computation.4 | async-start | bytes 11796480 | tf_op jit(solution)/shard_map/reduce_scatter | solution.py:138
  434.5 9.3 %copy-start.7 = (f32[768,768]{1,0:T(8,128)S(1)}, f32[768,768]{1,0:T(8,128)}, u32[]{:S(2)}) copy-start(f32[768,768]{1,0:T(8,128)} %fusion.42) | copy-start | bytes 7077892
  434.5 9.3 %copy-start.8 = (f32[768,768]{1,0:T(8,128)S(1)}, f32[768,768]{1,0:T(8,128)}, u32[]{:S(2)}) copy-start(f32[768,768]{1,0:T(8,128)} %fusion.45) | copy-start | bytes 7077892
  447.8 211.6 %all-reduce.18.cloned.1.call-start = ((), (), s32[]{:S(2)}) async-start(), calls=%async_computation.5 | async-start | bytes 5111808 | tf_op jit(solution)/shard_map/psum | solution.py:135
  448.7 100.8 %copy-start.11 = (f32[4,16,256]{2,1,0:T(8,128)S(1)}, f32[4,16,256]{2,1,0:T(8,128)}, u32[]{:S(2)}) copy-start(f32[4,16,256]{2,1,0:T(8,128)} %copy-done.10) | copy-start | bytes 196612
  541.2 36.3 %slice-start.4 = ((s8[6291456]{0:T(1024)(128)(4,1)}), s8[4194304]{0:T(1024)(128)(4,1)S(1)}, s32[]{:S(2)}) async-start(s8[6291456]{0:T(1024)(128)(4,1)} %bitcast.104), calls=%async_computation.10 | async-start | bytes 8388608
  549.5 28.0 %slice-start.5 = ((s8[6291456]{0:T(1024)(128)(4,1)}), s8[2097152]{0:T(1024)(128)(4,1)S(1)}, s32[]{:S(2)}) async-start(s8[6291456]{0:T(1024)(128)(4,1)} %bitcast.104), calls=%async_computation.11 | async-start | bytes 4194304
Sparse Core Ops, SparseCore 0:
  10.3 42.3 all-gather.1
  434.5 25.3 reduce-scatter.2
  462.7 78.4 reduce-scatter.4
  545.2 114.1 all-reduce.17
where the time goes:
time: 676 us; the launch traced here: 671 us
  other arithmetic  219 us (32%)
  matrix products  191 us (28%)
  waiting for transfers between devices  131 us (19%)
  local copies, waits for them, and re-layouts  55.2 us (8%)
  blocking collectives  44.2 us (7%)
  between operations  15.9 us (2%)
  starting transfers between devices  14.9 us (2%)
    reduce_scatter x1, waiting for transfers between devices, body(): lax.psum_scatter(summed[1], 'rows', scatter_dimension=0, tiled=True)  76.6 us
    psum x1, waiting for transfers between devices, body(): lax.psum((grad_terms[0], grad_terms[1], grad_terms[2], grad_terms[3]), 't...  52.6 us
    dot_general x4, matrix products, body(): jnp.einsum('rtd,de->rte', masked_list[offset], weight_blocks[offset], pre...  49.2 us
    another operation x2, other arithmetic, body(): stacked = jnp.stack(pooled, 0)  37.8 us
    dot_general x4, matrix products, body(): jnp.einsum('rtd,rte->de', masked_list[offset][:, 3:], conv_low, preferred...  37.3 us
    dot_general x4, matrix products, body(): jnp.einsum('rte,de->rtd', conv_low, weight_blocks[offset], preferred_elem...  34.6 us
    mul x2, other arithmetic, body(): keep_list[offset][..., None] * carried  33 us
    dot_general x1, matrix products, body(): jnp.einsum('brt,brtd->d', score_rows, stacked, precision=PRECISE)  27.9 us
  transfers between devices with their start and end apart: 9, of which 3 were waited for; matrix products, arithmetic and copies ran while one was open for 22% of the time, Pallas kernels for 0%

commit v1 on v0

v1 whole, which is shorter than its diff:
```python
import functools

import jax
import jax.numpy as jnp
from jax import lax
from jax.experimental import pallas as pl
from jax.experimental.pallas import tpu as pltpu
from jax.sharding import PartitionSpec as P

F32 = jnp.float32
BF16 = jnp.bfloat16
OFFSETS = 4
REACH = 5
SPAN = 8
EXTRA = 16
VMEM_LIMIT = 56 * 1024 * 1024
NT = (((1,), (1,)), ((), ()))
TN = (((0,), (0,)), ((), ()))
NN = (((1,), (0,)), ((), ()))


def dot(a, b, dims=NN, precision=None):
    return lax.dot_general(a, b, dims, precision=precision, preferred_element_type=F32)


def exact(a, b, dims=NN):
    return dot(a, b, dims, lax.Precision.HIGHEST)


def call(kernel, outs, *operands, scratch=(), scalars=1, flops=0, name=None):
    smem = pl.BlockSpec(memory_space=pltpu.SMEM)
    vmem = pl.BlockSpec(memory_space=pltpu.VMEM)
    moved = sum(a.size * a.dtype.itemsize for a in operands)
    result = pl.pallas_call(
        kernel,
        out_shape=[jax.ShapeDtypeStruct(s, t) for s, t in outs],
        in_specs=[smem] * scalars + [vmem] * (len(operands) - scalars),
        out_specs=[vmem] * len(outs),
        scratch_shapes=list(scratch),
        compiler_params=pltpu.CompilerParams(vmem_limit_bytes=VMEM_LIMIT),
        cost_estimate=pl.CostEstimate(flops=flops, bytes_accessed=moved, transcendentals=0),
        name=name,
    )(*operands)
    return result


def swap(value, axis, bit):
    count = lax.axis_size(axis)
    return lax.ppermute(value, axis, [(i, i ^ bit) for i in range(count)])


def gather_slots(value, axis, bits):
    slots = {0: value}
    for bit in bits:
        for m in list(slots):
            slots[m | bit] = swap(slots[m], axis, bit)
    return slots


def payload_kernel(where, table, score, bias, out):
    rows, width = table.shape
    shard = score.shape[1]
    out[:rows] = table[...].astype(BF16)
    source = lax.broadcasted_iota(jnp.int32, (shard, width), 0) + where[0] * shard
    column = lax.broadcasted_iota(jnp.int32, (shard, width), 1)
    place = (source == column).astype(BF16)
    both = jnp.concatenate(
        [jnp.broadcast_to(score[...], (8, shard)), jnp.broadcast_to(bias[...], (8, shard))], 0
    ).astype(BF16)
    out[rows:] = dot(both, place).astype(BF16)


def table_kernel(order, where, *refs):
    count = len(order)
    slots, (weight,) = refs[:count], refs[count : count + 1]
    product, scores, weight_low, table_low, vectors = refs[count + 1 :]
    rows = slots[0].shape[0] - EXTRA
    total = jnp.zeros((EXTRA, slots[0].shape[1]), F32)
    for slot, m in zip(slots, order):
        at = pl.multiple_of((where[0] ^ m) * rows, rows)
        table_low[pl.ds(at, rows), :] = slot[:rows]
        total = total + slot[rows:].astype(F32)
    vectors[...] = total.astype(BF16)
    weight_low[...] = weight[...].astype(BF16)
    full = dot(table_low[...], weight_low[...])
    product[...] = full.astype(BF16)
    scores[...] = exact(total[:8], full, NT)


def planes_kernel(where, ids, before, out):
    length = ids.shape[1]
    half = length // 2
    for m in range(SPAN):
        target = 2 * lax.broadcasted_iota(jnp.int32, (length, half), 1) + 1 - m
        source = lax.broadcasted_iota(jnp.int32, (length, half), 0)
        got = dot(ids[...], (source == target).astype(BF16))
        if m > 1:
            tail = before.shape[1]
            target = 2 * lax.broadcasted_iota(jnp.int32, (tail, half), 1) + 1 - m + tail
            source = lax.broadcasted_iota(jnp.int32, (tail, half), 0)
            got = got + dot(before[...], (source == target).astype(BF16))
        out[:, m * half : (m + 1) * half] = got


class Window:
    def __init__(self, planes, rows):
        half = planes.shape[1] // SPAN

        def part(which, m):
            return planes[which * rows : (which + 1) * rows, m * half : (m + 1) * half]

        self.bytes = [part(0, m) for m in range(SPAN)]
        self.segments = [part(1, m) for m in range(SPAN)]
        self.valid = [part(2, m) for m in range(SPAN)]
        self.mask = {
            (k, j): (self.segments[j + k] == self.segments[j]).astype(F32) * self.valid[j + k]
            for k in range(OFFSETS)
            for j in range(REACH)
        }
        self.keep, self.divide = [], []
        for side in range(2):
            keep = [self.mask[k, side] for k in range(OFFSETS)]
            counts, total = [], 0.0
            for k in range(OFFSETS):
                total = total + keep[k]
                counts.append(1.0 / jnp.maximum(total, 1.0))
            self.keep.append(keep)
            self.divide.append(counts)

    def pooled(self, side, values):
        means, total = [], 0.0
        for k in range(OFFSETS):
            total = total + self.keep[side][k] * values[side + k]
            means.append(total * self.divide[side][k])
        return means

    def spread(self, sides):
        result = [0.0] * REACH
        for side in range(2):
            carried = 0.0
            for k in reversed(range(OFFSETS)):
                carried = carried + sides[side][k] * self.divide[side][k]
                result[side + k] = result[side + k] + self.keep[side][k] * carried
        return result


def lookup(row, codes):
    index = codes.astype(jnp.int32)
    lanes = 128
    low = jnp.bitwise_and(index, lanes - 1)
    parts = [
        jnp.take_along_axis(
            jnp.broadcast_to(row[:, at : at + lanes], codes.shape), low, axis=1
        )
        for at in range(0, row.shape[1], lanes)
    ]
    return jnp.where(index >= lanes, parts[1], parts[0])


def packed_row(ref, plane, row):
    return jnp.broadcast_to(ref[plane, pl.ds(row, 1), :], (16, ref.shape[2])).astype(BF16)


def spread_rows(codes_ref, weights_ref, k, row, values):
    lanes = codes_ref.shape[2]
    blocks = values // 16
    name = (
        lax.broadcasted_iota(jnp.int32, (blocks, 16, lanes), 0) * 16
        + lax.broadcasted_iota(jnp.int32, (blocks, 16, lanes), 1)
    ).astype(F32).astype(BF16)
    total = jnp.zeros((blocks, 16, lanes), BF16)
    for j in range(REACH):
        code = packed_row(codes_ref, k + j, row)
        weight = packed_row(weights_ref, k * REACH + j, row)
        total = jnp.where(name == code[None], total + weight[None], total)
    return total.reshape(values, lanes)


def accumulate(codes_ref, weights_ref, total_ref, ks, cot, values, extra=None):
    rows, half = codes_ref.shape[1:]
    for chunk in range(rows // 2):
        pieces = [
            jnp.concatenate(
                [
                    spread_rows(codes_ref, weights_ref, k, 2 * chunk, values),
                    spread_rows(codes_ref, weights_ref, k, 2 * chunk + 1, values),
                ],
                1,
            )
            for k in ks
        ]
        if extra is not None:
            pieces.append(extra(chunk))
        left = jnp.concatenate(pieces, 0)
        part = dot(left, cot[2 * chunk * half : 2 * (chunk + 1) * half, :])
        if chunk == 0:
            total_ref[...] = part
        else:
            total_ref[...] += part


def split(value):
    high = value.astype(BF16)
    return high, (value - high.astype(F32)).astype(BF16)


def far_kernel(order, slots, values, group, *refs):
    scores = refs[: len(order)]
    planes, vectors, cot = refs[len(order) : len(order) + 3]
    out, codes, weights, probs, masks, averages = refs[len(order) + 3 : len(order) + 9]
    table, total = refs[len(order) + 9 :]
    rows = codes.shape[1]
    for score, m in zip(scores, order):
        table[group[0] ^ m] = score[...]
    window = Window(planes[...], rows)
    shared = jnp.sum(vectors[:8].astype(F32) * vectors[8:].astype(F32), 1, keepdims=True)[:1]
    conv_scores = [shared] * REACH
    for k in range(OFFSETS):
        row = table[k, :1, :]
        for m in range(k, k + REACH):
            found = lookup(row, window.bytes[m])
            conv_scores[m - k] = conv_scores[m - k] + window.mask[k, m - k] * found
    for m in range(SPAN):
        codes[m] = window.bytes[m]
    shares = []
    for side in range(2):
        block = window.pooled(side, conv_scores)
        top = functools.reduce(jnp.maximum, block)
        exps = [jnp.exp(b - top) for b in block]
        inverse = 1.0 / functools.reduce(jnp.add, exps)
        shares.append([e * inverse for e in exps])
        for k in range(OFFSETS):
            probs[side * OFFSETS + k] = shares[side][k]
    mixing = [0.5 * e for e in window.spread(shares)]
    averages[...] = functools.reduce(jnp.add, mixing)
    for k in range(OFFSETS):
        for j in range(REACH):
            masks[k * REACH + j] = window.mask[k, j]
            weights[k * REACH + j] = window.mask[k, j] * mixing[j]
    accumulate(codes, weights, total, [group[0] ^ m for m in slots], cot, values)
    for at in range(len(slots)):
        out[at] = total[at * values : (at + 1) * values].astype(BF16)


def near_kernel(slots, values, group, codes, weights, averages, cot, out, bias_out, total):
    half = codes.shape[2]

    def extra(chunk):
        line = jnp.concatenate(
            [averages[2 * chunk : 2 * chunk + 1, :], averages[2 * chunk + 1 : 2 * chunk + 2, :]], 1
        )
        line = jnp.broadcast_to(line, (EXTRA, 2 * half))
        high, low = split(line)
        at = lax.broadcasted_iota(jnp.int32, line.shape, 0)
        return jnp.where(at == 0, high.astype(F32), jnp.where(at == 1, low.astype(F32), 0.0)).astype(BF16)

    accumulate(codes, weights, total, [group[0] ^ m for m in slots], cot, values, extra)
    for at in range(len(slots)):
        out[at] = total[at * values : (at + 1) * values].astype(BF16)
    end = total[len(slots) * values :]
    bias_out[...] = jnp.broadcast_to(end[:1] + end[1:2], (8, end.shape[1]))


def score_kernel(order, values, group, *refs):
    products = refs[: len(order)]
    planes, vectors, probs, masks, codes, bias_part, cot = refs[len(order) : len(order) + 7]
    out, inner_ref, grads_ref, rows_ref = refs[len(order) + 7 :]
    rows, half = codes.shape[1:]
    biases = vectors[8:]
    blocks = values // 8
    name = (
        lax.broadcasted_iota(jnp.int32, (blocks, 8, half), 0) * 8
        + lax.broadcasted_iota(jnp.int32, (blocks, 8, half), 1)
    ).astype(F32)
    for chunk in range(rows // 2):
        here = cot[2 * chunk * half : 2 * (chunk + 1) * half, :]
        base = dot(biases, here, NT)
        found = {}
        for slot, m in zip(products, order):
            k = group[0] ^ m
            each = dot(slot[...], here, NT)
            for side in range(2):
                row = 2 * chunk + side
                mine = each[:, side * half : (side + 1) * half].reshape(blocks, 8, half)
                for j in range(REACH):
                    code = jnp.broadcast_to(codes[k + j, row : row + 1, :], (8, half))
                    picked = jnp.sum(jnp.where(name == code[None], mine, 0.0), 0)
                    mask = masks[k * REACH + j, row : row + 1, :]
                    found[j, side] = found.get((j, side), 0.0) + picked * mask
        for side in range(2):
            row = 2 * chunk + side
            for j in range(REACH):
                inner_ref[j, row : row + 1, :] = (
                    jnp.sum(found[j, side], 0, keepdims=True)
                    + base[:1, side * half : (side + 1) * half]
                )
    window = Window(planes[...], rows)
    inner_rows = [0.5 * inner_ref[j] for j in range(REACH)]
    sides = []
    for side in range(2):
        inner = window.pooled(side, inner_rows)
        share = [probs[side * OFFSETS + k] for k in range(OFFSETS)]
        mean = functools.reduce(jnp.add, [s * i for s, i in zip(share, inner)])
        sides.append([s * (i - mean) for s, i in zip(share, inner)])
    grads = window.spread(sides)
    overall = jnp.sum(jnp.sum(functools.reduce(jnp.add, grads), 1, keepdims=True), 0, keepdims=True)
    for k in range(OFFSETS):
        for j in range(REACH):
            grads_ref[k * REACH + j] = grads[j] * window.mask[k, j]
    ones = jnp.ones((8, half), F32)
    out[...] = jnp.zeros(out.shape, F32)
    for k in range(OFFSETS):
        total = jnp.zeros((blocks, 8, half), F32)
        for row in range(rows):
            for j in range(REACH):
                code = jnp.broadcast_to(codes[k + j, row : row + 1, :], (8, half))
                grad = jnp.broadcast_to(grads_ref[k * REACH + j, row : row + 1, :], (8, half))
                total = jnp.where(name == code[None], total + grad[None], total)
        line = exact(ones, total.reshape(values, half), NT)
        rows_ref[k] = line
        out[k : k + 1, :values] = line[:1]
    at = lax.broadcasted_iota(jnp.int32, (EXTRA, values), 0)
    score_grad = jnp.zeros((1, biases.shape[1]), F32)
    for slot, m in zip(products, order):
        line = jnp.broadcast_to(rows_ref[group[0] ^ m][:1], (EXTRA, values))
        high, low = split(line)
        both = jnp.where(at == 0, high.astype(F32), jnp.where(at == 1, low.astype(F32), 0.0))
        got = dot(both.astype(BF16), slot[...])
        score_grad = score_grad + got[:1] + got[1:2]
    score_grad = score_grad + overall * biases[:1].astype(F32)
    width = biases.shape[1]
    out[4:5, :width] = score_grad
    out[5:6, :width] = bias_part[:1] + overall * vectors[:1].astype(F32)


def output_kernel(order, values, group, *refs):
    products = refs[: len(order)]
    codes, weights, averages, vectors, out = refs[len(order) :]
    rows, half = codes.shape[1:]
    biases = vectors[8:].astype(F32)
    at = lax.broadcasted_iota(jnp.int32, (8, 2 * half), 0)
    first = lax.broadcasted_iota(jnp.int32, biases.shape, 0)
    biases = jnp.where(first < 2, biases, 0.0)
    for chunk in range(rows // 2):
        line = jnp.concatenate(
            [averages[2 * chunk : 2 * chunk + 1, :], averages[2 * chunk + 1 : 2 * chunk + 2, :]], 1
        )
        line = jnp.broadcast_to(line, (8, 2 * half))
        high, low = split(line)
        both = jnp.where(at == 0, high.astype(F32), jnp.where(at == 1, low.astype(F32), 0.0))
        total = dot(both, biases, TN)
        for slot, m in zip(products, order):
            k = group[0] ^ m
            left = jnp.concatenate(
                [
                    spread_rows(codes, weights, k, 2 * chunk, values),
                    spread_rows(codes, weights, k, 2 * chunk + 1, values),
                ],
                1,
            )
            total = total + dot(left, slot[...], TN)
        out[2 * chunk * half : 2 * (chunk + 1) * half, :] = total.astype(BF16)


def merge_kernel(bits, where, group, near, near_other, far_other, *refs):
    sums = refs[:-3]
    vectors, out, line = refs[-3:]
    values = near.shape[0]
    width = vectors.shape[1]
    line[...] = functools.reduce(jnp.add, [s[...] for s in sums])
    high, low = split(jnp.broadcast_to(line[pl.ds(group[0], 1), :values], (EXTRA, values)))
    at = lax.broadcasted_iota(jnp.int32, (EXTRA, values), 0)
    both = jnp.where(at == 0, high.astype(F32), jnp.where(at == 1, low.astype(F32), 0.0))
    scores = jnp.concatenate([vectors[:8], vectors[:8]], 0)
    total = dot(both.astype(BF16), scores, TN)
    total = total + near[...].astype(F32) + near_other[...].astype(F32) + far_other[...].astype(F32)
    total = total.astype(BF16)
    out[values:] = pack(jnp.concatenate([line[4:6, :width]] * 4, 0))
    size = values >> bits
    for actual in range(1 << bits):
        at = pl.multiple_of(reversed_bits(where[0] ^ actual, bits) * size, size)
        out[pl.ds(at, size), :] = total[actual * size : (actual + 1) * size]


def reversed_bits(number, bits):
    return sum((((number >> b) & 1) << (bits - 1 - b)) for b in range(bits))


def pack(rows):
    high, low = split(rows)
    return jnp.concatenate([high.astype(F32), low.astype(F32)], 0).astype(BF16)


def unpack(block):
    return block[:8].astype(F32) + block[8:].astype(F32)


def halve_kernel(where, mine, other, out):
    del where
    keep = out.shape[0] - EXTRA
    out[:keep] = (mine[:keep].astype(F32) + other[:keep].astype(F32)).astype(BF16)
    out[keep:] = pack(unpack(mine[mine.shape[0] - EXTRA :]) + unpack(other[keep:]))


def share_kernel(bits, where, group, block, weight_low, out, table_part):
    size = out.shape[0] >> bits
    for m in range(1 << bits):
        at = pl.multiple_of((where[0] ^ m) * size, size)
        place = reversed_bits(m, bits) * size
        out[pl.ds(at, size), :] = block[place : place + size]
    product = dot(out[...], weight_low[...], NT).astype(BF16)
    size = table_part.shape[0] // OFFSETS
    for actual in range(OFFSETS):
        at = pl.multiple_of((group[0] ^ actual) * size, size)
        table_part[pl.ds(at, size), :] = product[actual * size : (actual + 1) * size]


def weight_kernel(where, table_low, block, out):
    del where
    out[...] = dot(table_low[...], block[...], TN)


def bits_of(count):
    return [1 << at for at in reversed(range(count.bit_length() - 1))]


def body(byte_values, segment_ids, valid, table, conv_weight, conv_bias, score_weight, cotangent):
    rows_count, tract_count = lax.axis_size("rows"), lax.axis_size("tract")
    rows_at, tract_at = lax.axis_index("rows"), lax.axis_index("tract")
    values, width = table.shape[0] * rows_count, table.shape[1]
    rows, length = byte_values.shape
    half = length // 2
    copies = rows_count // OFFSETS
    me = rows_at[None].astype(jnp.int32)
    group = (rows_at // copies)[None].astype(jnp.int32)
    order = [0, 2, 1, 3]

    payload = call(
        payload_kernel, [((table.shape[0] + EXTRA, width), BF16)], me, table, score_weight[None], conv_bias[None],
        name="payload",
    )[0]
    slots = gather_slots(payload, "rows", bits_of(rows_count))
    ids = jnp.concatenate([byte_values, segment_ids, valid], 0)
    steps = [(i, i + 1) for i in range(tract_count - 1)]
    before = lax.ppermute(ids[:, half:], "tract", steps)
    planes = call(
        planes_kernel, [((3 * rows, SPAN * half), F32)], me, ids.astype(BF16), before.astype(BF16), name="planes"
    )[0]
    weight = conv_weight
    if copies > 1:
        near_by = [[g * copies + c for c in range(copies)] for g in range(OFFSETS)]
        weight = lax.all_gather(conv_weight.astype(BF16), "rows", axis=0, tiled=True, axis_index_groups=near_by)
    product, score_part, weight_low, table_low, vectors = call(
        functools.partial(table_kernel, list(slots)),
        [((values, width), BF16), ((8, values), F32), ((width, width), BF16), ((values, width), BF16), ((EXTRA, width), BF16)],
        me, *slots.values(), weight, name="products",
    )
    group_bits = [2 * copies, copies]
    score_slots = gather_slots(score_part, "rows", group_bits)
    score_slots = [score_slots[m * copies] for m in order]
    product_slots = gather_slots(product, "rows", group_bits)
    product_slots = [product_slots[m * copies] for m in order]

    cot = cotangent.reshape(rows * half, width)
    pair = [2, 3]
    far, codes, weights, probs, masks, averages = call(
        functools.partial(far_kernel, order, pair, values),
        [((2, values, width), BF16), ((SPAN, rows, half), F32), ((OFFSETS * REACH, rows, half), F32),
         ((2 * OFFSETS, rows, half), F32), ((OFFSETS * REACH, rows, half), F32), ((rows, half), F32)],
        group, *score_slots, planes, vectors, cot,
        scratch=[pltpu.VMEM((OFFSETS, 8, values), F32), pltpu.VMEM((2 * values, width), F32)],
        flops=2 * 2 * values * width * rows * half, name="far",
    )
    far_here = far[0] + swap(far[1], "rows", copies)
    far_other = swap(far_here, "rows", 2 * copies)
    near, bias_part = call(
        functools.partial(near_kernel, [0, 1], values),
        [((2, values, width), BF16), ((8, width), F32)],
        group, codes, weights, averages, cot,
        scratch=[pltpu.VMEM((2 * values + EXTRA, width), F32)],
        flops=2 * 2 * values * width * rows * half, name="near",
    )
    near_other = swap(near[1], "rows", copies)
    sums = call(
        functools.partial(score_kernel, order, values), [((8, 1024), F32)],
        group, *product_slots, planes, vectors, probs, masks, codes, bias_part, cot,
        scratch=[pltpu.VMEM((REACH, rows, half), F32), pltpu.VMEM((OFFSETS * REACH, rows, half), F32),
                 pltpu.VMEM((OFFSETS, 8, values), F32)],
        flops=4 * 2 * values * width * rows * half, name="scores",
    )[0]
    all_sums = list(gather_slots(sums, "rows", group_bits).values())

    exchanges = [("tract", 1 << at) for at in range(tract_count.bit_length() - 1)]
    exchanges += [("rows", 1 << at) for at in range(copies.bit_length() - 1)]
    halved = [e for at, e in enumerate(exchanges) if values >> (at + 1) >= 16]
    piece = jnp.zeros((1,), jnp.int32)
    for at, (axis, bit) in enumerate(halved):
        mine = tract_at if axis == "tract" else rows_at
        piece = piece + ((mine & bit) != 0).astype(jnp.int32) * (1 << at)
    block = call(
        functools.partial(merge_kernel, len(halved)), [((values + EXTRA, width), BF16)],
        piece, group, near[0], near_other, far_other, *all_sums, vectors,
        scratch=[pltpu.VMEM((8, 1024), F32)], scalars=2, name="merge",
    )[0]
    for axis, bit in halved:
        keep = (block.shape[0] - EXTRA) // 2
        other = swap(block[keep:], axis, bit)
        block = call(halve_kernel, [((keep + EXTRA, width), BF16)], me, block, other, name="halve")[0]
    for axis, bit in exchanges[len(halved) :]:
        other = swap(block, axis, bit)
        block = call(halve_kernel, [(block.shape, BF16)], me, block, other, name="whole")[0]
    ends = block[-EXTRA:].astype(F32)
    ends = ends[:2] + ends[8:10]
    block = block[:-EXTRA]
    for axis, bit in reversed(halved):
        block = jnp.concatenate([block, swap(block, axis, bit)], 0)

    full, table_part = call(
        functools.partial(share_kernel, len(halved)),
        [((values, width), BF16), ((values, width), BF16)], piece, group, block, weight_low,
        scalars=2, name="share",
    )
    for bit in group_bits:
        keep = table_part.shape[0] // 2
        other = swap(table_part[keep:].astype(BF16), "rows", bit)
        table_part = table_part[:keep].astype(F32) + other.astype(F32)
    out = call(
        functools.partial(output_kernel, order, values), [((rows * half, width), BF16)],
        group, *product_slots, codes, weights, averages, vectors,
        flops=4 * 2 * values * width * rows * half, name="output",
    )[0]
    if copies > 1:
        inside = rows_at % copies
        columns = lax.dynamic_slice_in_dim(table_low, inside * (width // copies), width // copies, 1)
        table_part = lax.dynamic_slice_in_dim(table_part, inside * table.shape[0], table.shape[0], 0)
    else:
        columns = table_low
    weight_grad = call(
        weight_kernel, [((conv_weight.shape[0], width), F32)], me, columns, full, name="weights",
    )[0]
    shard = conv_bias.shape[0]
    ends = lax.dynamic_slice_in_dim(ends, rows_at * shard, shard, 1)
    return out.reshape(cotangent.shape), table_part, weight_grad, ends[1], ends[0]


def solution(mesh):
    return jax.shard_map(
        body,
        mesh=mesh,
        in_specs=(
            P("rows", "tract"), P("rows", "tract"), P("rows", "tract"), P("rows", None),
            P("rows", None), P("rows"), P("rows"), P("rows", "tract", None),
        ),
        out_specs=(P("rows", "tract", None), P("rows", None), P("rows", None), P("rows"), P("rows")),
        check_vma=False,
    )
```

time: 676 us -> 132 us (0.20)
  other arithmetic: 219 us -> 4.55 us
  matrix products: 191 us -> 0 us
  waiting for transfers between devices: 131 us -> 31.1 us
  Pallas kernels: 0 us -> 52.9 us
  blocking collectives: 44.2 us -> 0 us
  local copies, waits for them, and re-layouts: 55.2 us -> 15.5 us
  between operations: 15.9 us -> 0.87 us
  starting transfers between devices: 14.9 us -> 26.5 us
    dot_general x16 -> x0, matrix products: 191 us -> none  [the longest x4 49.2 us: body(): jnp.einsum('rtd,de->rte', masked_list[offset], weight_blocks[offset], pre...]
    reduce_scatter x2 -> x0, waiting for transfers between devices: 76.6 us -> none  [the longest x1 76.6 us: body(): lax.psum_scatter(summed[1], 'rows', scatter_dimension=0, tiled=True)]
    another operation x4 -> x0, other arithmetic: 61.4 us -> none  [the longest x2 37.8 us: body(): stacked = jnp.stack(pooled, 0)]
    pallas_call x0 -> x13, Pallas kernels: none -> 52.9 us  [call(): pl.pallas_call(kernel, out_shape=[jax.ShapeDtypeStruct(s, t) for s, t in...]
    mul x5 -> x0, other arithmetic: 52.9 us -> none  [the longest x2 33 us: body(): keep_list[offset][..., None] * carried]
    psum x1 -> x0, waiting for transfers between devices: 52.6 us -> none  [body(): lax.psum((grad_terms[0], grad_terms[1], grad_terms[2], grad_terms[3]), 't...]
    reduce_sum x5 -> x0, other arithmetic: 42.5 us -> none  [the longest x1 25.2 us: body(): inner_prod = jnp.sum(stacked * upstream[None], -1)]
    add x3 -> x4, other arithmetic: 40.2 us -> 1.78 us  [the longest x2 1.66 us: body(): table_part = table_part[:keep].astype(F32) + other.astype(F32)]
  transfers between devices with their start and end apart: 9 -> 24, of which waited for: 3 -> 10; matrix products, arithmetic and copies ran while one was open for 22% -> 6% of each run, Pallas kernels for 0% -> 31%
where the time goes in v1:
time: 132 us; the launch traced here: 131 us
  Pallas kernels  52.9 us (40%)
  waiting for transfers between devices  31.1 us (24%)
  starting transfers between devices  26.5 us (20%)
  local copies, waits for them, and re-layouts  15.5 us (12%)
  other arithmetic  4.55 us (3%)
    pallas_call x13, Pallas kernels, call(): pl.pallas_call(kernel, out_shape=[jax.ShapeDtypeStruct(s, t) for s, t in...  52.9 us
    ppermute x23, waiting for transfers between devices, swap(): return lax.ppermute(value, axis, [(i, i ^ bit) for i in range(count)])  31.1 us
    ppermute x23, starting transfers between devices, swap(): return lax.ppermute(value, axis, [(i, i ^ bit) for i in range(count)])  22.9 us
    unnamed x38, local copies, waits for them, and re-layouts  6.77 us
    ppermute x1, starting transfers between devices, body(): before = lax.ppermute(ids[:, half:], 'tract', steps)  3.66 us
    slice x3, local copies, waits for them, and re-layouts, body(): other = swap(block[keep:], axis, bit)  2.75 us
  transfers between devices with their start and end apart: 24, of which 10 were waited for; matrix products, arithmetic and copies ran while one was open for 6% of the time, Pallas kernels for 31%

profile of v1, /device:TPU:0, one launch (start us, length us, event | category | flops | bytes accessed | tf_op | source)
XLA Modules:
  0.0 131.5 jit_solution(16455166144100518807)
XLA Ops:
  0.6 1.8 %payload.1.refs_0_ = bf16[80,768]{1,0:T(8,128)(2,1)} custom-call(s32[1]{0:T(128)} %bitcast.where.group, f32[64,768]{1,0:T(8,128)} %table.1, f32[1,192]{1,0:T(1,128)} %bitcast.16, f32[1,192]{1,0:T(1,128)} %bitcast.17), custom_call_target="tpu_custom_call" | custom-call | bytes 198148 | tf_op jit(solution)/shard_map/payload/pallas_call | solution.py:34
  2.4 2.9 %collective-permute-start = (bf16[80,768]{1,0:T(8,128)(2,1)}, bf16[80,768]{1,0:T(8,128)(2,1)S(1)}, u32[]{:S(2)}, u32[]{:S(2)}) collective-permute-start(bf16[80,768]{1,0:T(8,128)(2,1)} %payload.1.refs_0_), channel_id=1, source_target_pairs={{0,16},{8,24},{16,0},{24,8},{1,17},{9,25},{17,1},{25,9},{2,18},{10... | collective-permute-start | bytes 368648 | tf_op jit(solution)/shard_map/ppermute | solution.py:49
  5.3 0.7 constant_dynamic-update-slice_fusion.2
  6.1 2.8 %collective-permute-done.refs_1_ = bf16[80,768]{1,0:T(8,128)(2,1)S(1)} collective-permute-done((bf16[80,768]{1,0:T(8,128)(2,1)}, bf16[80,768]{1,0:T(8,128)(2,1)S(1)}, u32[]{:S(2)}, u32[]{:S(2)}) %collective-permute-start) | collective-permute-done | bytes 122912 | tf_op jit(solution)/shard_map/ppermute | solution.py:49
  8.9 0.7 constant_dynamic-update-slice_fusion.1
  9.6 0.7 constant_dynamic-update-slice_fusion
  10.3 3.7 %collective-permute-start.9 = (s32[48,128]{1,0:T(8,128)S(1)}, s32[48,128]{1,0:T(8,128)S(1)}, u32[]{:S(2)}, u32[]{:S(2)}) collective-permute-start(s32[48,128]{1,0:T(8,128)S(1)} %slice.73), channel_id=1, source_target_pairs={{0,1},{1,2},{2,3},{3,4},{4,5},{5,6},{6,7},{8,9},{9,10},{10,11},{11... | collective-permute-start | bytes 73736 | tf_op jit(solution)/shard_map/ppermute | solution.py:445
  14.0 0.6 copy-done.5
  14.7 0.7 copy-done.6
  15.3 4.3 %products.1 = (bf16[256,768]{1,0:T(8,128)(2,1)}, f32[8,256]{1,0:T(8,128)}, bf16[768,768]{1,0:T(8,128)(2,1)}, bf16[256,768]{1,0:T(8,128)(2,1)}, bf16[16,768]{1,0:T(8,128)(2,1)}) custom-call(s32[1]{0:T(128)} %bitcast.where.group, bf16[80,768]{1,0:T(8,128)(2,1)} %payload.1.refs_0_, bf16[80,768]{1,0:T(8,128)(2,1)} %copy-done.4, bf16[80,768]{1,0:T(8,128)(2,1)} %copy-done.5, ...), custom_call_target="tpu_custom_call" | custom-call | bytes 2850820 | tf_op jit(solution)/shard_map/products/pallas_call | solution.py:34
  19.6 1.5 %collective-permute-start.6 = (f32[8,256]{1,0:T(8,128)}, f32[8,256]{1,0:T(8,128)S(1)}, u32[]{:S(2)}, u32[]{:S(2)}) collective-permute-start(f32[8,256]{1,0:T(8,128)} %get-tuple-element.21.refs_0_), channel_id=1, source_target_pairs={{0,16},{8,24},{16,0},{24,8},{1,17},{9,25},{17,1},{25,9},{2,18},{10... | collective-permute-start | bytes 24584 | tf_op jit(solution)/shard_map/ppermute | solution.py:49
  21.1 2.4 %collective-permute-done.6.refs_1_ = f32[8,256]{1,0:T(8,128)S(1)} collective-permute-done((f32[8,256]{1,0:T(8,128)}, f32[8,256]{1,0:T(8,128)S(1)}, u32[]{:S(2)}, u32[]{:S(2)}) %collective-permute-start.6) | collective-permute-done | bytes 8224 | tf_op jit(solution)/shard_map/ppermute | solution.py:49
  23.5 0.6 convert_element_type.24.ids
  24.1 0.6 convert_element_type.25.before
  24.7 1.7 %planes.1.refs_4_ = f32[48,1024]{1,0:T(8,128)} custom-call(s32[1]{0:T(128)} %bitcast.where.group, bf16[48,256]{1,0:T(8,128)(2,1)} %convert_element_type.24.ids, bf16[48,128]{1,0:T(8,128)(2,1)} %convert_element_type.25.before), custom_call_target="tpu_custom_call" | custom-call | bytes 36868 | tf_op jit(solution)/shard_map/planes/pallas_call | solution.py:34
  26.4 0.5 collective-permute-start.4
  26.9 1.5 %collective-permute-start.3 = (bf16[256,768]{1,0:T(8,128)(2,1)}, bf16[256,768]{1,0:T(8,128)(2,1)S(1)}, u32[]{:S(2)}, u32[]{:S(2)}) collective-permute-start(bf16[256,768]{1,0:T(8,128)(2,1)} %get-tuple-element.20.refs_0_), channel_id=1, source_target_pairs={{0,16},{8,24},{16,0},{24,8},{1,17},{9,25},{17,1},{25,9},{2,18},{10... | collective-permute-start | bytes 1179656 | tf_op jit(solution)/shard_map/ppermute | solution.py:49
  28.4 0.6 copy-done.16
  29.0 5.2 %far.1 = (bf16[2,256,768]{2,1,0:T(8,128)(2,1)}, f32[8,16,128]{2,1,0:T(8,128)}, f32[20,16,128]{2,1,0:T(8,128)}, f32[8,16,128]{2,1,0:T(8,128)}, f32[20,16,128]{2,1,0:T(8,128)}, /*index=5*/f32[16,128]{1,0:T(8,128)}) custom-call(s32[1]{0:T(128)} %bitcast.where.group, f32[8,256]{1,0:T(8,128)} %get-tuple-element.21.refs_0_, f32[8,256]{1,0:T(8,128)} %copy-done.15, ...), custom_call_target="tpu_custom_call" | custom-call | flops 1610612736 | bytes 3399684 | tf_op jit(solution)/shard_map/far/pallas_call | solution.py:34
  34.2 1.0 slice_bitcast_fusion
  35.3 5.0 %near.1 = (bf16[2,256,768]{2,1,0:T(8,128)(2,1)}, f32[8,768]{1,0:T(8,128)}) custom-call(s32[1]{0:T(128)} %bitcast.where.group, f32[8,16,128]{2,1,0:T(8,128)} %get-tuple-element.23.refs_4_.codes.refs_8_, f32[20,16,128]{2,1,0:T(8,128)} %get-tuple-element.24.refs_5_.weights, f32[16,128]{1,0:T(8,128)} %get-tuple-element.25.refs_6_.averages, ...), custom_call_target="tpu_custom_call" | custom-call | flops 1610612736 | bytes 3383300 | tf_op jit(solution)/shard_map/near/pallas_call | solution.py:34
  40.3 0.5 collective-permute-start.5
  40.9 1.9 %slice_bitcast_fusion.1 = (bf16[256,768]{1,0:T(8,128)(2,1)S(1)}, bf16[256,768]{1,0:T(8,128)(2,1)}) fusion(bf16[2,256,768]{2,1,0:T(8,128)(2,1)} %get-tuple-element.26), kind=kLoop, calls=%fused_computation.4 | loop fusion | bytes 1572864 | tf_op jit(solution)/shard_map/squeeze | solution.py:483
  42.9 0.6 collective-permute-start.12
  43.6 0.7 copy-done.12
  44.3 0.2 copy-done.14
  44.4 14.2 %scores.1.refs_0_ = f32[8,1024]{1,0:T(8,128)} custom-call(s32[1]{0:T(128)} %bitcast.where.group, bf16[256,768]{1,0:T(8,128)(2,1)} %get-tuple-element.20.refs_0_, bf16[256,768]{1,0:T(8,128)(2,1)} %copy-done.13, bf16[256,768]{1,0:T(8,128)(2,1)} %copy-done.12, bf16[256,768]{1,0:T(8,128)(2,1)} %copy-done.14, f32[48,1024]{1,0:T(8,128)} %planes.1.refs_4_, ...), custom_call_target="tpu_custom_call" | custom-call | flops 3221225472 | bytes 5259268 | tf_op jit(solution)/shard_map/scores/pallas_call | solution.py:34
  58.6 1.5 %collective-permute-start.13 = (f32[8,1024]{1,0:T(8,128)}, f32[8,1024]{1,0:T(8,128)S(1)}, u32[]{:S(2)}, u32[]{:S(2)}) collective-permute-start(f32[8,1024]{1,0:T(8,128)} %scores.1.refs_0_), channel_id=1, source_target_pairs={{0,16},{8,24},{16,0},{24,8},{1,17},{9,25},{17,1},{25,9},{2,18},{10... | collective-permute-start | bytes 98312 | tf_op jit(solution)/shard_map/ppermute | solution.py:49
  60.1 2.6 %collective-permute-done.13.refs_1_ = f32[8,1024]{1,0:T(8,128)S(1)} collective-permute-done((f32[8,1024]{1,0:T(8,128)}, f32[8,1024]{1,0:T(8,128)S(1)}, u32[]{:S(2)}, u32[]{:S(2)}) %collective-permute-start.13) | collective-permute-done | bytes 32800 | tf_op jit(solution)/shard_map/ppermute | solution.py:49
  62.8 1.1 collective-permute-done.15.refs_3_
  64.0 0.6 copy-done.11
  64.6 2.4 %merge.1.mine = bf16[272,768]{1,0:T(8,128)(2,1)} custom-call(s32[1]{0:T(128)} %bitcast.5.where, s32[1]{0:T(128)} %bitcast.where.group, bf16[256,768]{1,0:T(8,128)(2,1)} %get-tuple-element.36.near, bf16[256,768]{1,0:T(8,128)(2,1)} %copy-done.1, bf16[256,768]{1,0:T(8,128)(2,1)} %copy-done.2, f32[8,1024]{1,0:T(8,128)} %scores.1.refs_0_, f32[8,1024]{1,0:T(8,128)} %copy-done.9, ...), custom_call_target="tpu_custom_call" | custom-call | bytes 1335304 | tf_op jit(solution)/shard_map/merge/pallas_call | solution.py:34
  67.0 0.9 slice.74
  67.9 1.6 %collective-permute-start.16 = (bf16[144,768]{1,0:T(8,128)(2,1)S(1)}, bf16[144,768]{1,0:T(8,128)(2,1)S(1)}, u32[]{:S(2)}, u32[]{:S(2)}) collective-permute-start(bf16[144,768]{1,0:T(8,128)(2,1)S(1)} %slice.74), channel_id=1, source_target_pairs={{0,1},{1,0},{2,3},{3,2},{4,5},{5,4},{6,7},{7,6},{8,9},{9,8},{10,11... | collective-permute-start | bytes 663560 | tf_op jit(solution)/shard_map/ppermute | solution.py:49
  69.5 6.0 %collective-permute-done.16.other = bf16[144,768]{1,0:T(8,128)(2,1)S(1)} collective-permute-done((bf16[144,768]{1,0:T(8,128)(2,1)S(1)}, bf16[144,768]{1,0:T(8,128)(2,1)S(1)}, u32[]{:S(2)}, u32[]{:S(2)}) %collective-permute-start.16) | collective-permute-done | bytes 221216 | tf_op jit(solution)/shard_map/ppermute | solution.py:49
  75.5 0.7 copy-done.3
  76.2 1.8 %halve.3.mine = bf16[144,768]{1,0:T(8,128)(2,1)} custom-call(s32[1]{0:T(128)} %bitcast.where.group, bf16[272,768]{1,0:T(8,128)(2,1)} %merge.1.mine, bf16[144,768]{1,0:T(8,128)(2,1)} %copy-done.3), custom_call_target="tpu_custom_call" | custom-call | bytes 638980 | tf_op jit(solution)/shard_map/halve/pallas_call | solution.py:34
  78.0 0.9 slice.75
  78.9 1.6 %collective-permute-start.17 = (bf16[80,768]{1,0:T(8,128)(2,1)S(1)}, bf16[80,768]{1,0:T(8,128)(2,1)S(1)}, u32[]{:S(2)}, u32[]{:S(2)}) collective-permute-start(bf16[80,768]{1,0:T(8,128)(2,1)S(1)} %slice.75), channel_id=1, source_target_pairs={{0,2},{1,3},{2,0},{3,1},{4,6},{5,7},{6,4},{7,5},{8,10},{9,11},{10,... | collective-permute-start | bytes 368648 | tf_op jit(solution)/shard_map/ppermute | solution.py:49
  80.5 3.3 %collective-permute-done.17.other = bf16[80,768]{1,0:T(8,128)(2,1)S(1)} collective-permute-done((bf16[80,768]{1,0:T(8,128)(2,1)S(1)}, bf16[80,768]{1,0:T(8,128)(2,1)S(1)}, u32[]{:S(2)}, u32[]{:S(2)}) %collective-permute-start.17) | collective-permute-done | bytes 122912 | tf_op jit(solution)/shard_map/ppermute | solution.py:49
  83.8 0.6 copy-done.7
  84.5 1.7 %halve.4.mine = bf16[80,768]{1,0:T(8,128)(2,1)} custom-call(s32[1]{0:T(128)} %bitcast.where.group, bf16[144,768]{1,0:T(8,128)(2,1)} %halve.3.mine, bf16[80,768]{1,0:T(8,128)(2,1)} %copy-done.7), custom_call_target="tpu_custom_call" | custom-call | bytes 344068 | tf_op jit(solution)/shard_map/halve/pallas_call | solution.py:34
  86.2 0.9 slice.76
  87.1 2.6 %collective-permute-start.18 = (bf16[48,768]{1,0:T(8,128)(2,1)S(1)}, bf16[48,768]{1,0:T(8,128)(2,1)S(1)}, u32[]{:S(2)}, u32[]{:S(2)}) collective-permute-start(bf16[48,768]{1,0:T(8,128)(2,1)S(1)} %slice.76), channel_id=1, source_target_pairs={{0,4},{1,5},{2,6},{3,7},{4,0},{5,1},{6,2},{7,3},{8,12},{9,13},{10,... | collective-permute-start | bytes 221192 | tf_op jit(solution)/shard_map/ppermute | solution.py:49
  89.7 2.7 %collective-permute-done.18.other = bf16[48,768]{1,0:T(8,128)(2,1)S(1)} collective-permute-done((bf16[48,768]{1,0:T(8,128)(2,1)S(1)}, bf16[48,768]{1,0:T(8,128)(2,1)S(1)}, u32[]{:S(2)}, u32[]{:S(2)}) %collective-permute-start.18) | collective-permute-done | bytes 73760 | tf_op jit(solution)/shard_map/ppermute | solution.py:49
  92.3 0.6 copy-done.8
  93.0 1.6 %halve.5 = bf16[48,768]{1,0:T(8,128)(2,1)} custom-call(s32[1]{0:T(128)} %bitcast.where.group, bf16[80,768]{1,0:T(8,128)(2,1)} %halve.4.mine, bf16[48,768]{1,0:T(8,128)(2,1)} %copy-done.8), custom_call_target="tpu_custom_call" | custom-call | bytes 196612 | tf_op jit(solution)/shard_map/halve/pallas_call | solution.py:34
  94.6 0.8 slice.77
  95.4 2.7 %collective-permute-start.19 = (bf16[32,768]{1,0:T(8,128)(2,1)S(1)}, bf16[32,768]{1,0:T(8,128)(2,1)S(1)}, u32[]{:S(2)}, u32[]{:S(2)}) collective-permute-start(bf16[32,768]{1,0:T(8,128)(2,1)S(1)} %slice.77), channel_id=1, source_target_pairs={{0,4},{1,5},{2,6},{3,7},{4,0},{5,1},{6,2},{7,3},{8,12},{9,13},{10,... | collective-permute-start | bytes 147464 | tf_op jit(solution)/shard_map/ppermute | solution.py:49
  98.0 2.4 %collective-permute-done.19 = bf16[32,768]{1,0:T(8,128)(2,1)S(1)} collective-permute-done((bf16[32,768]{1,0:T(8,128)(2,1)S(1)}, bf16[32,768]{1,0:T(8,128)(2,1)S(1)}, u32[]{:S(2)}, u32[]{:S(2)}) %collective-permute-start.19) | collective-permute-done | bytes 49184 | tf_op jit(solution)/shard_map/ppermute | solution.py:49
  100.5 2.1 %collective-permute-start.20 = (bf16[64,768]{1,0:T(8,128)(2,1)S(1)}, bf16[64,768]{1,0:T(8,128)(2,1)S(1)}, u32[]{:S(2)}, u32[]{:S(2)}) collective-permute-start(bf16[64,768]{1,0:T(8,128)(2,1)S(1)} %pad_maximum_fusion.2), channel_id=1, source_target_pairs={{0,2},{1,3},{2,0},{3,1},{4,6},{5,7},{6,4},{7,5},{8,10},{9,11},{10,... | collective-permute-start | bytes 294920 | tf_op jit(solution)/shard_map/ppermute | solution.py:49
  102.6 7.5 %output.1 = bf16[2048,768]{1,0:T(8,128)(2,1)} custom-call(s32[1]{0:T(128)} %bitcast.where.group, bf16[256,768]{1,0:T(8,128)(2,1)} %get-tuple-element.20.refs_0_, bf16[256,768]{1,0:T(8,128)(2,1)} %copy-done.13, bf16[256,768]{1,0:T(8,128)(2,1)} %copy-done.12, bf16[256,768]{1,0:T(8,128)(2,1)} %copy-done.14, ...), custom_call_target="tpu_custom_call" | custom-call | flops 3221225472 | bytes 1835012 | tf_op jit(solution)/shard_map/output/pallas_call | solution.py:34
  110.2 1.4 %collective-permute-start.21 = (bf16[128,768]{1,0:T(8,128)(2,1)S(1)}, bf16[128,768]{1,0:T(8,128)(2,1)S(1)}, u32[]{:S(2)}, u32[]{:S(2)}) collective-permute-start(bf16[128,768]{1,0:T(8,128)(2,1)S(1)} %pad_maximum_fusion.1), channel_id=1, source_target_pairs={{0,1},{1,0},{2,3},{3,2},{4,5},{5,4},{6,7},{7,6},{8,9},{9,8},{10,11... | collective-permute-start | bytes 589832 | tf_op jit(solution)/shard_map/ppermute | solution.py:49
  111.6 0.7 slice_convert_fusion.1
  112.3 3.6 %collective-permute-done.21 = bf16[128,768]{1,0:T(8,128)(2,1)S(1)} collective-permute-done((bf16[128,768]{1,0:T(8,128)(2,1)S(1)}, bf16[128,768]{1,0:T(8,128)(2,1)S(1)}, u32[]{:S(2)}, u32[]{:S(2)}) %collective-permute-start.21) | collective-permute-done | bytes 196640 | tf_op jit(solution)/shard_map/ppermute | solution.py:49
  115.9 0.8 pad_maximum_fusion.block
  116.7 2.7 %share.1 = (bf16[256,768]{1,0:T(8,128)(2,1)}, bf16[256,768]{1,0:T(8,128)(2,1)}) custom-call(s32[1]{0:T(128)} %bitcast.5.where, s32[1]{0:T(128)} %bitcast.where.group, bf16[256,768]{1,0:T(8,128)(2,1)} %pad_maximum_fusion.block, bf16[768,768]{1,0:T(8,128)(2,1)} %get-tuple-element.31.weight_low), custom_call_target="tpu_custom_call" | custom-call | bytes 1572872 | tf_op jit(solution)/shard_map/share/pallas_call | solution.py:34
  119.4 0.9 slice.65
  120.3 1.6 %collective-permute-start.22 = (bf16[128,768]{1,0:T(8,128)(2,1)S(1)}, bf16[128,768]{1,0:T(8,128)(2,1)S(1)}, u32[]{:S(2)}, u32[]{:S(2)}) collective-permute-start(bf16[128,768]{1,0:T(8,128)(2,1)S(1)} %slice.65), channel_id=1, source_target_pairs={{0,16},{8,24},{16,0},{24,8},{1,17},{9,25},{17,1},{25,9},{2,18},{10... | collective-permute-start | bytes 589832 | tf_op jit(solution)/shard_map/ppermute | solution.py:49
  122.0 4.1 %collective-permute-done.22 = bf16[128,768]{1,0:T(8,128)(2,1)S(1)} collective-permute-done((bf16[128,768]{1,0:T(8,128)(2,1)S(1)}, bf16[128,768]{1,0:T(8,128)(2,1)S(1)}, u32[]{:S(2)}, u32[]{:S(2)}) %collective-permute-start.22) | collective-permute-done | bytes 196640 | tf_op jit(solution)/shard_map/ppermute | solution.py:49
  126.1 1.0 convert_add_fusion
  127.2 0.6 fusion.1
  127.7 3.0 %weights.1 = f32[768,768]{1,0:T(8,128)} custom-call(s32[1]{0:T(128)} %bitcast.where.group, bf16[256,768]{1,0:T(8,128)(2,1)} %get-tuple-element.33.table_low, bf16[256,768]{1,0:T(8,128)(2,1)} %get-tuple-element.34.block), custom_call_target="tpu_custom_call" | custom-call | bytes 786436 | tf_op jit(solution)/shard_map/weights/pallas_call | solution.py:34
  130.8 0.7 slice_add_fusion
  (57 shorter events, 0.5 us)
Async XLA Ops:
  2.4 6.5 %collective-permute-start = (bf16[80,768]{1,0:T(8,128)(2,1)}, bf16[80,768]{1,0:T(8,128)(2,1)S(1)}, u32[]{:S(2)}, u32[]{:S(2)}) collective-permute-start(bf16[80,768]{1,0:T(8,128)(2,1)} %payload.1.refs_0_), channel_id=1, source_target_pairs={{0,16},{8,24},{16,0},{24,8},{1,17},{9,25},{17,1},{25,9},{2,18},{10... | collective-permute-start | bytes 368648 | tf_op jit(solution)/shard_map/ppermute | solution.py:49
  5.3 8.7 %collective-permute-start.1 = (bf16[80,768]{1,0:T(8,128)(2,1)}, bf16[80,768]{1,0:T(8,128)(2,1)S(1)}, u32[]{:S(2)}, u32[]{:S(2)}) collective-permute-start(bf16[80,768]{1,0:T(8,128)(2,1)} %payload.1.refs_0_), channel_id=1, source_target_pairs={{0,8},{8,0},{16,24},{24,16},{1,9},{9,1},{17,25},{25,17},{2,10},{10... | collective-permute-start | bytes 368648 | tf_op jit(solution)/shard_map/ppermute | solution.py:49
  8.9 5.2 %copy-start.4 = (bf16[80,768]{1,0:T(8,128)(2,1)}, bf16[80,768]{1,0:T(8,128)(2,1)S(1)}, u32[]{:S(2)}) copy-start(bf16[80,768]{1,0:T(8,128)(2,1)S(1)} %collective-permute-done.refs_1_) | copy-start | bytes 368644
  8.9 5.1 %collective-permute-start.2 = (bf16[80,768]{1,0:T(8,128)(2,1)S(1)}, bf16[80,768]{1,0:T(8,128)(2,1)S(1)}, u32[]{:S(2)}, u32[]{:S(2)}) collective-permute-start(bf16[80,768]{1,0:T(8,128)(2,1)S(1)} %collective-permute-done.refs_1_), channel_id=1, source_target_pairs={{0,8},{8,0},{16,24},{24,16},{1,9},{9,1},{17,25},{25,17},{2,10},{10... | collective-permute-start | bytes 368648 | tf_op jit(solution)/shard_map/ppermute | solution.py:49
  10.3 13.8 %collective-permute-start.9 = (s32[48,128]{1,0:T(8,128)S(1)}, s32[48,128]{1,0:T(8,128)S(1)}, u32[]{:S(2)}, u32[]{:S(2)}) collective-permute-start(s32[48,128]{1,0:T(8,128)S(1)} %slice.73), channel_id=1, source_target_pairs={{0,1},{1,2},{2,3},{3,4},{4,5},{5,6},{6,7},{8,9},{9,10},{10,11},{11... | collective-permute-start | bytes 73736 | tf_op jit(solution)/shard_map/ppermute | solution.py:445
  14.0 0.7 copy-start.5
  14.7 0.7 copy-start.6
  19.6 3.9 %collective-permute-start.6 = (f32[8,256]{1,0:T(8,128)}, f32[8,256]{1,0:T(8,128)S(1)}, u32[]{:S(2)}, u32[]{:S(2)}) collective-permute-start(f32[8,256]{1,0:T(8,128)} %get-tuple-element.21.refs_0_), channel_id=1, source_target_pairs={{0,16},{8,24},{16,0},{24,8},{1,17},{9,25},{17,1},{25,9},{2,18},{10... | collective-permute-start | bytes 24584 | tf_op jit(solution)/shard_map/ppermute | solution.py:49
  21.1 7.3 %collective-permute-start.7 = (f32[8,256]{1,0:T(8,128)}, f32[8,256]{1,0:T(8,128)S(1)}, u32[]{:S(2)}, u32[]{:S(2)}) collective-permute-start(f32[8,256]{1,0:T(8,128)} %get-tuple-element.21.refs_0_), channel_id=1, source_target_pairs={{0,8},{8,0},{16,24},{24,16},{1,9},{9,1},{17,25},{25,17},{2,10},{10... | collective-permute-start | bytes 24584 | tf_op jit(solution)/shard_map/ppermute | solution.py:49
  23.5 4.9 %copy-start.15 = (f32[8,256]{1,0:T(8,128)}, f32[8,256]{1,0:T(8,128)S(1)}, u32[]{:S(2)}) copy-start(f32[8,256]{1,0:T(8,128)S(1)} %collective-permute-done.6.refs_1_) | copy-start | bytes 24580
  23.5 4.9 %collective-permute-start.8 = (f32[8,256]{1,0:T(8,128)S(1)}, f32[8,256]{1,0:T(8,128)S(1)}, u32[]{:S(2)}, u32[]{:S(2)}) collective-permute-start(f32[8,256]{1,0:T(8,128)S(1)} %collective-permute-done.6.refs_1_), channel_id=1, source_target_pairs={{0,8},{8,0},{16,24},{24,16},{1,9},{9,1},{17,25},{25,17},{2,10},{10... | collective-permute-start | bytes 24584 | tf_op jit(solution)/shard_map/ppermute | solution.py:49
  26.4 17.1 %collective-permute-start.4 = (bf16[256,768]{1,0:T(8,128)(2,1)}, bf16[256,768]{1,0:T(8,128)(2,1)S(1)}, u32[]{:S(2)}, u32[]{:S(2)}) collective-permute-start(bf16[256,768]{1,0:T(8,128)(2,1)} %get-tuple-element.20.refs_0_), channel_id=1, source_target_pairs={{0,8},{8,0},{16,24},{24,16},{1,9},{9,1},{17,25},{25,17},{2,10},{10... | collective-permute-start | bytes 1179656 | tf_op jit(solution)/shard_map/ppermute | solution.py:49
  26.9 13.4 %collective-permute-start.3 = (bf16[256,768]{1,0:T(8,128)(2,1)}, bf16[256,768]{1,0:T(8,128)(2,1)S(1)}, u32[]{:S(2)}, u32[]{:S(2)}) collective-permute-start(bf16[256,768]{1,0:T(8,128)(2,1)} %get-tuple-element.20.refs_0_), channel_id=1, source_target_pairs={{0,16},{8,24},{16,0},{24,8},{1,17},{9,25},{17,1},{25,9},{2,18},{10... | collective-permute-start | bytes 1179656 | tf_op jit(solution)/shard_map/ppermute | solution.py:49
  28.4 0.6 copy-start.16
  28.4 0.6 copy-start.17
  35.2 7.7 %collective-permute-start.11 = (bf16[256,768]{1,0:T(8,128)(2,1)S(1)}, bf16[256,768]{1,0:T(8,128)(2,1)S(1)}, u32[]{:S(2)}, u32[]{:S(2)}) collective-permute-start(bf16[256,768]{1,0:T(8,128)(2,1)S(1)} %slice_bitcast_fusion), channel_id=1, source_target_pairs={{0,8},{8,0},{16,24},{24,16},{1,9},{9,1},{17,25},{25,17},{2,10},{10... | collective-permute-start | bytes 1179656 | tf_op jit(solution)/shard_map/ppermute | solution.py:49
  35.3 7.6 %copy-start = (bf16[2,256,768]{2,1,0:T(8,128)(2,1)S(1)}, bf16[2,256,768]{2,1,0:T(8,128)(2,1)}, u32[]{:S(2)}) copy-start(bf16[2,256,768]{2,1,0:T(8,128)(2,1)} %get-tuple-element.27) | copy-start | bytes 2359300
  40.3 3.3 %copy-start.13 = (bf16[256,768]{1,0:T(8,128)(2,1)}, bf16[256,768]{1,0:T(8,128)(2,1)S(1)}, u32[]{:S(2)}) copy-start(bf16[256,768]{1,0:T(8,128)(2,1)S(1)} %collective-permute-done.3.refs_1_) | copy-start | bytes 1179652
  40.3 3.2 %collective-permute-start.5 = (bf16[256,768]{1,0:T(8,128)(2,1)S(1)}, bf16[256,768]{1,0:T(8,128)(2,1)S(1)}, u32[]{:S(2)}, u32[]{:S(2)}) collective-permute-start(bf16[256,768]{1,0:T(8,128)(2,1)S(1)} %collective-permute-done.3.refs_1_), channel_id=1, source_target_pairs={{0,8},{8,0},{16,24},{24,16},{1,9},{9,1},{17,25},{25,17},{2,10},{10... | collective-permute-start | bytes 1179656 | tf_op jit(solution)/shard_map/ppermute | solution.py:49
  42.8 19.9 %collective-permute-start.10 = (bf16[256,768]{1,0:T(8,128)(2,1)S(1)}, bf16[256,768]{1,0:T(8,128)(2,1)S(1)}, u32[]{:S(2)}, u32[]{:S(2)}) collective-permute-start(bf16[256,768]{1,0:T(8,128)(2,1)S(1)} %get-tuple-element.35), channel_id=1, source_target_pairs={{0,8},{8,0},{16,24},{24,16},{1,9},{9,1},{17,25},{25,17},{2,10},{10... | collective-permute-start | bytes 1179656 | tf_op jit(solution)/shard_map/ppermute | solution.py:49
  42.9 19.8 %collective-permute-start.12 = (bf16[256,768]{1,0:T(8,128)(2,1)S(1)}, bf16[256,768]{1,0:T(8,128)(2,1)S(1)}, u32[]{:S(2)}, u32[]{:S(2)}) collective-permute-start(bf16[256,768]{1,0:T(8,128)(2,1)S(1)} %bitcast_add_fusion), channel_id=1, source_target_pairs={{0,16},{8,24},{16,0},{24,8},{1,17},{9,25},{17,1},{25,9},{2,18},{10... | collective-permute-start | bytes 1179656 | tf_op jit(solution)/shard_map/ppermute | solution.py:49
  43.5 0.7 copy-start.12
  43.6 0.9 copy-start.14
  58.6 4.1 %collective-permute-start.13 = (f32[8,1024]{1,0:T(8,128)}, f32[8,1024]{1,0:T(8,128)S(1)}, u32[]{:S(2)}, u32[]{:S(2)}) collective-permute-start(f32[8,1024]{1,0:T(8,128)} %scores.1.refs_0_), channel_id=1, source_target_pairs={{0,16},{8,24},{16,0},{24,8},{1,17},{9,25},{17,1},{25,9},{2,18},{10... | collective-permute-start | bytes 98312 | tf_op jit(solution)/shard_map/ppermute | solution.py:49
  60.1 2.7 %collective-permute-start.14 = (f32[8,1024]{1,0:T(8,128)}, f32[8,1024]{1,0:T(8,128)S(1)}, u32[]{:S(2)}, u32[]{:S(2)}) collective-permute-start(f32[8,1024]{1,0:T(8,128)} %scores.1.refs_0_), channel_id=1, source_target_pairs={{0,8},{8,0},{16,24},{24,16},{1,9},{9,1},{17,25},{25,17},{2,10},{10... | collective-permute-start | bytes 98312 | tf_op jit(solution)/shard_map/ppermute | solution.py:49
  62.7 1.2 copy-start.9
  62.7 1.2 collective-permute-start.15
  62.7 1.2 copy-start.1
  62.8 1.2 copy-start.2
  62.8 1.2 copy-start.10
  63.9 0.6 copy-start.11
  67.9 7.6 %collective-permute-start.16 = (bf16[144,768]{1,0:T(8,128)(2,1)S(1)}, bf16[144,768]{1,0:T(8,128)(2,1)S(1)}, u32[]{:S(2)}, u32[]{:S(2)}) collective-permute-start(bf16[144,768]{1,0:T(8,128)(2,1)S(1)} %slice.74), channel_id=1, source_target_pairs={{0,1},{1,0},{2,3},{3,2},{4,5},{5,4},{6,7},{7,6},{8,9},{9,8},{10,11... | collective-permute-start | bytes 663560 | tf_op jit(solution)/shard_map/ppermute | solution.py:49
  75.5 0.7 copy-start.3
  78.9 4.9 %collective-permute-start.17 = (bf16[80,768]{1,0:T(8,128)(2,1)S(1)}, bf16[80,768]{1,0:T(8,128)(2,1)S(1)}, u32[]{:S(2)}, u32[]{:S(2)}) collective-permute-start(bf16[80,768]{1,0:T(8,128)(2,1)S(1)} %slice.75), channel_id=1, source_target_pairs={{0,2},{1,3},{2,0},{3,1},{4,6},{5,7},{6,4},{7,5},{8,10},{9,11},{10,... | collective-permute-start | bytes 368648 | tf_op jit(solution)/shard_map/ppermute | solution.py:49
  83.8 0.6 copy-start.7
  87.1 5.3 %collective-permute-start.18 = (bf16[48,768]{1,0:T(8,128)(2,1)S(1)}, bf16[48,768]{1,0:T(8,128)(2,1)S(1)}, u32[]{:S(2)}, u32[]{:S(2)}) collective-permute-start(bf16[48,768]{1,0:T(8,128)(2,1)S(1)} %slice.76), channel_id=1, source_target_pairs={{0,4},{1,5},{2,6},{3,7},{4,0},{5,1},{6,2},{7,3},{8,12},{9,13},{10,... | collective-permute-start | bytes 221192 | tf_op jit(solution)/shard_map/ppermute | solution.py:49
  92.3 0.6 copy-start.8
  95.4 5.1 %collective-permute-start.19 = (bf16[32,768]{1,0:T(8,128)(2,1)S(1)}, bf16[32,768]{1,0:T(8,128)(2,1)S(1)}, u32[]{:S(2)}, u32[]{:S(2)}) collective-permute-start(bf16[32,768]{1,0:T(8,128)(2,1)S(1)} %slice.77), channel_id=1, source_target_pairs={{0,4},{1,5},{2,6},{3,7},{4,0},{5,1},{6,2},{7,3},{8,12},{9,13},{10,... | collective-permute-start | bytes 147464 | tf_op jit(solution)/shard_map/ppermute | solution.py:49
  100.5 9.7 %collective-permute-start.20 = (bf16[64,768]{1,0:T(8,128)(2,1)S(1)}, bf16[64,768]{1,0:T(8,128)(2,1)S(1)}, u32[]{:S(2)}, u32[]{:S(2)}) collective-permute-start(bf16[64,768]{1,0:T(8,128)(2,1)S(1)} %pad_maximum_fusion.2), channel_id=1, source_target_pairs={{0,2},{1,3},{2,0},{3,1},{4,6},{5,7},{6,4},{7,5},{8,10},{9,11},{10,... | collective-permute-start | bytes 294920 | tf_op jit(solution)/shard_map/ppermute | solution.py:49
  110.2 5.7 %collective-permute-start.21 = (bf16[128,768]{1,0:T(8,128)(2,1)S(1)}, bf16[128,768]{1,0:T(8,128)(2,1)S(1)}, u32[]{:S(2)}, u32[]{:S(2)}) collective-permute-start(bf16[128,768]{1,0:T(8,128)(2,1)S(1)} %pad_maximum_fusion.1), channel_id=1, source_target_pairs={{0,1},{1,0},{2,3},{3,2},{4,5},{5,4},{6,7},{7,6},{8,9},{9,8},{10,11... | collective-permute-start | bytes 589832 | tf_op jit(solution)/shard_map/ppermute | solution.py:49
  120.3 5.7 %collective-permute-start.22 = (bf16[128,768]{1,0:T(8,128)(2,1)S(1)}, bf16[128,768]{1,0:T(8,128)(2,1)S(1)}, u32[]{:S(2)}, u32[]{:S(2)}) collective-permute-start(bf16[128,768]{1,0:T(8,128)(2,1)S(1)} %slice.65), channel_id=1, source_target_pairs={{0,16},{8,24},{16,0},{24,8},{1,17},{9,25},{17,1},{25,9},{2,18},{10... | collective-permute-start | bytes 589832 | tf_op jit(solution)/shard_map/ppermute | solution.py:49
  127.1 3.7 %collective-permute-start.23 = (bf16[64,768]{1,0:T(8,128)(2,1)S(1)}, bf16[64,768]{1,0:T(8,128)(2,1)S(1)}, u32[]{:S(2)}, u32[]{:S(2)}) collective-permute-start(bf16[64,768]{1,0:T(8,128)(2,1)S(1)} %slice.93), channel_id=1, source_target_pairs={{0,8},{8,0},{16,24},{24,16},{1,9},{9,1},{17,25},{25,17},{2,10},{10... | collective-permute-start | bytes 294920 | tf_op jit(solution)/shard_map/ppermute | solution.py:49

commit v2 on v1

v2 whole, which is shorter than its diff:
```python
import functools

import jax
import jax.numpy as jnp
from jax import lax
from jax.experimental import pallas as pl
from jax.experimental.pallas import tpu as pltpu
from jax.sharding import PartitionSpec as P

F32 = jnp.float32
BF16 = jnp.bfloat16
OFFSETS = 4
REACH = 5
SPAN = 8
EXTRA = 16
HALVINGS = 2
EDGE = 3
VMEM_LIMIT = 16 * 1024 * 1024
LONG = 10**11
NT = (((1,), (1,)), ((), ()))
TN = (((0,), (0,)), ((), ()))
NN = (((1,), (0,)), ((), ()))


def dot(a, b, dims=NN, precision=None):
    return lax.dot_general(a, b, dims, precision=precision, preferred_element_type=F32)


def exact(a, b, dims=NN):
    return dot(a, b, dims, lax.Precision.HIGHEST)


def call(kernel, outs, *operands, scratch=(), cost=0, name=None, after=(), final=False):
    vmem = pl.BlockSpec(memory_space=pltpu.VMEM)
    hbm = pl.BlockSpec(memory_space=pltpu.HBM)
    stored = [isinstance(operand, tuple) for operand in operands]
    held = [
        pltpu.with_memory_space_constraint(operand[0] if far else operand, pltpu.HBM if far else pltpu.VMEM)
        for operand, far in zip(operands, stored)
    ]
    count = len(operands)

    def run(*refs):
        kernel(*refs[:count], *refs[count + len(after) :])

    return pl.pallas_call(
        run if after else kernel,
        out_shape=[jax.ShapeDtypeStruct(*o) if final else pltpu.VMEM(*o) for o in outs],
        in_specs=[hbm if far else vmem for far in stored] + [pl.BlockSpec(memory_space=pl.ANY)] * len(after),
        out_specs=[vmem] * len(outs),
        scratch_shapes=list(scratch),
        compiler_params=pltpu.CompilerParams(vmem_limit_bytes=VMEM_LIMIT),
        cost_estimate=pl.CostEstimate(flops=cost, bytes_accessed=0, transcendentals=0),
        name=name,
    )(*held, *after)


def swap(value, axis, bit):
    count = lax.axis_size(axis)
    return lax.ppermute(value, axis, [(i, i ^ bit) for i in range(count)])


def gather_slots(value, axis, bits):
    slots = {0: value}
    for bit in bits:
        for m in list(slots):
            slots[m | bit] = swap(slots[m], axis, bit)
    return slots


def row_index():
    return lax.axis_index("rows")


def group_index():
    return lax.axis_index("rows") // (lax.axis_size("rows") // OFFSETS)


def piece_index():
    return lax.axis_index("tract") % (1 << HALVINGS)


def load_kernel(rows, *refs):
    weight, table, score, bias = refs[:4]
    ids = refs[4:7]
    weight_low, table_low, score_here, bias_here, together, tail = refs[7:13]
    weight_here, table_here, ids_here, sems = refs[13:]
    parts = weight_here.shape[0]
    size = weight_here.shape[1]
    copies = [pltpu.make_async_copy(source, ids_here.at[at], sems.at[at]) for at, source in enumerate(ids)]
    copies.append(pltpu.make_async_copy(table, table_here, sems.at[3]))
    copies.append(pltpu.make_async_copy(score, score_here, sems.at[4]))
    copies.append(pltpu.make_async_copy(bias, bias_here, sems.at[5]))
    copies += [
        pltpu.make_async_copy(weight.at[pl.ds(at * size, size), :], weight_here.at[at], sems.at[6 + at]) for at in range(parts)
    ]
    for copy in copies:
        copy.start()
    length = ids_here.shape[2]
    for at in range(3):
        copies[at].wait()
        together[at * rows : (at + 1) * rows, :] = ids_here[at].astype(F32)
        tail[at * rows : (at + 1) * rows, :] = ids_here[at, :, length - tail.shape[1] :]
    copies[3].wait()
    table_low[...] = table_here[...].astype(BF16)
    copies[4].wait()
    copies[5].wait()
    for at in range(parts):
        copies[6 + at].wait()
        weight_low[at * size : (at + 1) * size, :] = weight_here[at].astype(BF16)


def kept_kernel(*refs):
    half = len(refs) // 2
    for value, out in zip(refs[:half], refs[half:]):
        out[...] = value[...]


def placed(parts, width):
    total = None
    for part, at in parts:
        shard = part.shape[1]
        source = lax.broadcasted_iota(jnp.int32, (shard, width), 0) + at * shard
        column = lax.broadcasted_iota(jnp.int32, (shard, width), 1)
        row = jnp.broadcast_to(part[...], (8, shard)).astype(BF16)
        got = dot(row, (source == column).astype(BF16))
        total = got if total is None else total + got
    return total


def scorer_kernel(order, near_order, *refs):
    scores = refs[: len(order)]
    biases = refs[len(order) : len(order) + len(near_order)]
    weight_low, scorer, out = refs[len(order) + len(near_order) :]
    width = out.shape[1]
    full = placed([(part, row_index() ^ m) for part, m in zip(scores, order)], width)
    bias = placed([(part, row_index() ^ m) for part, m in zip(biases, near_order)], width)
    full = jnp.concatenate([full, full], 0).astype(BF16)
    scorer[...] = full
    at = lax.broadcasted_iota(jnp.int32, bias.shape, 0)
    out[...] = jnp.where(at == 0, dot(full, weight_low[...], NT)[:8], bias)


def table_kernel(order, *refs):
    slots = refs[: len(order)]
    weight_low, product, table_low, table_turned = refs[len(order) :]
    rows = slots[0].shape[0]
    for slot, m in zip(slots, order):
        at = pl.multiple_of((row_index() ^ m) * rows, rows)
        table_low[pl.ds(at, rows), :] = slot[...].astype(BF16)
    product[...] = dot(table_low[...], weight_low[...]).astype(BF16)
    table_turned[...] = table_low[...].T


def planes_kernel(ids, before, out, hot):
    length = ids.shape[1]
    rows = ids.shape[0] // 3
    half = length // 2
    tail = before.shape[1]
    ids = ids[...].astype(BF16)
    earlier = before[...].astype(F32).astype(BF16)
    for m in range(SPAN):
        target = 2 * lax.broadcasted_iota(jnp.int32, (length, half), 1) + 1 - m
        source = lax.broadcasted_iota(jnp.int32, (length, half), 0)
        got = dot(ids, (source == target).astype(BF16))
        if m > 1:
            target = 2 * lax.broadcasted_iota(jnp.int32, (tail, half), 1) + 1 - m + tail
            source = lax.broadcasted_iota(jnp.int32, (tail, half), 0)
            got = got + dot(earlier, (source == target).astype(BF16))
        out[:, m * half : (m + 1) * half] = got
    values = hot.shape[0]
    name = names(values, half)
    for side in range(2):
        for row in range(rows):
            code = out[row : row + 1, side * half : (side + 1) * half]
            hot[:, (side * rows + row) * half : (side * rows + row + 1) * half] = one_hot(name, code)
    edge = gathered_edges([out[:rows, (SPAN - 2 + side) * half : (SPAN - 1 + side) * half] for side in range(2)])
    hot[:, 2 * rows * half :] = one_hot(name, edge)


def names(values, lanes):
    shape = (values // 16, 16, lanes)
    return (lax.broadcasted_iota(jnp.int32, shape, 0) * 16 + lax.broadcasted_iota(jnp.int32, shape, 1)).astype(F32).astype(BF16)


def one_hot(name, code):
    code = jnp.broadcast_to(code, name.shape[1:]).astype(BF16)
    return jnp.where(name == code[None], jnp.ones(name.shape, BF16), jnp.zeros(name.shape, BF16)).reshape(-1, name.shape[2])


def gathered_edges(planes):
    rows, lanes = planes[0].shape
    lane = lax.broadcasted_iota(jnp.int32, (rows, lanes), 1)
    row = lax.broadcasted_iota(jnp.int32, (rows, lanes), 0)
    total = jnp.zeros((rows, lanes), F32)
    for side, plane in enumerate(planes):
        for at in range(EDGE):
            place = (side * rows + row) * EDGE + at
            total = total + jnp.where(lane == place, plane[:, at : at + 1], 0.0)
    return jnp.sum(total, 0, keepdims=True)


class Window:
    def __init__(self, mask):
        self.mask = mask
        self.keep, self.divide = [], []
        for side in range(2):
            keep = [self.mask[k, side] for k in range(OFFSETS)]
            counts, total = [], 0.0
            for k in range(OFFSETS):
                total = total + keep[k]
                counts.append(1.0 / jnp.maximum(total, 1.0))
            self.keep.append(keep)
            self.divide.append(counts)

    def pooled(self, side, values):
        means, total = [], 0.0
        for k in range(OFFSETS):
            total = total + self.keep[side][k] * values[side + k]
            means.append(total * self.divide[side][k])
        return means

    def spread(self, sides):
        result = [0.0] * REACH
        for side in range(2):
            carried = 0.0
            for k in reversed(range(OFFSETS)):
                carried = carried + sides[side][k] * self.divide[side][k]
                result[side + k] = result[side + k] + self.keep[side][k] * carried
        return result


def window_of(planes, rows):
    half = planes.shape[1] // SPAN

    def part(which, m):
        return planes[which * rows : (which + 1) * rows, m * half : (m + 1) * half]

    segments = [part(1, m) for m in range(SPAN)]
    valid = [part(2, m) for m in range(SPAN)]
    mask = {
        (k, j): (segments[j + k] == segments[j]).astype(F32) * valid[j + k]
        for k in range(OFFSETS)
        for j in range(REACH)
    }
    return [part(0, m) for m in range(SPAN)], Window(mask)


CODES = 0
WEIGHTS = CODES + SPAN
MASKS = WEIGHTS + OFFSETS * REACH
PROBS = MASKS + OFFSETS * REACH
AVERAGE = PROBS + 2 * OFFSETS
PLANES = AVERAGE + 1


def lookup(row, codes):
    index = codes.astype(jnp.int32)
    lanes = 128
    low = jnp.bitwise_and(index, lanes - 1)
    parts = [
        jnp.take_along_axis(
            jnp.broadcast_to(row[:, at : at + lanes], codes.shape), low, axis=1
        )
        for at in range(0, row.shape[1], lanes)
    ]
    return jnp.where(index >= lanes, parts[1], parts[0])


def packed_row(ref, plane, row):
    return jnp.broadcast_to(ref[plane, pl.ds(row, 1), :], (16, ref.shape[2])).astype(BF16)


def spread_rows(plan, k, row, values):
    lanes = plan.shape[2]
    blocks = values // 16
    name = names(values, lanes)
    total = jnp.zeros((blocks, 16, lanes), BF16)
    for j in range(REACH):
        code = packed_row(plan, CODES + k + j, row)
        weight = packed_row(plan, WEIGHTS + k * REACH + j, row)
        total = jnp.where(name == code[None], total + weight[None], total)
    return total.reshape(values, lanes)


def accumulate(plan, total_ref, ks, cot, values, extra=None):
    rows, half = plan.shape[1:]
    for chunk in range(rows // 2):
        pieces = [
            jnp.concatenate(
                [
                    spread_rows(plan, k, 2 * chunk, values),
                    spread_rows(plan, k, 2 * chunk + 1, values),
                ],
                1,
            )
            for k in ks
        ]
        if extra is not None:
            pieces.append(extra(chunk))
        left = jnp.concatenate(pieces, 0)
        part = dot(left, cot[2 * chunk * half : 2 * (chunk + 1) * half, :])
        if chunk == 0:
            total_ref[...] = part
        else:
            total_ref[...] += part


def split(value):
    high = value.astype(BF16)
    return high, (value - high.astype(F32)).astype(BF16)


def thirds(value):
    high = value.astype(BF16)
    rest = value - high.astype(F32)
    middle = rest.astype(BF16)
    return high, middle, (rest - middle.astype(F32)).astype(BF16)


def far_kernel(order, slots, values, *refs):
    scorers = refs[: len(order)]
    table_low, planes, scorer, cot = refs[len(order) : len(order) + 4]
    own, sent, sent_too, plan, vectors, table, total = refs[len(order) + 4 :]
    rows = plan.shape[1]
    every = jnp.concatenate([s[...] for s in scorers], 0)
    parts = thirds(every)
    found = dot(jnp.concatenate(parts, 0), table_low[...], NT)
    count = every.shape[0]
    found = found[:count] + found[count : 2 * count] + found[2 * count :]
    for at, m in enumerate(order):
        table[group_index() ^ m] = found[at * 8 : (at + 1) * 8]
    codes, window = window_of(planes[...], rows)
    bias = functools.reduce(jnp.add, [s[1:2] for s in scorers])
    both = [scorer[:8].astype(F32), jnp.broadcast_to(bias, (8, bias.shape[1]))]
    vectors[...] = jnp.concatenate(both, 0).astype(BF16)
    shared = jnp.sum(both[0] * both[1], 1, keepdims=True)[:1]
    conv_scores = [shared] * REACH
    for k in range(OFFSETS):
        row = table[k, :1, :]
        for m in range(k, k + REACH):
            conv_scores[m - k] = conv_scores[m - k] + window.mask[k, m - k] * lookup(row, codes[m])
    for m in range(SPAN):
        plan[CODES + m] = codes[m]
    shares = []
    for side in range(2):
        block = window.pooled(side, conv_scores)
        top = functools.reduce(jnp.maximum, block)
        exps = [jnp.exp(b - top) for b in block]
        inverse = 1.0 / functools.reduce(jnp.add, exps)
        shares.append([e * inverse for e in exps])
        for k in range(OFFSETS):
            plan[PROBS + side * OFFSETS + k] = shares[side][k]
    mixing = [0.5 * e for e in window.spread(shares)]
    plan[AVERAGE] = functools.reduce(jnp.add, mixing)
    for k in range(OFFSETS):
        for j in range(REACH):
            plan[MASKS + k * REACH + j] = window.mask[k, j]
            plan[WEIGHTS + k * REACH + j] = window.mask[k, j] * mixing[j]
    accumulate(plan, total, [group_index() ^ m for m in slots], cot, values)
    own[...] = total[:values]
    sent[...] = total[values : values + values // 2].astype(BF16)
    sent_too[...] = total[values + values // 2 : 2 * values].astype(BF16)


def average_line(plan, chunk):
    return jnp.concatenate([plan[AVERAGE, row : row + 1, :] for row in (2 * chunk, 2 * chunk + 1)], 1)


def near_kernel(slots, values, plan, cot, own, sent, bias_out, total):
    half = plan.shape[2]

    def extra(chunk):
        line = jnp.broadcast_to(average_line(plan, chunk), (EXTRA, 2 * half))
        high, low = split(line)
        at = lax.broadcasted_iota(jnp.int32, line.shape, 0)
        return jnp.where(at == 0, high.astype(F32), jnp.where(at == 1, low.astype(F32), 0.0)).astype(BF16)

    accumulate(plan, total, [group_index() ^ m for m in slots], cot, values, extra)
    own[...] = total[:values]
    sent[...] = total[values : 2 * values].astype(BF16)
    end = total[len(slots) * values :]
    bias_out[...] = jnp.broadcast_to(end[:1] + end[1:2], (8, end.shape[1]))


def inner_kernel(order, values, *refs):
    products = refs[: len(order)]
    plan, vectors, cot = refs[len(order) : len(order) + 3]
    before, out = (refs[-2] if len(refs) > len(order) + 4 else None), refs[-1]
    rows, half = plan.shape[1:]
    blocks = values // 16
    name = names(values, half)
    for chunk in range(rows // 2):
        here = cot[2 * chunk * half : 2 * (chunk + 1) * half, :]
        base = dot(vectors[8:], here, NT) if before is None else None
        found = {}
        for slot, m in zip(products, order):
            k = group_index() ^ m
            each = dot(slot[...], here, NT).astype(BF16)
            for side in range(2):
                row = 2 * chunk + side
                mine = each[:, side * half : (side + 1) * half].reshape(blocks, 16, half)
                for j in range(REACH):
                    code = packed_row(plan, CODES + k + j, row)
                    picked = jnp.zeros((16, half), BF16)
                    for at in range(blocks):
                        picked = jnp.where(name[at] == code, mine[at], picked)
                    mask = plan[MASKS + k * REACH + j, row : row + 1, :]
                    found[j, side] = found.get((j, side), 0.0) + picked.astype(F32) * mask
        for side in range(2):
            row = 2 * chunk + side
            for j in range(REACH):
                if before is None:
                    start = base[:1, side * half : (side + 1) * half]
                else:
                    start = before[j, row : row + 1, :]
                out[j, row : row + 1, :] = jnp.sum(found[j, side], 0, keepdims=True) + start


def score_kernel(order, values, *refs):
    products = refs[: len(order)]
    inner_ref, plan, vectors, hot = refs[len(order) : len(order) + 4]
    out, flat, rows_ref = refs[len(order) + 4 :]
    rows, half = plan.shape[1:]
    biases = vectors[8:]
    window = Window({(k, j): plan[MASKS + k * REACH + j] for k in range(OFFSETS) for j in range(REACH)})
    inner_rows = [0.5 * inner_ref[j] for j in range(REACH)]
    sides = []
    for side in range(2):
        inner = window.pooled(side, inner_rows)
        share = [plan[PROBS + side * OFFSETS + k] for k in range(OFFSETS)]
        mean = functools.reduce(jnp.add, [s * i for s, i in zip(share, inner)])
        sides.append([s * (i - mean) for s, i in zip(share, inner)])
    grads = window.spread(sides)
    overall = jnp.sum(jnp.sum(functools.reduce(jnp.add, grads), 1, keepdims=True), 0, keepdims=True)
    lane = lax.broadcasted_iota(jnp.int32, (rows, half), 1)
    flat[...] = jnp.zeros(flat.shape, F32)
    for k in range(OFFSETS):
        edges = []
        for side in range(2):
            inside = jnp.zeros((rows, half), F32)
            edge = jnp.zeros((rows, half), F32)
            for m in range(side, SPAN, 2):
                if not 0 <= m - k < REACH:
                    continue
                value = grads[m - k] * window.mask[k, m - k]
                steps = m // 2
                if steps:
                    inside = inside + jnp.where(lane < half - steps, pltpu.roll(value, half - steps, 1), 0.0)
                    moved = pltpu.roll(value, EDGE - steps, 1) if steps < EDGE else value
                    edge = edge + jnp.where((lane >= EDGE - steps) & (lane < EDGE), moved, 0.0)
                else:
                    inside = inside + value
            for row in range(rows):
                at = (side * rows + row) * half
                flat[k : k + 1, at : at + half] = inside[row : row + 1, :]
            edges.append(edge)
        flat[k : k + 1, 2 * rows * half :] = gathered_edges(edges)
    high, low = split(flat[...])
    both = jnp.concatenate([high.astype(F32), low.astype(F32)], 0).astype(BF16)
    lines = dot(both, hot[...], NT)
    lines = lines[:8] + lines[8:]
    for k in range(OFFSETS):
        rows_ref[k] = jnp.broadcast_to(lines[k : k + 1], (8, values))
    width = biases.shape[1]
    score_grad = jnp.zeros((1, width), F32)
    for slot, m in zip(products, order):
        got = dot(pack(rows_ref[group_index() ^ m]), slot[...])
        score_grad = score_grad + got[:1] + got[8:9]
    out[...] = jnp.zeros(out.shape, F32)
    out[:1] = score_grad + overall * biases[:1].astype(F32)
    out[1:2] = overall * vectors[:1].astype(F32)
    for k in range(OFFSETS):
        out[2 + k : 3 + k, :values] = lines[k : k + 1]


def output_kernel(order, values, chunks_here, *refs):
    products = refs[: len(order)]
    plan, vectors = refs[len(order) : len(order) + 2]
    out, token, staged, sems = refs[-4:]
    token[...] = jnp.zeros(token.shape, F32)
    half = plan.shape[2]
    step = 2 * half
    biases = vectors[8:].astype(F32)
    at = lax.broadcasted_iota(jnp.int32, (8, step), 0)
    first = lax.broadcasted_iota(jnp.int32, biases.shape, 0)
    biases = jnp.where(first < 2, biases, 0.0)
    copies = []
    for place, chunk in enumerate(chunks_here):
        high, low = split(jnp.broadcast_to(average_line(plan, chunk), (8, step)))
        both = jnp.where(at == 0, high.astype(F32), jnp.where(at == 1, low.astype(F32), 0.0))
        total = dot(both, biases, TN)
        for slot, m in zip(products, order):
            k = group_index() ^ m
            left = jnp.concatenate([spread_rows(plan, k, row, values) for row in (2 * chunk, 2 * chunk + 1)], 1)
            total = total + dot(left, slot[...], TN)
        staged[place * step : (place + 1) * step, :] = total.astype(BF16)
        copies.append(
            pltpu.make_async_copy(
                staged.at[pl.ds(place * step, step), :], out.at[pl.ds(chunk * step, step), :], sems.at[place]
            )
        )
        copies[-1].start()
    for copy in copies:
        copy.wait()


def output_part(before, part, parts, order, values, products, plan, vectors, after):
    rows, half = plan.shape[1:]
    width = vectors.shape[1]
    each = rows // 2 // parts
    operands = [pltpu.with_memory_space_constraint(x, pltpu.VMEM) for x in (*products, plan, vectors)]
    operands += [] if before is None else [pltpu.with_memory_space_constraint(before, pltpu.HBM)]
    vmem = pl.BlockSpec(memory_space=pltpu.VMEM)
    elsewhere = pl.BlockSpec(memory_space=pl.ANY)
    count = len(products) + 2
    chunks_here = range(part * each, (part + 1) * each)

    def run(*refs):
        output_kernel(order, values, chunks_here, *refs[:count], *refs[-4:])

    return pl.pallas_call(
        run,
        out_shape=[jax.ShapeDtypeStruct((rows * half, width), BF16), pltpu.VMEM((8, 128), F32)],
        in_specs=[vmem] * count + [elsewhere] * (len(operands) - count + len(after)),
        out_specs=[elsewhere, vmem],
        input_output_aliases={} if before is None else {count: 0},
        scratch_shapes=[pltpu.VMEM((2 * half * each, width), BF16), pltpu.SemaphoreType.DMA((each,))],
        compiler_params=pltpu.CompilerParams(vmem_limit_bytes=VMEM_LIMIT),
        cost_estimate=pl.CostEstimate(flops=0, bytes_accessed=0, transcendentals=0),
        name="output",
    )(*operands, *after)


def reversed_bits(number, bits):
    return sum((((number >> b) & 1) << (bits - 1 - b)) for b in range(bits))


def chunks(bits, values, piece, group):
    block = values // OFFSETS
    size = block >> bits
    for actual in range(1 << bits):
        place = reversed_bits(piece ^ actual, bits) * OFFSETS * size
        for offset in range(OFFSETS):
            at = pl.multiple_of(place + (group ^ offset) * size, size)
            yield offset * block + actual * size, at, size


def pack(rows):
    high, low = split(rows)
    return jnp.concatenate([high.astype(F32), low.astype(F32)], 0).astype(BF16)


def unpack(block):
    return block[:8].astype(F32) + block[8:].astype(F32)


def merge_kernel(bits, near, near_other, far_other, sums, bias, keep, send, total):
    values = near.shape[0]
    summed = near[...] + near_other[...].astype(F32) + far_other[...].astype(F32)
    for source, at, size in chunks(bits, values, piece_index(), group_index()):
        total[pl.ds(at, size), :] = summed[source : source + size]
    part = keep.shape[0]
    keep[...] = total[:part]
    send[: values - part] = total[values - (values - part) :].astype(BF16)
    second = lax.broadcasted_iota(jnp.int32, bias.shape, 0) == 1
    send[values - part :] = pack(sums[...] + jnp.where(second, bias[...], 0.0))


def halve_kernel(mine, own_sent, other, keep, send):
    rows = mine.shape[0]
    total = mine[...] + other[:rows].astype(F32)
    part = keep.shape[0]
    keep[...] = total[:part]
    rest = send.shape[0] - EXTRA
    send[:rest] = total[rows - rest :].astype(BF16)
    send[rest:] = pack(unpack(own_sent[own_sent.shape[0] - EXTRA :]) + unpack(other[rows:]))


def whole_kernel(mine, other, send):
    rows = mine.shape[0] - EXTRA
    send[:rows] = (mine[:rows].astype(F32) + other[:rows].astype(F32)).astype(BF16)
    send[rows:] = pack(unpack(mine[rows:]) + unpack(other[rows:]))


def last_kernel(mine, other, block, sums):
    rows = block.shape[0]
    block[...] = (mine[:rows].astype(F32) + other[:rows].astype(F32)).astype(BF16)
    sums[...] = unpack(mine[rows:]) + unpack(other[rows:])


def share_kernel(block, sums, weight_low, keep, *sends):
    product = dot(block[...], weight_low[...], NT)
    rows = keep.shape[0]
    keep[...] = product[:rows]
    for at, send in enumerate(sends):
        send[:rows] = product[(at + 1) * rows : (at + 2) * rows].astype(BF16)
        send[rows:] = pack(sums[...])


def combine_kernel(keep, sums, *refs):
    others, (out, total) = refs[:-2], refs[-2:]
    rows = keep.shape[0]
    out[...] = functools.reduce(jnp.add, [keep[...]] + [o[:rows].astype(F32) for o in others]).astype(BF16)
    total[...] = functools.reduce(jnp.add, [sums[...]] + [unpack(o[rows:]) for o in others])


def added_kernel(mine, other, out):
    out[...] = (mine[...].astype(F32) + other[...].astype(F32)).astype(out.dtype)


def joined_kernel(mine, one, two, out):
    rows = one.shape[0]
    out[:rows] = (mine[:rows] + one[...].astype(F32)).astype(out.dtype)
    out[rows:] = (mine[rows:] + two[...].astype(F32)).astype(out.dtype)


def weight_kernel(bits, order, *refs):
    slots = refs[: len(order)]
    turned, vectors, sums, out, token, full = refs[len(order) :]
    token[...] = jnp.zeros(token.shape, F32)
    values = full.shape[0]
    placed = {m: slot for m, slot in zip(order, slots)}
    size = values // OFFSETS >> bits
    for m in range(1 << bits):
        for offset in range(OFFSETS):
            at = (group_index() ^ offset) * (values // OFFSETS) + (piece_index() ^ m) * size
            full[pl.ds(pl.multiple_of(at, size), size), :] = placed[m][offset * size : (offset + 1) * size]
    line = sums[pl.ds(group_index() + 2, 1), :values]
    scores = jnp.concatenate([vectors[:8], vectors[:8]], 0)
    first = lax.broadcasted_iota(jnp.int32, (8, values), 0) == 0
    through = dot(turned[...], pack(jnp.where(first, jnp.broadcast_to(line, first.shape), 0.0)), NT)
    high, low = split(through)
    out[...] = dot(turned[...], full[...]) + dot(high, scores) + dot(low, scores)


def table_grad_kernel(bits, order, offsets, *refs):
    slots = refs[: len(order)]
    scorers = refs[len(order) : len(order) + len(offsets)]
    sums, out, score_out, bias_out, table, full, rows_ref = refs[len(order) + len(offsets) :]
    values = full.shape[0]
    width = out.shape[1]
    high, low = split(sums[2 : 2 + OFFSETS, :values])
    for scorer, m in zip(scorers, offsets):
        rows_ref[group_index() ^ m] = scorer[...]
    right = jnp.concatenate([rows_ref[k, :1] for k in range(OFFSETS)], 0)
    right_high, right_low = split(right)
    left = jnp.concatenate([x.astype(F32) for x in (high, low, high, low)], 0).astype(BF16)
    right = jnp.concatenate([x.astype(F32) for x in (right_high, right_high, right_low, right_low)], 0).astype(BF16)
    full[...] = dot(left, right, TN)
    for slot, m in zip(slots, order):
        size = slot.shape[0]
        table[pl.ds(pl.multiple_of((piece_index() ^ m) * size, size), size), :] = slot[...].astype(F32)
    rows = out.shape[0]
    at = pl.multiple_of(row_index() * rows, rows)
    inside = row_index() * rows - group_index() * table.shape[0]
    out[...] = table[pl.ds(pl.multiple_of(inside, rows), rows), :] + full[pl.ds(at, rows), :]
    shard = score_out.shape[1]
    source = lax.broadcasted_iota(jnp.int32, (width, shard), 0)
    column = lax.broadcasted_iota(jnp.int32, (width, shard), 1) + row_index() * shard
    here = (source == column).astype(BF16)
    ends = functools.reduce(jnp.add, [dot(part, here) for part in thirds(sums[...])])
    score_out[...] = ends[:1]
    bias_out[...] = ends[1:2]


def bits_of(count):
    return [1 << at for at in reversed(range(count.bit_length() - 1))]


def body(byte_values, segment_ids, valid, table, conv_weight, conv_bias, score_weight, cotangent):
    rows_count, tract_count = lax.axis_size("rows"), lax.axis_size("tract")
    rows_at = lax.axis_index("rows")
    values, width = table.shape[0] * rows_count, table.shape[1]
    rows, length = byte_values.shape
    half = length // 2
    copies = rows_count // OFFSETS
    order = [0, 2, 1, 3]
    group_bits = [2 * copies, copies]
    near_bits = [bit for bit in bits_of(rows_count) if bit < copies]

    score_slots = gather_slots(score_weight[None], "rows", bits_of(rows_count))
    bias_slots = gather_slots(conv_bias[None], "rows", near_bits)
    weight = conv_weight
    if copies > 1:
        near_by = [[g * copies + c for c in range(copies)] for g in range(OFFSETS)]
        weight = lax.all_gather(conv_weight, "rows", axis=0, tiled=True, axis_index_groups=near_by)
    parts = 4
    shard = (1, conv_bias.shape[0])
    weight_low, shard_low, score_slots[0], bias_slots[0], ids, tail = call(
        functools.partial(load_kernel, rows),
        [(weight.shape, BF16), (table.shape, BF16), (shard, F32), (shard, F32), ((3 * rows, length), F32),
         ((3 * rows, 128), jnp.int32)],
        (weight,), (table,), (score_weight[None],), (conv_bias[None],), (byte_values,), (segment_ids,), (valid,),
        scratch=[pltpu.VMEM((parts, weight.shape[0] // parts, width), F32), pltpu.VMEM(table.shape, F32),
                 pltpu.VMEM((3, rows, length), jnp.int32), pltpu.SemaphoreType.DMA((6 + parts,))],
        name="load",
    )
    scorer, scored = call(
        functools.partial(scorer_kernel, list(score_slots), list(bias_slots)),
        [((EXTRA, width), BF16), ((8, width), F32)], *score_slots.values(), *bias_slots.values(), weight_low, name="scorer",
    )
    scorers = gather_slots(scored, "rows", group_bits)
    scorers = [scorers[m * copies] for m in order]
    tail = call(kept_kernel, [(tail.shape, jnp.int32)], tail, name="tail", after=[scored])[0]
    before = lax.ppermute(tail, "tract", [(i, i + 1) for i in range(tract_count - 1)])
    planes, hot = call(
        planes_kernel, [((3 * rows, SPAN * half), F32), ((values, 2 * rows * half + 128), BF16)],
        ids, before, name="planes", after=[scored],
    )
    table_slots = {0: shard_low}
    for bit in bits_of(rows_count):
        for m in list(table_slots):
            value = table_slots[m]
            if m:
                value = call(kept_kernel, [(table.shape, BF16)], value, name="table_low", after=[planes, scorers[1]])[0]
            table_slots[m | bit] = swap(value, "rows", bit)
    product, table_low, turned = call(
        functools.partial(table_kernel, list(table_slots)),
        [((values, width), BF16), ((values, width), BF16), ((width, values), BF16)],
        *table_slots.values(), weight_low, name="products", after=[scored],
    )

    cot = cotangent.reshape(rows * half, width)
    far, *far_sent, plan, vectors = call(
        functools.partial(far_kernel, order, [2, 3], values),
        [((values, width), F32), ((values // 2, width), BF16), ((values // 2, width), BF16), ((PLANES, rows, half), F32), ((EXTRA, width), BF16)],
        *scorers, table_low, planes, scorer, cot,
        scratch=[pltpu.VMEM((OFFSETS, 8, values), F32), pltpu.VMEM((2 * values, width), F32)], name="far",
    )
    far_sent = [swap(half_sent, "rows", copies) for half_sent in far_sent]
    far = call(joined_kernel, [((values, width), BF16)], far, *far_sent, name="far_sum")[0]
    far_other = swap(far, "rows", 2 * copies)
    near, near_sent, bias_part = call(
        functools.partial(near_kernel, [0, 1], values),
        [((values, width), F32), ((values, width), BF16), ((8, width), F32)], plan, cot,
        scratch=[pltpu.VMEM((2 * values + EXTRA, width), F32)], name="near", after=[far],
    )
    near_other = swap(near_sent, "rows", copies)

    products = {0: product, 1: swap(product, "rows", copies), 2: swap(product, "rows", 2 * copies)}
    inner = call(
        functools.partial(inner_kernel, [0, 1], values), [((REACH, rows, half), F32)],
        products[0], products[1], plan, vectors, cot, name="inner_near", after=[near_sent], cost=LONG,
    )[0]
    passed = call(kept_kernel, [((values, width), BF16)], products[2], name="passed", after=[near_sent])[0]
    products[3] = swap(passed, "rows", copies)
    inner = call(
        functools.partial(inner_kernel, [2, 3], values), [((REACH, rows, half), F32)],
        products[2], products[3], plan, vectors, cot, inner, name="inner_far",
    )[0]
    products = [products[m] for m in order]
    sums = call(
        functools.partial(score_kernel, order, values), [((8, width), F32)], *products, inner, plan, vectors, hot,
        scratch=[pltpu.VMEM((8, hot.shape[1]), F32), pltpu.VMEM((OFFSETS, 8, values), F32)], name="scores",
    )[0]

    exchanges = [("tract", 1 << at) for at in range(tract_count.bit_length() - 1)]
    exchanges += [("rows", 1 << at) for at in range(copies.bit_length() - 1)]
    halved, rest = exchanges[:HALVINGS], exchanges[HALVINGS:]
    size = values // 2
    keep, send = call(
        functools.partial(merge_kernel, HALVINGS), [((size, width), F32), ((size + EXTRA, width), BF16)],
        near, near_other, far_other, sums, bias_part, scratch=[pltpu.VMEM((values, width), F32)], name="merge",
    )
    out = None

    def fill(out, parts, after):
        for part in parts:
            out, token = output_part(out, part, 4, order, values, products, plan, vectors, after)
        return out, token

    for at, (axis, bit) in enumerate(halved):
        other = swap(send, axis, bit)
        out, token = fill(out, [0, 1] if at == 0 else [2], [send])
        last = at + 1 == HALVINGS
        size = size if last else size // 2
        keep, send = call(
            halve_kernel, [((size, width), F32), ((size + EXTRA, width), BF16)], keep, send, other, name="halve", after=[token],
        )
    out, token = fill(out, [3], [send])
    for axis, bit in rest[:-1]:
        other = swap(send, axis, bit)
        send = call(whole_kernel, [(send.shape, BF16)], send, other, name="whole")[0]
    other = swap(send, *rest[-1])
    block, sums = call(last_kernel, [((size, width), BF16), ((8, width), F32)], send, other, name="last", after=[token])

    part = size // OFFSETS
    table_keep, *table_sends = call(
        share_kernel, [((part, width), F32)] + [((part + EXTRA, width), BF16)] * (OFFSETS - 1), block, sums, weight_low, name="share",
    )
    table_others = [swap(send, "rows", (at + 1) * copies) for at, send in enumerate(table_sends)]
    blocks = {0: block} | {m: swap(block, "tract", m) for m in range(1, 1 << HALVINGS)}
    table_piece, sums = call(
        combine_kernel, [((part, width), BF16), ((8, width), F32)], table_keep, sums, *table_others, name="combine",
    )
    table_pieces = {0: table_piece} | {m: swap(table_piece, "tract", m) for m in range(1, 1 << HALVINGS)}
    if copies > 1:
        turned = lax.dynamic_slice_in_dim(turned, rows_at % copies * (width // copies), width // copies, 0)
    weight_grad, token = call(
        functools.partial(weight_kernel, HALVINGS, list(blocks)), [((conv_weight.shape[0], width), F32), ((8, 128), F32)],
        *blocks.values(), turned, vectors, sums, scratch=[pltpu.VMEM((values, width), BF16)], name="weights", final=True,
    )
    table_grad, score_grad, bias_grad = call(
        functools.partial(table_grad_kernel, HALVINGS, list(table_pieces), order),
        [(table.shape, F32), (shard, F32), (shard, F32)], *table_pieces.values(), *scorers, sums,
        scratch=[pltpu.VMEM((values // OFFSETS, width), F32), pltpu.VMEM((values, width), F32), pltpu.VMEM((OFFSETS, 8, width), F32)],
        name="table_grad", final=True, after=[token],
    )
    return out.reshape(cotangent.shape), table_grad, weight_grad, bias_grad[0], score_grad[0]


def solution(mesh):
    return jax.shard_map(
        body,
        mesh=mesh,
        in_specs=(
            P("rows", "tract"), P("rows", "tract"), P("rows", "tract"), P("rows", None),
            P("rows", None), P("rows"), P("rows"), P("rows", "tract", None),
        ),
        out_specs=(P("rows", "tract", None), P("rows", None), P("rows", None), P("rows"), P("rows")),
        check_vma=False,
    )
```

time: 132 us -> 77.1 us (0.58)
  Pallas kernels: 52.9 us -> 29.3 us
  local copies, waits for them, and re-layouts: 15.5 us -> 0.01 us
  waiting for transfers between devices: 31.1 us -> 21.9 us
  other arithmetic: 4.55 us -> 0 us
  starting transfers between devices: 26.5 us -> 24.9 us
    pallas_call x13 -> x25, Pallas kernels: 52.9 us -> 29.3 us  [the longest x21 20.4 us: call(): pl.pallas_call(run if after else kernel, out_shape=[jax.ShapeDtypeStruct(...]
    ppermute x23 -> x28, waiting for transfers between devices: 31.1 us -> 21.3 us  [swap(): return lax.ppermute(value, axis, [(i, i ^ bit) for i in range(count)])]
    unnamed x38 -> x2, local copies, waits for them, and re-layouts: 6.77 us -> 0.01 us
    slice x9 -> x0, local copies, waits for them, and re-layouts: 5.08 us -> none  [the longest x3 2.75 us: body(): other = swap(block[keep:], axis, bit)]
    squeeze x2 -> x0, local copies, waits for them, and re-layouts: 2.96 us -> none  [the longest x1 1.93 us: body(): near_other = swap(near[1], 'rows', copies)]
    convert_element_type x3 -> x0, other arithmetic: 1.95 us -> none  [the longest x1 0.74 us: body(): ends = block[-EXTRA:].astype(F32)]
    add x4 -> x0, other arithmetic: 1.78 us -> none  [the longest x2 1.66 us: body(): table_part = table_part[:keep].astype(F32) + other.astype(F32)]
    ppermute x23 -> x28, starting transfers between devices: 22.9 us -> 21.5 us  [swap(): return lax.ppermute(value, axis, [(i, i ^ bit) for i in range(count)])]
  transfers between devices with their start and end apart: 24 -> 29, of which waited for: 10 -> 16; matrix products, arithmetic and copies ran while one was open for 6% -> 0% of each run, Pallas kernels for 31% -> 31%
where the time goes in v2:
time: 77.1 us; the launch traced here: 77 us
  Pallas kernels  29.3 us (38%)
  starting transfers between devices  24.9 us (32%)
  waiting for transfers between devices  21.9 us (28%)
  between operations  0.85 us (1%)
    ppermute x28, starting transfers between devices, swap(): return lax.ppermute(value, axis, [(i, i ^ bit) for i in range(count)])  21.5 us
    ppermute x28, waiting for transfers between devices, swap(): return lax.ppermute(value, axis, [(i, i ^ bit) for i in range(count)])  21.3 us
    pallas_call x21, Pallas kernels, call(): pl.pallas_call(run if after else kernel, out_shape=[jax.ShapeDtypeStruct(...  20.4 us
    pallas_call x4, Pallas kernels, output_part(): pl.pallas_call(run, out_shape=[jax.ShapeDtypeStruct((rows * half, width),...  8.9 us
    ppermute x1, starting transfers between devices, body(): lax.ppermute(tail, 'tract', [(i, i + 1) for i in range(tract_count - 1)])  3.44 us
  transfers between devices with their start and end apart: 29, of which 16 were waited for; matrix products, arithmetic and copies ran while one was open for 0% of the time, Pallas kernels for 31%

profile of v2, /device:TPU:0, one launch (start us, length us, event | category | flops | bytes accessed | tf_op | source)
XLA Modules:
  0.0 77.0 jit_solution(16778812883147634343)
XLA Ops:
  0.6 2.0 %load.1 = (bf16[768,768]{1,0:T(8,128)(2,1)S(1)}, bf16[64,768]{1,0:T(8,128)(2,1)S(1)}, f32[1,192]{1,0:T(1,128)S(1)}, f32[1,192]{1,0:T(1,128)S(1)}, f32[48,256]{1,0:T(8,128)S(1)}, /*index=5*/s32[48,128]{1,0:T(8,128)S(1)}) custom-call(f32[768,768]{1,0:T(8,128)} %refs_0_.1, f32[64,768]{1,0:T(8,128)} %refs_1_.1, f32[1,192]{1,0:T(1,128)} %bitcast.12, ...), custom_call_target="tpu_custom_call" | custom-call | tf_op jit(solution)/shard_map/load/pallas_call | solution.py:46
  2.7 3.0 %collective-permute-start = (bf16[64,768]{1,0:T(8,128)(2,1)S(1)}, bf16[64,768]{1,0:T(8,128)(2,1)S(1)}, u32[]{:S(2)}, u32[]{:S(2)}) collective-permute-start(bf16[64,768]{1,0:T(8,128)(2,1)S(1)} %get-tuple-element.51.refs_0_), channel_id=1, source_target_pairs={{0,16},{8,24},{16,0},{24,8},{1,17},{9,25},{17,1},{25,9},{2,18},{10... | collective-permute-start | bytes 294920 | tf_op jit(solution)/shard_map/ppermute | solution.py:60
  5.7 0.1 collective-permute-start.2
  5.8 3.7 %collective-permute-done.2.refs_1_ = f32[1,192]{1,0:T(1,128)S(1)} collective-permute-done((f32[1,192]{1,0:T(1,128)}, f32[1,192]{1,0:T(1,128)S(1)}, u32[]{:S(2)}, u32[]{:S(2)}) %collective-permute-start.2) | collective-permute-done | bytes 800 | tf_op jit(solution)/shard_map/ppermute | solution.py:60
  9.5 0.0 collective-permute-start.4
  9.5 0.0 collective-permute-done.3.refs_2_
  9.5 1.1 %collective-permute-done.4.refs_3_ = f32[1,192]{1,0:T(1,128)S(1)} collective-permute-done((f32[1,192]{1,0:T(1,128)S(1)}, f32[1,192]{1,0:T(1,128)S(1)}, u32[]{:S(2)}, u32[]{:S(2)}) %collective-permute-start.4) | collective-permute-done | bytes 800 | tf_op jit(solution)/shard_map/ppermute | solution.py:60
  10.6 0.7 scorer.1
  11.3 3.4 %collective-permute-start.5 = (s32[48,128]{1,0:T(8,128)S(1)}, s32[48,128]{1,0:T(8,128)S(1)}, u32[]{:S(2)}, u32[]{:S(2)}) collective-permute-start(s32[48,128]{1,0:T(8,128)S(1)} %tail.1), channel_id=1, source_target_pairs={{0,1},{1,2},{2,3},{3,4},{4,5},{5,6},{6,7},{8,9},{9,10},{10,11},{11... | collective-permute-start | bytes 73736 | tf_op jit(solution)/shard_map/ppermute | solution.py:706
  14.7 0.9 %collective-permute-start.6 = (f32[8,768]{1,0:T(8,128)S(1)}, f32[8,768]{1,0:T(8,128)S(1)}, u32[]{:S(2)}, u32[]{:S(2)}) collective-permute-start(f32[8,768]{1,0:T(8,128)S(1)} %get-tuple-element.57.refs_1_.refs_2_.refs_5_.refs_0_.refs_4_), channel_id=1, source_target_pairs={{0,16},{8,24},{16,0},{24,8},{1,17},{9,25},{17,1},{25,9},{2,18},{10... | collective-permute-start | bytes 73736 | tf_op jit(solution)/shard_map/ppermute | solution.py:60
  15.7 0.0 collective-permute-start.1
  15.7 0.5 collective-permute-done.5.refs_1_
  16.2 0.6 planes.1
  16.8 1.8 %collective-permute-done.6.refs_2_.refs_1_.refs_5_ = f32[8,768]{1,0:T(8,128)S(1)} collective-permute-done((f32[8,768]{1,0:T(8,128)S(1)}, f32[8,768]{1,0:T(8,128)S(1)}, u32[]{:S(2)}, u32[]{:S(2)}) %collective-permute-start.6) | collective-permute-done | bytes 24608 | tf_op jit(solution)/shard_map/ppermute | solution.py:60
  18.6 0.1 collective-permute-start.7
  18.7 1.3 %collective-permute-done.7.refs_3_ = bf16[64,768]{1,0:T(8,128)(2,1)S(1)} collective-permute-done((bf16[64,768]{1,0:T(8,128)(2,1)S(1)}, bf16[64,768]{1,0:T(8,128)(2,1)S(1)}, u32[]{:S(2)}, u32[]{:S(2)}) %collective-permute-start.7) | collective-permute-done | bytes 98336 | tf_op jit(solution)/shard_map/ppermute | solution.py:60
  20.0 0.5 products.1
  20.5 0.9 %collective-permute-start.8 = (bf16[256,768]{1,0:T(8,128)(2,1)S(1)}, bf16[256,768]{1,0:T(8,128)(2,1)S(1)}, u32[]{:S(2)}, u32[]{:S(2)}) collective-permute-start(bf16[256,768]{1,0:T(8,128)(2,1)S(1)} %get-tuple-element.59.refs_0_), channel_id=1, source_target_pairs={{0,16},{8,24},{16,0},{24,8},{1,17},{9,25},{17,1},{25,9},{2,18},{10... | collective-permute-start | bytes 1179656 | tf_op jit(solution)/shard_map/ppermute | solution.py:60
  21.5 0.5 collective-permute-start.10
  22.0 1.2 %collective-permute-done.10.refs_2_.refs_6_ = f32[8,768]{1,0:T(8,128)S(1)} collective-permute-done((f32[8,768]{1,0:T(8,128)S(1)}, f32[8,768]{1,0:T(8,128)S(1)}, u32[]{:S(2)}, u32[]{:S(2)}) %collective-permute-start.10) | collective-permute-done | bytes 24608 | tf_op jit(solution)/shard_map/ppermute | solution.py:60
  23.2 0.0 collective-permute-done.11.refs_3_.refs_7_
  23.3 2.7 %far.1 = (f32[256,768]{1,0:T(8,128)S(1)}, bf16[128,768]{1,0:T(8,128)(2,1)S(1)}, bf16[128,768]{1,0:T(8,128)(2,1)S(1)}, f32[57,16,128]{2,1,0:T(8,128)S(1)}, bf16[16,768]{1,0:T(8,128)(2,1)S(1)}) custom-call(f32[8,768]{1,0:T(8,128)S(1)} %get-tuple-element.57.refs_1_.refs_2_.refs_5_.refs_0_.refs_4_, f32[8,768]{1,0:T(8,128)S(1)} %collective-permute-done.6.refs_2_.refs_1_.refs_5_, ...), custom_call_target="tpu_custom_call" | custom-call | tf_op jit(solution)/shard_map/far/pallas_call | solution.py:46
  26.0 0.2 collective-permute-start.12
  26.2 0.4 collective-permute-start.13
  26.6 0.9 %collective-permute-done.12.one = bf16[128,768]{1,0:T(8,128)(2,1)S(1)} collective-permute-done((bf16[128,768]{1,0:T(8,128)(2,1)S(1)}, bf16[128,768]{1,0:T(8,128)(2,1)S(1)}, u32[]{:S(2)}, u32[]{:S(2)}) %collective-permute-start.12) | collective-permute-done | bytes 196640 | tf_op jit(solution)/shard_map/ppermute | solution.py:60
  27.5 0.3 collective-permute-done.13.two
  27.8 0.1 far_sum.1.refs_2_
  27.9 1.2 %collective-permute-start.16 = (bf16[256,768]{1,0:T(8,128)(2,1)S(1)}, bf16[256,768]{1,0:T(8,128)(2,1)S(1)}, u32[]{:S(2)}, u32[]{:S(2)}) collective-permute-start(bf16[256,768]{1,0:T(8,128)(2,1)S(1)} %far_sum.1.refs_2_), channel_id=1, source_target_pairs={{0,16},{8,24},{16,0},{24,8},{1,17},{9,25},{17,1},{25,9},{2,18},{10... | collective-permute-start | bytes 1179656 | tf_op jit(solution)/shard_map/ppermute | solution.py:60
  29.1 2.0 %near.1 = (f32[256,768]{1,0:T(8,128)S(1)}, bf16[256,768]{1,0:T(8,128)(2,1)S(1)}, f32[8,768]{1,0:T(8,128)S(1)}) custom-call(f32[57,16,128]{2,1,0:T(8,128)S(1)} %get-tuple-element.62.refs_0_.refs_2_.refs_5_.refs_4_, bf16[2048,768]{1,0:T(8,128)(2,1)S(1)} %bitcast.7, bf16[256,768]{1,0:T(8,128)(2,1)S(1)} %far_sum.1.refs_2_), custom_call_target="tpu_custom_call" | custom-call | tf_op jit(solution)/shard_map/near/pallas_call | solution.py:46
  31.1 0.1 collective-permute-start.15
  31.2 1.4 %collective-permute-done.8.refs_0_.refs_1_ = bf16[256,768]{1,0:T(8,128)(2,1)S(1)} collective-permute-done((bf16[256,768]{1,0:T(8,128)(2,1)S(1)}, bf16[256,768]{1,0:T(8,128)(2,1)S(1)}, u32[]{:S(2)}, u32[]{:S(2)}) %collective-permute-start.8) | collective-permute-done | bytes 393248 | tf_op jit(solution)/shard_map/ppermute | solution.py:60
  32.6 0.1 collective-permute-start.14
  32.7 2.8 %inner_near.1.refs_5_ = f32[5,16,128]{2,1,0:T(8,128)S(1)} custom-call(bf16[256,768]{1,0:T(8,128)(2,1)S(1)} %get-tuple-element.59.refs_0_, bf16[256,768]{1,0:T(8,128)(2,1)S(1)} %collective-permute-done.9.refs_1_.refs_2_, f32[57,16,128]{2,1,0:T(8,128)S(1)} %get-tuple-element.62.refs_0_.refs_2_.refs_5_.refs_4_, ...), custom_call_target="tpu_custom_call" | custom-call | flops 99999997952 | tf_op jit(solution)/shard_map/inner_near/pallas_call | solution.py:46
  35.5 2.2 %inner_far.1.refs_4_ = f32[5,16,128]{2,1,0:T(8,128)S(1)} custom-call(bf16[256,768]{1,0:T(8,128)(2,1)S(1)} %collective-permute-done.8.refs_0_.refs_1_, bf16[256,768]{1,0:T(8,128)(2,1)S(1)} %collective-permute-done.14.refs_1_.refs_3_, f32[57,16,128]{2,1,0:T(8,128)S(1)} %get-tuple-element.62.refs_0_.refs_2_.refs_5_.refs_4_, ...), custom_call_target="tpu_custom_call" | custom-call | tf_op jit(solution)/shard_map/inner_far/pallas_call | solution.py:46
  37.7 1.4 %scores.1.sums = f32[8,768]{1,0:T(8,128)S(1)} custom-call(bf16[256,768]{1,0:T(8,128)(2,1)S(1)} %get-tuple-element.59.refs_0_, bf16[256,768]{1,0:T(8,128)(2,1)S(1)} %collective-permute-done.8.refs_0_.refs_1_, bf16[256,768]{1,0:T(8,128)(2,1)S(1)} %collective-permute-done.9.refs_1_.refs_2_, bf16[256,768]{1,0:T(8,128)(2,1)S(1)} %collective-permute-done.14.refs_1_.refs_3_, ...), custom_call_target="tpu_custom_call" | custom-call | tf_op jit(solution)/shard_map/scores/pallas_call | solution.py:46
  39.1 1.1 %collective-permute-done.16.far_other = bf16[256,768]{1,0:T(8,128)(2,1)S(1)} collective-permute-done((bf16[256,768]{1,0:T(8,128)(2,1)S(1)}, bf16[256,768]{1,0:T(8,128)(2,1)S(1)}, u32[]{:S(2)}, u32[]{:S(2)}) %collective-permute-start.16) | collective-permute-done | bytes 393248 | tf_op jit(solution)/shard_map/ppermute | solution.py:60
  40.2 0.3 merge.1
  40.5 1.6 %collective-permute-start.17 = (bf16[144,768]{1,0:T(8,128)(2,1)S(1)}, bf16[144,768]{1,0:T(8,128)(2,1)S(1)}, u32[]{:S(2)}, u32[]{:S(2)}) collective-permute-start(bf16[144,768]{1,0:T(8,128)(2,1)S(1)} %get-tuple-element.71.refs_6_.refs_7_.refs_1_), channel_id=1, source_target_pairs={{0,1},{1,0},{2,3},{3,2},{4,5},{5,4},{6,7},{7,6},{8,9},{9,8},{10,11... | collective-permute-start | bytes 663560 | tf_op jit(solution)/shard_map/ppermute | solution.py:60
  42.0 2.8 %output.4 = (bf16[2048,768]{1,0:T(8,128)(2,1)}, f32[8,128]{1,0:T(8,128)}) custom-call(bf16[256,768]{1,0:T(8,128)(2,1)S(1)} %get-tuple-element.59.refs_0_, bf16[256,768]{1,0:T(8,128)(2,1)S(1)} %collective-permute-done.8.refs_0_.refs_1_, bf16[256,768]{1,0:T(8,128)(2,1)S(1)} %collective-permute-done.9.refs_1_.refs_2_, ...), custom_call_target="tpu_custom_call" | custom-call | tf_op jit(solution)/shard_map/output/pallas_call | solution.py:522
  44.9 2.0 %output.5 = (bf16[2048,768]{1,0:T(8,128)(2,1)}, f32[8,128]{1,0:T(8,128)S(1)}) custom-call(bf16[256,768]{1,0:T(8,128)(2,1)S(1)} %get-tuple-element.59.refs_0_, bf16[256,768]{1,0:T(8,128)(2,1)S(1)} %collective-permute-done.8.refs_0_.refs_1_, bf16[256,768]{1,0:T(8,128)(2,1)S(1)} %collective-permute-done.9.refs_1_.refs_2_, ...), custom_call_target="tpu_custom_call", output_to_operand_aliasing={{0}: (6, {})} | custom-call | tf_op jit(solution)/shard_map/output/pallas_call | solution.py:522
  46.9 0.4 collective-permute-done.17.refs_2_
  47.3 0.1 halve.2
  47.4 1.7 %collective-permute-start.18 = (bf16[80,768]{1,0:T(8,128)(2,1)S(1)}, bf16[80,768]{1,0:T(8,128)(2,1)S(1)}, u32[]{:S(2)}, u32[]{:S(2)}) collective-permute-start(bf16[80,768]{1,0:T(8,128)(2,1)S(1)} %get-tuple-element.76.refs_7_.refs_1_), channel_id=1, source_target_pairs={{0,2},{1,3},{2,0},{3,1},{4,6},{5,7},{6,4},{7,5},{8,10},{9,11},{10,... | collective-permute-start | bytes 368648 | tf_op jit(solution)/shard_map/ppermute | solution.py:60
  49.0 2.0 %output.6 = (bf16[2048,768]{1,0:T(8,128)(2,1)}, f32[8,128]{1,0:T(8,128)S(1)}) custom-call(bf16[256,768]{1,0:T(8,128)(2,1)S(1)} %get-tuple-element.59.refs_0_, bf16[256,768]{1,0:T(8,128)(2,1)S(1)} %collective-permute-done.8.refs_0_.refs_1_, bf16[256,768]{1,0:T(8,128)(2,1)S(1)} %collective-permute-done.9.refs_1_.refs_2_, ...), custom_call_target="tpu_custom_call", output_to_operand_aliasing={{0}: (6, {})} | custom-call | tf_op jit(solution)/shard_map/output/pallas_call | solution.py:522
  51.0 1.3 %collective-permute-done.18.refs_2_ = bf16[80,768]{1,0:T(8,128)(2,1)S(1)} collective-permute-done((bf16[80,768]{1,0:T(8,128)(2,1)S(1)}, bf16[80,768]{1,0:T(8,128)(2,1)S(1)}, u32[]{:S(2)}, u32[]{:S(2)}) %collective-permute-start.18) | collective-permute-done | bytes 122912 | tf_op jit(solution)/shard_map/ppermute | solution.py:60
  52.3 0.7 halve.3
  53.0 2.6 %collective-permute-start.19 = (bf16[80,768]{1,0:T(8,128)(2,1)S(1)}, bf16[80,768]{1,0:T(8,128)(2,1)S(1)}, u32[]{:S(2)}, u32[]{:S(2)}) collective-permute-start(bf16[80,768]{1,0:T(8,128)(2,1)S(1)} %get-tuple-element.80.refs_7_.refs_0_), channel_id=1, source_target_pairs={{0,4},{1,5},{2,6},{3,7},{4,0},{5,1},{6,2},{7,3},{8,12},{9,13},{10,... | collective-permute-start | bytes 368648 | tf_op jit(solution)/shard_map/ppermute | solution.py:60
  55.6 2.0 %output.7 = (bf16[2048,768]{1,0:T(8,128)(2,1)}, f32[8,128]{1,0:T(8,128)S(1)}) custom-call(bf16[256,768]{1,0:T(8,128)(2,1)S(1)} %get-tuple-element.59.refs_0_, bf16[256,768]{1,0:T(8,128)(2,1)S(1)} %collective-permute-done.8.refs_0_.refs_1_, bf16[256,768]{1,0:T(8,128)(2,1)S(1)} %collective-permute-done.9.refs_1_.refs_2_, ...), custom_call_target="tpu_custom_call", output_to_operand_aliasing={{0}: (6, {})} | custom-call | tf_op jit(solution)/shard_map/output/pallas_call | solution.py:522
  57.6 2.5 %collective-permute-done.19.refs_1_ = bf16[80,768]{1,0:T(8,128)(2,1)S(1)} collective-permute-done((bf16[80,768]{1,0:T(8,128)(2,1)S(1)}, bf16[80,768]{1,0:T(8,128)(2,1)S(1)}, u32[]{:S(2)}, u32[]{:S(2)}) %collective-permute-start.19) | collective-permute-done | bytes 122912 | tf_op jit(solution)/shard_map/ppermute | solution.py:60
  60.1 0.5 share.1
  60.6 0.1 collective-permute-start.20
  60.7 1.6 %collective-permute-start.26 = (bf16[64,768]{1,0:T(8,128)(2,1)S(1)}, bf16[64,768]{1,0:T(8,128)(2,1)S(1)}, u32[]{:S(2)}, u32[]{:S(2)}) collective-permute-start(bf16[64,768]{1,0:T(8,128)(2,1)S(1)} %get-tuple-element.83.block.refs_0_), channel_id=1, source_target_pairs={{0,1},{1,0},{2,3},{3,2},{4,5},{5,4},{6,7},{7,6},{8,9},{9,8},{10,11... | collective-permute-start | bytes 294920 | tf_op jit(solution)/shard_map/ppermute | solution.py:60
  62.3 0.4 collective-permute-start.27
  62.6 1.6 %collective-permute-start.28 = (bf16[64,768]{1,0:T(8,128)(2,1)S(1)}, bf16[64,768]{1,0:T(8,128)(2,1)S(1)}, u32[]{:S(2)}, u32[]{:S(2)}) collective-permute-start(bf16[64,768]{1,0:T(8,128)(2,1)S(1)} %get-tuple-element.83.block.refs_0_), channel_id=1, source_target_pairs={{0,3},{1,2},{2,1},{3,0},{4,7},{5,6},{6,5},{7,4},{8,11},{9,10},{10,... | collective-permute-start | bytes 294920 | tf_op jit(solution)/shard_map/ppermute | solution.py:60
  64.2 0.9 %collective-permute-start.21 = (bf16[32,768]{1,0:T(8,128)(2,1)S(1)}, bf16[32,768]{1,0:T(8,128)(2,1)S(1)}, u32[]{:S(2)}, u32[]{:S(2)}) collective-permute-start(bf16[32,768]{1,0:T(8,128)(2,1)S(1)} %get-tuple-element.87), channel_id=1, source_target_pairs={{0,16},{8,24},{16,0},{24,8},{1,17},{9,25},{17,1},{25,9},{2,18},{10... | collective-permute-start | bytes 147464 | tf_op jit(solution)/shard_map/ppermute | solution.py:60
  65.1 0.1 collective-permute-start.22
  65.2 3.3 %collective-permute-done.21.refs_1_ = bf16[32,768]{1,0:T(8,128)(2,1)S(1)} collective-permute-done((bf16[32,768]{1,0:T(8,128)(2,1)S(1)}, bf16[32,768]{1,0:T(8,128)(2,1)S(1)}, u32[]{:S(2)}, u32[]{:S(2)}) %collective-permute-start.21) | collective-permute-done | bytes 49184 | tf_op jit(solution)/shard_map/ppermute | solution.py:60
  68.5 0.6 collective-permute-done.22.refs_2_
  69.2 1.6 %collective-permute-start.23 = (bf16[16,768]{1,0:T(8,128)(2,1)S(1)}, bf16[16,768]{1,0:T(8,128)(2,1)S(1)}, u32[]{:S(2)}, u32[]{:S(2)}) collective-permute-start(bf16[16,768]{1,0:T(8,128)(2,1)S(1)} %get-tuple-element.89.refs_0_), channel_id=1, source_target_pairs={{0,1},{1,0},{2,3},{3,2},{4,5},{5,4},{6,7},{7,6},{8,9},{9,8},{10,11... | collective-permute-start | bytes 73736 | tf_op jit(solution)/shard_map/ppermute | solution.py:60
  70.8 0.4 collective-permute-start.24
  71.2 1.6 %collective-permute-start.25 = (bf16[16,768]{1,0:T(8,128)(2,1)S(1)}, bf16[16,768]{1,0:T(8,128)(2,1)S(1)}, u32[]{:S(2)}, u32[]{:S(2)}) collective-permute-start(bf16[16,768]{1,0:T(8,128)(2,1)S(1)} %get-tuple-element.89.refs_0_), channel_id=1, source_target_pairs={{0,3},{1,2},{2,1},{3,0},{4,7},{5,6},{6,5},{7,4},{8,11},{9,10},{10,... | collective-permute-start | bytes 73736 | tf_op jit(solution)/shard_map/ppermute | solution.py:60
  72.8 2.7 %weights.1 = (f32[768,768]{1,0:T(8,128)}, f32[8,128]{1,0:T(8,128)S(1)}) custom-call(bf16[64,768]{1,0:T(8,128)(2,1)S(1)} %get-tuple-element.83.block.refs_0_, bf16[64,768]{1,0:T(8,128)(2,1)S(1)} %collective-permute-done.26.refs_1_, bf16[64,768]{1,0:T(8,128)(2,1)S(1)} %collective-permute-done.27.refs_2_, bf16[64,768]{1,0:T(8,128)(2,1)S(1)} %collective-permute-done.28.refs_3_, ...), custom_call_target="tpu_custom_call" | custom-call | tf_op jit(solution)/shard_map/weights/pallas_call | solution.py:46
  75.5 0.4 collective-permute-done.25.refs_3_
  75.9 1.1 %table_grad.1 = (f32[64,768]{1,0:T(8,128)}, f32[1,192]{1,0:T(1,128)}, f32[1,192]{1,0:T(1,128)}) custom-call(bf16[16,768]{1,0:T(8,128)(2,1)S(1)} %get-tuple-element.89.refs_0_, bf16[16,768]{1,0:T(8,128)(2,1)S(1)} %collective-permute-done.23.refs_1_, bf16[16,768]{1,0:T(8,128)(2,1)S(1)} %collective-permute-done.24.refs_2_, ...), custom_call_target="tpu_custom_call" | custom-call | tf_op jit(solution)/shard_map/table_grad/pallas_call | solution.py:46
  (21 shorter events, 0.1 us)
Async XLA Ops:
  0.6 22.6 %copy-start = (bf16[16,128,768]{2,1,0:T(8,128)(2,1)S(1)}, bf16[16,128,768]{2,1,0:T(8,128)(2,1)}, u32[]{:S(2)}) copy-start(bf16[16,128,768]{2,1,0:T(8,128)(2,1)} %param.15) | copy-start | bytes 9437188
  2.7 15.9 %collective-permute-start = (bf16[64,768]{1,0:T(8,128)(2,1)S(1)}, bf16[64,768]{1,0:T(8,128)(2,1)S(1)}, u32[]{:S(2)}, u32[]{:S(2)}) collective-permute-start(bf16[64,768]{1,0:T(8,128)(2,1)S(1)} %get-tuple-element.51.refs_0_), channel_id=1, source_target_pairs={{0,16},{8,24},{16,0},{24,8},{1,17},{9,25},{17,1},{25,9},{2,18},{10... | collective-permute-start | bytes 294920 | tf_op jit(solution)/shard_map/ppermute | solution.py:60
  5.7 3.8 %collective-permute-start.2 = (f32[1,192]{1,0:T(1,128)}, f32[1,192]{1,0:T(1,128)S(1)}, u32[]{:S(2)}, u32[]{:S(2)}) collective-permute-start(f32[1,192]{1,0:T(1,128)} %bitcast.13), channel_id=1, source_target_pairs={{0,16},{8,24},{16,0},{24,8},{1,17},{9,25},{17,1},{25,9},{2,18},{10... | collective-permute-start | bytes 2312 | tf_op jit(solution)/shard_map/ppermute | solution.py:60
  5.8 3.7 %collective-permute-start.3 = (f32[1,192]{1,0:T(1,128)}, f32[1,192]{1,0:T(1,128)S(1)}, u32[]{:S(2)}, u32[]{:S(2)}) collective-permute-start(f32[1,192]{1,0:T(1,128)} %bitcast.14), channel_id=1, source_target_pairs={{0,8},{8,0},{16,24},{24,16},{1,9},{9,1},{17,25},{25,17},{2,10},{10... | collective-permute-start | bytes 2312 | tf_op jit(solution)/shard_map/ppermute | solution.py:60
  9.5 1.1 %collective-permute-start.4 = (f32[1,192]{1,0:T(1,128)S(1)}, f32[1,192]{1,0:T(1,128)S(1)}, u32[]{:S(2)}, u32[]{:S(2)}) collective-permute-start(f32[1,192]{1,0:T(1,128)S(1)} %collective-permute-done.2.refs_1_), channel_id=1, source_target_pairs={{0,8},{8,0},{16,24},{24,16},{1,9},{9,1},{17,25},{25,17},{2,10},{10... | collective-permute-start | bytes 2312 | tf_op jit(solution)/shard_map/ppermute | solution.py:60
  11.3 5.0 %collective-permute-start.5 = (s32[48,128]{1,0:T(8,128)S(1)}, s32[48,128]{1,0:T(8,128)S(1)}, u32[]{:S(2)}, u32[]{:S(2)}) collective-permute-start(s32[48,128]{1,0:T(8,128)S(1)} %tail.1), channel_id=1, source_target_pairs={{0,1},{1,2},{2,3},{3,4},{4,5},{5,6},{6,7},{8,9},{9,10},{10,11},{11... | collective-permute-start | bytes 73736 | tf_op jit(solution)/shard_map/ppermute | solution.py:706
  14.7 3.9 %collective-permute-start.6 = (f32[8,768]{1,0:T(8,128)S(1)}, f32[8,768]{1,0:T(8,128)S(1)}, u32[]{:S(2)}, u32[]{:S(2)}) collective-permute-start(f32[8,768]{1,0:T(8,128)S(1)} %get-tuple-element.57.refs_1_.refs_2_.refs_5_.refs_0_.refs_4_), channel_id=1, source_target_pairs={{0,16},{8,24},{16,0},{24,8},{1,17},{9,25},{17,1},{25,9},{2,18},{10... | collective-permute-start | bytes 73736 | tf_op jit(solution)/shard_map/ppermute | solution.py:60
  15.7 3.0 %collective-permute-start.1 = (bf16[64,768]{1,0:T(8,128)(2,1)S(1)}, bf16[64,768]{1,0:T(8,128)(2,1)S(1)}, u32[]{:S(2)}, u32[]{:S(2)}) collective-permute-start(bf16[64,768]{1,0:T(8,128)(2,1)S(1)} %get-tuple-element.51.refs_0_), channel_id=1, source_target_pairs={{0,8},{8,0},{16,24},{24,16},{1,9},{9,1},{17,25},{25,17},{2,10},{10... | collective-permute-start | bytes 294920 | tf_op jit(solution)/shard_map/ppermute | solution.py:60
  18.6 1.4 %collective-permute-start.7 = (bf16[64,768]{1,0:T(8,128)(2,1)S(1)}, bf16[64,768]{1,0:T(8,128)(2,1)S(1)}, u32[]{:S(2)}, u32[]{:S(2)}) collective-permute-start(bf16[64,768]{1,0:T(8,128)(2,1)S(1)} %table_low.1), channel_id=1, source_target_pairs={{0,8},{8,0},{16,24},{24,16},{1,9},{9,1},{17,25},{25,17},{2,10},{10... | collective-permute-start | bytes 294920 | tf_op jit(solution)/shard_map/ppermute | solution.py:60
  20.5 12.0 %collective-permute-start.8 = (bf16[256,768]{1,0:T(8,128)(2,1)S(1)}, bf16[256,768]{1,0:T(8,128)(2,1)S(1)}, u32[]{:S(2)}, u32[]{:S(2)}) collective-permute-start(bf16[256,768]{1,0:T(8,128)(2,1)S(1)} %get-tuple-element.59.refs_0_), channel_id=1, source_target_pairs={{0,16},{8,24},{16,0},{24,8},{1,17},{9,25},{17,1},{25,9},{2,18},{10... | collective-permute-start | bytes 1179656 | tf_op jit(solution)/shard_map/ppermute | solution.py:60
  21.5 11.2 %collective-permute-start.9 = (bf16[256,768]{1,0:T(8,128)(2,1)S(1)}, bf16[256,768]{1,0:T(8,128)(2,1)S(1)}, u32[]{:S(2)}, u32[]{:S(2)}) collective-permute-start(bf16[256,768]{1,0:T(8,128)(2,1)S(1)} %get-tuple-element.59.refs_0_), channel_id=1, source_target_pairs={{0,8},{8,0},{16,24},{24,16},{1,9},{9,1},{17,25},{25,17},{2,10},{10... | collective-permute-start | bytes 1179656 | tf_op jit(solution)/shard_map/ppermute | solution.py:60
  21.5 1.8 %collective-permute-start.10 = (f32[8,768]{1,0:T(8,128)S(1)}, f32[8,768]{1,0:T(8,128)S(1)}, u32[]{:S(2)}, u32[]{:S(2)}) collective-permute-start(f32[8,768]{1,0:T(8,128)S(1)} %get-tuple-element.57.refs_1_.refs_2_.refs_5_.refs_0_.refs_4_), channel_id=1, source_target_pairs={{0,8},{8,0},{16,24},{24,16},{1,9},{9,1},{17,25},{25,17},{2,10},{10... | collective-permute-start | bytes 73736 | tf_op jit(solution)/shard_map/ppermute | solution.py:60
  22.0 1.3 %collective-permute-start.11 = (f32[8,768]{1,0:T(8,128)S(1)}, f32[8,768]{1,0:T(8,128)S(1)}, u32[]{:S(2)}, u32[]{:S(2)}) collective-permute-start(f32[8,768]{1,0:T(8,128)S(1)} %collective-permute-done.6.refs_2_.refs_1_.refs_5_), channel_id=1, source_target_pairs={{0,8},{8,0},{16,24},{24,16},{1,9},{9,1},{17,25},{25,17},{2,10},{10... | collective-permute-start | bytes 73736 | tf_op jit(solution)/shard_map/ppermute | solution.py:60
  26.0 1.5 %collective-permute-start.12 = (bf16[128,768]{1,0:T(8,128)(2,1)S(1)}, bf16[128,768]{1,0:T(8,128)(2,1)S(1)}, u32[]{:S(2)}, u32[]{:S(2)}) collective-permute-start(bf16[128,768]{1,0:T(8,128)(2,1)S(1)} %get-tuple-element.64), channel_id=1, source_target_pairs={{0,8},{8,0},{16,24},{24,16},{1,9},{9,1},{17,25},{25,17},{2,10},{10... | collective-permute-start | bytes 589832 | tf_op jit(solution)/shard_map/ppermute | solution.py:60
  26.2 1.6 %collective-permute-start.13 = (bf16[128,768]{1,0:T(8,128)(2,1)S(1)}, bf16[128,768]{1,0:T(8,128)(2,1)S(1)}, u32[]{:S(2)}, u32[]{:S(2)}) collective-permute-start(bf16[128,768]{1,0:T(8,128)(2,1)S(1)} %get-tuple-element.65), channel_id=1, source_target_pairs={{0,8},{8,0},{16,24},{24,16},{1,9},{9,1},{17,25},{25,17},{2,10},{10... | collective-permute-start | bytes 589832 | tf_op jit(solution)/shard_map/ppermute | solution.py:60
  27.9 12.3 %collective-permute-start.16 = (bf16[256,768]{1,0:T(8,128)(2,1)S(1)}, bf16[256,768]{1,0:T(8,128)(2,1)S(1)}, u32[]{:S(2)}, u32[]{:S(2)}) collective-permute-start(bf16[256,768]{1,0:T(8,128)(2,1)S(1)} %far_sum.1.refs_2_), channel_id=1, source_target_pairs={{0,16},{8,24},{16,0},{24,8},{1,17},{9,25},{17,1},{25,9},{2,18},{10... | collective-permute-start | bytes 1179656 | tf_op jit(solution)/shard_map/ppermute | solution.py:60
  31.1 8.0 %collective-permute-start.15 = (bf16[256,768]{1,0:T(8,128)(2,1)S(1)}, bf16[256,768]{1,0:T(8,128)(2,1)S(1)}, u32[]{:S(2)}, u32[]{:S(2)}) collective-permute-start(bf16[256,768]{1,0:T(8,128)(2,1)S(1)} %get-tuple-element.66.refs_1_.refs_5_), channel_id=1, source_target_pairs={{0,8},{8,0},{16,24},{24,16},{1,9},{9,1},{17,25},{25,17},{2,10},{10... | collective-permute-start | bytes 1179656 | tf_op jit(solution)/shard_map/ppermute | solution.py:60
  32.6 2.9 %collective-permute-start.14 = (bf16[256,768]{1,0:T(8,128)(2,1)S(1)}, bf16[256,768]{1,0:T(8,128)(2,1)S(1)}, u32[]{:S(2)}, u32[]{:S(2)}) collective-permute-start(bf16[256,768]{1,0:T(8,128)(2,1)S(1)} %passed.1), channel_id=1, source_target_pairs={{0,8},{8,0},{16,24},{24,16},{1,9},{9,1},{17,25},{25,17},{2,10},{10... | collective-permute-start | bytes 1179656 | tf_op jit(solution)/shard_map/ppermute | solution.py:60
  40.5 6.8 %collective-permute-start.17 = (bf16[144,768]{1,0:T(8,128)(2,1)S(1)}, bf16[144,768]{1,0:T(8,128)(2,1)S(1)}, u32[]{:S(2)}, u32[]{:S(2)}) collective-permute-start(bf16[144,768]{1,0:T(8,128)(2,1)S(1)} %get-tuple-element.71.refs_6_.refs_7_.refs_1_), channel_id=1, source_target_pairs={{0,1},{1,0},{2,3},{3,2},{4,5},{5,4},{6,7},{7,6},{8,9},{9,8},{10,11... | collective-permute-start | bytes 663560 | tf_op jit(solution)/shard_map/ppermute | solution.py:60
  47.4 4.9 %collective-permute-start.18 = (bf16[80,768]{1,0:T(8,128)(2,1)S(1)}, bf16[80,768]{1,0:T(8,128)(2,1)S(1)}, u32[]{:S(2)}, u32[]{:S(2)}) collective-permute-start(bf16[80,768]{1,0:T(8,128)(2,1)S(1)} %get-tuple-element.76.refs_7_.refs_1_), channel_id=1, source_target_pairs={{0,2},{1,3},{2,0},{3,1},{4,6},{5,7},{6,4},{7,5},{8,10},{9,11},{10,... | collective-permute-start | bytes 368648 | tf_op jit(solution)/shard_map/ppermute | solution.py:60
  53.0 7.1 %collective-permute-start.19 = (bf16[80,768]{1,0:T(8,128)(2,1)S(1)}, bf16[80,768]{1,0:T(8,128)(2,1)S(1)}, u32[]{:S(2)}, u32[]{:S(2)}) collective-permute-start(bf16[80,768]{1,0:T(8,128)(2,1)S(1)} %get-tuple-element.80.refs_7_.refs_0_), channel_id=1, source_target_pairs={{0,4},{1,5},{2,6},{3,7},{4,0},{5,1},{6,2},{7,3},{8,12},{9,13},{10,... | collective-permute-start | bytes 368648 | tf_op jit(solution)/shard_map/ppermute | solution.py:60
  60.6 4.5 %collective-permute-start.20 = (bf16[32,768]{1,0:T(8,128)(2,1)S(1)}, bf16[32,768]{1,0:T(8,128)(2,1)S(1)}, u32[]{:S(2)}, u32[]{:S(2)}) collective-permute-start(bf16[32,768]{1,0:T(8,128)(2,1)S(1)} %get-tuple-element.86), channel_id=1, source_target_pairs={{0,8},{8,0},{16,24},{24,16},{1,9},{9,1},{17,25},{25,17},{2,10},{10... | collective-permute-start | bytes 147464 | tf_op jit(solution)/shard_map/ppermute | solution.py:60
  60.7 10.5 %collective-permute-start.26 = (bf16[64,768]{1,0:T(8,128)(2,1)S(1)}, bf16[64,768]{1,0:T(8,128)(2,1)S(1)}, u32[]{:S(2)}, u32[]{:S(2)}) collective-permute-start(bf16[64,768]{1,0:T(8,128)(2,1)S(1)} %get-tuple-element.83.block.refs_0_), channel_id=1, source_target_pairs={{0,1},{1,0},{2,3},{3,2},{4,5},{5,4},{6,7},{7,6},{8,9},{9,8},{10,11... | collective-permute-start | bytes 294920 | tf_op jit(solution)/shard_map/ppermute | solution.py:60
  62.3 10.5 %collective-permute-start.27 = (bf16[64,768]{1,0:T(8,128)(2,1)S(1)}, bf16[64,768]{1,0:T(8,128)(2,1)S(1)}, u32[]{:S(2)}, u32[]{:S(2)}) collective-permute-start(bf16[64,768]{1,0:T(8,128)(2,1)S(1)} %get-tuple-element.83.block.refs_0_), channel_id=1, source_target_pairs={{0,2},{1,3},{2,0},{3,1},{4,6},{5,7},{6,4},{7,5},{8,10},{9,11},{10,... | collective-permute-start | bytes 294920 | tf_op jit(solution)/shard_map/ppermute | solution.py:60
  62.6 10.1 %collective-permute-start.28 = (bf16[64,768]{1,0:T(8,128)(2,1)S(1)}, bf16[64,768]{1,0:T(8,128)(2,1)S(1)}, u32[]{:S(2)}, u32[]{:S(2)}) collective-permute-start(bf16[64,768]{1,0:T(8,128)(2,1)S(1)} %get-tuple-element.83.block.refs_0_), channel_id=1, source_target_pairs={{0,3},{1,2},{2,1},{3,0},{4,7},{5,6},{6,5},{7,4},{8,11},{9,10},{10,... | collective-permute-start | bytes 294920 | tf_op jit(solution)/shard_map/ppermute | solution.py:60
  64.2 4.3 %collective-permute-start.21 = (bf16[32,768]{1,0:T(8,128)(2,1)S(1)}, bf16[32,768]{1,0:T(8,128)(2,1)S(1)}, u32[]{:S(2)}, u32[]{:S(2)}) collective-permute-start(bf16[32,768]{1,0:T(8,128)(2,1)S(1)} %get-tuple-element.87), channel_id=1, source_target_pairs={{0,16},{8,24},{16,0},{24,8},{1,17},{9,25},{17,1},{25,9},{2,18},{10... | collective-permute-start | bytes 147464 | tf_op jit(solution)/shard_map/ppermute | solution.py:60
  65.1 4.0 %collective-permute-start.22 = (bf16[32,768]{1,0:T(8,128)(2,1)S(1)}, bf16[32,768]{1,0:T(8,128)(2,1)S(1)}, u32[]{:S(2)}, u32[]{:S(2)}) collective-permute-start(bf16[32,768]{1,0:T(8,128)(2,1)S(1)} %get-tuple-element.88), channel_id=1, source_target_pairs={{0,24},{8,16},{16,8},{24,0},{1,25},{9,17},{17,9},{25,1},{2,26},{10... | collective-permute-start | bytes 147464 | tf_op jit(solution)/shard_map/ppermute | solution.py:60
  69.2 6.3 %collective-permute-start.23 = (bf16[16,768]{1,0:T(8,128)(2,1)S(1)}, bf16[16,768]{1,0:T(8,128)(2,1)S(1)}, u32[]{:S(2)}, u32[]{:S(2)}) collective-permute-start(bf16[16,768]{1,0:T(8,128)(2,1)S(1)} %get-tuple-element.89.refs_0_), channel_id=1, source_target_pairs={{0,1},{1,0},{2,3},{3,2},{4,5},{5,4},{6,7},{7,6},{8,9},{9,8},{10,11... | collective-permute-start | bytes 73736 | tf_op jit(solution)/shard_map/ppermute | solution.py:60
  70.8 4.7 %collective-permute-start.24 = (bf16[16,768]{1,0:T(8,128)(2,1)S(1)}, bf16[16,768]{1,0:T(8,128)(2,1)S(1)}, u32[]{:S(2)}, u32[]{:S(2)}) collective-permute-start(bf16[16,768]{1,0:T(8,128)(2,1)S(1)} %get-tuple-element.89.refs_0_), channel_id=1, source_target_pairs={{0,2},{1,3},{2,0},{3,1},{4,6},{5,7},{6,4},{7,5},{8,10},{9,11},{10,... | collective-permute-start | bytes 73736 | tf_op jit(solution)/shard_map/ppermute | solution.py:60
  71.2 4.7 %collective-permute-start.25 = (bf16[16,768]{1,0:T(8,128)(2,1)S(1)}, bf16[16,768]{1,0:T(8,128)(2,1)S(1)}, u32[]{:S(2)}, u32[]{:S(2)}) collective-permute-start(bf16[16,768]{1,0:T(8,128)(2,1)S(1)} %get-tuple-element.89.refs_0_), channel_id=1, source_target_pairs={{0,3},{1,2},{2,1},{3,0},{4,7},{5,6},{6,5},{7,4},{8,11},{9,10},{10,... | collective-permute-start | bytes 73736 | tf_op jit(solution)/shard_map/ppermute | solution.py:60

commit v3 on v2

--- a/solution.py
+++ b/solution.py
@@ -13,9 +13,10 @@
 REACH = 5
 SPAN = 8
 EXTRA = 16
-HALVINGS = 2
+PIECES = 4
 EDGE = 3
 VMEM_LIMIT = 16 * 1024 * 1024
+SENT = 48
 LONG = 10**11
 NT = (((1,), (1,)), ((), ()))
 TN = (((0,), (0,)), ((), ()))
@@ -30,7 +31,7 @@
     return dot(a, b, dims, lax.Precision.HIGHEST)
 
 
-def call(kernel, outs, *operands, scratch=(), cost=0, name=None, after=(), final=False):
+def call(kernel, outs, *operands, scratch=(), cost=0, name=None, after=(), final=0, copied=False):
     vmem = pl.BlockSpec(memory_space=pltpu.VMEM)
     hbm = pl.BlockSpec(memory_space=pltpu.HBM)
     stored = [isinstance(operand, tuple) for operand in operands]
@@ -45,9 +46,9 @@
 
     return pl.pallas_call(
         run if after else kernel,
-        out_shape=[jax.ShapeDtypeStruct(*o) if final else pltpu.VMEM(*o) for o in outs],
+        out_shape=[jax.ShapeDtypeStruct(*o) if at < final else pltpu.VMEM(*o) for at, o in enumerate(outs)],
         in_specs=[hbm if far else vmem for far in stored] + [pl.BlockSpec(memory_space=pl.ANY)] * len(after),
-        out_specs=[vmem] * len(outs),
+        out_specs=[hbm if at < final and copied else vmem for at in range(len(outs))],
         scratch_shapes=list(scratch),
         compiler_params=pltpu.CompilerParams(vmem_limit_bytes=VMEM_LIMIT),
         cost_estimate=pl.CostEstimate(flops=cost, bytes_accessed=0, transcendentals=0),
@@ -60,12 +61,35 @@
     return lax.ppermute(value, axis, [(i, i ^ bit) for i in range(count)])
 
 
-def gather_slots(value, axis, bits):
-    slots = {0: value}
+def stack_kernel(*refs):
+    out = refs[-1]
+    rows = refs[0].shape[0]
+    for at, value in enumerate(refs[:-1]):
+        out[at * rows : (at + 1) * rows] = value[...]
+
+
+def stacked(*values, name, after=()):
+    rows, width = values[0].shape
+    return call(stack_kernel, [((len(values) * rows, width), values[0].dtype)], *values, name=name, after=after)[0]
+
+
+def slots_of(bits):
+    order = [0]
     for bit in bits:
-        for m in list(slots):
-            slots[m | bit] = swap(slots[m], axis, bit)
-    return slots
+        order = order + [m | bit for m in order]
+    return order
+
+
+def gathered(value, axis, bits, name, after=()):
+    for bit in bits[:-1]:
+        value = stacked(value, swap(value, axis, bit), name=name, after=after)
+    return value, swap(value, axis, bits[-1])
+
+
+def pieces_of(refs, count):
+    each = count // len(refs)
+    rows = refs[0].shape[0] // each
+    return [ref.at[pl.ds(at * rows, rows), :] for ref in refs for at in range(each)]
 
 
 def row_index():
@@ -77,14 +101,14 @@
 
 
 def piece_index():
-    return lax.axis_index("tract") % (1 << HALVINGS)
+    return lax.axis_index("tract") % PIECES
 
 
 def load_kernel(rows, *refs):
     weight, table, score, bias = refs[:4]
     ids = refs[4:7]
-    weight_low, table_low, score_here, bias_here, together, tail = refs[7:13]
-    weight_here, table_here, ids_here, sems = refs[13:]
+    weight_low, table_low, score_here, bias_here, together = refs[7:12]
+    weight_here, table_here, ids_here, sems = refs[12:]
     parts = weight_here.shape[0]
     size = weight_here.shape[1]
     copies = [pltpu.make_async_copy(source, ids_here.at[at], sems.at[at]) for at, source in enumerate(ids)]
@@ -96,11 +120,9 @@
     ]
     for copy in copies:
         copy.start()
-    length = ids_here.shape[2]
     for at in range(3):
         copies[at].wait()
         together[at * rows : (at + 1) * rows, :] = ids_here[at].astype(F32)
-        tail[at * rows : (at + 1) * rows, :] = ids_here[at, :, length - tail.shape[1] :]
     copies[3].wait()
     table_low[...] = table_here[...].astype(BF16)
     copies[4].wait()
@@ -108,6 +130,11 @@
     for at in range(parts):
         copies[6 + at].wait()
         weight_low[at * size : (at + 1) * size, :] = weight_here[at].astype(BF16)
+
+
+def pair_kernel(first, second, out):
+    out[:8] = first[:8]
+    out[8:] = second[:8]
 
 
 def kept_kernel(*refs):
@@ -129,25 +156,28 @@
 
 
 def scorer_kernel(order, near_order, *refs):
-    scores = refs[: len(order)]
-    biases = refs[len(order) : len(order) + len(near_order)]
-    weight_low, scorer, out = refs[len(order) + len(near_order) :]
-    width = out.shape[1]
+    scores = pieces_of(refs[:2], len(order))
+    biases = refs[2 : 2 + len(near_order)]
+    weight_low, scorer, out = refs[2 + len(near_order) :]
+    width = scorer.shape[1]
     full = placed([(part, row_index() ^ m) for part, m in zip(scores, order)], width)
     bias = placed([(part, row_index() ^ m) for part, m in zip(biases, near_order)], width)
     full = jnp.concatenate([full, full], 0).astype(BF16)
     scorer[...] = full
     at = lax.broadcasted_iota(jnp.int32, bias.shape, 0)
-    out[...] = jnp.where(at == 0, dot(full, weight_low[...], NT)[:8], bias)
-
-
-def table_kernel(order, *refs):
-    slots = refs[: len(order)]
-    weight_low, product, table_low, table_turned = refs[len(order) :]
+    out[...] = jnp.zeros(out.shape, F32)
+    out[:8] = jnp.where(at == 0, dot(full, weight_low[...], NT)[:8], bias)
+
+
+def table_kernel(order, first, second, table_low):
+    slots = pieces_of((first, second), len(order))
     rows = slots[0].shape[0]
     for slot, m in zip(slots, order):
         at = pl.multiple_of((row_index() ^ m) * rows, rows)
-        table_low[pl.ds(at, rows), :] = slot[...].astype(BF16)
+        table_low[pl.ds(at, rows), :] = slot[...]
+
+
+def products_kernel(table_low, weight_low, product, table_turned):
     product[...] = dot(table_low[...], weight_low[...]).astype(BF16)
     table_turned[...] = table_low[...].T
 
@@ -156,9 +186,9 @@
     length = ids.shape[1]
     rows = ids.shape[0] // 3
     half = length // 2
-    tail = before.shape[1]
+    tail = 128
     ids = ids[...].astype(BF16)
-    earlier = before[...].astype(F32).astype(BF16)
+    earlier = before[:, length - tail :].astype(BF16)
     for m in range(SPAN):
         target = 2 * lax.broadcasted_iota(jnp.int32, (length, half), 1) + 1 - m
         source = lax.broadcasted_iota(jnp.int32, (length, half), 0)
@@ -318,12 +348,12 @@
     return high, middle, (rest - middle.astype(F32)).astype(BF16)
 
 
-def far_kernel(order, slots, values, *refs):
-    scorers = refs[: len(order)]
-    table_low, planes, scorer, cot = refs[len(order) : len(order) + 4]
-    own, sent, sent_too, plan, vectors, table, total = refs[len(order) + 4 :]
+def far_kernel(order, slot, values, *refs):
+    scorers = pieces_of(refs[:2], len(order))
+    table_low, planes, scorer, cot = refs[2:6]
+    sent_first, sent_second, plan, vectors, table, total = refs[6:]
     rows = plan.shape[1]
-    every = jnp.concatenate([s[...] for s in scorers], 0)
+    every = jnp.concatenate([s[:8] for s in scorers], 0)
     parts = thirds(every)
     found = dot(jnp.concatenate(parts, 0), table_low[...], NT)
     count = every.shape[0]
@@ -357,10 +387,13 @@
         for j in range(REACH):
             plan[MASKS + k * REACH + j] = window.mask[k, j]
             plan[WEIGHTS + k * REACH + j] = window.mask[k, j] * mixing[j]
-    accumulate(plan, total, [group_index() ^ m for m in slots], cot, values)
-    own[...] = total[:values]
-    sent[...] = total[values : values + values // 2].astype(BF16)
-    sent_too[...] = total[values + values // 2 : 2 * values].astype(BF16)
+    accumulate(plan, total, [group_index() ^ slot], cot, values)
+    for at, sent in enumerate((sent_first, sent_second)):
+        sent[...] = total[at * values // 2 : (at + 1) * values // 2].astype(BF16)
+
+
+def block_kernel(slot, values, plan, cot, out):
+    accumulate(plan, out, [group_index() ^ slot], cot, values)
 
 
 def average_line(plan, chunk):
@@ -384,9 +417,9 @@
 
 
 def inner_kernel(order, values, *refs):
-    products = refs[: len(order)]
-    plan, vectors, cot = refs[len(order) : len(order) + 3]
-    before, out = (refs[-2] if len(refs) > len(order) + 4 else None), refs[-1]
+    products = pieces_of(refs[:1], len(order))
+    plan, vectors, cot = refs[1:4]
+    before, out = (refs[-2] if len(refs) > 5 else None), refs[-1]
     rows, half = plan.shape[1:]
     blocks = values // 16
     name = names(values, half)
@@ -418,9 +451,9 @@
 
 
 def score_kernel(order, values, *refs):
-    products = refs[: len(order)]
-    inner_ref, plan, vectors, hot = refs[len(order) : len(order) + 4]
-    out, flat, rows_ref = refs[len(order) + 4 :]
+    products = pieces_of(refs[:2], len(order))
+    inner_ref, plan, vectors, hot = refs[2:6]
+    out, flat, rows_ref = refs[6:]
     rows, half = plan.shape[1:]
     biases = vectors[8:]
     window = Window({(k, j): plan[MASKS + k * REACH + j] for k in range(OFFSETS) for j in range(REACH)})
@@ -475,8 +508,8 @@
 
 
 def output_kernel(order, values, chunks_here, *refs):
-    products = refs[: len(order)]
-    plan, vectors = refs[len(order) : len(order) + 2]
+    products = pieces_of(refs[:2], len(order))
+    plan, vectors = refs[2:4]
     out, token, staged, sems = refs[-4:]
     token[...] = jnp.zeros(token.shape, F32)
     half = plan.shape[2]
@@ -532,17 +565,12 @@
     )(*operands, *after)
 
 
-def reversed_bits(number, bits):
-    return sum((((number >> b) & 1) << (bits - 1 - b)) for b in range(bits))
-
-
-def chunks(bits, values, piece, group):
+def chunks(values, piece, group):
     block = values // OFFSETS
-    size = block >> bits
-    for actual in range(1 << bits):
-        place = reversed_bits(piece ^ actual, bits) * OFFSETS * size
+    size = block // PIECES
+    for actual in range(PIECES):
         for offset in range(OFFSETS):
-            at = pl.multiple_of(place + (group ^ offset) * size, size)
+            at = pl.multiple_of((piece ^ actual) * OFFSETS * size + (group ^ offset) * size, size)
             yield offset * block + actual * size, at, size
 
 
@@ -555,26 +583,30 @@
     return block[:8].astype(F32) + block[8:].astype(F32)
 
 
-def merge_kernel(bits, near, near_other, far_other, sums, bias, keep, send, total):
+def merge_kernel(near, near_other, far_other, sums, bias, keep, *refs):
+    sends, total = refs[:-1], refs[-1]
     values = near.shape[0]
     summed = near[...] + near_other[...].astype(F32) + far_other[...].astype(F32)
-    for source, at, size in chunks(bits, values, piece_index(), group_index()):
+    for source, at, size in chunks(values, piece_index(), group_index()):
         total[pl.ds(at, size), :] = summed[source : source + size]
     part = keep.shape[0]
+    second = lax.broadcasted_iota(jnp.int32, bias.shape, 0) == 1
+    small = pack(sums[...] + jnp.where(second, bias[...], 0.0))
     keep[...] = total[:part]
-    send[: values - part] = total[values - (values - part) :].astype(BF16)
-    second = lax.broadcasted_iota(jnp.int32, bias.shape, 0) == 1
-    send[values - part :] = pack(sums[...] + jnp.where(second, bias[...], 0.0))
-
-
-def halve_kernel(mine, own_sent, other, keep, send):
-    rows = mine.shape[0]
-    total = mine[...] + other[:rows].astype(F32)
+    for at, send in enumerate(sends):
+        send[:part] = total[(at + 1) * part : (at + 2) * part].astype(BF16)
+        send[part:] = small
+
+
+def slice_kernel(keep, own, *refs):
+    others, send = refs[:-1], refs[-1]
     part = keep.shape[0]
-    keep[...] = total[:part]
-    rest = send.shape[0] - EXTRA
-    send[:rest] = total[rows - rest :].astype(BF16)
-    send[rest:] = pack(unpack(own_sent[own_sent.shape[0] - EXTRA :]) + unpack(other[rows:]))
+    total = functools.reduce(jnp.add, [keep[...]] + [o[:part].astype(F32) for o in others])
+    small = [unpack(x[part:]) for x in (own, *others)]
+    while len(small) > 1:
+        small = [small[at] + small[at + 1] for at in range(0, len(small), 2)]
+    send[:part] = total.astype(BF16)
+    send[part:] = pack(small[0])
 
 
 def whole_kernel(mine, other, send):
@@ -589,20 +621,27 @@
     sums[...] = unpack(mine[rows:]) + unpack(other[rows:])
 
 
-def share_kernel(block, sums, weight_low, keep, *sends):
+def share_kernel(block, sums, weight_low, keep, send):
     product = dot(block[...], weight_low[...], NT)
     rows = keep.shape[0]
     keep[...] = product[:rows]
-    for at, send in enumerate(sends):
-        send[:rows] = product[(at + 1) * rows : (at + 2) * rows].astype(BF16)
-        send[rows:] = pack(sums[...])
-
-
-def combine_kernel(keep, sums, *refs):
-    others, (out, total) = refs[:-2], refs[-2:]
+    send[:rows] = product[rows:].astype(BF16)
+    send[rows:] = pack(sums[...])
+
+
+def half_kernel(keep, sums, other, rest, send, total):
+    rows = rest.shape[0]
+    both = keep[...] + other[: 2 * rows].astype(F32)
+    total[...] = sums[...] + unpack(other[2 * rows :])
+    rest[...] = both[:rows]
+    send[:rows] = both[rows:].astype(BF16)
+    send[rows:] = pack(total[...])
+
+
+def combine_kernel(keep, sums, other, out, total):
     rows = keep.shape[0]
-    out[...] = functools.reduce(jnp.add, [keep[...]] + [o[:rows].astype(F32) for o in others]).astype(BF16)
-    total[...] = functools.reduce(jnp.add, [sums[...]] + [unpack(o[rows:]) for o in others])
+    out[...] = (keep[...] + other[:rows].astype(F32)).astype(BF16)
+    total[...] = sums[...] + unpack(other[rows:])
 
 
 def added_kernel(mine, other, out):
@@ -615,34 +654,43 @@
     out[rows:] = (mine[rows:] + two[...].astype(F32)).astype(out.dtype)
 
 
-def weight_kernel(bits, order, *refs):
+def weight_kernel(order, *refs):
     slots = refs[: len(order)]
-    turned, vectors, sums, out, token, full = refs[len(order) :]
+    turned, vectors, sums, out, token, full, staged, sems = refs[len(order) :]
     token[...] = jnp.zeros(token.shape, F32)
     values = full.shape[0]
     placed = {m: slot for m, slot in zip(order, slots)}
-    size = values // OFFSETS >> bits
-    for m in range(1 << bits):
+    size = values // OFFSETS // PIECES
+    for m in range(PIECES):
         for offset in range(OFFSETS):
             at = (group_index() ^ offset) * (values // OFFSETS) + (piece_index() ^ m) * size
             full[pl.ds(pl.multiple_of(at, size), size), :] = placed[m][offset * size : (offset + 1) * size]
     line = sums[pl.ds(group_index() + 2, 1), :values]
     scores = jnp.concatenate([vectors[:8], vectors[:8]], 0)
     first = lax.broadcasted_iota(jnp.int32, (8, values), 0) == 0
-    through = dot(turned[...], pack(jnp.where(first, jnp.broadcast_to(line, first.shape), 0.0)), NT)
-    high, low = split(through)
-    out[...] = dot(turned[...], full[...]) + dot(high, scores) + dot(low, scores)
-
-
-def table_grad_kernel(bits, order, offsets, *refs):
+    both = pack(jnp.where(first, jnp.broadcast_to(line, first.shape), 0.0))
+    parts = sems.shape[0]
+    step = turned.shape[0] // parts
+    copies = []
+    for part in range(parts):
+        here = turned[part * step : (part + 1) * step]
+        high, low = split(dot(here, both, NT))
+        staged[part] = dot(here, full[...]) + dot(high, scores) + dot(low, scores)
+        copies.append(pltpu.make_async_copy(staged.at[part], out.at[pl.ds(part * step, step), :], sems.at[part]))
+        copies[-1].start()
+    for copy in copies:
+        copy.wait()
+
+
+def table_grad_kernel(order, offsets, *refs):
     slots = refs[: len(order)]
-    scorers = refs[len(order) : len(order) + len(offsets)]
-    sums, out, score_out, bias_out, table, full, rows_ref = refs[len(order) + len(offsets) :]
+    scorers = pieces_of(refs[len(order) : len(order) + 2], len(offsets))
+    sums, out, score_out, bias_out, table, full, rows_ref = refs[len(order) + 2 :]
     values = full.shape[0]
     width = out.shape[1]
     high, low = split(sums[2 : 2 + OFFSETS, :values])
     for scorer, m in zip(scorers, offsets):
-        rows_ref[group_index() ^ m] = scorer[...]
+        rows_ref[group_index() ^ m] = scorer[:8]
     right = jnp.concatenate([rows_ref[k, :1] for k in range(OFFSETS)], 0)
     right_high, right_low = split(right)
     left = jnp.concatenate([x.astype(F32) for x in (high, low, high, low)], 0).astype(BF16)
@@ -679,55 +727,58 @@
     group_bits = [2 * copies, copies]
     near_bits = [bit for bit in bits_of(rows_count) if bit < copies]
 
-    score_slots = gather_slots(score_weight[None], "rows", bits_of(rows_count))
-    bias_slots = gather_slots(conv_bias[None], "rows", near_bits)
+    row_bits = bits_of(rows_count)
+    far_score = swap(score_weight[None], "rows", row_bits[0])
+    near_order = slots_of(near_bits)
+    biases = [conv_bias[None]]
+    for bit in near_bits:
+        biases = biases + [swap(value, "rows", bit) for value in biases]
     weight = conv_weight
     if copies > 1:
         near_by = [[g * copies + c for c in range(copies)] for g in range(OFFSETS)]
         weight = lax.all_gather(conv_weight, "rows", axis=0, tiled=True, axis_index_groups=near_by)
     parts = 4
     shard = (1, conv_bias.shape[0])
-    weight_low, shard_low, score_slots[0], bias_slots[0], ids, tail = call(
+    weight_low, table_low, score, biases[0], ids = call(
         functools.partial(load_kernel, rows),
-        [(weight.shape, BF16), (table.shape, BF16), (shard, F32), (shard, F32), ((3 * rows, length), F32),
-         ((3 * rows, 128), jnp.int32)],
+        [(weight.shape, BF16), (table.shape, BF16), (shard, F32), (shard, F32), ((3 * rows, length), F32)],
         (weight,), (table,), (score_weight[None],), (conv_bias[None],), (byte_values,), (segment_ids,), (valid,),
         scratch=[pltpu.VMEM((parts, weight.shape[0] // parts, width), F32), pltpu.VMEM(table.shape, F32),
                  pltpu.VMEM((3, rows, length), jnp.int32), pltpu.SemaphoreType.DMA((6 + parts,))],
         name="load",
     )
+    scores = gathered(stacked(score, far_score, name="score"), "rows", row_bits[1:], "score")
     scorer, scored = call(
-        functools.partial(scorer_kernel, list(score_slots), list(bias_slots)),
-        [((EXTRA, width), BF16), ((8, width), F32)], *score_slots.values(), *bias_slots.values(), weight_low, name="scorer",
-    )
-    scorers = gather_slots(scored, "rows", group_bits)
-    scorers = [scorers[m * copies] for m in order]
-    tail = call(kept_kernel, [(tail.shape, jnp.int32)], tail, name="tail", after=[scored])[0]
+        functools.partial(scorer_kernel, slots_of(row_bits), near_order),
+        [((EXTRA, width), BF16), ((SENT, width), F32)], *scores, *biases, weight_low, name="scorer",
+    )
+    far_scored = swap(scored, "rows", group_bits[0])
+    table_low = stacked(table_low, name="table_low", after=[far_score])
+    far_table = swap(table_low, "rows", row_bits[0])
+    table_low = stacked(table_low, far_table, name="table_pair", after=[scored])
+    table_low = call(
+        functools.partial(table_kernel, slots_of(row_bits)), [((values, width), BF16)],
+        *gathered(table_low, "rows", row_bits[1:], "table_pair"), name="table",
+    )[0]
+    product, turned = call(
+        products_kernel, [((values, width), BF16), ((width, values), BF16)], table_low, weight_low, name="products", after=[],
+    )
+    tail = stacked(ids, name="tail", after=[product])
     before = lax.ppermute(tail, "tract", [(i, i + 1) for i in range(tract_count - 1)])
     planes, hot = call(
-        planes_kernel, [((3 * rows, SPAN * half), F32), ((values, 2 * rows * half + 128), BF16)],
-        ids, before, name="planes", after=[scored],
-    )
-    table_slots = {0: shard_low}
-    for bit in bits_of(rows_count):
-        for m in list(table_slots):
-            value = table_slots[m]
-            if m:
-                value = call(kept_kernel, [(table.shape, BF16)], value, name="table_low", after=[planes, scorers[1]])[0]
-            table_slots[m | bit] = swap(value, "rows", bit)
-    product, table_low, turned = call(
-        functools.partial(table_kernel, list(table_slots)),
-        [((values, width), BF16), ((values, width), BF16), ((width, values), BF16)],
-        *table_slots.values(), weight_low, name="products", after=[scored],
-    )
+        planes_kernel, [((3 * rows, SPAN * half), F32), ((values, 2 * rows * half + 128), BF16)], ids, before, name="planes",
+    )
+    scorers = call(pair_kernel, [((16, width), F32)], scored, far_scored, name="scored")[0]
+    scorers = scorers, swap(scorers, "rows", group_bits[1])
 
     cot = cotangent.reshape(rows * half, width)
-    far, *far_sent, plan, vectors = call(
-        functools.partial(far_kernel, order, [2, 3], values),
-        [((values, width), F32), ((values // 2, width), BF16), ((values // 2, width), BF16), ((PLANES, rows, half), F32), ((EXTRA, width), BF16)],
+    *far_sent, plan, vectors = call(
+        functools.partial(far_kernel, order, 3, values),
+        [((values // 2, width), BF16), ((values // 2, width), BF16), ((PLANES, rows, half), F32), ((EXTRA, width), BF16)],
         *scorers, table_low, planes, scorer, cot,
-        scratch=[pltpu.VMEM((OFFSETS, 8, values), F32), pltpu.VMEM((2 * values, width), F32)], name="far",
-    )
+        scratch=[pltpu.VMEM((OFFSETS, 8, values), F32), pltpu.VMEM((values, width), F32)], name="far",
+    )
+    far = call(functools.partial(block_kernel, 2, values), [((values, width), F32)], plan, cot, name="far_own")[0]
     far_sent = [swap(half_sent, "rows", copies) for half_sent in far_sent]
     far = call(joined_kernel, [((values, width), BF16)], far, *far_sent, name="far_sum")[0]
     far_other = swap(far, "rows", 2 * copies)
@@ -738,47 +789,40 @@
     )
     near_other = swap(near_sent, "rows", copies)
 
-    products = {0: product, 1: swap(product, "rows", copies), 2: swap(product, "rows", 2 * copies)}
+    far_product = swap(product, "rows", 2 * copies)
+    product = stacked(product, far_product, name="passed", after=[near_sent])
+    products = product, swap(product, "rows", copies)
     inner = call(
-        functools.partial(inner_kernel, [0, 1], values), [((REACH, rows, half), F32)],
-        products[0], products[1], plan, vectors, cot, name="inner_near", after=[near_sent], cost=LONG,
+        functools.partial(inner_kernel, [0, 2], values), [((REACH, rows, half), F32)],
+        products[0], plan, vectors, cot, name="inner_near", cost=LONG,
     )[0]
-    passed = call(kept_kernel, [((values, width), BF16)], products[2], name="passed", after=[near_sent])[0]
-    products[3] = swap(passed, "rows", copies)
     inner = call(
-        functools.partial(inner_kernel, [2, 3], values), [((REACH, rows, half), F32)],
-        products[2], products[3], plan, vectors, cot, inner, name="inner_far",
+        functools.partial(inner_kernel, [1, 3], values), [((REACH, rows, half), F32)],
+        products[1], plan, vectors, cot, inner, name="inner_far",
     )[0]
-    products = [products[m] for m in order]
     sums = call(
         functools.partial(score_kernel, order, values), [((8, width), F32)], *products, inner, plan, vectors, hot,
         scratch=[pltpu.VMEM((8, hot.shape[1]), F32), pltpu.VMEM((OFFSETS, 8, values), F32)], name="scores",
     )[0]
 
-    exchanges = [("tract", 1 << at) for at in range(tract_count.bit_length() - 1)]
-    exchanges += [("rows", 1 << at) for at in range(copies.bit_length() - 1)]
-    halved, rest = exchanges[:HALVINGS], exchanges[HALVINGS:]
-    size = values // 2
-    keep, send = call(
-        functools.partial(merge_kernel, HALVINGS), [((size, width), F32), ((size + EXTRA, width), BF16)],
+    rest = [("tract", 1 << at) for at in range(PIECES.bit_length() - 1, tract_count.bit_length() - 1)]
+    rest += [("rows", 1 << at) for at in range(copies.bit_length() - 1)]
+    size = values // PIECES
+    keep, *sends = call(
+        merge_kernel, [((size, width), F32)] + [((size + EXTRA, width), BF16)] * (PIECES - 1),
         near, near_other, far_other, sums, bias_part, scratch=[pltpu.VMEM((values, width), F32)], name="merge",
     )
-    out = None
-
-    def fill(out, parts, after):
-        for part in parts:
-            out, token = output_part(out, part, 4, order, values, products, plan, vectors, after)
+    others = [swap(send, "tract", at + 1) for at, send in enumerate(sends)]
+    parts = 2
+
+    def fill(out, which, after):
+        for part in which:
+            out, token = output_part(out, part, parts, order, values, products, plan, vectors, [after])
         return out, token
 
-    for at, (axis, bit) in enumerate(halved):
-        other = swap(send, axis, bit)
-        out, token = fill(out, [0, 1] if at == 0 else [2], [send])
-        last = at + 1 == HALVINGS
-        size = size if last else size // 2
-        keep, send = call(
-            halve_kernel, [((size, width), F32), ((size + EXTRA, width), BF16)], keep, send, other, name="halve", after=[token],
-        )
-    out, token = fill(out, [3], [send])
+    out, token = fill(None, [0], keep)
+    send = call(slice_kernel, [((size + EXTRA, width), BF16)], keep, sends[0], *others, name="slice", after=[token])[0]
+    out, token = fill(out, [1], send)
     for axis, bit in rest[:-1]:
         other = swap(send, axis, bit)
         send = call(whole_kernel, [(send.shape, BF16)], send, other, name="whole")[0]
@@ -786,26 +830,32 @@
     block, sums = call(last_kernel, [((size, width), BF16), ((8, width), F32)], send, other, name="last", after=[token])
 
     part = size // OFFSETS
-    table_keep, *table_sends = call(
-        share_kernel, [((part, width), F32)] + [((part + EXTRA, width), BF16)] * (OFFSETS - 1), block, sums, weight_low, name="share",
-    )
-    table_others = [swap(send, "rows", (at + 1) * copies) for at, send in enumerate(table_sends)]
-    blocks = {0: block} | {m: swap(block, "tract", m) for m in range(1, 1 << HALVINGS)}
-    table_piece, sums = call(
-        combine_kernel, [((part, width), BF16), ((8, width), F32)], table_keep, sums, *table_others, name="combine",
-    )
-    table_pieces = {0: table_piece} | {m: swap(table_piece, "tract", m) for m in range(1, 1 << HALVINGS)}
+    keep, send = call(
+        share_kernel, [((2 * part, width), F32), ((2 * part + EXTRA, width), BF16)], block, sums, weight_low, name="share",
+    )
+    other = swap(send, "rows", group_bits[0])
+    blocks = {0: block} | {m: swap(block, "tract", m) for m in range(1, PIECES)}
+    keep, send, sums = call(
+        half_kernel, [((part, width), F32), ((part + EXTRA, width), BF16), ((8, width), F32)], keep, sums, other, name="half",
+    )
+    other = swap(send, "rows", group_bits[1])
+    table_piece, sums = call(combine_kernel, [((part, width), BF16), ((8, width), F32)], keep, sums, other, name="combine")
+    table_pieces = {0: table_piece} | {m: swap(table_piece, "tract", m) for m in range(1, PIECES)}
     if copies > 1:
         turned = lax.dynamic_slice_in_dim(turned, rows_at % copies * (width // copies), width // copies, 0)
+    weight_rows = conv_weight.shape[0]
+    steps = 3
     weight_grad, token = call(
-        functools.partial(weight_kernel, HALVINGS, list(blocks)), [((conv_weight.shape[0], width), F32), ((8, 128), F32)],
-        *blocks.values(), turned, vectors, sums, scratch=[pltpu.VMEM((values, width), BF16)], name="weights", final=True,
+        functools.partial(weight_kernel, list(blocks)), [((weight_rows, width), F32), ((8, 128), F32)],
+        *blocks.values(), turned, vectors, sums,
+        scratch=[pltpu.VMEM((values, width), BF16), pltpu.VMEM((steps, weight_rows // steps, width), F32),
+                 pltpu.SemaphoreType.DMA((steps,))], name="weights", final=1, copied=True,
     )
     table_grad, score_grad, bias_grad = call(
-        functools.partial(table_grad_kernel, HALVINGS, list(table_pieces), order),
+        functools.partial(table_grad_kernel, list(table_pieces), order),
         [(table.shape, F32), (shard, F32), (shard, F32)], *table_pieces.values(), *scorers, sums,
         scratch=[pltpu.VMEM((values // OFFSETS, width), F32), pltpu.VMEM((values, width), F32), pltpu.VMEM((OFFSETS, 8, width), F32)],
-        name="table_grad", final=True, after=[token],
+        name="table_grad", final=3, after=[token],
     )
     return out.reshape(cotangent.shape), table_grad, weight_grad, bias_grad[0], score_grad[0]
 

time: 77.1 us -> 68.1 us (0.88)
  waiting for transfers between devices: 21.9 us -> 11.9 us
  starting transfers between devices: 24.9 us -> 29.1 us
  Pallas kernels: 29.3 us -> 25.9 us
    ppermute x28 -> x24, waiting for transfers between devices: 21.3 us -> 10.3 us  [swap(): return lax.ppermute(value, axis, [(i, i ^ bit) for i in range(count)])]
    ppermute x28 -> x24, starting transfers between devices: 21.5 us -> 25.7 us  [swap(): return lax.ppermute(value, axis, [(i, i ^ bit) for i in range(count)])]
    pallas_call x4 -> x2, Pallas kernels: 8.9 us -> 6.59 us  [output_part(): pl.pallas_call(run, out_shape=[jax.ShapeDtypeStruct((rows * half, width),...]
    pallas_call x21 -> x26, Pallas kernels: 20.4 us -> 19.3 us  [call(): pl.pallas_call(run if after else kernel, out_shape=[jax.ShapeDtypeStruct(...]
    ppermute x1, waiting for transfers between devices: 0.55 us -> 1.63 us  [body(): lax.ppermute(tail, 'tract', [(i, i + 1) for i in range(tract_count - 1)])]
  transfers between devices with their start and end apart: 29 -> 25, of which waited for: 16 -> 11; matrix products, arithmetic and copies ran while one was open for 0% -> 0% of each run, Pallas kernels for 31% -> 35%
where the time goes in v3:
time: 68.1 us; the launch traced here: 67.9 us
  starting transfers between devices  29.1 us (43%)
  Pallas kernels  25.9 us (38%)
  waiting for transfers between devices  11.9 us (17%)
  between operations  0.92 us (1%)
    ppermute x24, starting transfers between devices, swap(): return lax.ppermute(value, axis, [(i, i ^ bit) for i in range(count)])  25.7 us
    pallas_call x26, Pallas kernels, call(): pl.pallas_call(run if after else kernel, out_shape=[jax.ShapeDtypeStruct(...  19.3 us
    ppermute x24, waiting for transfers between devices, swap(): return lax.ppermute(value, axis, [(i, i ^ bit) for i in range(count)])  10.3 us
    pallas_call x2, Pallas kernels, output_part(): pl.pallas_call(run, out_shape=[jax.ShapeDtypeStruct((rows * half, width),...  6.59 us
    ppermute x1, starting transfers between devices, body(): lax.ppermute(tail, 'tract', [(i, i + 1) for i in range(tract_count - 1)])  3.42 us
    ppermute x1, waiting for transfers between devices, body(): lax.ppermute(tail, 'tract', [(i, i + 1) for i in range(tract_count - 1)])  1.63 us
  transfers between devices with their start and end apart: 25, of which 11 were waited for; matrix products, arithmetic and copies ran while one was open for 0% of the time, Pallas kernels for 35%

profile of v3, /device:TPU:0, one launch (start us, length us, event | category | flops | bytes accessed | tf_op | source)
XLA Modules:
  0.0 67.9 jit_solution(9932338589901697174)
XLA Ops:
  0.6 3.0 %collective-permute-start = (f32[1,192]{1,0:T(1,128)}, f32[1,192]{1,0:T(1,128)S(1)}, u32[]{:S(2)}, u32[]{:S(2)}) collective-permute-start(f32[1,192]{1,0:T(1,128)} %bitcast.13), channel_id=1, source_target_pairs={{0,16},{8,24},{16,0},{24,8},{1,17},{9,25},{17,1},{25,9},{2,18},{10... | collective-permute-start | bytes 2312 | tf_op jit(solution)/shard_map/ppermute | solution.py:61
  3.6 1.9 %load.1 = (bf16[768,768]{1,0:T(8,128)(2,1)S(1)}, bf16[64,768]{1,0:T(8,128)(2,1)S(1)}, f32[1,192]{1,0:T(1,128)S(1)}, f32[1,192]{1,0:T(1,128)S(1)}, f32[48,256]{1,0:T(8,128)S(1)}) custom-call(f32[768,768]{1,0:T(8,128)} %refs_0_.1, f32[64,768]{1,0:T(8,128)} %refs_1_.1, f32[1,192]{1,0:T(1,128)} %bitcast.14, f32[1,192]{1,0:T(1,128)} %bitcast.12, ...), custom_call_target="tpu_custom_call" | custom-call | tf_op jit(solution)/shard_map/load/pallas_call | solution.py:47
  5.5 0.0 collective-permute-done.refs_1_
  5.6 1.9 %collective-permute-start.1 = (bf16[64,768]{1,0:T(8,128)(2,1)S(1)}, bf16[64,768]{1,0:T(8,128)(2,1)S(1)}, u32[]{:S(2)}, u32[]{:S(2)}) collective-permute-start(bf16[64,768]{1,0:T(8,128)(2,1)S(1)} %table_low.1.refs_0_), channel_id=1, source_target_pairs={{0,16},{8,24},{16,0},{24,8},{1,17},{9,25},{17,1},{25,9},{2,18},{10... | collective-permute-start | bytes 294920 | tf_op jit(solution)/shard_map/ppermute | solution.py:61
  7.5 0.0 collective-permute-start.2
  7.5 1.2 %collective-permute-done.2.refs_1_ = f32[2,192]{1,0:T(2,128)S(1)} collective-permute-done((f32[2,192]{1,0:T(2,128)S(1)}, f32[2,192]{1,0:T(2,128)S(1)}, u32[]{:S(2)}, u32[]{:S(2)}) %collective-permute-start.2) | collective-permute-done | bytes 1568 | tf_op jit(solution)/shard_map/ppermute | solution.py:61
  8.7 0.7 scorer.1
  9.3 0.9 %collective-permute-done.1.refs_1_ = bf16[64,768]{1,0:T(8,128)(2,1)S(1)} collective-permute-done((bf16[64,768]{1,0:T(8,128)(2,1)S(1)}, bf16[64,768]{1,0:T(8,128)(2,1)S(1)}, u32[]{:S(2)}, u32[]{:S(2)}) %collective-permute-start.1) | collective-permute-done | bytes 98336 | tf_op jit(solution)/shard_map/ppermute | solution.py:61
  10.3 0.1 collective-permute-start.3
  10.3 1.9 %collective-permute-start.5 = (f32[48,768]{1,0:T(8,128)S(1)}, f32[48,768]{1,0:T(8,128)S(1)}, u32[]{:S(2)}, u32[]{:S(2)}) collective-permute-start(f32[48,768]{1,0:T(8,128)S(1)} %get-tuple-element.49.refs_2_.first), channel_id=1, source_target_pairs={{0,16},{8,24},{16,0},{24,8},{1,17},{9,25},{17,1},{25,9},{2,18},{10... | collective-permute-start | bytes 442376 | tf_op jit(solution)/shard_map/ppermute | solution.py:61
  12.3 0.0 collective-permute-done.3.second
  12.3 0.5 products.1
  12.8 1.4 %collective-permute-start.4 = (bf16[256,768]{1,0:T(8,128)(2,1)S(1)}, bf16[256,768]{1,0:T(8,128)(2,1)S(1)}, u32[]{:S(2)}, u32[]{:S(2)}) collective-permute-start(bf16[256,768]{1,0:T(8,128)(2,1)S(1)} %get-tuple-element.50.refs_1_.refs_0_), channel_id=1, source_target_pairs={{0,16},{8,24},{16,0},{24,8},{1,17},{9,25},{17,1},{25,9},{2,18},{10... | collective-permute-start | bytes 1179656 | tf_op jit(solution)/shard_map/ppermute | solution.py:61
  14.2 3.4 %collective-permute-start.7 = (f32[48,256]{1,0:T(8,128)S(1)}, f32[48,256]{1,0:T(8,128)S(1)}, u32[]{:S(2)}, u32[]{:S(2)}) collective-permute-start(f32[48,256]{1,0:T(8,128)S(1)} %tail.1), channel_id=1, source_target_pairs={{0,1},{1,2},{2,3},{3,4},{4,5},{5,6},{6,7},{8,9},{9,10},{10,11},{11... | collective-permute-start | bytes 147464 | tf_op jit(solution)/shard_map/ppermute | solution.py:767
  17.7 0.1 collective-permute-start.6
  17.8 1.6 %collective-permute-done.7.before = f32[48,256]{1,0:T(8,128)S(1)} collective-permute-done((f32[48,256]{1,0:T(8,128)S(1)}, f32[48,256]{1,0:T(8,128)S(1)}, u32[]{:S(2)}, u32[]{:S(2)}) %collective-permute-start.7) | collective-permute-done | bytes 49184 | tf_op jit(solution)/shard_map/ppermute | solution.py:767
  19.4 0.6 planes.1
  20.0 0.0 collective-permute-done.6.refs_1_.refs_5_
  20.0 1.8 %far.1 = (bf16[128,768]{1,0:T(8,128)(2,1)S(1)}, bf16[128,768]{1,0:T(8,128)(2,1)S(1)}, f32[57,16,128]{2,1,0:T(8,128)S(1)}, bf16[16,768]{1,0:T(8,128)(2,1)S(1)}) custom-call(f32[16,768]{1,0:T(8,128)S(1)} %scored.1.refs_0_.refs_4_, f32[16,768]{1,0:T(8,128)S(1)} %collective-permute-done.6.refs_1_.refs_5_, bf16[256,768]{1,0:T(8,128)(2,1)S(1)} %table.1.table_low.refs_2_, ...), custom_call_target="tpu_custom_call" | custom-call | tf_op jit(solution)/shard_map/far/pallas_call | solution.py:47
  21.8 0.1 collective-permute-start.8
  21.9 0.5 collective-permute-start.9
  22.4 1.0 %far_own.1.mine = f32[256,768]{1,0:T(8,128)S(1)} custom-call(f32[57,16,128]{2,1,0:T(8,128)S(1)} %get-tuple-element.54.plan.refs_0_.refs_1_.refs_3_.refs_2_, bf16[2048,768]{1,0:T(8,128)(2,1)S(1)} %bitcast.7), custom_call_target="tpu_custom_call" | custom-call | tf_op jit(solution)/shard_map/far_own/pallas_call | solution.py:47
  23.4 0.0 collective-permute-done.8.one
  23.4 0.2 collective-permute-done.9.two
  23.6 0.1 far_sum.1.refs_2_
  23.7 0.7 %collective-permute-start.12 = (bf16[256,768]{1,0:T(8,128)(2,1)S(1)}, bf16[256,768]{1,0:T(8,128)(2,1)S(1)}, u32[]{:S(2)}, u32[]{:S(2)}) collective-permute-start(bf16[256,768]{1,0:T(8,128)(2,1)S(1)} %far_sum.1.refs_2_), channel_id=1, source_target_pairs={{0,16},{8,24},{16,0},{24,8},{1,17},{9,25},{17,1},{25,9},{2,18},{10... | collective-permute-start | bytes 1179656 | tf_op jit(solution)/shard_map/ppermute | solution.py:61
  24.4 2.0 %near.1 = (f32[256,768]{1,0:T(8,128)S(1)}, bf16[256,768]{1,0:T(8,128)(2,1)S(1)}, f32[8,768]{1,0:T(8,128)S(1)}) custom-call(f32[57,16,128]{2,1,0:T(8,128)S(1)} %get-tuple-element.54.plan.refs_0_.refs_1_.refs_3_.refs_2_, bf16[2048,768]{1,0:T(8,128)(2,1)S(1)} %bitcast.8, bf16[256,768]{1,0:T(8,128)(2,1)S(1)} %far_sum.1.refs_2_), custom_call_target="tpu_custom_call" | custom-call | tf_op jit(solution)/shard_map/near/pallas_call | solution.py:47
  26.4 0.1 collective-permute-start.11
  26.5 0.1 passed.1.refs_0_
  26.5 0.5 collective-permute-start.10
  27.1 2.8 %inner_near.1.refs_4_ = f32[5,16,128]{2,1,0:T(8,128)S(1)} custom-call(bf16[512,768]{1,0:T(8,128)(2,1)S(1)} %passed.1.refs_0_, f32[57,16,128]{2,1,0:T(8,128)S(1)} %get-tuple-element.54.plan.refs_0_.refs_1_.refs_3_.refs_2_, bf16[16,768]{1,0:T(8,128)(2,1)S(1)} %get-tuple-element.58.refs_2_.refs_4_.refs_3_.refs_5_, bf16[2048,768]{1,0:T(8,128)(2,1)S(1)} %bitcast.9), custom_call_target="tpu_custom_call" | custom-call | flops 99999997952 | tf_op jit(solution)/shard_map/inner_near/pallas_call | solution.py:47
  29.9 0.0 collective-permute-done.10.refs_0_.refs_1_
  29.9 2.1 %inner_far.1.refs_2_ = f32[5,16,128]{2,1,0:T(8,128)S(1)} custom-call(bf16[512,768]{1,0:T(8,128)(2,1)S(1)} %collective-permute-done.10.refs_0_.refs_1_, f32[57,16,128]{2,1,0:T(8,128)S(1)} %get-tuple-element.54.plan.refs_0_.refs_1_.refs_3_.refs_2_, bf16[16,768]{1,0:T(8,128)(2,1)S(1)} %get-tuple-element.58.refs_2_.refs_4_.refs_3_.refs_5_, ...), custom_call_target="tpu_custom_call" | custom-call | tf_op jit(solution)/shard_map/inner_far/pallas_call | solution.py:47
  32.0 1.4 %scores.1.sums = f32[8,768]{1,0:T(8,128)S(1)} custom-call(bf16[512,768]{1,0:T(8,128)(2,1)S(1)} %passed.1.refs_0_, bf16[512,768]{1,0:T(8,128)(2,1)S(1)} %collective-permute-done.10.refs_0_.refs_1_, f32[5,16,128]{2,1,0:T(8,128)S(1)} %inner_far.1.refs_2_, f32[57,16,128]{2,1,0:T(8,128)S(1)} %get-tuple-element.54.plan.refs_0_.refs_1_.refs_3_.refs_2_, ...), custom_call_target="tpu_custom_call" | custom-call | tf_op jit(solution)/shard_map/scores/pallas_call | solution.py:47
  33.4 1.5 %collective-permute-done.12.far_other = bf16[256,768]{1,0:T(8,128)(2,1)S(1)} collective-permute-done((bf16[256,768]{1,0:T(8,128)(2,1)S(1)}, bf16[256,768]{1,0:T(8,128)(2,1)S(1)}, u32[]{:S(2)}, u32[]{:S(2)}) %collective-permute-start.12) | collective-permute-done | bytes 393248 | tf_op jit(solution)/shard_map/ppermute | solution.py:61
  35.0 0.3 merge.1
  35.3 3.4 %collective-permute-start.14 = (bf16[80,768]{1,0:T(8,128)(2,1)S(1)}, bf16[80,768]{1,0:T(8,128)(2,1)S(1)}, u32[]{:S(2)}, u32[]{:S(2)}) collective-permute-start(bf16[80,768]{1,0:T(8,128)(2,1)S(1)} %get-tuple-element.65), channel_id=1, source_target_pairs={{0,2},{1,3},{2,0},{3,1},{4,6},{5,7},{6,4},{7,5},{8,10},{9,11},{10,... | collective-permute-start | bytes 368648 | tf_op jit(solution)/shard_map/ppermute | solution.py:61
  38.6 0.5 collective-permute-start.15
  39.1 1.0 %collective-permute-start.13 = (bf16[80,768]{1,0:T(8,128)(2,1)S(1)}, bf16[80,768]{1,0:T(8,128)(2,1)S(1)}, u32[]{:S(2)}, u32[]{:S(2)}) collective-permute-start(bf16[80,768]{1,0:T(8,128)(2,1)S(1)} %get-tuple-element.64.refs_1_), channel_id=1, source_target_pairs={{0,1},{1,0},{2,3},{3,2},{4,5},{5,4},{6,7},{7,6},{8,9},{9,8},{10,11... | collective-permute-start | bytes 368648 | tf_op jit(solution)/shard_map/ppermute | solution.py:61
  40.1 3.4 %output.2 = (bf16[2048,768]{1,0:T(8,128)(2,1)}, f32[8,128]{1,0:T(8,128)S(1)}) custom-call(bf16[512,768]{1,0:T(8,128)(2,1)S(1)} %passed.1.refs_0_, bf16[512,768]{1,0:T(8,128)(2,1)S(1)} %collective-permute-done.10.refs_0_.refs_1_, f32[57,16,128]{2,1,0:T(8,128)S(1)} %get-tuple-element.54.plan.refs_0_.refs_1_.refs_3_.refs_2_, ...), custom_call_target="tpu_custom_call" | custom-call | tf_op jit(solution)/shard_map/output/pallas_call | solution.py:555
  43.6 1.1 %collective-permute-done.15.refs_4_ = bf16[80,768]{1,0:T(8,128)(2,1)S(1)} collective-permute-done((bf16[80,768]{1,0:T(8,128)(2,1)S(1)}, bf16[80,768]{1,0:T(8,128)(2,1)S(1)}, u32[]{:S(2)}, u32[]{:S(2)}) %collective-permute-start.15) | collective-permute-done | bytes 122912 | tf_op jit(solution)/shard_map/ppermute | solution.py:61
  44.7 1.2 %collective-permute-done.13.refs_2_ = bf16[80,768]{1,0:T(8,128)(2,1)S(1)} collective-permute-done((bf16[80,768]{1,0:T(8,128)(2,1)S(1)}, bf16[80,768]{1,0:T(8,128)(2,1)S(1)}, u32[]{:S(2)}, u32[]{:S(2)}) %collective-permute-start.13) | collective-permute-done | bytes 122912 | tf_op jit(solution)/shard_map/ppermute | solution.py:61
  45.9 0.1 slice.1.refs_5_.refs_0_
  45.9 2.7 %collective-permute-start.16 = (bf16[80,768]{1,0:T(8,128)(2,1)S(1)}, bf16[80,768]{1,0:T(8,128)(2,1)S(1)}, u32[]{:S(2)}, u32[]{:S(2)}) collective-permute-start(bf16[80,768]{1,0:T(8,128)(2,1)S(1)} %slice.1.refs_5_.refs_0_), channel_id=1, source_target_pairs={{0,4},{1,5},{2,6},{3,7},{4,0},{5,1},{6,2},{7,3},{8,12},{9,13},{10,... | collective-permute-start | bytes 368648 | tf_op jit(solution)/shard_map/ppermute | solution.py:61
  48.6 3.2 %output.3 = (bf16[2048,768]{1,0:T(8,128)(2,1)}, f32[8,128]{1,0:T(8,128)S(1)}) custom-call(bf16[512,768]{1,0:T(8,128)(2,1)S(1)} %passed.1.refs_0_, bf16[512,768]{1,0:T(8,128)(2,1)S(1)} %collective-permute-done.10.refs_0_.refs_1_, f32[57,16,128]{2,1,0:T(8,128)S(1)} %get-tuple-element.54.plan.refs_0_.refs_1_.refs_3_.refs_2_, ...), custom_call_target="tpu_custom_call", output_to_operand_aliasing={{0}: (4, {})} | custom-call | tf_op jit(solution)/shard_map/output/pallas_call | solution.py:555
  51.8 1.5 %collective-permute-done.16.refs_1_ = bf16[80,768]{1,0:T(8,128)(2,1)S(1)} collective-permute-done((bf16[80,768]{1,0:T(8,128)(2,1)S(1)}, bf16[80,768]{1,0:T(8,128)(2,1)S(1)}, u32[]{:S(2)}, u32[]{:S(2)}) %collective-permute-start.16) | collective-permute-done | bytes 122912 | tf_op jit(solution)/shard_map/ppermute | solution.py:61
  53.4 0.5 share.1
  53.9 0.7 %collective-permute-start.17 = (bf16[48,768]{1,0:T(8,128)(2,1)S(1)}, bf16[48,768]{1,0:T(8,128)(2,1)S(1)}, u32[]{:S(2)}, u32[]{:S(2)}) collective-permute-start(bf16[48,768]{1,0:T(8,128)(2,1)S(1)} %get-tuple-element.73), channel_id=1, source_target_pairs={{0,16},{8,24},{16,0},{24,8},{1,17},{9,25},{17,1},{25,9},{2,18},{10... | collective-permute-start | bytes 221192 | tf_op jit(solution)/shard_map/ppermute | solution.py:61
  54.6 1.8 %collective-permute-start.24 = (bf16[64,768]{1,0:T(8,128)(2,1)S(1)}, bf16[64,768]{1,0:T(8,128)(2,1)S(1)}, u32[]{:S(2)}, u32[]{:S(2)}) collective-permute-start(bf16[64,768]{1,0:T(8,128)(2,1)S(1)} %get-tuple-element.70.block.refs_0_), channel_id=1, source_target_pairs={{0,3},{1,2},{2,1},{3,0},{4,7},{5,6},{6,5},{7,4},{8,11},{9,10},{10,... | collective-permute-start | bytes 294920 | tf_op jit(solution)/shard_map/ppermute | solution.py:61
  56.4 1.5 %collective-permute-start.23 = (bf16[64,768]{1,0:T(8,128)(2,1)S(1)}, bf16[64,768]{1,0:T(8,128)(2,1)S(1)}, u32[]{:S(2)}, u32[]{:S(2)}) collective-permute-start(bf16[64,768]{1,0:T(8,128)(2,1)S(1)} %get-tuple-element.70.block.refs_0_), channel_id=1, source_target_pairs={{0,2},{1,3},{2,0},{3,1},{4,6},{5,7},{6,4},{7,5},{8,10},{9,11},{10,... | collective-permute-start | bytes 294920 | tf_op jit(solution)/shard_map/ppermute | solution.py:61
  57.9 0.2 collective-permute-start.22
  58.1 0.2 collective-permute-done.17.other
  58.3 0.1 collective-permute-start.18
  58.4 1.2 %collective-permute-done.18.other = bf16[32,768]{1,0:T(8,128)(2,1)S(1)} collective-permute-done((bf16[32,768]{1,0:T(8,128)(2,1)S(1)}, bf16[32,768]{1,0:T(8,128)(2,1)S(1)}, u32[]{:S(2)}, u32[]{:S(2)}) %collective-permute-start.18) | collective-permute-done | bytes 49184 | tf_op jit(solution)/shard_map/ppermute | solution.py:61
  59.6 1.9 %collective-permute-start.21 = (bf16[16,768]{1,0:T(8,128)(2,1)S(1)}, bf16[16,768]{1,0:T(8,128)(2,1)S(1)}, u32[]{:S(2)}, u32[]{:S(2)}) collective-permute-start(bf16[16,768]{1,0:T(8,128)(2,1)S(1)} %get-tuple-element.77.refs_0_), channel_id=1, source_target_pairs={{0,3},{1,2},{2,1},{3,0},{4,7},{5,6},{6,5},{7,4},{8,11},{9,10},{10,... | collective-permute-start | bytes 73736 | tf_op jit(solution)/shard_map/ppermute | solution.py:61
  61.5 1.5 %collective-permute-start.20 = (bf16[16,768]{1,0:T(8,128)(2,1)S(1)}, bf16[16,768]{1,0:T(8,128)(2,1)S(1)}, u32[]{:S(2)}, u32[]{:S(2)}) collective-permute-start(bf16[16,768]{1,0:T(8,128)(2,1)S(1)} %get-tuple-element.77.refs_0_), channel_id=1, source_target_pairs={{0,2},{1,3},{2,0},{3,1},{4,6},{5,7},{6,4},{7,5},{8,10},{9,11},{10,... | collective-permute-start | bytes 73736 | tf_op jit(solution)/shard_map/ppermute | solution.py:61
  62.9 0.0 collective-permute-done.24.refs_3_
  62.9 0.2 collective-permute-start.19
  63.2 0.0 collective-permute-done.23.refs_2_
  63.2 0.0 collective-permute-done.22.refs_1_
  63.2 2.3 %weights.1 = (f32[768,768]{1,0:T(8,128)}, f32[8,128]{1,0:T(8,128)S(1)}) custom-call(bf16[64,768]{1,0:T(8,128)(2,1)S(1)} %get-tuple-element.70.block.refs_0_, bf16[64,768]{1,0:T(8,128)(2,1)S(1)} %collective-permute-done.22.refs_1_, bf16[64,768]{1,0:T(8,128)(2,1)S(1)} %collective-permute-done.23.refs_2_, bf16[64,768]{1,0:T(8,128)(2,1)S(1)} %collective-permute-done.24.refs_3_, ...), custom_call_target="tpu_custom_call" | custom-call | tf_op jit(solution)/shard_map/weights/pallas_call | solution.py:47
  65.5 0.0 collective-permute-done.20.refs_2_
  65.5 1.2 %collective-permute-done.19.refs_1_ = bf16[16,768]{1,0:T(8,128)(2,1)S(1)} collective-permute-done((bf16[16,768]{1,0:T(8,128)(2,1)S(1)}, bf16[16,768]{1,0:T(8,128)(2,1)S(1)}, u32[]{:S(2)}, u32[]{:S(2)}) %collective-permute-start.19) | collective-permute-done | bytes 24608 | tf_op jit(solution)/shard_map/ppermute | solution.py:61
  66.8 1.1 %table_grad.1 = (f32[64,768]{1,0:T(8,128)}, f32[1,192]{1,0:T(1,128)}, f32[1,192]{1,0:T(1,128)}) custom-call(bf16[16,768]{1,0:T(8,128)(2,1)S(1)} %get-tuple-element.77.refs_0_, bf16[16,768]{1,0:T(8,128)(2,1)S(1)} %collective-permute-done.19.refs_1_, bf16[16,768]{1,0:T(8,128)(2,1)S(1)} %collective-permute-done.20.refs_2_, ...), custom_call_target="tpu_custom_call" | custom-call | tf_op jit(solution)/shard_map/table_grad/pallas_call | solution.py:47
  (16 shorter events, 0.2 us)
Async XLA Ops:
  0.6 4.9 %collective-permute-start = (f32[1,192]{1,0:T(1,128)}, f32[1,192]{1,0:T(1,128)S(1)}, u32[]{:S(2)}, u32[]{:S(2)}) collective-permute-start(f32[1,192]{1,0:T(1,128)} %bitcast.13), channel_id=1, source_target_pairs={{0,16},{8,24},{16,0},{24,8},{1,17},{9,25},{17,1},{25,9},{2,18},{10... | collective-permute-start | bytes 2312 | tf_op jit(solution)/shard_map/ppermute | solution.py:61
  5.6 4.7 %collective-permute-start.1 = (bf16[64,768]{1,0:T(8,128)(2,1)S(1)}, bf16[64,768]{1,0:T(8,128)(2,1)S(1)}, u32[]{:S(2)}, u32[]{:S(2)}) collective-permute-start(bf16[64,768]{1,0:T(8,128)(2,1)S(1)} %table_low.1.refs_0_), channel_id=1, source_target_pairs={{0,16},{8,24},{16,0},{24,8},{1,17},{9,25},{17,1},{25,9},{2,18},{10... | collective-permute-start | bytes 294920 | tf_op jit(solution)/shard_map/ppermute | solution.py:61
  7.5 1.2 %collective-permute-start.2 = (f32[2,192]{1,0:T(2,128)S(1)}, f32[2,192]{1,0:T(2,128)S(1)}, u32[]{:S(2)}, u32[]{:S(2)}) collective-permute-start(f32[2,192]{1,0:T(2,128)S(1)} %score.1.refs_0_), channel_id=1, source_target_pairs={{0,8},{8,0},{16,24},{24,16},{1,9},{9,1},{17,25},{25,17},{2,10},{10... | collective-permute-start | bytes 4616 | tf_op jit(solution)/shard_map/ppermute | solution.py:61
  8.7 11.3 %copy-start = (bf16[16,128,768]{2,1,0:T(8,128)(2,1)S(1)}, bf16[16,128,768]{2,1,0:T(8,128)(2,1)}, u32[]{:S(2)}) copy-start(bf16[16,128,768]{2,1,0:T(8,128)(2,1)} %param.15) | copy-start | bytes 9437188
  10.3 2.0 %collective-permute-start.3 = (bf16[128,768]{1,0:T(8,128)(2,1)S(1)}, bf16[128,768]{1,0:T(8,128)(2,1)S(1)}, u32[]{:S(2)}, u32[]{:S(2)}) collective-permute-start(bf16[128,768]{1,0:T(8,128)(2,1)S(1)} %table_pair.1.first), channel_id=1, source_target_pairs={{0,8},{8,0},{16,24},{24,16},{1,9},{9,1},{17,25},{25,17},{2,10},{10... | collective-permute-start | bytes 589832 | tf_op jit(solution)/shard_map/ppermute | solution.py:61
  10.3 7.3 %collective-permute-start.5 = (f32[48,768]{1,0:T(8,128)S(1)}, f32[48,768]{1,0:T(8,128)S(1)}, u32[]{:S(2)}, u32[]{:S(2)}) collective-permute-start(f32[48,768]{1,0:T(8,128)S(1)} %get-tuple-element.49.refs_2_.first), channel_id=1, source_target_pairs={{0,16},{8,24},{16,0},{24,8},{1,17},{9,25},{17,1},{25,9},{2,18},{10... | collective-permute-start | bytes 442376 | tf_op jit(solution)/shard_map/ppermute | solution.py:61
  12.8 13.7 %collective-permute-start.4 = (bf16[256,768]{1,0:T(8,128)(2,1)S(1)}, bf16[256,768]{1,0:T(8,128)(2,1)S(1)}, u32[]{:S(2)}, u32[]{:S(2)}) collective-permute-start(bf16[256,768]{1,0:T(8,128)(2,1)S(1)} %get-tuple-element.50.refs_1_.refs_0_), channel_id=1, source_target_pairs={{0,16},{8,24},{16,0},{24,8},{1,17},{9,25},{17,1},{25,9},{2,18},{10... | collective-permute-start | bytes 1179656 | tf_op jit(solution)/shard_map/ppermute | solution.py:61
  14.2 5.2 %collective-permute-start.7 = (f32[48,256]{1,0:T(8,128)S(1)}, f32[48,256]{1,0:T(8,128)S(1)}, u32[]{:S(2)}, u32[]{:S(2)}) collective-permute-start(f32[48,256]{1,0:T(8,128)S(1)} %tail.1), channel_id=1, source_target_pairs={{0,1},{1,2},{2,3},{3,4},{4,5},{5,6},{6,7},{8,9},{9,10},{10,11},{11... | collective-permute-start | bytes 147464 | tf_op jit(solution)/shard_map/ppermute | solution.py:767
  17.7 2.3 %collective-permute-start.6 = (f32[16,768]{1,0:T(8,128)S(1)}, f32[16,768]{1,0:T(8,128)S(1)}, u32[]{:S(2)}, u32[]{:S(2)}) collective-permute-start(f32[16,768]{1,0:T(8,128)S(1)} %scored.1.refs_0_.refs_4_), channel_id=1, source_target_pairs={{0,8},{8,0},{16,24},{24,16},{1,9},{9,1},{17,25},{25,17},{2,10},{10... | collective-permute-start | bytes 147464 | tf_op jit(solution)/shard_map/ppermute | solution.py:61
  21.8 1.6 %collective-permute-start.8 = (bf16[128,768]{1,0:T(8,128)(2,1)S(1)}, bf16[128,768]{1,0:T(8,128)(2,1)S(1)}, u32[]{:S(2)}, u32[]{:S(2)}) collective-permute-start(bf16[128,768]{1,0:T(8,128)(2,1)S(1)} %get-tuple-element.55), channel_id=1, source_target_pairs={{0,8},{8,0},{16,24},{24,16},{1,9},{9,1},{17,25},{25,17},{2,10},{10... | collective-permute-start | bytes 589832 | tf_op jit(solution)/shard_map/ppermute | solution.py:61
  21.9 1.7 %collective-permute-start.9 = (bf16[128,768]{1,0:T(8,128)(2,1)S(1)}, bf16[128,768]{1,0:T(8,128)(2,1)S(1)}, u32[]{:S(2)}, u32[]{:S(2)}) collective-permute-start(bf16[128,768]{1,0:T(8,128)(2,1)S(1)} %get-tuple-element.56), channel_id=1, source_target_pairs={{0,8},{8,0},{16,24},{24,16},{1,9},{9,1},{17,25},{25,17},{2,10},{10... | collective-permute-start | bytes 589832 | tf_op jit(solution)/shard_map/ppermute | solution.py:61
  23.7 11.3 %collective-permute-start.12 = (bf16[256,768]{1,0:T(8,128)(2,1)S(1)}, bf16[256,768]{1,0:T(8,128)(2,1)S(1)}, u32[]{:S(2)}, u32[]{:S(2)}) collective-permute-start(bf16[256,768]{1,0:T(8,128)(2,1)S(1)} %far_sum.1.refs_2_), channel_id=1, source_target_pairs={{0,16},{8,24},{16,0},{24,8},{1,17},{9,25},{17,1},{25,9},{2,18},{10... | collective-permute-start | bytes 1179656 | tf_op jit(solution)/shard_map/ppermute | solution.py:61
  26.4 8.6 %collective-permute-start.11 = (bf16[256,768]{1,0:T(8,128)(2,1)S(1)}, bf16[256,768]{1,0:T(8,128)(2,1)S(1)}, u32[]{:S(2)}, u32[]{:S(2)}) collective-permute-start(bf16[256,768]{1,0:T(8,128)(2,1)S(1)} %get-tuple-element.57.refs_2_), channel_id=1, source_target_pairs={{0,8},{8,0},{16,24},{24,16},{1,9},{9,1},{17,25},{25,17},{2,10},{10... | collective-permute-start | bytes 1179656 | tf_op jit(solution)/shard_map/ppermute | solution.py:61
  26.5 3.4 %collective-permute-start.10 = (bf16[512,768]{1,0:T(8,128)(2,1)S(1)}, bf16[512,768]{1,0:T(8,128)(2,1)S(1)}, u32[]{:S(2)}, u32[]{:S(2)}) collective-permute-start(bf16[512,768]{1,0:T(8,128)(2,1)S(1)} %passed.1.refs_0_), channel_id=1, source_target_pairs={{0,8},{8,0},{16,24},{24,16},{1,9},{9,1},{17,25},{25,17},{2,10},{10... | collective-permute-start | bytes 2359304 | tf_op jit(solution)/shard_map/ppermute | solution.py:61
  35.3 8.3 %collective-permute-start.14 = (bf16[80,768]{1,0:T(8,128)(2,1)S(1)}, bf16[80,768]{1,0:T(8,128)(2,1)S(1)}, u32[]{:S(2)}, u32[]{:S(2)}) collective-permute-start(bf16[80,768]{1,0:T(8,128)(2,1)S(1)} %get-tuple-element.65), channel_id=1, source_target_pairs={{0,2},{1,3},{2,0},{3,1},{4,6},{5,7},{6,4},{7,5},{8,10},{9,11},{10,... | collective-permute-start | bytes 368648 | tf_op jit(solution)/shard_map/ppermute | solution.py:61
  38.6 6.1 %collective-permute-start.15 = (bf16[80,768]{1,0:T(8,128)(2,1)S(1)}, bf16[80,768]{1,0:T(8,128)(2,1)S(1)}, u32[]{:S(2)}, u32[]{:S(2)}) collective-permute-start(bf16[80,768]{1,0:T(8,128)(2,1)S(1)} %get-tuple-element.66), channel_id=1, source_target_pairs={{0,3},{1,2},{2,1},{3,0},{4,7},{5,6},{6,5},{7,4},{8,11},{9,10},{10,... | collective-permute-start | bytes 368648 | tf_op jit(solution)/shard_map/ppermute | solution.py:61
  39.1 6.8 %collective-permute-start.13 = (bf16[80,768]{1,0:T(8,128)(2,1)S(1)}, bf16[80,768]{1,0:T(8,128)(2,1)S(1)}, u32[]{:S(2)}, u32[]{:S(2)}) collective-permute-start(bf16[80,768]{1,0:T(8,128)(2,1)S(1)} %get-tuple-element.64.refs_1_), channel_id=1, source_target_pairs={{0,1},{1,0},{2,3},{3,2},{4,5},{5,4},{6,7},{7,6},{8,9},{9,8},{10,11... | collective-permute-start | bytes 368648 | tf_op jit(solution)/shard_map/ppermute | solution.py:61
  45.9 7.4 %collective-permute-start.16 = (bf16[80,768]{1,0:T(8,128)(2,1)S(1)}, bf16[80,768]{1,0:T(8,128)(2,1)S(1)}, u32[]{:S(2)}, u32[]{:S(2)}) collective-permute-start(bf16[80,768]{1,0:T(8,128)(2,1)S(1)} %slice.1.refs_5_.refs_0_), channel_id=1, source_target_pairs={{0,4},{1,5},{2,6},{3,7},{4,0},{5,1},{6,2},{7,3},{8,12},{9,13},{10,... | collective-permute-start | bytes 368648 | tf_op jit(solution)/shard_map/ppermute | solution.py:61
  53.9 4.4 %collective-permute-start.17 = (bf16[48,768]{1,0:T(8,128)(2,1)S(1)}, bf16[48,768]{1,0:T(8,128)(2,1)S(1)}, u32[]{:S(2)}, u32[]{:S(2)}) collective-permute-start(bf16[48,768]{1,0:T(8,128)(2,1)S(1)} %get-tuple-element.73), channel_id=1, source_target_pairs={{0,16},{8,24},{16,0},{24,8},{1,17},{9,25},{17,1},{25,9},{2,18},{10... | collective-permute-start | bytes 221192 | tf_op jit(solution)/shard_map/ppermute | solution.py:61
  54.6 8.4 %collective-permute-start.24 = (bf16[64,768]{1,0:T(8,128)(2,1)S(1)}, bf16[64,768]{1,0:T(8,128)(2,1)S(1)}, u32[]{:S(2)}, u32[]{:S(2)}) collective-permute-start(bf16[64,768]{1,0:T(8,128)(2,1)S(1)} %get-tuple-element.70.block.refs_0_), channel_id=1, source_target_pairs={{0,3},{1,2},{2,1},{3,0},{4,7},{5,6},{6,5},{7,4},{8,11},{9,10},{10,... | collective-permute-start | bytes 294920 | tf_op jit(solution)/shard_map/ppermute | solution.py:61
  56.4 6.8 %collective-permute-start.23 = (bf16[64,768]{1,0:T(8,128)(2,1)S(1)}, bf16[64,768]{1,0:T(8,128)(2,1)S(1)}, u32[]{:S(2)}, u32[]{:S(2)}) collective-permute-start(bf16[64,768]{1,0:T(8,128)(2,1)S(1)} %get-tuple-element.70.block.refs_0_), channel_id=1, source_target_pairs={{0,2},{1,3},{2,0},{3,1},{4,6},{5,7},{6,4},{7,5},{8,10},{9,11},{10,... | collective-permute-start | bytes 294920 | tf_op jit(solution)/shard_map/ppermute | solution.py:61
  57.9 5.3 %collective-permute-start.22 = (bf16[64,768]{1,0:T(8,128)(2,1)S(1)}, bf16[64,768]{1,0:T(8,128)(2,1)S(1)}, u32[]{:S(2)}, u32[]{:S(2)}) collective-permute-start(bf16[64,768]{1,0:T(8,128)(2,1)S(1)} %get-tuple-element.70.block.refs_0_), channel_id=1, source_target_pairs={{0,1},{1,0},{2,3},{3,2},{4,5},{5,4},{6,7},{7,6},{8,9},{9,8},{10,11... | collective-permute-start | bytes 294920 | tf_op jit(solution)/shard_map/ppermute | solution.py:61
  58.3 1.3 %collective-permute-start.18 = (bf16[32,768]{1,0:T(8,128)(2,1)S(1)}, bf16[32,768]{1,0:T(8,128)(2,1)S(1)}, u32[]{:S(2)}, u32[]{:S(2)}) collective-permute-start(bf16[32,768]{1,0:T(8,128)(2,1)S(1)} %get-tuple-element.76), channel_id=1, source_target_pairs={{0,8},{8,0},{16,24},{24,16},{1,9},{9,1},{17,25},{25,17},{2,10},{10... | collective-permute-start | bytes 147464 | tf_op jit(solution)/shard_map/ppermute | solution.py:61
  59.6 5.9 %collective-permute-start.21 = (bf16[16,768]{1,0:T(8,128)(2,1)S(1)}, bf16[16,768]{1,0:T(8,128)(2,1)S(1)}, u32[]{:S(2)}, u32[]{:S(2)}) collective-permute-start(bf16[16,768]{1,0:T(8,128)(2,1)S(1)} %get-tuple-element.77.refs_0_), channel_id=1, source_target_pairs={{0,3},{1,2},{2,1},{3,0},{4,7},{5,6},{6,5},{7,4},{8,11},{9,10},{10,... | collective-permute-start | bytes 73736 | tf_op jit(solution)/shard_map/ppermute | solution.py:61
  61.5 4.0 %collective-permute-start.20 = (bf16[16,768]{1,0:T(8,128)(2,1)S(1)}, bf16[16,768]{1,0:T(8,128)(2,1)S(1)}, u32[]{:S(2)}, u32[]{:S(2)}) collective-permute-start(bf16[16,768]{1,0:T(8,128)(2,1)S(1)} %get-tuple-element.77.refs_0_), channel_id=1, source_target_pairs={{0,2},{1,3},{2,0},{3,1},{4,6},{5,7},{6,4},{7,5},{8,10},{9,11},{10,... | collective-permute-start | bytes 73736 | tf_op jit(solution)/shard_map/ppermute | solution.py:61
  62.9 3.8 %collective-permute-start.19 = (bf16[16,768]{1,0:T(8,128)(2,1)S(1)}, bf16[16,768]{1,0:T(8,128)(2,1)S(1)}, u32[]{:S(2)}, u32[]{:S(2)}) collective-permute-start(bf16[16,768]{1,0:T(8,128)(2,1)S(1)} %get-tuple-element.77.refs_0_), channel_id=1, source_target_pairs={{0,1},{1,0},{2,3},{3,2},{4,5},{5,4},{6,7},{7,6},{8,9},{9,8},{10,11... | collective-permute-start | bytes 73736 | tf_op jit(solution)/shard_map/ppermute | solution.py:61

commit v4 on v3

--- a/solution.py
+++ b/solution.py
@@ -105,31 +105,29 @@
 
 
 def load_kernel(rows, *refs):
-    weight, table, score, bias = refs[:4]
-    ids = refs[4:7]
-    weight_low, table_low, score_here, bias_here, together = refs[7:12]
-    weight_here, table_here, ids_here, sems = refs[12:]
-    parts = weight_here.shape[0]
-    size = weight_here.shape[1]
-    copies = [pltpu.make_async_copy(source, ids_here.at[at], sems.at[at]) for at, source in enumerate(ids)]
-    copies.append(pltpu.make_async_copy(table, table_here, sems.at[3]))
-    copies.append(pltpu.make_async_copy(score, score_here, sems.at[4]))
-    copies.append(pltpu.make_async_copy(bias, bias_here, sems.at[5]))
-    copies += [
-        pltpu.make_async_copy(weight.at[pl.ds(at * size, size), :], weight_here.at[at], sems.at[6 + at]) for at in range(parts)
+    sources = refs[:6]
+    table_low, score_here, bias_here, together, table_here, ids_here, sems = refs[6:]
+    targets = [table_here, score_here, bias_here] + [ids_here.at[at] for at in range(3)]
+    copies = [pltpu.make_async_copy(source, target, sems.at[at]) for at, (source, target) in enumerate(zip(sources, targets))]
+    for copy in copies:
+        copy.start()
+    for copy in copies:
+        copy.wait()
+    table_low[...] = table_here[...].astype(BF16)
+    for at in range(3):
+        together[at * rows : (at + 1) * rows, :] = ids_here[at].astype(F32)
+
+
+def weight_low_kernel(weight, out, here, sems):
+    parts, size = here.shape[:2]
+    copies = [
+        pltpu.make_async_copy(weight.at[pl.ds(at * size, size), :], here.at[at], sems.at[at]) for at in range(parts)
     ]
     for copy in copies:
         copy.start()
-    for at in range(3):
+    for at in range(parts):
         copies[at].wait()
-        together[at * rows : (at + 1) * rows, :] = ids_here[at].astype(F32)
-    copies[3].wait()
-    table_low[...] = table_here[...].astype(BF16)
-    copies[4].wait()
-    copies[5].wait()
-    for at in range(parts):
-        copies[6 + at].wait()
-        weight_low[at * size : (at + 1) * size, :] = weight_here[at].astype(BF16)
+        out[at * size : (at + 1) * size, :] = here[at].astype(BF16)
 
 
 def pair_kernel(first, second, out):
@@ -182,30 +180,33 @@
     table_turned[...] = table_low[...].T
 
 
-def planes_kernel(ids, before, out, hot):
+def planes_kernel(ids, out, hot):
     length = ids.shape[1]
     rows = ids.shape[0] // 3
     half = length // 2
-    tail = 128
-    ids = ids[...].astype(BF16)
-    earlier = before[:, length - tail :].astype(BF16)
+    own = ids[...].astype(BF16)
     for m in range(SPAN):
         target = 2 * lax.broadcasted_iota(jnp.int32, (length, half), 1) + 1 - m
         source = lax.broadcasted_iota(jnp.int32, (length, half), 0)
-        got = dot(ids, (source == target).astype(BF16))
-        if m > 1:
-            target = 2 * lax.broadcasted_iota(jnp.int32, (tail, half), 1) + 1 - m + tail
-            source = lax.broadcasted_iota(jnp.int32, (tail, half), 0)
-            got = got + dot(earlier, (source == target).astype(BF16))
-        out[:, m * half : (m + 1) * half] = got
-    values = hot.shape[0]
-    name = names(values, half)
+        out[:, m * half : (m + 1) * half] = dot(own, (source == target).astype(BF16))
+    name = names(hot.shape[0], half)
     for side in range(2):
         for row in range(rows):
             code = out[row : row + 1, side * half : (side + 1) * half]
             hot[:, (side * rows + row) * half : (side * rows + row + 1) * half] = one_hot(name, code)
-    edge = gathered_edges([out[:rows, (SPAN - 2 + side) * half : (SPAN - 1 + side) * half] for side in range(2)])
-    hot[:, 2 * rows * half :] = one_hot(name, edge)
+
+
+def halo_kernel(planes, before, out):
+    tail = 128
+    earlier = before[:, before.shape[1] - tail :].astype(BF16)
+    half = planes.shape[1] // SPAN
+    for m in range(SPAN):
+        part = planes[:, m * half : (m + 1) * half]
+        if m > 1:
+            target = 2 * lax.broadcasted_iota(jnp.int32, (tail, half), 1) + 1 - m + tail
+            source = lax.broadcasted_iota(jnp.int32, (tail, half), 0)
+            part = part + dot(earlier, (source == target).astype(BF16))
+        out[:, m * half : (m + 1) * half] = part
 
 
 def names(values, lanes):
@@ -261,19 +262,14 @@
 
 
 def window_of(planes, rows):
-    half = planes.shape[1] // SPAN
-
-    def part(which, m):
-        return planes[which * rows : (which + 1) * rows, m * half : (m + 1) * half]
-
-    segments = [part(1, m) for m in range(SPAN)]
-    valid = [part(2, m) for m in range(SPAN)]
+    segments = [plane[rows : 2 * rows] for plane in planes]
+    valid = [plane[2 * rows :] for plane in planes]
     mask = {
         (k, j): (segments[j + k] == segments[j]).astype(F32) * valid[j + k]
         for k in range(OFFSETS)
         for j in range(REACH)
     }
-    return [part(0, m) for m in range(SPAN)], Window(mask)
+    return [plane[:rows] for plane in planes], Window(mask)
 
 
 CODES = 0
@@ -360,7 +356,8 @@
     found = found[:count] + found[count : 2 * count] + found[2 * count :]
     for at, m in enumerate(order):
         table[group_index() ^ m] = found[at * 8 : (at + 1) * 8]
-    codes, window = window_of(planes[...], rows)
+    half = planes.shape[1] // SPAN
+    codes, window = window_of([planes[:, m * half : (m + 1) * half] for m in range(SPAN)], rows)
     bias = functools.reduce(jnp.add, [s[1:2] for s in scorers])
     both = [scorer[:8].astype(F32), jnp.broadcast_to(bias, (8, bias.shape[1]))]
     vectors[...] = jnp.concatenate(both, 0).astype(BF16)
@@ -416,20 +413,21 @@
     bias_out[...] = jnp.broadcast_to(end[:1] + end[1:2], (8, end.shape[1]))
 
 
-def inner_kernel(order, values, *refs):
-    products = pieces_of(refs[:1], len(order))
-    plan, vectors, cot = refs[1:4]
-    before, out = (refs[-2] if len(refs) > 5 else None), refs[-1]
+def inner_kernel(order, values, products, plan, vectors, cot, *refs):
+    before, out = (refs[0] if len(refs) > 1 else None), refs[-1]
     rows, half = plan.shape[1:]
     blocks = values // 16
     name = names(values, half)
+    left = products[...]
+    if before is None:
+        left = jnp.concatenate([left, vectors[...]], 0)
     for chunk in range(rows // 2):
         here = cot[2 * chunk * half : 2 * (chunk + 1) * half, :]
-        base = dot(vectors[8:], here, NT) if before is None else None
+        both = dot(left, here, NT)
         found = {}
-        for slot, m in zip(products, order):
+        for place, m in enumerate(order):
             k = group_index() ^ m
-            each = dot(slot[...], here, NT).astype(BF16)
+            each = both[place * values : (place + 1) * values].astype(BF16)
             for side in range(2):
                 row = 2 * chunk + side
                 mine = each[:, side * half : (side + 1) * half].reshape(blocks, 16, half)
@@ -444,7 +442,8 @@
             row = 2 * chunk + side
             for j in range(REACH):
                 if before is None:
-                    start = base[:1, side * half : (side + 1) * half]
+                    at = len(order) * values + 8
+                    start = both[at : at + 1, side * half : (side + 1) * half]
                 else:
                     start = before[j, row : row + 1, :]
                 out[j, row : row + 1, :] = jnp.sum(found[j, side], 0, keepdims=True) + start
@@ -491,7 +490,8 @@
         flat[k : k + 1, 2 * rows * half :] = gathered_edges(edges)
     high, low = split(flat[...])
     both = jnp.concatenate([high.astype(F32), low.astype(F32)], 0).astype(BF16)
-    lines = dot(both, hot[...], NT)
+    edge = gathered_edges([plan[CODES + SPAN - 2 + side] for side in range(2)])
+    lines = dot(both[:, : hot.shape[1]], hot[...], NT) + dot(both[:, hot.shape[1] :], one_hot(names(values, half), edge), NT)
     lines = lines[:8] + lines[8:]
     for k in range(OFFSETS):
         rows_ref[k] = jnp.broadcast_to(lines[k : k + 1], (8, values))
@@ -583,19 +583,24 @@
     return block[:8].astype(F32) + block[8:].astype(F32)
 
 
-def merge_kernel(near, near_other, far_other, sums, bias, keep, *refs):
-    sends, total = refs[:-1], refs[-1]
-    values = near.shape[0]
-    summed = near[...] + near_other[...].astype(F32) + far_other[...].astype(F32)
-    for source, at, size in chunks(values, piece_index(), group_index()):
-        total[pl.ds(at, size), :] = summed[source : source + size]
-    part = keep.shape[0]
+def small_sums(sums, bias):
     second = lax.broadcasted_iota(jnp.int32, bias.shape, 0) == 1
-    small = pack(sums[...] + jnp.where(second, bias[...], 0.0))
-    keep[...] = total[:part]
-    for at, send in enumerate(sends):
-        send[:part] = total[(at + 1) * part : (at + 2) * part].astype(BF16)
-        send[part:] = small
+    return pack(sums[...] + jnp.where(second, bias[...], 0.0))
+
+
+def sent_kernel(slots, near, far, sums, bias, *sends):
+    size = near.shape[0] // PIECES
+    for at, (slot, send) in enumerate(zip(slots, sends)):
+        total = near[slot * size : (slot + 1) * size] + far[at * size : (at + 1) * size].astype(F32)
+        send[:size] = total.astype(BF16)
+        send[size:] = small_sums(sums, bias)
+
+
+def rest_kernel(near, far, sums, bias, keep, send):
+    size = keep.shape[0]
+    keep[...] = near[:size] + far[:size].astype(F32)
+    send[:size] = (near[2 * size : 3 * size] + far[size:].astype(F32)).astype(BF16)
+    send[size:] = small_sums(sums, bias)
 
 
 def slice_kernel(keep, own, *refs):
@@ -648,68 +653,83 @@
     out[...] = (mine[...].astype(F32) + other[...].astype(F32)).astype(out.dtype)
 
 
-def joined_kernel(mine, one, two, out):
+def arrange(source, target, group):
+    values = source.shape[0]
+    for at, place, size in chunks(values, piece_index(), group):
+        target[pl.ds(place, size), :] = source[at : at + size]
+
+
+def far_sum_kernel(mine, one, two, first, second, total):
     rows = one.shape[0]
-    out[:rows] = (mine[:rows] + one[...].astype(F32)).astype(out.dtype)
-    out[rows:] = (mine[rows:] + two[...].astype(F32)).astype(out.dtype)
-
-
-def weight_kernel(order, *refs):
+    halves = [mine[:rows] + one[...].astype(F32), mine[rows:] + two[...].astype(F32)]
+    arrange(jnp.concatenate(halves, 0), total, group_index() ^ 2)
+    size = total.shape[0] // PIECES
+    for out, slots in ((first, (1, 3)), (second, (0, 2))):
+        for at, slot in enumerate(slots):
+            out[at * size : (at + 1) * size] = total[slot * size : (slot + 1) * size].astype(BF16)
+
+
+def near_sum_kernel(near, other, total):
+    arrange(near[...] + other[...].astype(F32), total, group_index())
+
+
+def weight_kernel(order, offsets, *refs):
     slots = refs[: len(order)]
-    turned, vectors, sums, out, token, full, staged, sems = refs[len(order) :]
-    token[...] = jnp.zeros(token.shape, F32)
-    values = full.shape[0]
-    placed = {m: slot for m, slot in zip(order, slots)}
-    size = values // OFFSETS // PIECES
-    for m in range(PIECES):
+    turned, vectors, sums = refs[len(order) : len(order) + 3]
+    scorers = pieces_of(refs[len(order) + 3 : len(order) + 5], len(offsets))
+    out, score_out, bias_out, ranks, full, staged, rows_ref, ends, sems = refs[len(order) + 5 :]
+    values, width = full.shape
+    group, piece = group_index(), piece_index()
+    block = values // OFFSETS
+    size = block // PIECES
+    copies = []
+
+    def send(source, target):
+        copies.append(pltpu.make_async_copy(source, target, sems.at[len(copies)]))
+        copies[-1].start()
+
+    for m, slot in zip(order, slots):
         for offset in range(OFFSETS):
-            at = (group_index() ^ offset) * (values // OFFSETS) + (piece_index() ^ m) * size
-            full[pl.ds(pl.multiple_of(at, size), size), :] = placed[m][offset * size : (offset + 1) * size]
-    line = sums[pl.ds(group_index() + 2, 1), :values]
+            at = (group ^ offset) * block + (piece ^ m) * size
+            full[pl.ds(pl.multiple_of(at, size), size), :] = slot[offset * size : (offset + 1) * size]
+    line = sums[pl.ds(group + 2, 1), :values]
     scores = jnp.concatenate([vectors[:8], vectors[:8]], 0)
     first = lax.broadcasted_iota(jnp.int32, (8, values), 0) == 0
     both = pack(jnp.where(first, jnp.broadcast_to(line, first.shape), 0.0))
-    parts = sems.shape[0]
-    step = turned.shape[0] // parts
-    copies = []
+    parts, step = staged.shape[:2]
     for part in range(parts):
         here = turned[part * step : (part + 1) * step]
         high, low = split(dot(here, both, NT))
         staged[part] = dot(here, full[...]) + dot(high, scores) + dot(low, scores)
-        copies.append(pltpu.make_async_copy(staged.at[part], out.at[pl.ds(part * step, step), :], sems.at[part]))
-        copies[-1].start()
-    for copy in copies:
-        copy.wait()
-
-
-def table_grad_kernel(order, offsets, *refs):
-    slots = refs[: len(order)]
-    scorers = pieces_of(refs[len(order) : len(order) + 2], len(offsets))
-    sums, out, score_out, bias_out, table, full, rows_ref = refs[len(order) + 2 :]
-    values = full.shape[0]
-    width = out.shape[1]
-    high, low = split(sums[2 : 2 + OFFSETS, :values])
-    for scorer, m in zip(scorers, offsets):
-        rows_ref[group_index() ^ m] = scorer[:8]
-    right = jnp.concatenate([rows_ref[k, :1] for k in range(OFFSETS)], 0)
-    right_high, right_low = split(right)
-    left = jnp.concatenate([x.astype(F32) for x in (high, low, high, low)], 0).astype(BF16)
-    right = jnp.concatenate([x.astype(F32) for x in (right_high, right_high, right_low, right_low)], 0).astype(BF16)
-    full[...] = dot(left, right, TN)
-    for slot, m in zip(slots, order):
-        size = slot.shape[0]
-        table[pl.ds(pl.multiple_of((piece_index() ^ m) * size, size), size), :] = slot[...].astype(F32)
-    rows = out.shape[0]
-    at = pl.multiple_of(row_index() * rows, rows)
-    inside = row_index() * rows - group_index() * table.shape[0]
-    out[...] = table[pl.ds(pl.multiple_of(inside, rows), rows), :] + full[pl.ds(at, rows), :]
+        send(staged.at[part], out.at[pl.ds(part * step, step), :])
     shard = score_out.shape[1]
     source = lax.broadcasted_iota(jnp.int32, (width, shard), 0)
     column = lax.broadcasted_iota(jnp.int32, (width, shard), 1) + row_index() * shard
     here = (source == column).astype(BF16)
-    ends = functools.reduce(jnp.add, [dot(part, here) for part in thirds(sums[...])])
-    score_out[...] = ends[:1]
-    bias_out[...] = ends[1:2]
+    ends[...] = functools.reduce(jnp.add, [dot(part, here) for part in thirds(sums[...])])
+    send(ends.at[pl.ds(0, 1), :], score_out)
+    send(ends.at[pl.ds(1, 1), :], bias_out)
+    for scorer, m in zip(scorers, offsets):
+        rows_ref[group ^ m] = scorer[...]
+    high, low = split(sums[2 : 2 + OFFSETS, :values])
+    right_high, right_low = split(jnp.concatenate([rows_ref[k, :1] for k in range(OFFSETS)], 0))
+    left = jnp.concatenate([x.astype(F32) for x in (high, low, high, low)], 0).astype(BF16)
+    right = jnp.concatenate([x.astype(F32) for x in (right_high, right_high, right_low, right_low)], 0).astype(BF16)
+    ranks[...] = dot(left, right, TN)
+    for copy in copies:
+        copy.wait()
+
+
+def table_grad_kernel(order, *refs):
+    slots, (ranks, out, table) = refs[: len(order)], refs[len(order) :]
+    group, block = group_index(), table.shape[0]
+    for slot, m in zip(slots, order):
+        size = slot.shape[0]
+        at = pl.multiple_of((piece_index() ^ m) * size, size)
+        table[pl.ds(at, size), :] = slot[...].astype(F32) + ranks[pl.ds(pl.multiple_of(group * block, block) + at, size), :]
+    rows = out.shape[0]
+    inside = row_index() * rows - group * block
+    out[...] = table[pl.ds(pl.multiple_of(inside, rows), rows), :]
 
 
 def bits_of(count):
@@ -737,16 +757,20 @@
     if copies > 1:
         near_by = [[g * copies + c for c in range(copies)] for g in range(OFFSETS)]
         weight = lax.all_gather(conv_weight, "rows", axis=0, tiled=True, axis_index_groups=near_by)
+    shard = (1, conv_bias.shape[0])
+    table_low, score, biases[0], ids = call(
+        functools.partial(load_kernel, rows),
+        [(table.shape, BF16), (shard, F32), (shard, F32), ((3 * rows, length), F32)],
+        (table,), (score_weight[None],), (conv_bias[None],), (byte_values,), (segment_ids,), (valid,),
+        scratch=[pltpu.VMEM(table.shape, F32), pltpu.VMEM((3, rows, length), jnp.int32), pltpu.SemaphoreType.DMA((6,))],
+        name="load",
+    )
     parts = 4
-    shard = (1, conv_bias.shape[0])
-    weight_low, table_low, score, biases[0], ids = call(
-        functools.partial(load_kernel, rows),
-        [(weight.shape, BF16), (table.shape, BF16), (shard, F32), (shard, F32), ((3 * rows, length), F32)],
-        (weight,), (table,), (score_weight[None],), (conv_bias[None],), (byte_values,), (segment_ids,), (valid,),
-        scratch=[pltpu.VMEM((parts, weight.shape[0] // parts, width), F32), pltpu.VMEM(table.shape, F32),
-                 pltpu.VMEM((3, rows, length), jnp.int32), pltpu.SemaphoreType.DMA((6 + parts,))],
-        name="load",
-    )
+    weight_low = call(
+        weight_low_kernel, [(weight.shape, BF16)], (weight,),
+        scratch=[pltpu.VMEM((parts, weight.shape[0] // parts, width), F32), pltpu.SemaphoreType.DMA((parts,))],
+        name="weight_low", after=[table_low],
+    )[0]
     scores = gathered(stacked(score, far_score, name="score"), "rows", row_bits[1:], "score")
     scorer, scored = call(
         functools.partial(scorer_kernel, slots_of(row_bits), near_order),
@@ -766,8 +790,9 @@
     tail = stacked(ids, name="tail", after=[product])
     before = lax.ppermute(tail, "tract", [(i, i + 1) for i in range(tract_count - 1)])
     planes, hot = call(
-        planes_kernel, [((3 * rows, SPAN * half), F32), ((values, 2 * rows * half + 128), BF16)], ids, before, name="planes",
-    )
+        planes_kernel, [((3 * rows, SPAN * half), F32), ((values, 2 * rows * half), BF16)], ids, name="planes", after=[product],
+    )
+    planes = call(halo_kernel, [(planes.shape, F32)], planes, before, name="halo")[0]
     scorers = call(pair_kernel, [((16, width), F32)], scored, far_scored, name="scored")[0]
     scorers = scorers, swap(scorers, "rows", group_bits[1])
 
@@ -780,17 +805,20 @@
     )
     far = call(functools.partial(block_kernel, 2, values), [((values, width), F32)], plan, cot, name="far_own")[0]
     far_sent = [swap(half_sent, "rows", copies) for half_sent in far_sent]
-    far = call(joined_kernel, [((values, width), BF16)], far, *far_sent, name="far_sum")[0]
-    far_other = swap(far, "rows", 2 * copies)
+    far = call(
+        far_sum_kernel, [((values // 2, width), BF16)] * 2, far, *far_sent,
+        scratch=[pltpu.VMEM((values, width), F32)], name="far_sum",
+    )
+    far_others = [swap(part, "rows", 2 * copies) for part in far]
+    far_product = swap(product, "rows", 2 * copies)
     near, near_sent, bias_part = call(
         functools.partial(near_kernel, [0, 1], values),
         [((values, width), F32), ((values, width), BF16), ((8, width), F32)], plan, cot,
-        scratch=[pltpu.VMEM((2 * values + EXTRA, width), F32)], name="near", after=[far],
+        scratch=[pltpu.VMEM((2 * values + EXTRA, width), F32)], name="near", after=[far_product],
     )
     near_other = swap(near_sent, "rows", copies)
 
-    far_product = swap(product, "rows", 2 * copies)
-    product = stacked(product, far_product, name="passed", after=[near_sent])
+    product = stacked(product, far_product, name="passed")
     products = product, swap(product, "rows", copies)
     inner = call(
         functools.partial(inner_kernel, [0, 2], values), [((REACH, rows, half), F32)],
@@ -802,16 +830,19 @@
     )[0]
     sums = call(
         functools.partial(score_kernel, order, values), [((8, width), F32)], *products, inner, plan, vectors, hot,
-        scratch=[pltpu.VMEM((8, hot.shape[1]), F32), pltpu.VMEM((OFFSETS, 8, values), F32)], name="scores",
+        scratch=[pltpu.VMEM((8, hot.shape[1] + half), F32), pltpu.VMEM((OFFSETS, 8, values), F32)], name="scores",
     )[0]
 
     rest = [("tract", 1 << at) for at in range(PIECES.bit_length() - 1, tract_count.bit_length() - 1)]
     rest += [("rows", 1 << at) for at in range(copies.bit_length() - 1)]
     size = values // PIECES
-    keep, *sends = call(
-        merge_kernel, [((size, width), F32)] + [((size + EXTRA, width), BF16)] * (PIECES - 1),
-        near, near_other, far_other, sums, bias_part, scratch=[pltpu.VMEM((values, width), F32)], name="merge",
-    )
+    near = call(near_sum_kernel, [((values, width), F32)], near, near_other, name="near_sum")[0]
+    sent = ((size + EXTRA, width), BF16)
+    send_one, send_three = call(
+        functools.partial(sent_kernel, (1, 3)), [sent, sent], near, far_others[0], sums, bias_part, name="merge",
+    )
+    keep, send_two = call(rest_kernel, [((size, width), F32), sent], near, far_others[1], sums, bias_part, name="rest")
+    sends = [send_one, send_two, send_three]
     others = [swap(send, "tract", at + 1) for at, send in enumerate(sends)]
     parts = 2
 
@@ -845,18 +876,18 @@
         turned = lax.dynamic_slice_in_dim(turned, rows_at % copies * (width // copies), width // copies, 0)
     weight_rows = conv_weight.shape[0]
     steps = 3
-    weight_grad, token = call(
-        functools.partial(weight_kernel, list(blocks)), [((weight_rows, width), F32), ((8, 128), F32)],
-        *blocks.values(), turned, vectors, sums,
+    weight_grad, score_grad, bias_grad, ranks = call(
+        functools.partial(weight_kernel, list(blocks), order),
+        [((weight_rows, width), F32), (shard, F32), (shard, F32), ((values, width), F32)],
+        *blocks.values(), turned, vectors, sums, *scorers,
         scratch=[pltpu.VMEM((values, width), BF16), pltpu.VMEM((steps, weight_rows // steps, width), F32),
-                 pltpu.SemaphoreType.DMA((steps,))], name="weights", final=1, copied=True,
-    )
-    table_grad, score_grad, bias_grad = call(
-        functools.partial(table_grad_kernel, list(table_pieces), order),
-        [(table.shape, F32), (shard, F32), (shard, F32)], *table_pieces.values(), *scorers, sums,
-        scratch=[pltpu.VMEM((values // OFFSETS, width), F32), pltpu.VMEM((values, width), F32), pltpu.VMEM((OFFSETS, 8, width), F32)],
-        name="table_grad", final=3, after=[token],
-    )
+                 pltpu.VMEM((OFFSETS, 8, width), F32), pltpu.VMEM((8, shard[1]), F32), pltpu.SemaphoreType.DMA((steps + 2,))],
+        name="weights", final=3, copied=True,
+    )
+    table_grad = call(
+        functools.partial(table_grad_kernel, list(table_pieces)), [(table.shape, F32)], *table_pieces.values(), ranks,
+        scratch=[pltpu.VMEM((values // OFFSETS, width), F32)], name="table_grad", final=1,
+    )[0]
     return out.reshape(cotangent.shape), table_grad, weight_grad, bias_grad[0], score_grad[0]
 
 

time: 68.1 us -> 66.7 us (0.979)
  waiting for transfers between devices: 11.9 us -> 8.03 us
  starting transfers between devices: 29.1 us -> 31.2 us
    ppermute x24 -> x25, waiting for transfers between devices: 10.3 us -> 7.11 us  [swap(): return lax.ppermute(value, axis, [(i, i ^ bit) for i in range(count)])]
    ppermute x24 -> x25, starting transfers between devices: 25.7 us -> 27.8 us  [swap(): return lax.ppermute(value, axis, [(i, i ^ bit) for i in range(count)])]
    ppermute x1, waiting for transfers between devices: 1.63 us -> 0.92 us  [body(): lax.ppermute(tail, 'tract', [(i, i + 1) for i in range(tract_count - 1)])]
    pallas_call x26 -> x30, Pallas kernels: 19.3 us -> 19.6 us  [call(): pl.pallas_call(run if after else kernel, out_shape=[jax.ShapeDtypeStruct(...]
  transfers between devices with their start and end apart: 25 -> 26, of which waited for: 11 -> 11; matrix products, arithmetic and copies ran while one was open for 0% -> 0% of each run, Pallas kernels for 35% -> 38%
where the time goes in v4:
time: 66.7 us; the launch traced here: 66.5 us
  starting transfers between devices  31.2 us (47%)
  Pallas kernels  26.4 us (40%)
  waiting for transfers between devices  8.03 us (12%)
  between operations  0.93 us (1%)
    ppermute x25, starting transfers between devices, swap(): return lax.ppermute(value, axis, [(i, i ^ bit) for i in range(count)])  27.8 us
    pallas_call x30, Pallas kernels, call(): pl.pallas_call(run if after else kernel, out_shape=[jax.ShapeDtypeStruct(...  19.6 us
    ppermute x25, waiting for transfers between devices, swap(): return lax.ppermute(value, axis, [(i, i ^ bit) for i in range(count)])  7.11 us
    pallas_call x2, Pallas kernels, output_part(): pl.pallas_call(run, out_shape=[jax.ShapeDtypeStruct((rows * half, width),...  6.78 us
    ppermute x1, starting transfers between devices, body(): lax.ppermute(tail, 'tract', [(i, i + 1) for i in range(tract_count - 1)])  3.41 us
  transfers between devices with their start and end apart: 26, of which 11 were waited for; matrix products, arithmetic and copies ran while one was open for 0% of the time, Pallas kernels for 38%

profile of v4, /device:TPU:0, one launch (start us, length us, event | category | flops | bytes accessed | tf_op | source)
XLA Modules:
  0.0 66.5 jit_solution(17456796054851970048)
XLA Ops:
  0.6 3.0 %collective-permute-start = (f32[1,192]{1,0:T(1,128)}, f32[1,192]{1,0:T(1,128)S(1)}, u32[]{:S(2)}, u32[]{:S(2)}) collective-permute-start(f32[1,192]{1,0:T(1,128)} %bitcast.13), channel_id=1, source_target_pairs={{0,16},{8,24},{16,0},{24,8},{1,17},{9,25},{17,1},{25,9},{2,18},{10... | collective-permute-start | bytes 2312 | tf_op jit(solution)/shard_map/ppermute | solution.py:61
  3.6 1.0 %load.1 = (bf16[64,768]{1,0:T(8,128)(2,1)S(1)}, f32[1,192]{1,0:T(1,128)S(1)}, f32[1,192]{1,0:T(1,128)S(1)}, f32[48,256]{1,0:T(8,128)S(1)}) custom-call(f32[64,768]{1,0:T(8,128)} %refs_0_.2, f32[1,192]{1,0:T(1,128)} %bitcast.14, f32[1,192]{1,0:T(1,128)} %bitcast.12, s32[16,256]{1,0:T(8,128)} %refs_3_.1, s32[16,256]{1,0:T(8,128)} %refs_4_.1, s32[16,256]{1,0:T(8,128)} %refs_5_.1), custom_call_target="tpu_custom_call" | custom-call | tf_op jit(solution)/shard_map/load/pallas_call | solution.py:47
  4.6 0.8 %collective-permute-done.refs_1_ = f32[1,192]{1,0:T(1,128)S(1)} collective-permute-done((f32[1,192]{1,0:T(1,128)}, f32[1,192]{1,0:T(1,128)S(1)}, u32[]{:S(2)}, u32[]{:S(2)}) %collective-permute-start) | collective-permute-done | bytes 800 | tf_op jit(solution)/shard_map/ppermute | solution.py:61
  5.4 2.1 %collective-permute-start.1 = (bf16[64,768]{1,0:T(8,128)(2,1)S(1)}, bf16[64,768]{1,0:T(8,128)(2,1)S(1)}, u32[]{:S(2)}, u32[]{:S(2)}) collective-permute-start(bf16[64,768]{1,0:T(8,128)(2,1)S(1)} %table_low.1.refs_0_), channel_id=1, source_target_pairs={{0,16},{8,24},{16,0},{24,8},{1,17},{9,25},{17,1},{25,9},{2,18},{10... | collective-permute-start | bytes 294920 | tf_op jit(solution)/shard_map/ppermute | solution.py:61
  7.5 0.0 collective-permute-start.2
  7.5 1.7 %weight_low.1.refs_3_ = bf16[768,768]{1,0:T(8,128)(2,1)S(1)} custom-call(f32[768,768]{1,0:T(8,128)} %refs_0_.3, bf16[64,768]{1,0:T(8,128)(2,1)S(1)} %get-tuple-element.45.refs_0_.refs_1_), custom_call_target="tpu_custom_call" | custom-call | tf_op jit(solution)/shard_map/weight_low/pallas_call | solution.py:47
  9.2 0.0 collective-permute-done.2.refs_1_
  9.2 0.7 %scorer.1 = (bf16[16,768]{1,0:T(8,128)(2,1)S(1)}, f32[48,768]{1,0:T(8,128)S(1)}) custom-call(f32[2,192]{1,0:T(2,128)S(1)} %score.1.refs_0_, f32[2,192]{1,0:T(2,128)S(1)} %collective-permute-done.2.refs_1_, f32[1,192]{1,0:T(1,128)S(1)} %get-tuple-element.47.refs_2_, bf16[768,768]{1,0:T(8,128)(2,1)S(1)} %weight_low.1.refs_3_), custom_call_target="tpu_custom_call" | custom-call | tf_op jit(solution)/shard_map/scorer/pallas_call | solution.py:47
  9.9 0.2 collective-permute-done.1.refs_1_
  10.1 0.4 collective-permute-start.3
  10.5 1.8 %collective-permute-start.6 = (f32[48,768]{1,0:T(8,128)S(1)}, f32[48,768]{1,0:T(8,128)S(1)}, u32[]{:S(2)}, u32[]{:S(2)}) collective-permute-start(f32[48,768]{1,0:T(8,128)S(1)} %get-tuple-element.48.refs_2_.first), channel_id=1, source_target_pairs={{0,16},{8,24},{16,0},{24,8},{1,17},{9,25},{17,1},{25,9},{2,18},{10... | collective-permute-start | bytes 442376 | tf_op jit(solution)/shard_map/ppermute | solution.py:61
  12.3 0.0 collective-permute-done.3.second
  12.3 0.5 products.1
  12.8 1.4 %collective-permute-start.4 = (bf16[256,768]{1,0:T(8,128)(2,1)S(1)}, bf16[256,768]{1,0:T(8,128)(2,1)S(1)}, u32[]{:S(2)}, u32[]{:S(2)}) collective-permute-start(bf16[256,768]{1,0:T(8,128)(2,1)S(1)} %get-tuple-element.49.refs_0_.refs_1_), channel_id=1, source_target_pairs={{0,16},{8,24},{16,0},{24,8},{1,17},{9,25},{17,1},{25,9},{2,18},{10... | collective-permute-start | bytes 1179656 | tf_op jit(solution)/shard_map/ppermute | solution.py:61
  14.2 3.4 %collective-permute-start.8 = (f32[48,256]{1,0:T(8,128)S(1)}, f32[48,256]{1,0:T(8,128)S(1)}, u32[]{:S(2)}, u32[]{:S(2)}) collective-permute-start(f32[48,256]{1,0:T(8,128)S(1)} %tail.1), channel_id=1, source_target_pairs={{0,1},{1,2},{2,3},{3,4},{4,5},{5,6},{6,7},{8,9},{9,10},{10,11},{11... | collective-permute-start | bytes 147464 | tf_op jit(solution)/shard_map/ppermute | solution.py:791
  17.7 0.1 collective-permute-start.7
  17.8 0.7 %planes.1 = (f32[48,1024]{1,0:T(8,128)S(1)}, bf16[256,4096]{1,0:T(8,128)(2,1)S(1)}) custom-call(f32[48,256]{1,0:T(8,128)S(1)} %get-tuple-element.50.refs_0_, bf16[256,768]{1,0:T(8,128)(2,1)S(1)} %get-tuple-element.49.refs_0_.refs_1_), custom_call_target="tpu_custom_call" | custom-call | tf_op jit(solution)/shard_map/planes/pallas_call | solution.py:47
  18.5 0.9 %collective-permute-done.8.before = f32[48,256]{1,0:T(8,128)S(1)} collective-permute-done((f32[48,256]{1,0:T(8,128)S(1)}, f32[48,256]{1,0:T(8,128)S(1)}, u32[]{:S(2)}, u32[]{:S(2)}) %collective-permute-start.8) | collective-permute-done | bytes 49184 | tf_op jit(solution)/shard_map/ppermute | solution.py:791
  19.4 0.2 halo.1.refs_3_
  19.6 0.0 collective-permute-done.7.refs_1_.refs_8_
  19.6 1.8 %far.1 = (bf16[128,768]{1,0:T(8,128)(2,1)S(1)}, bf16[128,768]{1,0:T(8,128)(2,1)S(1)}, f32[57,16,128]{2,1,0:T(8,128)S(1)}, bf16[16,768]{1,0:T(8,128)(2,1)S(1)}) custom-call(f32[16,768]{1,0:T(8,128)S(1)} %scored.1.refs_0_.refs_7_, f32[16,768]{1,0:T(8,128)S(1)} %collective-permute-done.7.refs_1_.refs_8_, bf16[256,768]{1,0:T(8,128)(2,1)S(1)} %table.1.table_low.refs_2_, ...), custom_call_target="tpu_custom_call" | custom-call | tf_op jit(solution)/shard_map/far/pallas_call | solution.py:47
  21.4 0.1 collective-permute-start.10
  21.5 0.5 collective-permute-start.11
  22.0 1.0 %far_own.1.mine = f32[256,768]{1,0:T(8,128)S(1)} custom-call(f32[57,16,128]{2,1,0:T(8,128)S(1)} %get-tuple-element.53.refs_0_.plan.refs_3_.refs_2_, bf16[2048,768]{1,0:T(8,128)(2,1)S(1)} %bitcast.7), custom_call_target="tpu_custom_call" | custom-call | tf_op jit(solution)/shard_map/far_own/pallas_call | solution.py:47
  23.0 0.0 collective-permute-done.10.one
  23.0 0.2 collective-permute-done.11.two
  23.2 0.1 far_sum.1
  23.4 0.7 %collective-permute-start.12 = (bf16[128,768]{1,0:T(8,128)(2,1)S(1)}, bf16[128,768]{1,0:T(8,128)(2,1)S(1)}, u32[]{:S(2)}, u32[]{:S(2)}) collective-permute-start(bf16[128,768]{1,0:T(8,128)(2,1)S(1)} %get-tuple-element.59), channel_id=1, source_target_pairs={{0,16},{8,24},{16,0},{24,8},{1,17},{9,25},{17,1},{25,9},{2,18},{10... | collective-permute-start | bytes 589832 | tf_op jit(solution)/shard_map/ppermute | solution.py:61
  24.1 1.4 %collective-permute-start.13 = (bf16[128,768]{1,0:T(8,128)(2,1)S(1)}, bf16[128,768]{1,0:T(8,128)(2,1)S(1)}, u32[]{:S(2)}, u32[]{:S(2)}) collective-permute-start(bf16[128,768]{1,0:T(8,128)(2,1)S(1)} %get-tuple-element.64), channel_id=1, source_target_pairs={{0,16},{8,24},{16,0},{24,8},{1,17},{9,25},{17,1},{25,9},{2,18},{10... | collective-permute-start | bytes 589832 | tf_op jit(solution)/shard_map/ppermute | solution.py:61
  25.4 0.0 collective-permute-done.4.refs_1_.refs_2_
  25.5 0.1 passed.1.products.refs_0_
  25.5 0.1 collective-permute-start.5
  25.6 2.0 %near.1 = (f32[256,768]{1,0:T(8,128)S(1)}, bf16[256,768]{1,0:T(8,128)(2,1)S(1)}, f32[8,768]{1,0:T(8,128)S(1)}) custom-call(f32[57,16,128]{2,1,0:T(8,128)S(1)} %get-tuple-element.53.refs_0_.plan.refs_3_.refs_2_, bf16[2048,768]{1,0:T(8,128)(2,1)S(1)} %bitcast.8, bf16[256,768]{1,0:T(8,128)(2,1)S(1)} %collective-permute-done.4.refs_1_.refs_2_), custom_call_target="tpu_custom_call" | custom-call | tf_op jit(solution)/shard_map/near/pallas_call | solution.py:47
  27.6 0.6 collective-permute-start.9
  28.1 2.2 %inner_near.1.refs_0_ = f32[5,16,128]{2,1,0:T(8,128)S(1)} custom-call(bf16[512,768]{1,0:T(8,128)(2,1)S(1)} %passed.1.products.refs_0_, f32[57,16,128]{2,1,0:T(8,128)S(1)} %get-tuple-element.53.refs_0_.plan.refs_3_.refs_2_, bf16[16,768]{1,0:T(8,128)(2,1)S(1)} %get-tuple-element.54.vectors.refs_4_.refs_3_.refs_5_, bf16[2048,768]{1,0:T(8,128)(2,1)S(1)} %bitcast.9), custom_call_target="tpu_custom_call" | custom-call | flops 99999997952 | tf_op jit(solution)/shard_map/inner_near/pallas_call | solution.py:47
  30.3 0.1 near_sum.1.near
  30.4 2.1 %inner_far.1.refs_2_ = f32[5,16,128]{2,1,0:T(8,128)S(1)} custom-call(bf16[512,768]{1,0:T(8,128)(2,1)S(1)} %collective-permute-done.5.products.refs_1_, f32[57,16,128]{2,1,0:T(8,128)S(1)} %get-tuple-element.53.refs_0_.plan.refs_3_.refs_2_, bf16[16,768]{1,0:T(8,128)(2,1)S(1)} %get-tuple-element.54.vectors.refs_4_.refs_3_.refs_5_, ...), custom_call_target="tpu_custom_call" | custom-call | tf_op jit(solution)/shard_map/inner_far/pallas_call | solution.py:47
  32.6 1.6 %scores.1.sums = f32[8,768]{1,0:T(8,128)S(1)} custom-call(bf16[512,768]{1,0:T(8,128)(2,1)S(1)} %passed.1.products.refs_0_, bf16[512,768]{1,0:T(8,128)(2,1)S(1)} %collective-permute-done.5.products.refs_1_, f32[5,16,128]{2,1,0:T(8,128)S(1)} %inner_far.1.refs_2_, f32[57,16,128]{2,1,0:T(8,128)S(1)} %get-tuple-element.53.refs_0_.plan.refs_3_.refs_2_, ...), custom_call_target="tpu_custom_call" | custom-call | tf_op jit(solution)/shard_map/scores/pallas_call | solution.py:47
  34.2 0.5 collective-permute-done.13.far
  34.7 0.1 merge.1
  34.7 3.4 %collective-permute-start.16 = (bf16[80,768]{1,0:T(8,128)(2,1)S(1)}, bf16[80,768]{1,0:T(8,128)(2,1)S(1)}, u32[]{:S(2)}, u32[]{:S(2)}) collective-permute-start(bf16[80,768]{1,0:T(8,128)(2,1)S(1)} %get-tuple-element.67), channel_id=1, source_target_pairs={{0,3},{1,2},{2,1},{3,0},{4,7},{5,6},{6,5},{7,4},{8,11},{9,10},{10,... | collective-permute-start | bytes 368648 | tf_op jit(solution)/shard_map/ppermute | solution.py:61
  38.1 1.4 %collective-permute-start.14 = (bf16[80,768]{1,0:T(8,128)(2,1)S(1)}, bf16[80,768]{1,0:T(8,128)(2,1)S(1)}, u32[]{:S(2)}, u32[]{:S(2)}) collective-permute-start(bf16[80,768]{1,0:T(8,128)(2,1)S(1)} %get-tuple-element.65.refs_1_), channel_id=1, source_target_pairs={{0,1},{1,0},{2,3},{3,2},{4,5},{5,4},{6,7},{7,6},{8,9},{9,8},{10,11... | collective-permute-start | bytes 368648 | tf_op jit(solution)/shard_map/ppermute | solution.py:61
  39.6 0.1 collective-permute-start.15
  39.7 3.5 %output.2 = (bf16[2048,768]{1,0:T(8,128)(2,1)}, f32[8,128]{1,0:T(8,128)S(1)}) custom-call(bf16[512,768]{1,0:T(8,128)(2,1)S(1)} %passed.1.products.refs_0_, bf16[512,768]{1,0:T(8,128)(2,1)S(1)} %collective-permute-done.5.products.refs_1_, f32[57,16,128]{2,1,0:T(8,128)S(1)} %get-tuple-element.53.refs_0_.plan.refs_3_.refs_2_, ...), custom_call_target="tpu_custom_call" | custom-call | tf_op jit(solution)/shard_map/output/pallas_call | solution.py:555
  43.2 0.6 collective-permute-done.14.refs_2_
  43.8 0.7 %collective-permute-done.15.refs_3_ = bf16[80,768]{1,0:T(8,128)(2,1)S(1)} collective-permute-done((bf16[80,768]{1,0:T(8,128)(2,1)S(1)}, bf16[80,768]{1,0:T(8,128)(2,1)S(1)}, u32[]{:S(2)}, u32[]{:S(2)}) %collective-permute-start.15) | collective-permute-done | bytes 122912 | tf_op jit(solution)/shard_map/ppermute | solution.py:61
  44.5 0.1 slice.1.refs_5_.refs_0_
  44.6 3.0 %collective-permute-start.17 = (bf16[80,768]{1,0:T(8,128)(2,1)S(1)}, bf16[80,768]{1,0:T(8,128)(2,1)S(1)}, u32[]{:S(2)}, u32[]{:S(2)}) collective-permute-start(bf16[80,768]{1,0:T(8,128)(2,1)S(1)} %slice.1.refs_5_.refs_0_), channel_id=1, source_target_pairs={{0,4},{1,5},{2,6},{3,7},{4,0},{5,1},{6,2},{7,3},{8,12},{9,13},{10,... | collective-permute-start | bytes 368648 | tf_op jit(solution)/shard_map/ppermute | solution.py:61
  47.6 3.3 %output.3 = (bf16[2048,768]{1,0:T(8,128)(2,1)}, f32[8,128]{1,0:T(8,128)S(1)}) custom-call(bf16[512,768]{1,0:T(8,128)(2,1)S(1)} %passed.1.products.refs_0_, bf16[512,768]{1,0:T(8,128)(2,1)S(1)} %collective-permute-done.5.products.refs_1_, f32[57,16,128]{2,1,0:T(8,128)S(1)} %get-tuple-element.53.refs_0_.plan.refs_3_.refs_2_, ...), custom_call_target="tpu_custom_call", output_to_operand_aliasing={{0}: (4, {})} | custom-call | tf_op jit(solution)/shard_map/output/pallas_call | solution.py:555
  50.9 2.1 %collective-permute-done.17.refs_1_ = bf16[80,768]{1,0:T(8,128)(2,1)S(1)} collective-permute-done((bf16[80,768]{1,0:T(8,128)(2,1)S(1)}, bf16[80,768]{1,0:T(8,128)(2,1)S(1)}, u32[]{:S(2)}, u32[]{:S(2)}) %collective-permute-start.17) | collective-permute-done | bytes 122912 | tf_op jit(solution)/shard_map/ppermute | solution.py:61
  53.0 0.5 share.1
  53.5 0.7 %collective-permute-start.18 = (bf16[48,768]{1,0:T(8,128)(2,1)S(1)}, bf16[48,768]{1,0:T(8,128)(2,1)S(1)}, u32[]{:S(2)}, u32[]{:S(2)}) collective-permute-start(bf16[48,768]{1,0:T(8,128)(2,1)S(1)} %get-tuple-element.74), channel_id=1, source_target_pairs={{0,16},{8,24},{16,0},{24,8},{1,17},{9,25},{17,1},{25,9},{2,18},{10... | collective-permute-start | bytes 221192 | tf_op jit(solution)/shard_map/ppermute | solution.py:61
  54.3 1.3 %collective-permute-start.25 = (bf16[64,768]{1,0:T(8,128)(2,1)S(1)}, bf16[64,768]{1,0:T(8,128)(2,1)S(1)}, u32[]{:S(2)}, u32[]{:S(2)}) collective-permute-start(bf16[64,768]{1,0:T(8,128)(2,1)S(1)} %get-tuple-element.71.block.refs_0_), channel_id=1, source_target_pairs={{0,3},{1,2},{2,1},{3,0},{4,7},{5,6},{6,5},{7,4},{8,11},{9,10},{10,... | collective-permute-start | bytes 294920 | tf_op jit(solution)/shard_map/ppermute | solution.py:61
  55.5 1.4 %collective-permute-start.24 = (bf16[64,768]{1,0:T(8,128)(2,1)S(1)}, bf16[64,768]{1,0:T(8,128)(2,1)S(1)}, u32[]{:S(2)}, u32[]{:S(2)}) collective-permute-start(bf16[64,768]{1,0:T(8,128)(2,1)S(1)} %get-tuple-element.71.block.refs_0_), channel_id=1, source_target_pairs={{0,2},{1,3},{2,0},{3,1},{4,6},{5,7},{6,4},{7,5},{8,10},{9,11},{10,... | collective-permute-start | bytes 294920 | tf_op jit(solution)/shard_map/ppermute | solution.py:61
  56.9 0.9 %collective-permute-start.23 = (bf16[64,768]{1,0:T(8,128)(2,1)S(1)}, bf16[64,768]{1,0:T(8,128)(2,1)S(1)}, u32[]{:S(2)}, u32[]{:S(2)}) collective-permute-start(bf16[64,768]{1,0:T(8,128)(2,1)S(1)} %get-tuple-element.71.block.refs_0_), channel_id=1, source_target_pairs={{0,1},{1,0},{2,3},{3,2},{4,5},{5,4},{6,7},{7,6},{8,9},{9,8},{10,11... | collective-permute-start | bytes 294920 | tf_op jit(solution)/shard_map/ppermute | solution.py:61
  57.8 0.2 collective-permute-done.18.other
  57.9 0.1 collective-permute-start.19
  58.0 1.2 %collective-permute-done.19.other = bf16[32,768]{1,0:T(8,128)(2,1)S(1)} collective-permute-done((bf16[32,768]{1,0:T(8,128)(2,1)S(1)}, bf16[32,768]{1,0:T(8,128)(2,1)S(1)}, u32[]{:S(2)}, u32[]{:S(2)}) %collective-permute-start.19) | collective-permute-done | bytes 49184 | tf_op jit(solution)/shard_map/ppermute | solution.py:61
  59.2 1.3 %collective-permute-start.22 = (bf16[16,768]{1,0:T(8,128)(2,1)S(1)}, bf16[16,768]{1,0:T(8,128)(2,1)S(1)}, u32[]{:S(2)}, u32[]{:S(2)}) collective-permute-start(bf16[16,768]{1,0:T(8,128)(2,1)S(1)} %get-tuple-element.78.refs_0_), channel_id=1, source_target_pairs={{0,3},{1,2},{2,1},{3,0},{4,7},{5,6},{6,5},{7,4},{8,11},{9,10},{10,... | collective-permute-start | bytes 73736 | tf_op jit(solution)/shard_map/ppermute | solution.py:61
  60.6 1.4 %collective-permute-start.21 = (bf16[16,768]{1,0:T(8,128)(2,1)S(1)}, bf16[16,768]{1,0:T(8,128)(2,1)S(1)}, u32[]{:S(2)}, u32[]{:S(2)}) collective-permute-start(bf16[16,768]{1,0:T(8,128)(2,1)S(1)} %get-tuple-element.78.refs_0_), channel_id=1, source_target_pairs={{0,2},{1,3},{2,0},{3,1},{4,6},{5,7},{6,4},{7,5},{8,10},{9,11},{10,... | collective-permute-start | bytes 73736 | tf_op jit(solution)/shard_map/ppermute | solution.py:61
  62.0 0.8 %collective-permute-start.20 = (bf16[16,768]{1,0:T(8,128)(2,1)S(1)}, bf16[16,768]{1,0:T(8,128)(2,1)S(1)}, u32[]{:S(2)}, u32[]{:S(2)}) collective-permute-start(bf16[16,768]{1,0:T(8,128)(2,1)S(1)} %get-tuple-element.78.refs_0_), channel_id=1, source_target_pairs={{0,1},{1,0},{2,3},{3,2},{4,5},{5,4},{6,7},{7,6},{8,9},{9,8},{10,11... | collective-permute-start | bytes 73736 | tf_op jit(solution)/shard_map/ppermute | solution.py:61
  62.8 2.3 %weights.1 = (f32[768,768]{1,0:T(8,128)}, f32[1,192]{1,0:T(1,128)}, f32[1,192]{1,0:T(1,128)}, f32[256,768]{1,0:T(8,128)S(1)}) custom-call(bf16[64,768]{1,0:T(8,128)(2,1)S(1)} %get-tuple-element.71.block.refs_0_, bf16[64,768]{1,0:T(8,128)(2,1)S(1)} %collective-permute-done.23.refs_1_, bf16[64,768]{1,0:T(8,128)(2,1)S(1)} %collective-permute-done.24.refs_2_, ...), custom_call_target="tpu_custom_call" | custom-call | tf_op jit(solution)/shard_map/weights/pallas_call | solution.py:47
  65.2 0.6 collective-permute-done.20.refs_1_
  65.8 0.7 %table_grad.1 = f32[64,768]{1,0:T(8,128)} custom-call(bf16[16,768]{1,0:T(8,128)(2,1)S(1)} %get-tuple-element.78.refs_0_, bf16[16,768]{1,0:T(8,128)(2,1)S(1)} %collective-permute-done.20.refs_1_, bf16[16,768]{1,0:T(8,128)(2,1)S(1)} %collective-permute-done.21.refs_2_, bf16[16,768]{1,0:T(8,128)(2,1)S(1)} %collective-permute-done.22.refs_3_, ...), custom_call_target="tpu_custom_call" | custom-call | tf_op jit(solution)/shard_map/table_grad/pallas_call | solution.py:47
  (22 shorter events, 0.2 us)
Async XLA Ops:
  0.6 4.8 %collective-permute-start = (f32[1,192]{1,0:T(1,128)}, f32[1,192]{1,0:T(1,128)S(1)}, u32[]{:S(2)}, u32[]{:S(2)}) collective-permute-start(f32[1,192]{1,0:T(1,128)} %bitcast.13), channel_id=1, source_target_pairs={{0,16},{8,24},{16,0},{24,8},{1,17},{9,25},{17,1},{25,9},{2,18},{10... | collective-permute-start | bytes 2312 | tf_op jit(solution)/shard_map/ppermute | solution.py:61
  5.4 4.7 %collective-permute-start.1 = (bf16[64,768]{1,0:T(8,128)(2,1)S(1)}, bf16[64,768]{1,0:T(8,128)(2,1)S(1)}, u32[]{:S(2)}, u32[]{:S(2)}) collective-permute-start(bf16[64,768]{1,0:T(8,128)(2,1)S(1)} %table_low.1.refs_0_), channel_id=1, source_target_pairs={{0,16},{8,24},{16,0},{24,8},{1,17},{9,25},{17,1},{25,9},{2,18},{10... | collective-permute-start | bytes 294920 | tf_op jit(solution)/shard_map/ppermute | solution.py:61
  7.5 1.7 %collective-permute-start.2 = (f32[2,192]{1,0:T(2,128)S(1)}, f32[2,192]{1,0:T(2,128)S(1)}, u32[]{:S(2)}, u32[]{:S(2)}) collective-permute-start(f32[2,192]{1,0:T(2,128)S(1)} %score.1.refs_0_), channel_id=1, source_target_pairs={{0,8},{8,0},{16,24},{24,16},{1,9},{9,1},{17,25},{25,17},{2,10},{10... | collective-permute-start | bytes 4616 | tf_op jit(solution)/shard_map/ppermute | solution.py:61
  9.9 9.8 %copy-start = (bf16[16,128,768]{2,1,0:T(8,128)(2,1)S(1)}, bf16[16,128,768]{2,1,0:T(8,128)(2,1)}, u32[]{:S(2)}) copy-start(bf16[16,128,768]{2,1,0:T(8,128)(2,1)} %param.15) | copy-start | bytes 9437188
  10.1 2.2 %collective-permute-start.3 = (bf16[128,768]{1,0:T(8,128)(2,1)S(1)}, bf16[128,768]{1,0:T(8,128)(2,1)S(1)}, u32[]{:S(2)}, u32[]{:S(2)}) collective-permute-start(bf16[128,768]{1,0:T(8,128)(2,1)S(1)} %table_pair.1.first), channel_id=1, source_target_pairs={{0,8},{8,0},{16,24},{24,16},{1,9},{9,1},{17,25},{25,17},{2,10},{10... | collective-permute-start | bytes 589832 | tf_op jit(solution)/shard_map/ppermute | solution.py:61
  10.5 7.2 %collective-permute-start.6 = (f32[48,768]{1,0:T(8,128)S(1)}, f32[48,768]{1,0:T(8,128)S(1)}, u32[]{:S(2)}, u32[]{:S(2)}) collective-permute-start(f32[48,768]{1,0:T(8,128)S(1)} %get-tuple-element.48.refs_2_.first), channel_id=1, source_target_pairs={{0,16},{8,24},{16,0},{24,8},{1,17},{9,25},{17,1},{25,9},{2,18},{10... | collective-permute-start | bytes 442376 | tf_op jit(solution)/shard_map/ppermute | solution.py:61
  12.8 12.6 %collective-permute-start.4 = (bf16[256,768]{1,0:T(8,128)(2,1)S(1)}, bf16[256,768]{1,0:T(8,128)(2,1)S(1)}, u32[]{:S(2)}, u32[]{:S(2)}) collective-permute-start(bf16[256,768]{1,0:T(8,128)(2,1)S(1)} %get-tuple-element.49.refs_0_.refs_1_), channel_id=1, source_target_pairs={{0,16},{8,24},{16,0},{24,8},{1,17},{9,25},{17,1},{25,9},{2,18},{10... | collective-permute-start | bytes 1179656 | tf_op jit(solution)/shard_map/ppermute | solution.py:61
  14.2 5.2 %collective-permute-start.8 = (f32[48,256]{1,0:T(8,128)S(1)}, f32[48,256]{1,0:T(8,128)S(1)}, u32[]{:S(2)}, u32[]{:S(2)}) collective-permute-start(f32[48,256]{1,0:T(8,128)S(1)} %tail.1), channel_id=1, source_target_pairs={{0,1},{1,2},{2,3},{3,4},{4,5},{5,6},{6,7},{8,9},{9,10},{10,11},{11... | collective-permute-start | bytes 147464 | tf_op jit(solution)/shard_map/ppermute | solution.py:791
  17.7 1.9 %collective-permute-start.7 = (f32[16,768]{1,0:T(8,128)S(1)}, f32[16,768]{1,0:T(8,128)S(1)}, u32[]{:S(2)}, u32[]{:S(2)}) collective-permute-start(f32[16,768]{1,0:T(8,128)S(1)} %scored.1.refs_0_.refs_7_), channel_id=1, source_target_pairs={{0,8},{8,0},{16,24},{24,16},{1,9},{9,1},{17,25},{25,17},{2,10},{10... | collective-permute-start | bytes 147464 | tf_op jit(solution)/shard_map/ppermute | solution.py:61
  21.4 1.6 %collective-permute-start.10 = (bf16[128,768]{1,0:T(8,128)(2,1)S(1)}, bf16[128,768]{1,0:T(8,128)(2,1)S(1)}, u32[]{:S(2)}, u32[]{:S(2)}) collective-permute-start(bf16[128,768]{1,0:T(8,128)(2,1)S(1)} %get-tuple-element.57), channel_id=1, source_target_pairs={{0,8},{8,0},{16,24},{24,16},{1,9},{9,1},{17,25},{25,17},{2,10},{10... | collective-permute-start | bytes 589832 | tf_op jit(solution)/shard_map/ppermute | solution.py:61
  21.5 1.7 %collective-permute-start.11 = (bf16[128,768]{1,0:T(8,128)(2,1)S(1)}, bf16[128,768]{1,0:T(8,128)(2,1)S(1)}, u32[]{:S(2)}, u32[]{:S(2)}) collective-permute-start(bf16[128,768]{1,0:T(8,128)(2,1)S(1)} %get-tuple-element.58), channel_id=1, source_target_pairs={{0,8},{8,0},{16,24},{24,16},{1,9},{9,1},{17,25},{25,17},{2,10},{10... | collective-permute-start | bytes 589832 | tf_op jit(solution)/shard_map/ppermute | solution.py:61
  23.4 16.2 %collective-permute-start.12 = (bf16[128,768]{1,0:T(8,128)(2,1)S(1)}, bf16[128,768]{1,0:T(8,128)(2,1)S(1)}, u32[]{:S(2)}, u32[]{:S(2)}) collective-permute-start(bf16[128,768]{1,0:T(8,128)(2,1)S(1)} %get-tuple-element.59), channel_id=1, source_target_pairs={{0,16},{8,24},{16,0},{24,8},{1,17},{9,25},{17,1},{25,9},{2,18},{10... | collective-permute-start | bytes 589832 | tf_op jit(solution)/shard_map/ppermute | solution.py:61
  24.1 10.6 %collective-permute-start.13 = (bf16[128,768]{1,0:T(8,128)(2,1)S(1)}, bf16[128,768]{1,0:T(8,128)(2,1)S(1)}, u32[]{:S(2)}, u32[]{:S(2)}) collective-permute-start(bf16[128,768]{1,0:T(8,128)(2,1)S(1)} %get-tuple-element.64), channel_id=1, source_target_pairs={{0,16},{8,24},{16,0},{24,8},{1,17},{9,25},{17,1},{25,9},{2,18},{10... | collective-permute-start | bytes 589832 | tf_op jit(solution)/shard_map/ppermute | solution.py:61
  25.5 4.9 %collective-permute-start.5 = (bf16[512,768]{1,0:T(8,128)(2,1)S(1)}, bf16[512,768]{1,0:T(8,128)(2,1)S(1)}, u32[]{:S(2)}, u32[]{:S(2)}) collective-permute-start(bf16[512,768]{1,0:T(8,128)(2,1)S(1)} %passed.1.products.refs_0_), channel_id=1, source_target_pairs={{0,8},{8,0},{16,24},{24,16},{1,9},{9,1},{17,25},{25,17},{2,10},{10... | collective-permute-start | bytes 2359304 | tf_op jit(solution)/shard_map/ppermute | solution.py:61
  27.6 2.7 %collective-permute-start.9 = (bf16[256,768]{1,0:T(8,128)(2,1)S(1)}, bf16[256,768]{1,0:T(8,128)(2,1)S(1)}, u32[]{:S(2)}, u32[]{:S(2)}) collective-permute-start(bf16[256,768]{1,0:T(8,128)(2,1)S(1)} %get-tuple-element.56), channel_id=1, source_target_pairs={{0,8},{8,0},{16,24},{24,16},{1,9},{9,1},{17,25},{25,17},{2,10},{10... | collective-permute-start | bytes 1179656 | tf_op jit(solution)/shard_map/ppermute | solution.py:61
  34.7 8.4 %collective-permute-start.16 = (bf16[80,768]{1,0:T(8,128)(2,1)S(1)}, bf16[80,768]{1,0:T(8,128)(2,1)S(1)}, u32[]{:S(2)}, u32[]{:S(2)}) collective-permute-start(bf16[80,768]{1,0:T(8,128)(2,1)S(1)} %get-tuple-element.67), channel_id=1, source_target_pairs={{0,3},{1,2},{2,1},{3,0},{4,7},{5,6},{6,5},{7,4},{8,11},{9,10},{10,... | collective-permute-start | bytes 368648 | tf_op jit(solution)/shard_map/ppermute | solution.py:61
  38.1 5.7 %collective-permute-start.14 = (bf16[80,768]{1,0:T(8,128)(2,1)S(1)}, bf16[80,768]{1,0:T(8,128)(2,1)S(1)}, u32[]{:S(2)}, u32[]{:S(2)}) collective-permute-start(bf16[80,768]{1,0:T(8,128)(2,1)S(1)} %get-tuple-element.65.refs_1_), channel_id=1, source_target_pairs={{0,1},{1,0},{2,3},{3,2},{4,5},{5,4},{6,7},{7,6},{8,9},{9,8},{10,11... | collective-permute-start | bytes 368648 | tf_op jit(solution)/shard_map/ppermute | solution.py:61
  39.6 4.9 %collective-permute-start.15 = (bf16[80,768]{1,0:T(8,128)(2,1)S(1)}, bf16[80,768]{1,0:T(8,128)(2,1)S(1)}, u32[]{:S(2)}, u32[]{:S(2)}) collective-permute-start(bf16[80,768]{1,0:T(8,128)(2,1)S(1)} %get-tuple-element.66), channel_id=1, source_target_pairs={{0,2},{1,3},{2,0},{3,1},{4,6},{5,7},{6,4},{7,5},{8,10},{9,11},{10,... | collective-permute-start | bytes 368648 | tf_op jit(solution)/shard_map/ppermute | solution.py:61
  44.6 8.4 %collective-permute-start.17 = (bf16[80,768]{1,0:T(8,128)(2,1)S(1)}, bf16[80,768]{1,0:T(8,128)(2,1)S(1)}, u32[]{:S(2)}, u32[]{:S(2)}) collective-permute-start(bf16[80,768]{1,0:T(8,128)(2,1)S(1)} %slice.1.refs_5_.refs_0_), channel_id=1, source_target_pairs={{0,4},{1,5},{2,6},{3,7},{4,0},{5,1},{6,2},{7,3},{8,12},{9,13},{10,... | collective-permute-start | bytes 368648 | tf_op jit(solution)/shard_map/ppermute | solution.py:61
  53.5 4.4 %collective-permute-start.18 = (bf16[48,768]{1,0:T(8,128)(2,1)S(1)}, bf16[48,768]{1,0:T(8,128)(2,1)S(1)}, u32[]{:S(2)}, u32[]{:S(2)}) collective-permute-start(bf16[48,768]{1,0:T(8,128)(2,1)S(1)} %get-tuple-element.74), channel_id=1, source_target_pairs={{0,16},{8,24},{16,0},{24,8},{1,17},{9,25},{17,1},{25,9},{2,18},{10... | collective-permute-start | bytes 221192 | tf_op jit(solution)/shard_map/ppermute | solution.py:61
  54.3 7.7 %collective-permute-start.25 = (bf16[64,768]{1,0:T(8,128)(2,1)S(1)}, bf16[64,768]{1,0:T(8,128)(2,1)S(1)}, u32[]{:S(2)}, u32[]{:S(2)}) collective-permute-start(bf16[64,768]{1,0:T(8,128)(2,1)S(1)} %get-tuple-element.71.block.refs_0_), channel_id=1, source_target_pairs={{0,3},{1,2},{2,1},{3,0},{4,7},{5,6},{6,5},{7,4},{8,11},{9,10},{10,... | collective-permute-start | bytes 294920 | tf_op jit(solution)/shard_map/ppermute | solution.py:61
  55.5 7.3 %collective-permute-start.24 = (bf16[64,768]{1,0:T(8,128)(2,1)S(1)}, bf16[64,768]{1,0:T(8,128)(2,1)S(1)}, u32[]{:S(2)}, u32[]{:S(2)}) collective-permute-start(bf16[64,768]{1,0:T(8,128)(2,1)S(1)} %get-tuple-element.71.block.refs_0_), channel_id=1, source_target_pairs={{0,2},{1,3},{2,0},{3,1},{4,6},{5,7},{6,4},{7,5},{8,10},{9,11},{10,... | collective-permute-start | bytes 294920 | tf_op jit(solution)/shard_map/ppermute | solution.py:61
  56.9 5.9 %collective-permute-start.23 = (bf16[64,768]{1,0:T(8,128)(2,1)S(1)}, bf16[64,768]{1,0:T(8,128)(2,1)S(1)}, u32[]{:S(2)}, u32[]{:S(2)}) collective-permute-start(bf16[64,768]{1,0:T(8,128)(2,1)S(1)} %get-tuple-element.71.block.refs_0_), channel_id=1, source_target_pairs={{0,1},{1,0},{2,3},{3,2},{4,5},{5,4},{6,7},{7,6},{8,9},{9,8},{10,11... | collective-permute-start | bytes 294920 | tf_op jit(solution)/shard_map/ppermute | solution.py:61
  57.9 1.3 %collective-permute-start.19 = (bf16[32,768]{1,0:T(8,128)(2,1)S(1)}, bf16[32,768]{1,0:T(8,128)(2,1)S(1)}, u32[]{:S(2)}, u32[]{:S(2)}) collective-permute-start(bf16[32,768]{1,0:T(8,128)(2,1)S(1)} %get-tuple-element.77), channel_id=1, source_target_pairs={{0,8},{8,0},{16,24},{24,16},{1,9},{9,1},{17,25},{25,17},{2,10},{10... | collective-permute-start | bytes 147464 | tf_op jit(solution)/shard_map/ppermute | solution.py:61
  59.2 5.9 %collective-permute-start.22 = (bf16[16,768]{1,0:T(8,128)(2,1)S(1)}, bf16[16,768]{1,0:T(8,128)(2,1)S(1)}, u32[]{:S(2)}, u32[]{:S(2)}) collective-permute-start(bf16[16,768]{1,0:T(8,128)(2,1)S(1)} %get-tuple-element.78.refs_0_), channel_id=1, source_target_pairs={{0,3},{1,2},{2,1},{3,0},{4,7},{5,6},{6,5},{7,4},{8,11},{9,10},{10,... | collective-permute-start | bytes 73736 | tf_op jit(solution)/shard_map/ppermute | solution.py:61
  60.6 4.6 %collective-permute-start.21 = (bf16[16,768]{1,0:T(8,128)(2,1)S(1)}, bf16[16,768]{1,0:T(8,128)(2,1)S(1)}, u32[]{:S(2)}, u32[]{:S(2)}) collective-permute-start(bf16[16,768]{1,0:T(8,128)(2,1)S(1)} %get-tuple-element.78.refs_0_), channel_id=1, source_target_pairs={{0,2},{1,3},{2,0},{3,1},{4,6},{5,7},{6,4},{7,5},{8,10},{9,11},{10,... | collective-permute-start | bytes 73736 | tf_op jit(solution)/shard_map/ppermute | solution.py:61
  62.0 3.8 %collective-permute-start.20 = (bf16[16,768]{1,0:T(8,128)(2,1)S(1)}, bf16[16,768]{1,0:T(8,128)(2,1)S(1)}, u32[]{:S(2)}, u32[]{:S(2)}) collective-permute-start(bf16[16,768]{1,0:T(8,128)(2,1)S(1)} %get-tuple-element.78.refs_0_), channel_id=1, source_target_pairs={{0,1},{1,0},{2,3},{3,2},{4,5},{5,4},{6,7},{7,6},{8,9},{9,8},{10,11... | collective-permute-start | bytes 73736 | tf_op jit(solution)/shard_map/ppermute | solution.py:61

commit v5 on v4

--- a/solution.py
+++ b/solution.py
@@ -13,6 +13,7 @@
 REACH = 5
 SPAN = 8
 EXTRA = 16
+SMALL = 8
 PIECES = 4
 EDGE = 3
 VMEM_LIMIT = 16 * 1024 * 1024
@@ -449,12 +450,8 @@
                 out[j, row : row + 1, :] = jnp.sum(found[j, side], 0, keepdims=True) + start
 
 
-def score_kernel(order, values, *refs):
-    products = pieces_of(refs[:2], len(order))
-    inner_ref, plan, vectors, hot = refs[2:6]
-    out, flat, rows_ref = refs[6:]
+def score_kernel(values, inner_ref, plan, vectors, hot, out, flat):
     rows, half = plan.shape[1:]
-    biases = vectors[8:]
     window = Window({(k, j): plan[MASKS + k * REACH + j] for k in range(OFFSETS) for j in range(REACH)})
     inner_rows = [0.5 * inner_ref[j] for j in range(REACH)]
     sides = []
@@ -493,18 +490,13 @@
     edge = gathered_edges([plan[CODES + SPAN - 2 + side] for side in range(2)])
     lines = dot(both[:, : hot.shape[1]], hot[...], NT) + dot(both[:, hot.shape[1] :], one_hot(names(values, half), edge), NT)
     lines = lines[:8] + lines[8:]
-    for k in range(OFFSETS):
-        rows_ref[k] = jnp.broadcast_to(lines[k : k + 1], (8, values))
-    width = biases.shape[1]
-    score_grad = jnp.zeros((1, width), F32)
-    for slot, m in zip(products, order):
-        got = dot(pack(rows_ref[group_index() ^ m]), slot[...])
-        score_grad = score_grad + got[:1] + got[8:9]
+    width = vectors.shape[1]
     out[...] = jnp.zeros(out.shape, F32)
-    out[:1] = score_grad + overall * biases[:1].astype(F32)
-    out[1:2] = overall * vectors[:1].astype(F32)
-    for k in range(OFFSETS):
-        out[2 + k : 3 + k, :values] = lines[k : k + 1]
+    out[:1] = overall * vectors[:1].astype(F32)
+    for k in range(OFFSETS + 1):
+        row, lane = small_place(k, values, width)
+        part = lines[k : k + 1] if k < OFFSETS else jnp.broadcast_to(overall, (1, values))
+        out[row : row + 1, lane : lane + values] = part
 
 
 def output_kernel(order, values, chunks_here, *refs):
@@ -579,13 +571,23 @@
     return jnp.concatenate([high.astype(F32), low.astype(F32)], 0).astype(BF16)
 
 
-def unpack(block):
-    return block[:8].astype(F32) + block[8:].astype(F32)
+def small_place(at, values, width):
+    per = width // values
+    return 1 + at // per, at % per * values
+
+
+def small_pack(rows):
+    high, low = split(rows)
+    return jnp.concatenate([high.astype(F32), low.astype(F32)], 0).astype(BF16)
+
+
+def small_unpack(block):
+    return block[: SMALL // 2].astype(F32) + block[SMALL // 2 :].astype(F32)
 
 
 def small_sums(sums, bias):
-    second = lax.broadcasted_iota(jnp.int32, bias.shape, 0) == 1
-    return pack(sums[...] + jnp.where(second, bias[...], 0.0))
+    first = lax.broadcasted_iota(jnp.int32, sums.shape, 0) == 0
+    return small_pack(sums[...] + jnp.where(first, bias[: sums.shape[0]], 0.0))
 
 
 def sent_kernel(slots, near, far, sums, bias, *sends):
@@ -607,23 +609,23 @@
     others, send = refs[:-1], refs[-1]
     part = keep.shape[0]
     total = functools.reduce(jnp.add, [keep[...]] + [o[:part].astype(F32) for o in others])
-    small = [unpack(x[part:]) for x in (own, *others)]
+    small = [small_unpack(x[part:]) for x in (own, *others)]
     while len(small) > 1:
         small = [small[at] + small[at + 1] for at in range(0, len(small), 2)]
     send[:part] = total.astype(BF16)
-    send[part:] = pack(small[0])
+    send[part:] = small_pack(small[0])
 
 
 def whole_kernel(mine, other, send):
-    rows = mine.shape[0] - EXTRA
+    rows = mine.shape[0] - SMALL
     send[:rows] = (mine[:rows].astype(F32) + other[:rows].astype(F32)).astype(BF16)
-    send[rows:] = pack(unpack(mine[rows:]) + unpack(other[rows:]))
+    send[rows:] = small_pack(small_unpack(mine[rows:]) + small_unpack(other[rows:]))
 
 
 def last_kernel(mine, other, block, sums):
     rows = block.shape[0]
     block[...] = (mine[:rows].astype(F32) + other[:rows].astype(F32)).astype(BF16)
-    sums[...] = unpack(mine[rows:]) + unpack(other[rows:])
+    sums[...] = small_unpack(mine[rows:]) + small_unpack(other[rows:])
 
 
 def share_kernel(block, sums, weight_low, keep, send):
@@ -631,22 +633,22 @@
     rows = keep.shape[0]
     keep[...] = product[:rows]
     send[:rows] = product[rows:].astype(BF16)
-    send[rows:] = pack(sums[...])
+    send[rows:] = small_pack(sums[...])
 
 
 def half_kernel(keep, sums, other, rest, send, total):
     rows = rest.shape[0]
     both = keep[...] + other[: 2 * rows].astype(F32)
-    total[...] = sums[...] + unpack(other[2 * rows :])
+    total[...] = sums[...] + small_unpack(other[2 * rows :])
     rest[...] = both[:rows]
     send[:rows] = both[rows:].astype(BF16)
-    send[rows:] = pack(total[...])
+    send[rows:] = small_pack(total[...])
 
 
 def combine_kernel(keep, sums, other, out, total):
     rows = keep.shape[0]
     out[...] = (keep[...] + other[:rows].astype(F32)).astype(BF16)
-    total[...] = sums[...] + unpack(other[rows:])
+    total[...] = sums[...] + small_unpack(other[rows:])
 
 
 def added_kernel(mine, other, out):
@@ -677,7 +679,8 @@
     slots = refs[: len(order)]
     turned, vectors, sums = refs[len(order) : len(order) + 3]
     scorers = pieces_of(refs[len(order) + 3 : len(order) + 5], len(offsets))
-    out, score_out, bias_out, ranks, full, staged, rows_ref, ends, sems = refs[len(order) + 5 :]
+    products = pieces_of(refs[len(order) + 5 : len(order) + 7], len(offsets))
+    out, score_out, bias_out, ranks, full, staged, rows_ref, lines, ends, sems = refs[len(order) + 7 :]
     values, width = full.shape
     group, piece = group_index(), piece_index()
     block = values // OFFSETS
@@ -692,7 +695,10 @@
         for offset in range(OFFSETS):
             at = (group ^ offset) * block + (piece ^ m) * size
             full[pl.ds(pl.multiple_of(at, size), size), :] = slot[offset * size : (offset + 1) * size]
-    line = sums[pl.ds(group + 2, 1), :values]
+    for k in range(OFFSETS):
+        row, lane = small_place(k, values, width)
+        lines[k : k + 1] = sums[row : row + 1, lane : lane + values]
+    line = lines[pl.ds(group, 1), :]
     scores = jnp.concatenate([vectors[:8], vectors[:8]], 0)
     first = lax.broadcasted_iota(jnp.int32, (8, values), 0) == 0
     both = pack(jnp.where(first, jnp.broadcast_to(line, first.shape), 0.0))
@@ -706,12 +712,19 @@
     source = lax.broadcasted_iota(jnp.int32, (width, shard), 0)
     column = lax.broadcasted_iota(jnp.int32, (width, shard), 1) + row_index() * shard
     here = (source == column).astype(BF16)
-    ends[...] = functools.reduce(jnp.add, [dot(part, here) for part in thirds(sums[...])])
+    row, lane = small_place(OFFSETS, values, width)
+    score_grad = sums[row : row + 1, lane : lane + 1] * vectors[8:9].astype(F32)
+    for product, m in zip(products, offsets):
+        got = dot(pack(jnp.broadcast_to(lines[pl.ds(group ^ m, 1), :], (8, values))), product[...])
+        score_grad = score_grad + got[:1] + got[8:9]
+    at = lax.broadcasted_iota(jnp.int32, (8, width), 0)
+    small = jnp.where(at == 0, score_grad, jnp.where(at == 1, sums[:1], 0.0))
+    ends[...] = functools.reduce(jnp.add, [dot(part, here) for part in thirds(small)])
     send(ends.at[pl.ds(0, 1), :], score_out)
     send(ends.at[pl.ds(1, 1), :], bias_out)
     for scorer, m in zip(scorers, offsets):
         rows_ref[group ^ m] = scorer[...]
-    high, low = split(sums[2 : 2 + OFFSETS, :values])
+    high, low = split(lines[:OFFSETS])
     right_high, right_low = split(jnp.concatenate([rows_ref[k, :1] for k in range(OFFSETS)], 0))
     left = jnp.concatenate([x.astype(F32) for x in (high, low, high, low)], 0).astype(BF16)
     right = jnp.concatenate([x.astype(F32) for x in (right_high, right_high, right_low, right_low)], 0).astype(BF16)
@@ -814,7 +827,7 @@
     near, near_sent, bias_part = call(
         functools.partial(near_kernel, [0, 1], values),
         [((values, width), F32), ((values, width), BF16), ((8, width), F32)], plan, cot,
-        scratch=[pltpu.VMEM((2 * values + EXTRA, width), F32)], name="near", after=[far_product],
+        scratch=[pltpu.VMEM((2 * values + EXTRA, width), F32)], name="near", after=[far_product, far[1]],
     )
     near_other = swap(near_sent, "rows", copies)
 
@@ -829,15 +842,15 @@
         products[1], plan, vectors, cot, inner, name="inner_far",
     )[0]
     sums = call(
-        functools.partial(score_kernel, order, values), [((8, width), F32)], *products, inner, plan, vectors, hot,
-        scratch=[pltpu.VMEM((8, hot.shape[1] + half), F32), pltpu.VMEM((OFFSETS, 8, values), F32)], name="scores",
+        functools.partial(score_kernel, values), [((SMALL // 2, width), F32)], inner, plan, vectors, hot,
+        scratch=[pltpu.VMEM((8, hot.shape[1] + half), F32)], name="scores",
     )[0]
 
     rest = [("tract", 1 << at) for at in range(PIECES.bit_length() - 1, tract_count.bit_length() - 1)]
     rest += [("rows", 1 << at) for at in range(copies.bit_length() - 1)]
     size = values // PIECES
     near = call(near_sum_kernel, [((values, width), F32)], near, near_other, name="near_sum")[0]
-    sent = ((size + EXTRA, width), BF16)
+    sent = ((size + SMALL, width), BF16)
     send_one, send_three = call(
         functools.partial(sent_kernel, (1, 3)), [sent, sent], near, far_others[0], sums, bias_part, name="merge",
     )
@@ -852,25 +865,25 @@
         return out, token
 
     out, token = fill(None, [0], keep)
-    send = call(slice_kernel, [((size + EXTRA, width), BF16)], keep, sends[0], *others, name="slice", after=[token])[0]
+    send = call(slice_kernel, [((size + SMALL, width), BF16)], keep, sends[0], *others, name="slice", after=[token])[0]
     out, token = fill(out, [1], send)
     for axis, bit in rest[:-1]:
         other = swap(send, axis, bit)
         send = call(whole_kernel, [(send.shape, BF16)], send, other, name="whole")[0]
     other = swap(send, *rest[-1])
-    block, sums = call(last_kernel, [((size, width), BF16), ((8, width), F32)], send, other, name="last", after=[token])
+    block, sums = call(last_kernel, [((size, width), BF16), ((SMALL // 2, width), F32)], send, other, name="last", after=[token])
 
     part = size // OFFSETS
     keep, send = call(
-        share_kernel, [((2 * part, width), F32), ((2 * part + EXTRA, width), BF16)], block, sums, weight_low, name="share",
+        share_kernel, [((2 * part, width), F32), ((2 * part + SMALL, width), BF16)], block, sums, weight_low, name="share",
     )
     other = swap(send, "rows", group_bits[0])
     blocks = {0: block} | {m: swap(block, "tract", m) for m in range(1, PIECES)}
     keep, send, sums = call(
-        half_kernel, [((part, width), F32), ((part + EXTRA, width), BF16), ((8, width), F32)], keep, sums, other, name="half",
+        half_kernel, [((part, width), F32), ((part + SMALL, width), BF16), ((SMALL // 2, width), F32)], keep, sums, other, name="half",
     )
     other = swap(send, "rows", group_bits[1])
-    table_piece, sums = call(combine_kernel, [((part, width), BF16), ((8, width), F32)], keep, sums, other, name="combine")
+    table_piece, sums = call(combine_kernel, [((part, width), BF16), ((SMALL // 2, width), F32)], keep, sums, other, name="combine")
     table_pieces = {0: table_piece} | {m: swap(table_piece, "tract", m) for m in range(1, PIECES)}
     if copies > 1:
         turned = lax.dynamic_slice_in_dim(turned, rows_at % copies * (width // copies), width // copies, 0)
@@ -879,9 +892,10 @@
     weight_grad, score_grad, bias_grad, ranks = call(
         functools.partial(weight_kernel, list(blocks), order),
         [((weight_rows, width), F32), (shard, F32), (shard, F32), ((values, width), F32)],
-        *blocks.values(), turned, vectors, sums, *scorers,
+        *blocks.values(), turned, vectors, sums, *scorers, *products,
         scratch=[pltpu.VMEM((values, width), BF16), pltpu.VMEM((steps, weight_rows // steps, width), F32),
-                 pltpu.VMEM((OFFSETS, 8, width), F32), pltpu.VMEM((8, shard[1]), F32), pltpu.SemaphoreType.DMA((steps + 2,))],
+                 pltpu.VMEM((OFFSETS, 8, width), F32), pltpu.VMEM((8, values), F32), pltpu.VMEM((8, shard[1]), F32),
+                 pltpu.SemaphoreType.DMA((steps + 2,))],
         name="weights", final=3, copied=True,
     )
     table_grad = call(

time: 66.7 us -> 65 us (0.975)
  Pallas kernels: 26.4 us -> 25.5 us
  waiting for transfers between devices: 8.03 us -> 7.19 us
    ppermute x25, waiting for transfers between devices: 7.11 us -> 6.26 us  [swap(): return lax.ppermute(value, axis, [(i, i ^ bit) for i in range(count)])]
  transfers between devices with their start and end apart: 26 -> 26, of which waited for: 11 -> 10; matrix products, arithmetic and copies ran while one was open for 0% -> 0% of each run, Pallas kernels for 38% -> 37%
where the time goes in v5:
time: 65 us; the launch traced here: 64.8 us
  starting transfers between devices  31.1 us (48%)
  Pallas kernels  25.5 us (39%)
  waiting for transfers between devices  7.19 us (11%)
  between operations  0.94 us (1%)
    ppermute x25, starting transfers between devices, swap(): return lax.ppermute(value, axis, [(i, i ^ bit) for i in range(count)])  27.7 us
    pallas_call x30, Pallas kernels, call(): pl.pallas_call(run if after else kernel, out_shape=[jax.ShapeDtypeStruct(...  19 us
    pallas_call x2, Pallas kernels, output_part(): pl.pallas_call(run, out_shape=[jax.ShapeDtypeStruct((rows * half, width),...  6.48 us
    ppermute x25, waiting for transfers between devices, swap(): return lax.ppermute(value, axis, [(i, i ^ bit) for i in range(count)])  6.26 us
    ppermute x1, starting transfers between devices, body(): lax.ppermute(tail, 'tract', [(i, i + 1) for i in range(tract_count - 1)])  3.41 us
  transfers between devices with their start and end apart: 26, of which 10 were waited for; matrix products, arithmetic and copies ran while one was open for 0% of the time, Pallas kernels for 37%

profile of v5, /device:TPU:0, one launch (start us, length us, event | category | flops | bytes accessed | tf_op | source)
XLA Modules:
  0.0 64.8 jit_solution(17759401505872239230)
XLA Ops:
  0.6 3.0 %collective-permute-start = (f32[1,192]{1,0:T(1,128)}, f32[1,192]{1,0:T(1,128)S(1)}, u32[]{:S(2)}, u32[]{:S(2)}) collective-permute-start(f32[1,192]{1,0:T(1,128)} %bitcast.13), channel_id=1, source_target_pairs={{0,16},{8,24},{16,0},{24,8},{1,17},{9,25},{17,1},{25,9},{2,18},{10... | collective-permute-start | bytes 2312 | tf_op jit(solution)/shard_map/ppermute | solution.py:62
  3.6 1.0 %load.1 = (bf16[64,768]{1,0:T(8,128)(2,1)S(1)}, f32[1,192]{1,0:T(1,128)S(1)}, f32[1,192]{1,0:T(1,128)S(1)}, f32[48,256]{1,0:T(8,128)S(1)}) custom-call(f32[64,768]{1,0:T(8,128)} %refs_0_.2, f32[1,192]{1,0:T(1,128)} %bitcast.14, f32[1,192]{1,0:T(1,128)} %bitcast.12, s32[16,256]{1,0:T(8,128)} %refs_3_.1, s32[16,256]{1,0:T(8,128)} %refs_4_.1, s32[16,256]{1,0:T(8,128)} %refs_5_.1), custom_call_target="tpu_custom_call" | custom-call | tf_op jit(solution)/shard_map/load/pallas_call | solution.py:48
  4.6 0.8 %collective-permute-done.refs_1_ = f32[1,192]{1,0:T(1,128)S(1)} collective-permute-done((f32[1,192]{1,0:T(1,128)}, f32[1,192]{1,0:T(1,128)S(1)}, u32[]{:S(2)}, u32[]{:S(2)}) %collective-permute-start) | collective-permute-done | bytes 800 | tf_op jit(solution)/shard_map/ppermute | solution.py:62
  5.4 2.1 %collective-permute-start.1 = (bf16[64,768]{1,0:T(8,128)(2,1)S(1)}, bf16[64,768]{1,0:T(8,128)(2,1)S(1)}, u32[]{:S(2)}, u32[]{:S(2)}) collective-permute-start(bf16[64,768]{1,0:T(8,128)(2,1)S(1)} %table_low.1.refs_0_), channel_id=1, source_target_pairs={{0,16},{8,24},{16,0},{24,8},{1,17},{9,25},{17,1},{25,9},{2,18},{10... | collective-permute-start | bytes 294920 | tf_op jit(solution)/shard_map/ppermute | solution.py:62
  7.5 0.0 collective-permute-start.2
  7.5 1.7 %weight_low.1.refs_3_ = bf16[768,768]{1,0:T(8,128)(2,1)S(1)} custom-call(f32[768,768]{1,0:T(8,128)} %refs_0_.3, bf16[64,768]{1,0:T(8,128)(2,1)S(1)} %get-tuple-element.45.refs_0_.refs_1_), custom_call_target="tpu_custom_call" | custom-call | tf_op jit(solution)/shard_map/weight_low/pallas_call | solution.py:48
  9.2 0.0 collective-permute-done.2.refs_1_
  9.2 0.7 %scorer.1 = (bf16[16,768]{1,0:T(8,128)(2,1)S(1)}, f32[48,768]{1,0:T(8,128)S(1)}) custom-call(f32[2,192]{1,0:T(2,128)S(1)} %score.1.refs_0_, f32[2,192]{1,0:T(2,128)S(1)} %collective-permute-done.2.refs_1_, f32[1,192]{1,0:T(1,128)S(1)} %get-tuple-element.47.refs_2_, bf16[768,768]{1,0:T(8,128)(2,1)S(1)} %weight_low.1.refs_3_), custom_call_target="tpu_custom_call" | custom-call | tf_op jit(solution)/shard_map/scorer/pallas_call | solution.py:48
  9.9 0.2 collective-permute-done.1.refs_1_
  10.1 0.4 collective-permute-start.3
  10.5 1.8 %collective-permute-start.6 = (f32[48,768]{1,0:T(8,128)S(1)}, f32[48,768]{1,0:T(8,128)S(1)}, u32[]{:S(2)}, u32[]{:S(2)}) collective-permute-start(f32[48,768]{1,0:T(8,128)S(1)} %get-tuple-element.48.refs_2_.first), channel_id=1, source_target_pairs={{0,16},{8,24},{16,0},{24,8},{1,17},{9,25},{17,1},{25,9},{2,18},{10... | collective-permute-start | bytes 442376 | tf_op jit(solution)/shard_map/ppermute | solution.py:62
  12.3 0.0 collective-permute-done.3.second
  12.3 0.5 products.1
  12.8 1.4 %collective-permute-start.4 = (bf16[256,768]{1,0:T(8,128)(2,1)S(1)}, bf16[256,768]{1,0:T(8,128)(2,1)S(1)}, u32[]{:S(2)}, u32[]{:S(2)}) collective-permute-start(bf16[256,768]{1,0:T(8,128)(2,1)S(1)} %get-tuple-element.49.refs_0_.refs_1_), channel_id=1, source_target_pairs={{0,16},{8,24},{16,0},{24,8},{1,17},{9,25},{17,1},{25,9},{2,18},{10... | collective-permute-start | bytes 1179656 | tf_op jit(solution)/shard_map/ppermute | solution.py:62
  14.2 3.4 %collective-permute-start.8 = (f32[48,256]{1,0:T(8,128)S(1)}, f32[48,256]{1,0:T(8,128)S(1)}, u32[]{:S(2)}, u32[]{:S(2)}) collective-permute-start(f32[48,256]{1,0:T(8,128)S(1)} %tail.1), channel_id=1, source_target_pairs={{0,1},{1,2},{2,3},{3,4},{4,5},{5,6},{6,7},{8,9},{9,10},{10,11},{11... | collective-permute-start | bytes 147464 | tf_op jit(solution)/shard_map/ppermute | solution.py:804
  17.7 0.0 collective-permute-done.6.second
  17.7 0.1 collective-permute-start.7
  17.8 0.7 %planes.1 = (f32[48,1024]{1,0:T(8,128)S(1)}, bf16[256,4096]{1,0:T(8,128)(2,1)S(1)}) custom-call(f32[48,256]{1,0:T(8,128)S(1)} %get-tuple-element.50.refs_0_, bf16[256,768]{1,0:T(8,128)(2,1)S(1)} %get-tuple-element.49.refs_0_.refs_1_), custom_call_target="tpu_custom_call" | custom-call | tf_op jit(solution)/shard_map/planes/pallas_call | solution.py:48
  18.5 0.9 %collective-permute-done.8.before = f32[48,256]{1,0:T(8,128)S(1)} collective-permute-done((f32[48,256]{1,0:T(8,128)S(1)}, f32[48,256]{1,0:T(8,128)S(1)}, u32[]{:S(2)}, u32[]{:S(2)}) %collective-permute-start.8) | collective-permute-done | bytes 49184 | tf_op jit(solution)/shard_map/ppermute | solution.py:804
  19.4 0.2 halo.1.refs_3_
  19.6 1.8 %far.1 = (bf16[128,768]{1,0:T(8,128)(2,1)S(1)}, bf16[128,768]{1,0:T(8,128)(2,1)S(1)}, f32[57,16,128]{2,1,0:T(8,128)S(1)}, bf16[16,768]{1,0:T(8,128)(2,1)S(1)}) custom-call(f32[16,768]{1,0:T(8,128)S(1)} %scored.1.refs_0_.refs_7_, f32[16,768]{1,0:T(8,128)S(1)} %collective-permute-done.7.refs_1_.refs_8_, bf16[256,768]{1,0:T(8,128)(2,1)S(1)} %table.1.table_low.refs_2_, ...), custom_call_target="tpu_custom_call" | custom-call | tf_op jit(solution)/shard_map/far/pallas_call | solution.py:48
  21.4 0.1 collective-permute-start.9
  21.5 0.5 collective-permute-start.10
  22.0 1.0 %far_own.1.mine = f32[256,768]{1,0:T(8,128)S(1)} custom-call(f32[57,16,128]{2,1,0:T(8,128)S(1)} %get-tuple-element.53.plan.refs_0_.refs_2_, bf16[2048,768]{1,0:T(8,128)(2,1)S(1)} %bitcast.7), custom_call_target="tpu_custom_call" | custom-call | tf_op jit(solution)/shard_map/far_own/pallas_call | solution.py:48
  23.0 0.2 collective-permute-done.10.two
  23.2 0.1 far_sum.1
  23.4 0.7 %collective-permute-start.13 = (bf16[128,768]{1,0:T(8,128)(2,1)S(1)}, bf16[128,768]{1,0:T(8,128)(2,1)S(1)}, u32[]{:S(2)}, u32[]{:S(2)}) collective-permute-start(bf16[128,768]{1,0:T(8,128)(2,1)S(1)} %get-tuple-element.64), channel_id=1, source_target_pairs={{0,16},{8,24},{16,0},{24,8},{1,17},{9,25},{17,1},{25,9},{2,18},{10... | collective-permute-start | bytes 589832 | tf_op jit(solution)/shard_map/ppermute | solution.py:62
  24.1 1.4 %collective-permute-start.12 = (bf16[128,768]{1,0:T(8,128)(2,1)S(1)}, bf16[128,768]{1,0:T(8,128)(2,1)S(1)}, u32[]{:S(2)}, u32[]{:S(2)}) collective-permute-start(bf16[128,768]{1,0:T(8,128)(2,1)S(1)} %get-tuple-element.57.refs_3_), channel_id=1, source_target_pairs={{0,16},{8,24},{16,0},{24,8},{1,17},{9,25},{17,1},{25,9},{2,18},{10... | collective-permute-start | bytes 589832 | tf_op jit(solution)/shard_map/ppermute | solution.py:62
  25.4 0.0 collective-permute-done.4.refs_1_.refs_2_
  25.5 0.1 passed.1.products.refs_0_.refs_9_
  25.5 0.1 collective-permute-start.5
  25.6 2.0 %near.1 = (f32[256,768]{1,0:T(8,128)S(1)}, bf16[256,768]{1,0:T(8,128)(2,1)S(1)}, f32[8,768]{1,0:T(8,128)S(1)}) custom-call(f32[57,16,128]{2,1,0:T(8,128)S(1)} %get-tuple-element.53.plan.refs_0_.refs_2_, bf16[2048,768]{1,0:T(8,128)(2,1)S(1)} %bitcast.8, bf16[256,768]{1,0:T(8,128)(2,1)S(1)} %collective-permute-done.4.refs_1_.refs_2_, ...), custom_call_target="tpu_custom_call" | custom-call | tf_op jit(solution)/shard_map/near/pallas_call | solution.py:48
  27.6 0.6 collective-permute-start.11
  28.1 2.2 %inner_near.1.refs_0_ = f32[5,16,128]{2,1,0:T(8,128)S(1)} custom-call(bf16[512,768]{1,0:T(8,128)(2,1)S(1)} %passed.1.products.refs_0_.refs_9_, f32[57,16,128]{2,1,0:T(8,128)S(1)} %get-tuple-element.53.plan.refs_0_.refs_2_, bf16[16,768]{1,0:T(8,128)(2,1)S(1)} %get-tuple-element.54.vectors.refs_3_.refs_5_, bf16[2048,768]{1,0:T(8,128)(2,1)S(1)} %bitcast.9), custom_call_target="tpu_custom_call" | custom-call | flops 99999997952 | tf_op jit(solution)/shard_map/inner_near/pallas_call | solution.py:48
  30.3 0.1 near_sum.1.near
  30.4 2.1 %inner_far.1.inner_ref = f32[5,16,128]{2,1,0:T(8,128)S(1)} custom-call(bf16[512,768]{1,0:T(8,128)(2,1)S(1)} %collective-permute-done.5.products.refs_1_.refs_10_, f32[57,16,128]{2,1,0:T(8,128)S(1)} %get-tuple-element.53.plan.refs_0_.refs_2_, bf16[16,768]{1,0:T(8,128)(2,1)S(1)} %get-tuple-element.54.vectors.refs_3_.refs_5_, bf16[2048,768]{1,0:T(8,128)(2,1)S(1)} %bitcast.10, ...), custom_call_target="tpu_custom_call" | custom-call | tf_op jit(solution)/shard_map/inner_far/pallas_call | solution.py:48
  32.5 0.9 %scores.1.sums = f32[4,768]{1,0:T(4,128)S(1)} custom-call(f32[5,16,128]{2,1,0:T(8,128)S(1)} %inner_far.1.inner_ref, f32[57,16,128]{2,1,0:T(8,128)S(1)} %get-tuple-element.53.plan.refs_0_.refs_2_, bf16[16,768]{1,0:T(8,128)(2,1)S(1)} %get-tuple-element.54.vectors.refs_3_.refs_5_, bf16[256,4096]{1,0:T(8,128)(2,1)S(1)} %get-tuple-element.60.hot), custom_call_target="tpu_custom_call" | custom-call | tf_op jit(solution)/shard_map/scores/pallas_call | solution.py:48
  33.5 0.1 merge.1
  33.6 3.4 %collective-permute-start.16 = (bf16[72,768]{1,0:T(8,128)(2,1)S(1)}, bf16[72,768]{1,0:T(8,128)(2,1)S(1)}, u32[]{:S(2)}, u32[]{:S(2)}) collective-permute-start(bf16[72,768]{1,0:T(8,128)(2,1)S(1)} %get-tuple-element.67), channel_id=1, source_target_pairs={{0,3},{1,2},{2,1},{3,0},{4,7},{5,6},{6,5},{7,4},{8,11},{9,10},{10,... | collective-permute-start | bytes 331784 | tf_op jit(solution)/shard_map/ppermute | solution.py:62
  37.0 1.4 %collective-permute-start.14 = (bf16[72,768]{1,0:T(8,128)(2,1)S(1)}, bf16[72,768]{1,0:T(8,128)(2,1)S(1)}, u32[]{:S(2)}, u32[]{:S(2)}) collective-permute-start(bf16[72,768]{1,0:T(8,128)(2,1)S(1)} %get-tuple-element.65.refs_1_), channel_id=1, source_target_pairs={{0,1},{1,0},{2,3},{3,2},{4,5},{5,4},{6,7},{7,6},{8,9},{9,8},{10,11... | collective-permute-start | bytes 331784 | tf_op jit(solution)/shard_map/ppermute | solution.py:62
  38.4 0.0 collective-permute-done.12.far
  38.4 0.1 collective-permute-start.15
  38.5 3.3 %output.2 = (bf16[2048,768]{1,0:T(8,128)(2,1)}, f32[8,128]{1,0:T(8,128)S(1)}) custom-call(bf16[512,768]{1,0:T(8,128)(2,1)S(1)} %passed.1.products.refs_0_.refs_9_, bf16[512,768]{1,0:T(8,128)(2,1)S(1)} %collective-permute-done.5.products.refs_1_.refs_10_, f32[57,16,128]{2,1,0:T(8,128)S(1)} %get-tuple-element.53.plan.refs_0_.refs_2_, ...), custom_call_target="tpu_custom_call" | custom-call | tf_op jit(solution)/shard_map/output/pallas_call | solution.py:547
  41.9 0.7 %collective-permute-done.14.refs_2_ = bf16[72,768]{1,0:T(8,128)(2,1)S(1)} collective-permute-done((bf16[72,768]{1,0:T(8,128)(2,1)S(1)}, bf16[72,768]{1,0:T(8,128)(2,1)S(1)}, u32[]{:S(2)}, u32[]{:S(2)}) %collective-permute-start.14) | collective-permute-done | bytes 110624 | tf_op jit(solution)/shard_map/ppermute | solution.py:62
  42.6 0.7 %collective-permute-done.15.refs_3_ = bf16[72,768]{1,0:T(8,128)(2,1)S(1)} collective-permute-done((bf16[72,768]{1,0:T(8,128)(2,1)S(1)}, bf16[72,768]{1,0:T(8,128)(2,1)S(1)}, u32[]{:S(2)}, u32[]{:S(2)}) %collective-permute-start.15) | collective-permute-done | bytes 110624 | tf_op jit(solution)/shard_map/ppermute | solution.py:62
  43.2 0.1 slice.1.refs_5_.refs_0_
  43.3 3.0 %collective-permute-start.17 = (bf16[72,768]{1,0:T(8,128)(2,1)S(1)}, bf16[72,768]{1,0:T(8,128)(2,1)S(1)}, u32[]{:S(2)}, u32[]{:S(2)}) collective-permute-start(bf16[72,768]{1,0:T(8,128)(2,1)S(1)} %slice.1.refs_5_.refs_0_), channel_id=1, source_target_pairs={{0,4},{1,5},{2,6},{3,7},{4,0},{5,1},{6,2},{7,3},{8,12},{9,13},{10,... | collective-permute-start | bytes 331784 | tf_op jit(solution)/shard_map/ppermute | solution.py:62
  46.3 3.1 %output.3 = (bf16[2048,768]{1,0:T(8,128)(2,1)}, f32[8,128]{1,0:T(8,128)S(1)}) custom-call(bf16[512,768]{1,0:T(8,128)(2,1)S(1)} %passed.1.products.refs_0_.refs_9_, bf16[512,768]{1,0:T(8,128)(2,1)S(1)} %collective-permute-done.5.products.refs_1_.refs_10_, f32[57,16,128]{2,1,0:T(8,128)S(1)} %get-tuple-element.53.plan.refs_0_.refs_2_, ...), custom_call_target="tpu_custom_call", output_to_operand_aliasing={{0}: (4, {})} | custom-call | tf_op jit(solution)/shard_map/output/pallas_call | solution.py:547
  49.5 2.1 %collective-permute-done.17.refs_1_ = bf16[72,768]{1,0:T(8,128)(2,1)S(1)} collective-permute-done((bf16[72,768]{1,0:T(8,128)(2,1)S(1)}, bf16[72,768]{1,0:T(8,128)(2,1)S(1)}, u32[]{:S(2)}, u32[]{:S(2)}) %collective-permute-start.17) | collective-permute-done | bytes 110624 | tf_op jit(solution)/shard_map/ppermute | solution.py:62
  51.6 0.5 share.1
  52.0 0.7 %collective-permute-start.18 = (bf16[40,768]{1,0:T(8,128)(2,1)S(1)}, bf16[40,768]{1,0:T(8,128)(2,1)S(1)}, u32[]{:S(2)}, u32[]{:S(2)}) collective-permute-start(bf16[40,768]{1,0:T(8,128)(2,1)S(1)} %get-tuple-element.74), channel_id=1, source_target_pairs={{0,16},{8,24},{16,0},{24,8},{1,17},{9,25},{17,1},{25,9},{2,18},{10... | collective-permute-start | bytes 184328 | tf_op jit(solution)/shard_map/ppermute | solution.py:62
  52.7 1.2 %collective-permute-start.25 = (bf16[64,768]{1,0:T(8,128)(2,1)S(1)}, bf16[64,768]{1,0:T(8,128)(2,1)S(1)}, u32[]{:S(2)}, u32[]{:S(2)}) collective-permute-start(bf16[64,768]{1,0:T(8,128)(2,1)S(1)} %get-tuple-element.71.block.refs_0_), channel_id=1, source_target_pairs={{0,3},{1,2},{2,1},{3,0},{4,7},{5,6},{6,5},{7,4},{8,11},{9,10},{10,... | collective-permute-start | bytes 294920 | tf_op jit(solution)/shard_map/ppermute | solution.py:62
  53.9 1.4 %collective-permute-start.24 = (bf16[64,768]{1,0:T(8,128)(2,1)S(1)}, bf16[64,768]{1,0:T(8,128)(2,1)S(1)}, u32[]{:S(2)}, u32[]{:S(2)}) collective-permute-start(bf16[64,768]{1,0:T(8,128)(2,1)S(1)} %get-tuple-element.71.block.refs_0_), channel_id=1, source_target_pairs={{0,2},{1,3},{2,0},{3,1},{4,6},{5,7},{6,4},{7,5},{8,10},{9,11},{10,... | collective-permute-start | bytes 294920 | tf_op jit(solution)/shard_map/ppermute | solution.py:62
  55.3 0.9 %collective-permute-start.23 = (bf16[64,768]{1,0:T(8,128)(2,1)S(1)}, bf16[64,768]{1,0:T(8,128)(2,1)S(1)}, u32[]{:S(2)}, u32[]{:S(2)}) collective-permute-start(bf16[64,768]{1,0:T(8,128)(2,1)S(1)} %get-tuple-element.71.block.refs_0_), channel_id=1, source_target_pairs={{0,1},{1,0},{2,3},{3,2},{4,5},{5,4},{6,7},{7,6},{8,9},{9,8},{10,11... | collective-permute-start | bytes 294920 | tf_op jit(solution)/shard_map/ppermute | solution.py:62
  56.2 0.1 collective-permute-done.18.other
  56.3 0.1 collective-permute-start.19
  56.4 1.2 %collective-permute-done.19.other = bf16[24,768]{1,0:T(8,128)(2,1)S(1)} collective-permute-done((bf16[24,768]{1,0:T(8,128)(2,1)S(1)}, bf16[24,768]{1,0:T(8,128)(2,1)S(1)}, u32[]{:S(2)}, u32[]{:S(2)}) %collective-permute-start.19) | collective-permute-done | bytes 36896 | tf_op jit(solution)/shard_map/ppermute | solution.py:62
  57.6 1.2 %collective-permute-start.22 = (bf16[16,768]{1,0:T(8,128)(2,1)S(1)}, bf16[16,768]{1,0:T(8,128)(2,1)S(1)}, u32[]{:S(2)}, u32[]{:S(2)}) collective-permute-start(bf16[16,768]{1,0:T(8,128)(2,1)S(1)} %get-tuple-element.78.refs_0_), channel_id=1, source_target_pairs={{0,3},{1,2},{2,1},{3,0},{4,7},{5,6},{6,5},{7,4},{8,11},{9,10},{10,... | collective-permute-start | bytes 73736 | tf_op jit(solution)/shard_map/ppermute | solution.py:62
  58.9 1.4 %collective-permute-start.21 = (bf16[16,768]{1,0:T(8,128)(2,1)S(1)}, bf16[16,768]{1,0:T(8,128)(2,1)S(1)}, u32[]{:S(2)}, u32[]{:S(2)}) collective-permute-start(bf16[16,768]{1,0:T(8,128)(2,1)S(1)} %get-tuple-element.78.refs_0_), channel_id=1, source_target_pairs={{0,2},{1,3},{2,0},{3,1},{4,6},{5,7},{6,4},{7,5},{8,10},{9,11},{10,... | collective-permute-start | bytes 73736 | tf_op jit(solution)/shard_map/ppermute | solution.py:62
  60.2 1.0 %collective-permute-start.20 = (bf16[16,768]{1,0:T(8,128)(2,1)S(1)}, bf16[16,768]{1,0:T(8,128)(2,1)S(1)}, u32[]{:S(2)}, u32[]{:S(2)}) collective-permute-start(bf16[16,768]{1,0:T(8,128)(2,1)S(1)} %get-tuple-element.78.refs_0_), channel_id=1, source_target_pairs={{0,1},{1,0},{2,3},{3,2},{4,5},{5,4},{6,7},{7,6},{8,9},{9,8},{10,11... | collective-permute-start | bytes 73736 | tf_op jit(solution)/shard_map/ppermute | solution.py:62
  61.2 0.0 collective-permute-done.23.refs_1_
  61.2 2.5 %weights.1 = (f32[768,768]{1,0:T(8,128)}, f32[1,192]{1,0:T(1,128)}, f32[1,192]{1,0:T(1,128)}, f32[256,768]{1,0:T(8,128)S(1)}) custom-call(bf16[64,768]{1,0:T(8,128)(2,1)S(1)} %get-tuple-element.71.block.refs_0_, bf16[64,768]{1,0:T(8,128)(2,1)S(1)} %collective-permute-done.23.refs_1_, bf16[64,768]{1,0:T(8,128)(2,1)S(1)} %collective-permute-done.24.refs_2_, ...), custom_call_target="tpu_custom_call" | custom-call | tf_op jit(solution)/shard_map/weights/pallas_call | solution.py:48
  63.7 0.4 collective-permute-done.20.refs_1_
  64.1 0.7 %table_grad.1 = f32[64,768]{1,0:T(8,128)} custom-call(bf16[16,768]{1,0:T(8,128)(2,1)S(1)} %get-tuple-element.78.refs_0_, bf16[16,768]{1,0:T(8,128)(2,1)S(1)} %collective-permute-done.20.refs_1_, bf16[16,768]{1,0:T(8,128)(2,1)S(1)} %collective-permute-done.21.refs_2_, bf16[16,768]{1,0:T(8,128)(2,1)S(1)} %collective-permute-done.22.refs_3_, ...), custom_call_target="tpu_custom_call" | custom-call | tf_op jit(solution)/shard_map/table_grad/pallas_call | solution.py:48
  (22 shorter events, 0.2 us)
Async XLA Ops:
  0.6 4.8 %collective-permute-start = (f32[1,192]{1,0:T(1,128)}, f32[1,192]{1,0:T(1,128)S(1)}, u32[]{:S(2)}, u32[]{:S(2)}) collective-permute-start(f32[1,192]{1,0:T(1,128)} %bitcast.13), channel_id=1, source_target_pairs={{0,16},{8,24},{16,0},{24,8},{1,17},{9,25},{17,1},{25,9},{2,18},{10... | collective-permute-start | bytes 2312 | tf_op jit(solution)/shard_map/ppermute | solution.py:62
  5.4 4.7 %collective-permute-start.1 = (bf16[64,768]{1,0:T(8,128)(2,1)S(1)}, bf16[64,768]{1,0:T(8,128)(2,1)S(1)}, u32[]{:S(2)}, u32[]{:S(2)}) collective-permute-start(bf16[64,768]{1,0:T(8,128)(2,1)S(1)} %table_low.1.refs_0_), channel_id=1, source_target_pairs={{0,16},{8,24},{16,0},{24,8},{1,17},{9,25},{17,1},{25,9},{2,18},{10... | collective-permute-start | bytes 294920 | tf_op jit(solution)/shard_map/ppermute | solution.py:62
  7.5 1.7 %collective-permute-start.2 = (f32[2,192]{1,0:T(2,128)S(1)}, f32[2,192]{1,0:T(2,128)S(1)}, u32[]{:S(2)}, u32[]{:S(2)}) collective-permute-start(f32[2,192]{1,0:T(2,128)S(1)} %score.1.refs_0_), channel_id=1, source_target_pairs={{0,8},{8,0},{16,24},{24,16},{1,9},{9,1},{17,25},{25,17},{2,10},{10... | collective-permute-start | bytes 4616 | tf_op jit(solution)/shard_map/ppermute | solution.py:62
  9.9 9.8 %copy-start = (bf16[16,128,768]{2,1,0:T(8,128)(2,1)S(1)}, bf16[16,128,768]{2,1,0:T(8,128)(2,1)}, u32[]{:S(2)}) copy-start(bf16[16,128,768]{2,1,0:T(8,128)(2,1)} %param.15) | copy-start | bytes 9437188
  10.1 2.2 %collective-permute-start.3 = (bf16[128,768]{1,0:T(8,128)(2,1)S(1)}, bf16[128,768]{1,0:T(8,128)(2,1)S(1)}, u32[]{:S(2)}, u32[]{:S(2)}) collective-permute-start(bf16[128,768]{1,0:T(8,128)(2,1)S(1)} %table_pair.1.first), channel_id=1, source_target_pairs={{0,8},{8,0},{16,24},{24,16},{1,9},{9,1},{17,25},{25,17},{2,10},{10... | collective-permute-start | bytes 589832 | tf_op jit(solution)/shard_map/ppermute | solution.py:62
  10.5 7.2 %collective-permute-start.6 = (f32[48,768]{1,0:T(8,128)S(1)}, f32[48,768]{1,0:T(8,128)S(1)}, u32[]{:S(2)}, u32[]{:S(2)}) collective-permute-start(f32[48,768]{1,0:T(8,128)S(1)} %get-tuple-element.48.refs_2_.first), channel_id=1, source_target_pairs={{0,16},{8,24},{16,0},{24,8},{1,17},{9,25},{17,1},{25,9},{2,18},{10... | collective-permute-start | bytes 442376 | tf_op jit(solution)/shard_map/ppermute | solution.py:62
  12.8 12.6 %collective-permute-start.4 = (bf16[256,768]{1,0:T(8,128)(2,1)S(1)}, bf16[256,768]{1,0:T(8,128)(2,1)S(1)}, u32[]{:S(2)}, u32[]{:S(2)}) collective-permute-start(bf16[256,768]{1,0:T(8,128)(2,1)S(1)} %get-tuple-element.49.refs_0_.refs_1_), channel_id=1, source_target_pairs={{0,16},{8,24},{16,0},{24,8},{1,17},{9,25},{17,1},{25,9},{2,18},{10... | collective-permute-start | bytes 1179656 | tf_op jit(solution)/shard_map/ppermute | solution.py:62
  14.2 5.2 %collective-permute-start.8 = (f32[48,256]{1,0:T(8,128)S(1)}, f32[48,256]{1,0:T(8,128)S(1)}, u32[]{:S(2)}, u32[]{:S(2)}) collective-permute-start(f32[48,256]{1,0:T(8,128)S(1)} %tail.1), channel_id=1, source_target_pairs={{0,1},{1,2},{2,3},{3,4},{4,5},{5,6},{6,7},{8,9},{9,10},{10,11},{11... | collective-permute-start | bytes 147464 | tf_op jit(solution)/shard_map/ppermute | solution.py:804
  17.7 1.9 %collective-permute-start.7 = (f32[16,768]{1,0:T(8,128)S(1)}, f32[16,768]{1,0:T(8,128)S(1)}, u32[]{:S(2)}, u32[]{:S(2)}) collective-permute-start(f32[16,768]{1,0:T(8,128)S(1)} %scored.1.refs_0_.refs_7_), channel_id=1, source_target_pairs={{0,8},{8,0},{16,24},{24,16},{1,9},{9,1},{17,25},{25,17},{2,10},{10... | collective-permute-start | bytes 147464 | tf_op jit(solution)/shard_map/ppermute | solution.py:62
  21.4 1.6 %collective-permute-start.9 = (bf16[128,768]{1,0:T(8,128)(2,1)S(1)}, bf16[128,768]{1,0:T(8,128)(2,1)S(1)}, u32[]{:S(2)}, u32[]{:S(2)}) collective-permute-start(bf16[128,768]{1,0:T(8,128)(2,1)S(1)} %get-tuple-element.55), channel_id=1, source_target_pairs={{0,8},{8,0},{16,24},{24,16},{1,9},{9,1},{17,25},{25,17},{2,10},{10... | collective-permute-start | bytes 589832 | tf_op jit(solution)/shard_map/ppermute | solution.py:62
  21.5 1.7 %collective-permute-start.10 = (bf16[128,768]{1,0:T(8,128)(2,1)S(1)}, bf16[128,768]{1,0:T(8,128)(2,1)S(1)}, u32[]{:S(2)}, u32[]{:S(2)}) collective-permute-start(bf16[128,768]{1,0:T(8,128)(2,1)S(1)} %get-tuple-element.56), channel_id=1, source_target_pairs={{0,8},{8,0},{16,24},{24,16},{1,9},{9,1},{17,25},{25,17},{2,10},{10... | collective-permute-start | bytes 589832 | tf_op jit(solution)/shard_map/ppermute | solution.py:62
  23.4 10.1 %collective-permute-start.13 = (bf16[128,768]{1,0:T(8,128)(2,1)S(1)}, bf16[128,768]{1,0:T(8,128)(2,1)S(1)}, u32[]{:S(2)}, u32[]{:S(2)}) collective-permute-start(bf16[128,768]{1,0:T(8,128)(2,1)S(1)} %get-tuple-element.64), channel_id=1, source_target_pairs={{0,16},{8,24},{16,0},{24,8},{1,17},{9,25},{17,1},{25,9},{2,18},{10... | collective-permute-start | bytes 589832 | tf_op jit(solution)/shard_map/ppermute | solution.py:62
  24.1 14.3 %collective-permute-start.12 = (bf16[128,768]{1,0:T(8,128)(2,1)S(1)}, bf16[128,768]{1,0:T(8,128)(2,1)S(1)}, u32[]{:S(2)}, u32[]{:S(2)}) collective-permute-start(bf16[128,768]{1,0:T(8,128)(2,1)S(1)} %get-tuple-element.57.refs_3_), channel_id=1, source_target_pairs={{0,16},{8,24},{16,0},{24,8},{1,17},{9,25},{17,1},{25,9},{2,18},{10... | collective-permute-start | bytes 589832 | tf_op jit(solution)/shard_map/ppermute | solution.py:62
  25.5 4.9 %collective-permute-start.5 = (bf16[512,768]{1,0:T(8,128)(2,1)S(1)}, bf16[512,768]{1,0:T(8,128)(2,1)S(1)}, u32[]{:S(2)}, u32[]{:S(2)}) collective-permute-start(bf16[512,768]{1,0:T(8,128)(2,1)S(1)} %passed.1.products.refs_0_.refs_9_), channel_id=1, source_target_pairs={{0,8},{8,0},{16,24},{24,16},{1,9},{9,1},{17,25},{25,17},{2,10},{10... | collective-permute-start | bytes 2359304 | tf_op jit(solution)/shard_map/ppermute | solution.py:62
  27.6 2.7 %collective-permute-start.11 = (bf16[256,768]{1,0:T(8,128)(2,1)S(1)}, bf16[256,768]{1,0:T(8,128)(2,1)S(1)}, u32[]{:S(2)}, u32[]{:S(2)}) collective-permute-start(bf16[256,768]{1,0:T(8,128)(2,1)S(1)} %get-tuple-element.59), channel_id=1, source_target_pairs={{0,8},{8,0},{16,24},{24,16},{1,9},{9,1},{17,25},{25,17},{2,10},{10... | collective-permute-start | bytes 1179656 | tf_op jit(solution)/shard_map/ppermute | solution.py:62
  33.6 8.3 %collective-permute-start.16 = (bf16[72,768]{1,0:T(8,128)(2,1)S(1)}, bf16[72,768]{1,0:T(8,128)(2,1)S(1)}, u32[]{:S(2)}, u32[]{:S(2)}) collective-permute-start(bf16[72,768]{1,0:T(8,128)(2,1)S(1)} %get-tuple-element.67), channel_id=1, source_target_pairs={{0,3},{1,2},{2,1},{3,0},{4,7},{5,6},{6,5},{7,4},{8,11},{9,10},{10,... | collective-permute-start | bytes 331784 | tf_op jit(solution)/shard_map/ppermute | solution.py:62
  37.0 5.6 %collective-permute-start.14 = (bf16[72,768]{1,0:T(8,128)(2,1)S(1)}, bf16[72,768]{1,0:T(8,128)(2,1)S(1)}, u32[]{:S(2)}, u32[]{:S(2)}) collective-permute-start(bf16[72,768]{1,0:T(8,128)(2,1)S(1)} %get-tuple-element.65.refs_1_), channel_id=1, source_target_pairs={{0,1},{1,0},{2,3},{3,2},{4,5},{5,4},{6,7},{7,6},{8,9},{9,8},{10,11... | collective-permute-start | bytes 331784 | tf_op jit(solution)/shard_map/ppermute | solution.py:62
  38.4 4.8 %collective-permute-start.15 = (bf16[72,768]{1,0:T(8,128)(2,1)S(1)}, bf16[72,768]{1,0:T(8,128)(2,1)S(1)}, u32[]{:S(2)}, u32[]{:S(2)}) collective-permute-start(bf16[72,768]{1,0:T(8,128)(2,1)S(1)} %get-tuple-element.66), channel_id=1, source_target_pairs={{0,2},{1,3},{2,0},{3,1},{4,6},{5,7},{6,4},{7,5},{8,10},{9,11},{10,... | collective-permute-start | bytes 331784 | tf_op jit(solution)/shard_map/ppermute | solution.py:62
  43.3 8.2 %collective-permute-start.17 = (bf16[72,768]{1,0:T(8,128)(2,1)S(1)}, bf16[72,768]{1,0:T(8,128)(2,1)S(1)}, u32[]{:S(2)}, u32[]{:S(2)}) collective-permute-start(bf16[72,768]{1,0:T(8,128)(2,1)S(1)} %slice.1.refs_5_.refs_0_), channel_id=1, source_target_pairs={{0,4},{1,5},{2,6},{3,7},{4,0},{5,1},{6,2},{7,3},{8,12},{9,13},{10,... | collective-permute-start | bytes 331784 | tf_op jit(solution)/shard_map/ppermute | solution.py:62
  52.0 4.3 %collective-permute-start.18 = (bf16[40,768]{1,0:T(8,128)(2,1)S(1)}, bf16[40,768]{1,0:T(8,128)(2,1)S(1)}, u32[]{:S(2)}, u32[]{:S(2)}) collective-permute-start(bf16[40,768]{1,0:T(8,128)(2,1)S(1)} %get-tuple-element.74), channel_id=1, source_target_pairs={{0,16},{8,24},{16,0},{24,8},{1,17},{9,25},{17,1},{25,9},{2,18},{10... | collective-permute-start | bytes 184328 | tf_op jit(solution)/shard_map/ppermute | solution.py:62
  52.7 7.5 %collective-permute-start.25 = (bf16[64,768]{1,0:T(8,128)(2,1)S(1)}, bf16[64,768]{1,0:T(8,128)(2,1)S(1)}, u32[]{:S(2)}, u32[]{:S(2)}) collective-permute-start(bf16[64,768]{1,0:T(8,128)(2,1)S(1)} %get-tuple-element.71.block.refs_0_), channel_id=1, source_target_pairs={{0,3},{1,2},{2,1},{3,0},{4,7},{5,6},{6,5},{7,4},{8,11},{9,10},{10,... | collective-permute-start | bytes 294920 | tf_op jit(solution)/shard_map/ppermute | solution.py:62
  53.9 7.3 %collective-permute-start.24 = (bf16[64,768]{1,0:T(8,128)(2,1)S(1)}, bf16[64,768]{1,0:T(8,128)(2,1)S(1)}, u32[]{:S(2)}, u32[]{:S(2)}) collective-permute-start(bf16[64,768]{1,0:T(8,128)(2,1)S(1)} %get-tuple-element.71.block.refs_0_), channel_id=1, source_target_pairs={{0,2},{1,3},{2,0},{3,1},{4,6},{5,7},{6,4},{7,5},{8,10},{9,11},{10,... | collective-permute-start | bytes 294920 | tf_op jit(solution)/shard_map/ppermute | solution.py:62
  55.3 5.9 %collective-permute-start.23 = (bf16[64,768]{1,0:T(8,128)(2,1)S(1)}, bf16[64,768]{1,0:T(8,128)(2,1)S(1)}, u32[]{:S(2)}, u32[]{:S(2)}) collective-permute-start(bf16[64,768]{1,0:T(8,128)(2,1)S(1)} %get-tuple-element.71.block.refs_0_), channel_id=1, source_target_pairs={{0,1},{1,0},{2,3},{3,2},{4,5},{5,4},{6,7},{7,6},{8,9},{9,8},{10,11... | collective-permute-start | bytes 294920 | tf_op jit(solution)/shard_map/ppermute | solution.py:62
  56.3 1.3 %collective-permute-start.19 = (bf16[24,768]{1,0:T(8,128)(2,1)S(1)}, bf16[24,768]{1,0:T(8,128)(2,1)S(1)}, u32[]{:S(2)}, u32[]{:S(2)}) collective-permute-start(bf16[24,768]{1,0:T(8,128)(2,1)S(1)} %get-tuple-element.77), channel_id=1, source_target_pairs={{0,8},{8,0},{16,24},{24,16},{1,9},{9,1},{17,25},{25,17},{2,10},{10... | collective-permute-start | bytes 110600 | tf_op jit(solution)/shard_map/ppermute | solution.py:62
  57.6 6.1 %collective-permute-start.22 = (bf16[16,768]{1,0:T(8,128)(2,1)S(1)}, bf16[16,768]{1,0:T(8,128)(2,1)S(1)}, u32[]{:S(2)}, u32[]{:S(2)}) collective-permute-start(bf16[16,768]{1,0:T(8,128)(2,1)S(1)} %get-tuple-element.78.refs_0_), channel_id=1, source_target_pairs={{0,3},{1,2},{2,1},{3,0},{4,7},{5,6},{6,5},{7,4},{8,11},{9,10},{10,... | collective-permute-start | bytes 73736 | tf_op jit(solution)/shard_map/ppermute | solution.py:62
  58.9 4.8 %collective-permute-start.21 = (bf16[16,768]{1,0:T(8,128)(2,1)S(1)}, bf16[16,768]{1,0:T(8,128)(2,1)S(1)}, u32[]{:S(2)}, u32[]{:S(2)}) collective-permute-start(bf16[16,768]{1,0:T(8,128)(2,1)S(1)} %get-tuple-element.78.refs_0_), channel_id=1, source_target_pairs={{0,2},{1,3},{2,0},{3,1},{4,6},{5,7},{6,4},{7,5},{8,10},{9,11},{10,... | collective-permute-start | bytes 73736 | tf_op jit(solution)/shard_map/ppermute | solution.py:62
  60.2 3.8 %collective-permute-start.20 = (bf16[16,768]{1,0:T(8,128)(2,1)S(1)}, bf16[16,768]{1,0:T(8,128)(2,1)S(1)}, u32[]{:S(2)}, u32[]{:S(2)}) collective-permute-start(bf16[16,768]{1,0:T(8,128)(2,1)S(1)} %get-tuple-element.78.refs_0_), channel_id=1, source_target_pairs={{0,1},{1,0},{2,3},{3,2},{4,5},{5,4},{6,7},{7,6},{8,9},{9,8},{10,11... | collective-permute-start | bytes 73736 | tf_op jit(solution)/shard_map/ppermute | solution.py:62

commit v6 on v5

--- a/solution.py
+++ b/solution.py
@@ -628,8 +628,12 @@
     sums[...] = small_unpack(mine[rows:]) + small_unpack(other[rows:])
 
 
-def share_kernel(block, sums, weight_low, keep, send):
-    product = dot(block[...], weight_low[...], NT)
+def turned_kernel(value, out):
+    out[...] = value[...].T
+
+
+def share_kernel(block, sums, weight_turned, keep, send):
+    product = dot(block[...], weight_turned[...])
     rows = keep.shape[0]
     keep[...] = product[:rows]
     send[:rows] = product[rows:].astype(BF16)
@@ -699,14 +703,14 @@
         row, lane = small_place(k, values, width)
         lines[k : k + 1] = sums[row : row + 1, lane : lane + values]
     line = lines[pl.ds(group, 1), :]
-    scores = jnp.concatenate([vectors[:8], vectors[:8]], 0)
+    scores = vectors[:1].astype(F32)
     first = lax.broadcasted_iota(jnp.int32, (8, values), 0) == 0
     both = pack(jnp.where(first, jnp.broadcast_to(line, first.shape), 0.0))
     parts, step = staged.shape[:2]
     for part in range(parts):
         here = turned[part * step : (part + 1) * step]
-        high, low = split(dot(here, both, NT))
-        staged[part] = dot(here, full[...]) + dot(high, scores) + dot(low, scores)
+        through = dot(here, both, NT)
+        staged[part] = dot(here, full[...]) + (through[:, :1] + through[:, 8:9]) * scores
         send(staged.at[part], out.at[pl.ds(part * step, step), :])
     shard = score_out.shape[1]
     source = lax.broadcasted_iota(jnp.int32, (width, shard), 0)
@@ -865,8 +869,9 @@
         return out, token
 
     out, token = fill(None, [0], keep)
-    send = call(slice_kernel, [((size + SMALL, width), BF16)], keep, sends[0], *others, name="slice", after=[token])[0]
+    send = call(slice_kernel, [((size + SMALL, width), BF16)], keep, sends[2], *others, name="slice", after=[token])[0]
     out, token = fill(out, [1], send)
+    weight_turned = call(turned_kernel, [(weight_low.shape, BF16)], weight_low, name="turned", after=[token])[0]
     for axis, bit in rest[:-1]:
         other = swap(send, axis, bit)
         send = call(whole_kernel, [(send.shape, BF16)], send, other, name="whole")[0]
@@ -875,7 +880,7 @@
 
     part = size // OFFSETS
     keep, send = call(
-        share_kernel, [((2 * part, width), F32), ((2 * part + SMALL, width), BF16)], block, sums, weight_low, name="share",
+        share_kernel, [((2 * part, width), F32), ((2 * part + SMALL, width), BF16)], block, sums, weight_turned, name="share",
     )
     other = swap(send, "rows", group_bits[0])
     blocks = {0: block} | {m: swap(block, "tract", m) for m in range(1, PIECES)}

time: 65 us -> 64.3 us (0.989)
    pallas_call x30 -> x31, Pallas kernels: 19 us -> 18.6 us  [call(): pl.pallas_call(run if after else kernel, out_shape=[jax.ShapeDtypeStruct(...]
where the time goes in v6:
time: 64.3 us; the launch traced here: 64.1 us
  starting transfers between devices  31.5 us (49%)
  Pallas kernels  25.1 us (39%)
  waiting for transfers between devices  6.56 us (10%)
  between operations  0.95 us (1%)
    ppermute x25, starting transfers between devices, swap(): return lax.ppermute(value, axis, [(i, i ^ bit) for i in range(count)])  28.1 us
    pallas_call x31, Pallas kernels, call(): pl.pallas_call(run if after else kernel, out_shape=[jax.ShapeDtypeStruct(...  18.6 us
    pallas_call x2, Pallas kernels, output_part(): pl.pallas_call(run, out_shape=[jax.ShapeDtypeStruct((rows * half, width),...  6.48 us
    ppermute x25, waiting for transfers between devices, swap(): return lax.ppermute(value, axis, [(i, i ^ bit) for i in range(count)])  5.63 us
    ppermute x1, starting transfers between devices, body(): lax.ppermute(tail, 'tract', [(i, i + 1) for i in range(tract_count - 1)])  3.41 us
  transfers between devices with their start and end apart: 26, of which 10 were waited for; matrix products, arithmetic and copies ran while one was open for 0% of the time, Pallas kernels for 37%

profile of v6, /device:TPU:0, one launch (start us, length us, event | category | flops | bytes accessed | tf_op | source)
XLA Modules:
  0.0 64.1 jit_solution(13628907812469615060)
XLA Ops:
  0.6 3.0 %collective-permute-start = (f32[1,192]{1,0:T(1,128)}, f32[1,192]{1,0:T(1,128)S(1)}, u32[]{:S(2)}, u32[]{:S(2)}) collective-permute-start(f32[1,192]{1,0:T(1,128)} %bitcast.13), channel_id=1, source_target_pairs={{0,16},{8,24},{16,0},{24,8},{1,17},{9,25},{17,1},{25,9},{2,18},{10... | collective-permute-start | bytes 2312 | tf_op jit(solution)/shard_map/ppermute | solution.py:62
  3.6 1.0 %load.1 = (bf16[64,768]{1,0:T(8,128)(2,1)S(1)}, f32[1,192]{1,0:T(1,128)S(1)}, f32[1,192]{1,0:T(1,128)S(1)}, f32[48,256]{1,0:T(8,128)S(1)}) custom-call(f32[64,768]{1,0:T(8,128)} %refs_0_.2, f32[1,192]{1,0:T(1,128)} %bitcast.14, f32[1,192]{1,0:T(1,128)} %bitcast.12, s32[16,256]{1,0:T(8,128)} %refs_3_.1, s32[16,256]{1,0:T(8,128)} %refs_4_.1, s32[16,256]{1,0:T(8,128)} %refs_5_.1), custom_call_target="tpu_custom_call" | custom-call | tf_op jit(solution)/shard_map/load/pallas_call | solution.py:48
  4.6 0.8 %collective-permute-done.refs_1_ = f32[1,192]{1,0:T(1,128)S(1)} collective-permute-done((f32[1,192]{1,0:T(1,128)}, f32[1,192]{1,0:T(1,128)S(1)}, u32[]{:S(2)}, u32[]{:S(2)}) %collective-permute-start) | collective-permute-done | bytes 800 | tf_op jit(solution)/shard_map/ppermute | solution.py:62
  5.4 2.1 %collective-permute-start.1 = (bf16[64,768]{1,0:T(8,128)(2,1)S(1)}, bf16[64,768]{1,0:T(8,128)(2,1)S(1)}, u32[]{:S(2)}, u32[]{:S(2)}) collective-permute-start(bf16[64,768]{1,0:T(8,128)(2,1)S(1)} %table_low.1.refs_0_), channel_id=1, source_target_pairs={{0,16},{8,24},{16,0},{24,8},{1,17},{9,25},{17,1},{25,9},{2,18},{10... | collective-permute-start | bytes 294920 | tf_op jit(solution)/shard_map/ppermute | solution.py:62
  7.5 0.0 collective-permute-start.2
  7.5 1.7 %weight_low.1.refs_3_.refs_0_ = bf16[768,768]{1,0:T(8,128)(2,1)S(1)} custom-call(f32[768,768]{1,0:T(8,128)} %refs_0_.3, bf16[64,768]{1,0:T(8,128)(2,1)S(1)} %get-tuple-element.45.refs_0_.refs_1_), custom_call_target="tpu_custom_call" | custom-call | tf_op jit(solution)/shard_map/weight_low/pallas_call | solution.py:48
  9.2 0.0 collective-permute-done.2.refs_1_
  9.2 0.7 %scorer.1 = (bf16[16,768]{1,0:T(8,128)(2,1)S(1)}, f32[48,768]{1,0:T(8,128)S(1)}) custom-call(f32[2,192]{1,0:T(2,128)S(1)} %score.1.refs_0_, f32[2,192]{1,0:T(2,128)S(1)} %collective-permute-done.2.refs_1_, f32[1,192]{1,0:T(1,128)S(1)} %get-tuple-element.47.refs_2_, bf16[768,768]{1,0:T(8,128)(2,1)S(1)} %weight_low.1.refs_3_.refs_0_), custom_call_target="tpu_custom_call" | custom-call | tf_op jit(solution)/shard_map/scorer/pallas_call | solution.py:48
  9.9 0.2 collective-permute-done.1.refs_1_
  10.1 0.4 collective-permute-start.3
  10.5 1.8 %collective-permute-start.6 = (f32[48,768]{1,0:T(8,128)S(1)}, f32[48,768]{1,0:T(8,128)S(1)}, u32[]{:S(2)}, u32[]{:S(2)}) collective-permute-start(f32[48,768]{1,0:T(8,128)S(1)} %get-tuple-element.48.refs_2_.first), channel_id=1, source_target_pairs={{0,16},{8,24},{16,0},{24,8},{1,17},{9,25},{17,1},{25,9},{2,18},{10... | collective-permute-start | bytes 442376 | tf_op jit(solution)/shard_map/ppermute | solution.py:62
  12.3 0.5 products.1
  12.8 1.4 %collective-permute-start.4 = (bf16[256,768]{1,0:T(8,128)(2,1)S(1)}, bf16[256,768]{1,0:T(8,128)(2,1)S(1)}, u32[]{:S(2)}, u32[]{:S(2)}) collective-permute-start(bf16[256,768]{1,0:T(8,128)(2,1)S(1)} %get-tuple-element.49.refs_0_.refs_1_), channel_id=1, source_target_pairs={{0,16},{8,24},{16,0},{24,8},{1,17},{9,25},{17,1},{25,9},{2,18},{10... | collective-permute-start | bytes 1179656 | tf_op jit(solution)/shard_map/ppermute | solution.py:62
  14.2 3.4 %collective-permute-start.8 = (f32[48,256]{1,0:T(8,128)S(1)}, f32[48,256]{1,0:T(8,128)S(1)}, u32[]{:S(2)}, u32[]{:S(2)}) collective-permute-start(f32[48,256]{1,0:T(8,128)S(1)} %tail.1), channel_id=1, source_target_pairs={{0,1},{1,2},{2,3},{3,4},{4,5},{5,6},{6,7},{8,9},{9,10},{10,11},{11... | collective-permute-start | bytes 147464 | tf_op jit(solution)/shard_map/ppermute | solution.py:808
  17.7 0.1 collective-permute-start.7
  17.8 0.7 %planes.1 = (f32[48,1024]{1,0:T(8,128)S(1)}, bf16[256,4096]{1,0:T(8,128)(2,1)S(1)}) custom-call(f32[48,256]{1,0:T(8,128)S(1)} %get-tuple-element.50.refs_0_, bf16[256,768]{1,0:T(8,128)(2,1)S(1)} %get-tuple-element.49.refs_0_.refs_1_), custom_call_target="tpu_custom_call" | custom-call | tf_op jit(solution)/shard_map/planes/pallas_call | solution.py:48
  18.5 0.9 %collective-permute-done.8.before = f32[48,256]{1,0:T(8,128)S(1)} collective-permute-done((f32[48,256]{1,0:T(8,128)S(1)}, f32[48,256]{1,0:T(8,128)S(1)}, u32[]{:S(2)}, u32[]{:S(2)}) %collective-permute-start.8) | collective-permute-done | bytes 49184 | tf_op jit(solution)/shard_map/ppermute | solution.py:808
  19.4 0.2 halo.1.refs_3_
  19.6 0.0 collective-permute-done.7.refs_1_.refs_8_
  19.6 1.8 %far.1 = (bf16[128,768]{1,0:T(8,128)(2,1)S(1)}, bf16[128,768]{1,0:T(8,128)(2,1)S(1)}, f32[57,16,128]{2,1,0:T(8,128)S(1)}, bf16[16,768]{1,0:T(8,128)(2,1)S(1)}) custom-call(f32[16,768]{1,0:T(8,128)S(1)} %scored.1.refs_0_.refs_7_, f32[16,768]{1,0:T(8,128)S(1)} %collective-permute-done.7.refs_1_.refs_8_, bf16[256,768]{1,0:T(8,128)(2,1)S(1)} %table.1.table_low.refs_2_, ...), custom_call_target="tpu_custom_call" | custom-call | tf_op jit(solution)/shard_map/far/pallas_call | solution.py:48
  21.4 0.1 collective-permute-start.9
  21.5 0.5 collective-permute-start.10
  22.0 1.0 %far_own.1.mine = f32[256,768]{1,0:T(8,128)S(1)} custom-call(f32[57,16,128]{2,1,0:T(8,128)S(1)} %get-tuple-element.53.plan.refs_0_.refs_2_, bf16[2048,768]{1,0:T(8,128)(2,1)S(1)} %bitcast.7), custom_call_target="tpu_custom_call" | custom-call | tf_op jit(solution)/shard_map/far_own/pallas_call | solution.py:48
  23.0 0.2 collective-permute-done.10.two
  23.2 0.1 far_sum.1
  23.4 0.7 %collective-permute-start.13 = (bf16[128,768]{1,0:T(8,128)(2,1)S(1)}, bf16[128,768]{1,0:T(8,128)(2,1)S(1)}, u32[]{:S(2)}, u32[]{:S(2)}) collective-permute-start(bf16[128,768]{1,0:T(8,128)(2,1)S(1)} %get-tuple-element.64), channel_id=1, source_target_pairs={{0,16},{8,24},{16,0},{24,8},{1,17},{9,25},{17,1},{25,9},{2,18},{10... | collective-permute-start | bytes 589832 | tf_op jit(solution)/shard_map/ppermute | solution.py:62
  24.1 1.4 %collective-permute-start.12 = (bf16[128,768]{1,0:T(8,128)(2,1)S(1)}, bf16[128,768]{1,0:T(8,128)(2,1)S(1)}, u32[]{:S(2)}, u32[]{:S(2)}) collective-permute-start(bf16[128,768]{1,0:T(8,128)(2,1)S(1)} %get-tuple-element.57.refs_3_), channel_id=1, source_target_pairs={{0,16},{8,24},{16,0},{24,8},{1,17},{9,25},{17,1},{25,9},{2,18},{10... | collective-permute-start | bytes 589832 | tf_op jit(solution)/shard_map/ppermute | solution.py:62
  25.5 0.1 passed.1.products.refs_0_.refs_9_
  25.5 0.1 collective-permute-start.5
  25.6 2.0 %near.1 = (f32[256,768]{1,0:T(8,128)S(1)}, bf16[256,768]{1,0:T(8,128)(2,1)S(1)}, f32[8,768]{1,0:T(8,128)S(1)}) custom-call(f32[57,16,128]{2,1,0:T(8,128)S(1)} %get-tuple-element.53.plan.refs_0_.refs_2_, bf16[2048,768]{1,0:T(8,128)(2,1)S(1)} %bitcast.8, bf16[256,768]{1,0:T(8,128)(2,1)S(1)} %collective-permute-done.4.refs_1_.refs_2_, ...), custom_call_target="tpu_custom_call" | custom-call | tf_op jit(solution)/shard_map/near/pallas_call | solution.py:48
  27.6 0.6 collective-permute-start.11
  28.1 2.2 %inner_near.1.refs_0_ = f32[5,16,128]{2,1,0:T(8,128)S(1)} custom-call(bf16[512,768]{1,0:T(8,128)(2,1)S(1)} %passed.1.products.refs_0_.refs_9_, f32[57,16,128]{2,1,0:T(8,128)S(1)} %get-tuple-element.53.plan.refs_0_.refs_2_, bf16[16,768]{1,0:T(8,128)(2,1)S(1)} %get-tuple-element.54.vectors.refs_3_.refs_5_, bf16[2048,768]{1,0:T(8,128)(2,1)S(1)} %bitcast.9), custom_call_target="tpu_custom_call" | custom-call | flops 99999997952 | tf_op jit(solution)/shard_map/inner_near/pallas_call | solution.py:48
  30.3 0.1 near_sum.1.near
  30.4 2.1 %inner_far.1.inner_ref = f32[5,16,128]{2,1,0:T(8,128)S(1)} custom-call(bf16[512,768]{1,0:T(8,128)(2,1)S(1)} %collective-permute-done.5.products.refs_1_.refs_10_, f32[57,16,128]{2,1,0:T(8,128)S(1)} %get-tuple-element.53.plan.refs_0_.refs_2_, bf16[16,768]{1,0:T(8,128)(2,1)S(1)} %get-tuple-element.54.vectors.refs_3_.refs_5_, bf16[2048,768]{1,0:T(8,128)(2,1)S(1)} %bitcast.10, ...), custom_call_target="tpu_custom_call" | custom-call | tf_op jit(solution)/shard_map/inner_far/pallas_call | solution.py:48
  32.5 0.9 %scores.1.sums = f32[4,768]{1,0:T(4,128)S(1)} custom-call(f32[5,16,128]{2,1,0:T(8,128)S(1)} %inner_far.1.inner_ref, f32[57,16,128]{2,1,0:T(8,128)S(1)} %get-tuple-element.53.plan.refs_0_.refs_2_, bf16[16,768]{1,0:T(8,128)(2,1)S(1)} %get-tuple-element.54.vectors.refs_3_.refs_5_, bf16[256,4096]{1,0:T(8,128)(2,1)S(1)} %get-tuple-element.60.hot), custom_call_target="tpu_custom_call" | custom-call | tf_op jit(solution)/shard_map/scores/pallas_call | solution.py:48
  33.5 0.1 merge.1
  33.6 2.4 %collective-permute-start.14 = (bf16[72,768]{1,0:T(8,128)(2,1)S(1)}, bf16[72,768]{1,0:T(8,128)(2,1)S(1)}, u32[]{:S(2)}, u32[]{:S(2)}) collective-permute-start(bf16[72,768]{1,0:T(8,128)(2,1)S(1)} %get-tuple-element.66), channel_id=1, source_target_pairs={{0,1},{1,0},{2,3},{3,2},{4,5},{5,4},{6,7},{7,6},{8,9},{9,8},{10,11... | collective-permute-start | bytes 331784 | tf_op jit(solution)/shard_map/ppermute | solution.py:62
  36.0 2.4 %collective-permute-start.16 = (bf16[72,768]{1,0:T(8,128)(2,1)S(1)}, bf16[72,768]{1,0:T(8,128)(2,1)S(1)}, u32[]{:S(2)}, u32[]{:S(2)}) collective-permute-start(bf16[72,768]{1,0:T(8,128)(2,1)S(1)} %get-tuple-element.65.refs_1_), channel_id=1, source_target_pairs={{0,3},{1,2},{2,1},{3,0},{4,7},{5,6},{6,5},{7,4},{8,11},{9,10},{10,... | collective-permute-start | bytes 331784 | tf_op jit(solution)/shard_map/ppermute | solution.py:62
  38.4 0.0 collective-permute-done.12.far
  38.4 0.1 rest.1
  38.4 0.1 collective-permute-start.15
  38.5 3.3 %output.2 = (bf16[2048,768]{1,0:T(8,128)(2,1)}, f32[8,128]{1,0:T(8,128)S(1)}) custom-call(bf16[512,768]{1,0:T(8,128)(2,1)S(1)} %passed.1.products.refs_0_.refs_9_, bf16[512,768]{1,0:T(8,128)(2,1)S(1)} %collective-permute-done.5.products.refs_1_.refs_10_, f32[57,16,128]{2,1,0:T(8,128)S(1)} %get-tuple-element.53.plan.refs_0_.refs_2_, ...), custom_call_target="tpu_custom_call" | custom-call | tf_op jit(solution)/shard_map/output/pallas_call | solution.py:547
  41.9 0.7 %collective-permute-done.16.refs_4_ = bf16[72,768]{1,0:T(8,128)(2,1)S(1)} collective-permute-done((bf16[72,768]{1,0:T(8,128)(2,1)S(1)}, bf16[72,768]{1,0:T(8,128)(2,1)S(1)}, u32[]{:S(2)}, u32[]{:S(2)}) %collective-permute-start.16) | collective-permute-done | bytes 110624 | tf_op jit(solution)/shard_map/ppermute | solution.py:62
  42.6 0.7 %collective-permute-done.15.refs_3_ = bf16[72,768]{1,0:T(8,128)(2,1)S(1)} collective-permute-done((bf16[72,768]{1,0:T(8,128)(2,1)S(1)}, bf16[72,768]{1,0:T(8,128)(2,1)S(1)}, u32[]{:S(2)}, u32[]{:S(2)}) %collective-permute-start.15) | collective-permute-done | bytes 110624 | tf_op jit(solution)/shard_map/ppermute | solution.py:62
  43.3 0.1 slice.1.refs_5_.refs_0_
  43.3 3.3 %collective-permute-start.17 = (bf16[72,768]{1,0:T(8,128)(2,1)S(1)}, bf16[72,768]{1,0:T(8,128)(2,1)S(1)}, u32[]{:S(2)}, u32[]{:S(2)}) collective-permute-start(bf16[72,768]{1,0:T(8,128)(2,1)S(1)} %slice.1.refs_5_.refs_0_), channel_id=1, source_target_pairs={{0,4},{1,5},{2,6},{3,7},{4,0},{5,1},{6,2},{7,3},{8,12},{9,13},{10,... | collective-permute-start | bytes 331784 | tf_op jit(solution)/shard_map/ppermute | solution.py:62
  46.6 3.1 %output.3 = (bf16[2048,768]{1,0:T(8,128)(2,1)}, f32[8,128]{1,0:T(8,128)S(1)}) custom-call(bf16[512,768]{1,0:T(8,128)(2,1)S(1)} %passed.1.products.refs_0_.refs_9_, bf16[512,768]{1,0:T(8,128)(2,1)S(1)} %collective-permute-done.5.products.refs_1_.refs_10_, f32[57,16,128]{2,1,0:T(8,128)S(1)} %get-tuple-element.53.plan.refs_0_.refs_2_, ...), custom_call_target="tpu_custom_call", output_to_operand_aliasing={{0}: (4, {})} | custom-call | tf_op jit(solution)/shard_map/output/pallas_call | solution.py:547
  49.8 0.4 turned.1.weight_turned
  50.2 1.2 %collective-permute-done.17.refs_1_ = bf16[72,768]{1,0:T(8,128)(2,1)S(1)} collective-permute-done((bf16[72,768]{1,0:T(8,128)(2,1)S(1)}, bf16[72,768]{1,0:T(8,128)(2,1)S(1)}, u32[]{:S(2)}, u32[]{:S(2)}) %collective-permute-start.17) | collective-permute-done | bytes 110624 | tf_op jit(solution)/shard_map/ppermute | solution.py:62
  51.4 0.3 share.1
  51.7 0.7 %collective-permute-start.18 = (bf16[40,768]{1,0:T(8,128)(2,1)S(1)}, bf16[40,768]{1,0:T(8,128)(2,1)S(1)}, u32[]{:S(2)}, u32[]{:S(2)}) collective-permute-start(bf16[40,768]{1,0:T(8,128)(2,1)S(1)} %get-tuple-element.74), channel_id=1, source_target_pairs={{0,16},{8,24},{16,0},{24,8},{1,17},{9,25},{17,1},{25,9},{2,18},{10... | collective-permute-start | bytes 184328 | tf_op jit(solution)/shard_map/ppermute | solution.py:62
  52.5 0.7 %collective-permute-start.25 = (bf16[64,768]{1,0:T(8,128)(2,1)S(1)}, bf16[64,768]{1,0:T(8,128)(2,1)S(1)}, u32[]{:S(2)}, u32[]{:S(2)}) collective-permute-start(bf16[64,768]{1,0:T(8,128)(2,1)S(1)} %get-tuple-element.71.block.refs_0_), channel_id=1, source_target_pairs={{0,3},{1,2},{2,1},{3,0},{4,7},{5,6},{6,5},{7,4},{8,11},{9,10},{10,... | collective-permute-start | bytes 294920 | tf_op jit(solution)/shard_map/ppermute | solution.py:62
  53.1 1.5 %collective-permute-start.24 = (bf16[64,768]{1,0:T(8,128)(2,1)S(1)}, bf16[64,768]{1,0:T(8,128)(2,1)S(1)}, u32[]{:S(2)}, u32[]{:S(2)}) collective-permute-start(bf16[64,768]{1,0:T(8,128)(2,1)S(1)} %get-tuple-element.71.block.refs_0_), channel_id=1, source_target_pairs={{0,2},{1,3},{2,0},{3,1},{4,6},{5,7},{6,4},{7,5},{8,10},{9,11},{10,... | collective-permute-start | bytes 294920 | tf_op jit(solution)/shard_map/ppermute | solution.py:62
  54.6 1.4 %collective-permute-start.23 = (bf16[64,768]{1,0:T(8,128)(2,1)S(1)}, bf16[64,768]{1,0:T(8,128)(2,1)S(1)}, u32[]{:S(2)}, u32[]{:S(2)}) collective-permute-start(bf16[64,768]{1,0:T(8,128)(2,1)S(1)} %get-tuple-element.71.block.refs_0_), channel_id=1, source_target_pairs={{0,1},{1,0},{2,3},{3,2},{4,5},{5,4},{6,7},{7,6},{8,9},{9,8},{10,11... | collective-permute-start | bytes 294920 | tf_op jit(solution)/shard_map/ppermute | solution.py:62
  55.9 0.1 collective-permute-done.18.other
  56.0 0.1 collective-permute-start.19
  56.1 1.2 %collective-permute-done.19.other = bf16[24,768]{1,0:T(8,128)(2,1)S(1)} collective-permute-done((bf16[24,768]{1,0:T(8,128)(2,1)S(1)}, bf16[24,768]{1,0:T(8,128)(2,1)S(1)}, u32[]{:S(2)}, u32[]{:S(2)}) %collective-permute-start.19) | collective-permute-done | bytes 36896 | tf_op jit(solution)/shard_map/ppermute | solution.py:62
  57.3 0.7 %collective-permute-start.22 = (bf16[16,768]{1,0:T(8,128)(2,1)S(1)}, bf16[16,768]{1,0:T(8,128)(2,1)S(1)}, u32[]{:S(2)}, u32[]{:S(2)}) collective-permute-start(bf16[16,768]{1,0:T(8,128)(2,1)S(1)} %get-tuple-element.78.refs_0_), channel_id=1, source_target_pairs={{0,3},{1,2},{2,1},{3,0},{4,7},{5,6},{6,5},{7,4},{8,11},{9,10},{10,... | collective-permute-start | bytes 73736 | tf_op jit(solution)/shard_map/ppermute | solution.py:62
  58.0 1.5 %collective-permute-start.21 = (bf16[16,768]{1,0:T(8,128)(2,1)S(1)}, bf16[16,768]{1,0:T(8,128)(2,1)S(1)}, u32[]{:S(2)}, u32[]{:S(2)}) collective-permute-start(bf16[16,768]{1,0:T(8,128)(2,1)S(1)} %get-tuple-element.78.refs_0_), channel_id=1, source_target_pairs={{0,2},{1,3},{2,0},{3,1},{4,6},{5,7},{6,4},{7,5},{8,10},{9,11},{10,... | collective-permute-start | bytes 73736 | tf_op jit(solution)/shard_map/ppermute | solution.py:62
  59.5 1.4 %collective-permute-start.20 = (bf16[16,768]{1,0:T(8,128)(2,1)S(1)}, bf16[16,768]{1,0:T(8,128)(2,1)S(1)}, u32[]{:S(2)}, u32[]{:S(2)}) collective-permute-start(bf16[16,768]{1,0:T(8,128)(2,1)S(1)} %get-tuple-element.78.refs_0_), channel_id=1, source_target_pairs={{0,1},{1,0},{2,3},{3,2},{4,5},{5,4},{6,7},{7,6},{8,9},{9,8},{10,11... | collective-permute-start | bytes 73736 | tf_op jit(solution)/shard_map/ppermute | solution.py:62
  60.9 1.8 %weights.1 = (f32[768,768]{1,0:T(8,128)}, f32[1,192]{1,0:T(1,128)}, f32[1,192]{1,0:T(1,128)}, f32[256,768]{1,0:T(8,128)S(1)}) custom-call(bf16[64,768]{1,0:T(8,128)(2,1)S(1)} %get-tuple-element.71.block.refs_0_, bf16[64,768]{1,0:T(8,128)(2,1)S(1)} %collective-permute-done.23.refs_1_, bf16[64,768]{1,0:T(8,128)(2,1)S(1)} %collective-permute-done.24.refs_2_, ...), custom_call_target="tpu_custom_call" | custom-call | tf_op jit(solution)/shard_map/weights/pallas_call | solution.py:48
  62.8 0.0 collective-permute-done.21.refs_2_
  62.8 0.6 collective-permute-done.20.refs_1_
  63.4 0.7 %table_grad.1 = f32[64,768]{1,0:T(8,128)} custom-call(bf16[16,768]{1,0:T(8,128)(2,1)S(1)} %get-tuple-element.78.refs_0_, bf16[16,768]{1,0:T(8,128)(2,1)S(1)} %collective-permute-done.20.refs_1_, bf16[16,768]{1,0:T(8,128)(2,1)S(1)} %collective-permute-done.21.refs_2_, bf16[16,768]{1,0:T(8,128)(2,1)S(1)} %collective-permute-done.22.refs_3_, ...), custom_call_target="tpu_custom_call" | custom-call | tf_op jit(solution)/shard_map/table_grad/pallas_call | solution.py:48
  (23 shorter events, 0.2 us)
Async XLA Ops:
  0.6 4.8 %collective-permute-start = (f32[1,192]{1,0:T(1,128)}, f32[1,192]{1,0:T(1,128)S(1)}, u32[]{:S(2)}, u32[]{:S(2)}) collective-permute-start(f32[1,192]{1,0:T(1,128)} %bitcast.13), channel_id=1, source_target_pairs={{0,16},{8,24},{16,0},{24,8},{1,17},{9,25},{17,1},{25,9},{2,18},{10... | collective-permute-start | bytes 2312 | tf_op jit(solution)/shard_map/ppermute | solution.py:62
  5.4 4.7 %collective-permute-start.1 = (bf16[64,768]{1,0:T(8,128)(2,1)S(1)}, bf16[64,768]{1,0:T(8,128)(2,1)S(1)}, u32[]{:S(2)}, u32[]{:S(2)}) collective-permute-start(bf16[64,768]{1,0:T(8,128)(2,1)S(1)} %table_low.1.refs_0_), channel_id=1, source_target_pairs={{0,16},{8,24},{16,0},{24,8},{1,17},{9,25},{17,1},{25,9},{2,18},{10... | collective-permute-start | bytes 294920 | tf_op jit(solution)/shard_map/ppermute | solution.py:62
  7.5 1.7 %collective-permute-start.2 = (f32[2,192]{1,0:T(2,128)S(1)}, f32[2,192]{1,0:T(2,128)S(1)}, u32[]{:S(2)}, u32[]{:S(2)}) collective-permute-start(f32[2,192]{1,0:T(2,128)S(1)} %score.1.refs_0_), channel_id=1, source_target_pairs={{0,8},{8,0},{16,24},{24,16},{1,9},{9,1},{17,25},{25,17},{2,10},{10... | collective-permute-start | bytes 4616 | tf_op jit(solution)/shard_map/ppermute | solution.py:62
  9.9 9.8 %copy-start = (bf16[16,128,768]{2,1,0:T(8,128)(2,1)S(1)}, bf16[16,128,768]{2,1,0:T(8,128)(2,1)}, u32[]{:S(2)}) copy-start(bf16[16,128,768]{2,1,0:T(8,128)(2,1)} %param.15) | copy-start | bytes 9437188
  10.1 2.2 %collective-permute-start.3 = (bf16[128,768]{1,0:T(8,128)(2,1)S(1)}, bf16[128,768]{1,0:T(8,128)(2,1)S(1)}, u32[]{:S(2)}, u32[]{:S(2)}) collective-permute-start(bf16[128,768]{1,0:T(8,128)(2,1)S(1)} %table_pair.1.first), channel_id=1, source_target_pairs={{0,8},{8,0},{16,24},{24,16},{1,9},{9,1},{17,25},{25,17},{2,10},{10... | collective-permute-start | bytes 589832 | tf_op jit(solution)/shard_map/ppermute | solution.py:62
  10.5 7.2 %collective-permute-start.6 = (f32[48,768]{1,0:T(8,128)S(1)}, f32[48,768]{1,0:T(8,128)S(1)}, u32[]{:S(2)}, u32[]{:S(2)}) collective-permute-start(f32[48,768]{1,0:T(8,128)S(1)} %get-tuple-element.48.refs_2_.first), channel_id=1, source_target_pairs={{0,16},{8,24},{16,0},{24,8},{1,17},{9,25},{17,1},{25,9},{2,18},{10... | collective-permute-start | bytes 442376 | tf_op jit(solution)/shard_map/ppermute | solution.py:62
  12.8 12.6 %collective-permute-start.4 = (bf16[256,768]{1,0:T(8,128)(2,1)S(1)}, bf16[256,768]{1,0:T(8,128)(2,1)S(1)}, u32[]{:S(2)}, u32[]{:S(2)}) collective-permute-start(bf16[256,768]{1,0:T(8,128)(2,1)S(1)} %get-tuple-element.49.refs_0_.refs_1_), channel_id=1, source_target_pairs={{0,16},{8,24},{16,0},{24,8},{1,17},{9,25},{17,1},{25,9},{2,18},{10... | collective-permute-start | bytes 1179656 | tf_op jit(solution)/shard_map/ppermute | solution.py:62
  14.2 5.2 %collective-permute-start.8 = (f32[48,256]{1,0:T(8,128)S(1)}, f32[48,256]{1,0:T(8,128)S(1)}, u32[]{:S(2)}, u32[]{:S(2)}) collective-permute-start(f32[48,256]{1,0:T(8,128)S(1)} %tail.1), channel_id=1, source_target_pairs={{0,1},{1,2},{2,3},{3,4},{4,5},{5,6},{6,7},{8,9},{9,10},{10,11},{11... | collective-permute-start | bytes 147464 | tf_op jit(solution)/shard_map/ppermute | solution.py:808
  17.7 1.9 %collective-permute-start.7 = (f32[16,768]{1,0:T(8,128)S(1)}, f32[16,768]{1,0:T(8,128)S(1)}, u32[]{:S(2)}, u32[]{:S(2)}) collective-permute-start(f32[16,768]{1,0:T(8,128)S(1)} %scored.1.refs_0_.refs_7_), channel_id=1, source_target_pairs={{0,8},{8,0},{16,24},{24,16},{1,9},{9,1},{17,25},{25,17},{2,10},{10... | collective-permute-start | bytes 147464 | tf_op jit(solution)/shard_map/ppermute | solution.py:62
  21.4 1.6 %collective-permute-start.9 = (bf16[128,768]{1,0:T(8,128)(2,1)S(1)}, bf16[128,768]{1,0:T(8,128)(2,1)S(1)}, u32[]{:S(2)}, u32[]{:S(2)}) collective-permute-start(bf16[128,768]{1,0:T(8,128)(2,1)S(1)} %get-tuple-element.55), channel_id=1, source_target_pairs={{0,8},{8,0},{16,24},{24,16},{1,9},{9,1},{17,25},{25,17},{2,10},{10... | collective-permute-start | bytes 589832 | tf_op jit(solution)/shard_map/ppermute | solution.py:62
  21.5 1.7 %collective-permute-start.10 = (bf16[128,768]{1,0:T(8,128)(2,1)S(1)}, bf16[128,768]{1,0:T(8,128)(2,1)S(1)}, u32[]{:S(2)}, u32[]{:S(2)}) collective-permute-start(bf16[128,768]{1,0:T(8,128)(2,1)S(1)} %get-tuple-element.56), channel_id=1, source_target_pairs={{0,8},{8,0},{16,24},{24,16},{1,9},{9,1},{17,25},{25,17},{2,10},{10... | collective-permute-start | bytes 589832 | tf_op jit(solution)/shard_map/ppermute | solution.py:62
  23.4 10.1 %collective-permute-start.13 = (bf16[128,768]{1,0:T(8,128)(2,1)S(1)}, bf16[128,768]{1,0:T(8,128)(2,1)S(1)}, u32[]{:S(2)}, u32[]{:S(2)}) collective-permute-start(bf16[128,768]{1,0:T(8,128)(2,1)S(1)} %get-tuple-element.64), channel_id=1, source_target_pairs={{0,16},{8,24},{16,0},{24,8},{1,17},{9,25},{17,1},{25,9},{2,18},{10... | collective-permute-start | bytes 589832 | tf_op jit(solution)/shard_map/ppermute | solution.py:62
  24.1 14.3 %collective-permute-start.12 = (bf16[128,768]{1,0:T(8,128)(2,1)S(1)}, bf16[128,768]{1,0:T(8,128)(2,1)S(1)}, u32[]{:S(2)}, u32[]{:S(2)}) collective-permute-start(bf16[128,768]{1,0:T(8,128)(2,1)S(1)} %get-tuple-element.57.refs_3_), channel_id=1, source_target_pairs={{0,16},{8,24},{16,0},{24,8},{1,17},{9,25},{17,1},{25,9},{2,18},{10... | collective-permute-start | bytes 589832 | tf_op jit(solution)/shard_map/ppermute | solution.py:62
  25.5 4.9 %collective-permute-start.5 = (bf16[512,768]{1,0:T(8,128)(2,1)S(1)}, bf16[512,768]{1,0:T(8,128)(2,1)S(1)}, u32[]{:S(2)}, u32[]{:S(2)}) collective-permute-start(bf16[512,768]{1,0:T(8,128)(2,1)S(1)} %passed.1.products.refs_0_.refs_9_), channel_id=1, source_target_pairs={{0,8},{8,0},{16,24},{24,16},{1,9},{9,1},{17,25},{25,17},{2,10},{10... | collective-permute-start | bytes 2359304 | tf_op jit(solution)/shard_map/ppermute | solution.py:62
  27.6 2.7 %collective-permute-start.11 = (bf16[256,768]{1,0:T(8,128)(2,1)S(1)}, bf16[256,768]{1,0:T(8,128)(2,1)S(1)}, u32[]{:S(2)}, u32[]{:S(2)}) collective-permute-start(bf16[256,768]{1,0:T(8,128)(2,1)S(1)} %get-tuple-element.59), channel_id=1, source_target_pairs={{0,8},{8,0},{16,24},{24,16},{1,9},{9,1},{17,25},{25,17},{2,10},{10... | collective-permute-start | bytes 1179656 | tf_op jit(solution)/shard_map/ppermute | solution.py:62
  33.6 8.3 %collective-permute-start.14 = (bf16[72,768]{1,0:T(8,128)(2,1)S(1)}, bf16[72,768]{1,0:T(8,128)(2,1)S(1)}, u32[]{:S(2)}, u32[]{:S(2)}) collective-permute-start(bf16[72,768]{1,0:T(8,128)(2,1)S(1)} %get-tuple-element.66), channel_id=1, source_target_pairs={{0,1},{1,0},{2,3},{3,2},{4,5},{5,4},{6,7},{7,6},{8,9},{9,8},{10,11... | collective-permute-start | bytes 331784 | tf_op jit(solution)/shard_map/ppermute | solution.py:62
  36.0 6.6 %collective-permute-start.16 = (bf16[72,768]{1,0:T(8,128)(2,1)S(1)}, bf16[72,768]{1,0:T(8,128)(2,1)S(1)}, u32[]{:S(2)}, u32[]{:S(2)}) collective-permute-start(bf16[72,768]{1,0:T(8,128)(2,1)S(1)} %get-tuple-element.65.refs_1_), channel_id=1, source_target_pairs={{0,3},{1,2},{2,1},{3,0},{4,7},{5,6},{6,5},{7,4},{8,11},{9,10},{10,... | collective-permute-start | bytes 331784 | tf_op jit(solution)/shard_map/ppermute | solution.py:62
  38.4 4.8 %collective-permute-start.15 = (bf16[72,768]{1,0:T(8,128)(2,1)S(1)}, bf16[72,768]{1,0:T(8,128)(2,1)S(1)}, u32[]{:S(2)}, u32[]{:S(2)}) collective-permute-start(bf16[72,768]{1,0:T(8,128)(2,1)S(1)} %get-tuple-element.67), channel_id=1, source_target_pairs={{0,2},{1,3},{2,0},{3,1},{4,6},{5,7},{6,4},{7,5},{8,10},{9,11},{10,... | collective-permute-start | bytes 331784 | tf_op jit(solution)/shard_map/ppermute | solution.py:62
  43.3 8.0 %collective-permute-start.17 = (bf16[72,768]{1,0:T(8,128)(2,1)S(1)}, bf16[72,768]{1,0:T(8,128)(2,1)S(1)}, u32[]{:S(2)}, u32[]{:S(2)}) collective-permute-start(bf16[72,768]{1,0:T(8,128)(2,1)S(1)} %slice.1.refs_5_.refs_0_), channel_id=1, source_target_pairs={{0,4},{1,5},{2,6},{3,7},{4,0},{5,1},{6,2},{7,3},{8,12},{9,13},{10,... | collective-permute-start | bytes 331784 | tf_op jit(solution)/shard_map/ppermute | solution.py:62
  51.7 4.3 %collective-permute-start.18 = (bf16[40,768]{1,0:T(8,128)(2,1)S(1)}, bf16[40,768]{1,0:T(8,128)(2,1)S(1)}, u32[]{:S(2)}, u32[]{:S(2)}) collective-permute-start(bf16[40,768]{1,0:T(8,128)(2,1)S(1)} %get-tuple-element.74), channel_id=1, source_target_pairs={{0,16},{8,24},{16,0},{24,8},{1,17},{9,25},{17,1},{25,9},{2,18},{10... | collective-permute-start | bytes 184328 | tf_op jit(solution)/shard_map/ppermute | solution.py:62
  52.5 7.1 %collective-permute-start.25 = (bf16[64,768]{1,0:T(8,128)(2,1)S(1)}, bf16[64,768]{1,0:T(8,128)(2,1)S(1)}, u32[]{:S(2)}, u32[]{:S(2)}) collective-permute-start(bf16[64,768]{1,0:T(8,128)(2,1)S(1)} %get-tuple-element.71.block.refs_0_), channel_id=1, source_target_pairs={{0,3},{1,2},{2,1},{3,0},{4,7},{5,6},{6,5},{7,4},{8,11},{9,10},{10,... | collective-permute-start | bytes 294920 | tf_op jit(solution)/shard_map/ppermute | solution.py:62
  53.1 7.8 %collective-permute-start.24 = (bf16[64,768]{1,0:T(8,128)(2,1)S(1)}, bf16[64,768]{1,0:T(8,128)(2,1)S(1)}, u32[]{:S(2)}, u32[]{:S(2)}) collective-permute-start(bf16[64,768]{1,0:T(8,128)(2,1)S(1)} %get-tuple-element.71.block.refs_0_), channel_id=1, source_target_pairs={{0,2},{1,3},{2,0},{3,1},{4,6},{5,7},{6,4},{7,5},{8,10},{9,11},{10,... | collective-permute-start | bytes 294920 | tf_op jit(solution)/shard_map/ppermute | solution.py:62
  54.6 6.3 %collective-permute-start.23 = (bf16[64,768]{1,0:T(8,128)(2,1)S(1)}, bf16[64,768]{1,0:T(8,128)(2,1)S(1)}, u32[]{:S(2)}, u32[]{:S(2)}) collective-permute-start(bf16[64,768]{1,0:T(8,128)(2,1)S(1)} %get-tuple-element.71.block.refs_0_), channel_id=1, source_target_pairs={{0,1},{1,0},{2,3},{3,2},{4,5},{5,4},{6,7},{7,6},{8,9},{9,8},{10,11... | collective-permute-start | bytes 294920 | tf_op jit(solution)/shard_map/ppermute | solution.py:62
  56.0 1.3 %collective-permute-start.19 = (bf16[24,768]{1,0:T(8,128)(2,1)S(1)}, bf16[24,768]{1,0:T(8,128)(2,1)S(1)}, u32[]{:S(2)}, u32[]{:S(2)}) collective-permute-start(bf16[24,768]{1,0:T(8,128)(2,1)S(1)} %get-tuple-element.77), channel_id=1, source_target_pairs={{0,8},{8,0},{16,24},{24,16},{1,9},{9,1},{17,25},{25,17},{2,10},{10... | collective-permute-start | bytes 110600 | tf_op jit(solution)/shard_map/ppermute | solution.py:62
  57.3 5.4 %collective-permute-start.22 = (bf16[16,768]{1,0:T(8,128)(2,1)S(1)}, bf16[16,768]{1,0:T(8,128)(2,1)S(1)}, u32[]{:S(2)}, u32[]{:S(2)}) collective-permute-start(bf16[16,768]{1,0:T(8,128)(2,1)S(1)} %get-tuple-element.78.refs_0_), channel_id=1, source_target_pairs={{0,3},{1,2},{2,1},{3,0},{4,7},{5,6},{6,5},{7,4},{8,11},{9,10},{10,... | collective-permute-start | bytes 73736 | tf_op jit(solution)/shard_map/ppermute | solution.py:62
  58.0 4.7 %collective-permute-start.21 = (bf16[16,768]{1,0:T(8,128)(2,1)S(1)}, bf16[16,768]{1,0:T(8,128)(2,1)S(1)}, u32[]{:S(2)}, u32[]{:S(2)}) collective-permute-start(bf16[16,768]{1,0:T(8,128)(2,1)S(1)} %get-tuple-element.78.refs_0_), channel_id=1, source_target_pairs={{0,2},{1,3},{2,0},{3,1},{4,6},{5,7},{6,4},{7,5},{8,10},{9,11},{10,... | collective-permute-start | bytes 73736 | tf_op jit(solution)/shard_map/ppermute | solution.py:62
  59.5 3.8 %collective-permute-start.20 = (bf16[16,768]{1,0:T(8,128)(2,1)S(1)}, bf16[16,768]{1,0:T(8,128)(2,1)S(1)}, u32[]{:S(2)}, u32[]{:S(2)}) collective-permute-start(bf16[16,768]{1,0:T(8,128)(2,1)S(1)} %get-tuple-element.78.refs_0_), channel_id=1, source_target_pairs={{0,1},{1,0},{2,3},{3,2},{4,5},{5,4},{6,7},{7,6},{8,9},{9,8},{10,11... | collective-permute-start | bytes 73736 | tf_op jit(solution)/shard_map/ppermute | solution.py:62

commit v7 on v6

--- a/solution.py
+++ b/solution.py
@@ -66,7 +66,7 @@
     out = refs[-1]
     rows = refs[0].shape[0]
     for at, value in enumerate(refs[:-1]):
-        out[at * rows : (at + 1) * rows] = value[...]
+        out[at * rows : (at + 1) * rows] = value[...].astype(out.dtype)
 
 
 def stacked(*values, name, after=()):
@@ -780,7 +780,7 @@
         [(table.shape, BF16), (shard, F32), (shard, F32), ((3 * rows, length), F32)],
         (table,), (score_weight[None],), (conv_bias[None],), (byte_values,), (segment_ids,), (valid,),
         scratch=[pltpu.VMEM(table.shape, F32), pltpu.VMEM((3, rows, length), jnp.int32), pltpu.SemaphoreType.DMA((6,))],
-        name="load",
+        name="load", cost=LONG,
     )
     parts = 4
     weight_low = call(
@@ -794,9 +794,10 @@
         [((EXTRA, width), BF16), ((SENT, width), F32)], *scores, *biases, weight_low, name="scorer",
     )
     far_scored = swap(scored, "rows", group_bits[0])
-    table_low = stacked(table_low, name="table_low", after=[far_score])
-    far_table = swap(table_low, "rows", row_bits[0])
-    table_low = stacked(table_low, far_table, name="table_pair", after=[scored])
+    far_table = swap(table, "rows", row_bits[0])
+    table_low = call(
+        stack_kernel, [((2 * table.shape[0], width), BF16)], table_low, far_table, name="table_pair", after=[scored],
+    )[0]
     table_low = call(
         functools.partial(table_kernel, slots_of(row_bits)), [((values, width), BF16)],
         *gathered(table_low, "rows", row_bits[1:], "table_pair"), name="table",

time: 64.3 us -> 63.7 us (level)
  starting transfers between devices: 31.5 us -> 27 us
  waiting for transfers between devices: 6.56 us -> 10.4 us
    ppermute x25, starting transfers between devices: 28.1 us -> 23.6 us  [swap(): return lax.ppermute(value, axis, [(i, i ^ bit) for i in range(count)])]
    ppermute x25, waiting for transfers between devices: 5.63 us -> 10 us  [swap(): return lax.ppermute(value, axis, [(i, i ^ bit) for i in range(count)])]
    pallas_call x31 -> x30, Pallas kernels: 18.6 us -> 18.6 us  [call(): pl.pallas_call(run if after else kernel, out_shape=[jax.ShapeDtypeStruct(...]
  transfers between devices with their start and end apart: 26 -> 26, of which waited for: 10 -> 12; matrix products, arithmetic and copies ran while one was open for 0% -> 0% of each run, Pallas kernels for 37% -> 38%
where the time goes in v7:
time: 63.7 us; the launch traced here: 63.5 us
  starting transfers between devices  27 us (42%)
  Pallas kernels  25.1 us (39%)
  waiting for transfers between devices  10.4 us (16%)
  between operations  0.92 us (1%)
    ppermute x25, starting transfers between devices, swap(): return lax.ppermute(value, axis, [(i, i ^ bit) for i in range(count)])  23.6 us
    pallas_call x30, Pallas kernels, call(): pl.pallas_call(run if after else kernel, out_shape=[jax.ShapeDtypeStruct(...  18.6 us
    ppermute x25, waiting for transfers between devices, swap(): return lax.ppermute(value, axis, [(i, i ^ bit) for i in range(count)])  10 us
    pallas_call x2, Pallas kernels, output_part(): pl.pallas_call(run, out_shape=[jax.ShapeDtypeStruct((rows * half, width),...  6.48 us
    ppermute x1, starting transfers between devices, body(): lax.ppermute(tail, 'tract', [(i, i + 1) for i in range(tract_count - 1)])  3.41 us
  transfers between devices with their start and end apart: 26, of which 12 were waited for; matrix products, arithmetic and copies ran while one was open for 0% of the time, Pallas kernels for 38%

profile of v7, /device:TPU:0, one launch (start us, length us, event | category | flops | bytes accessed | tf_op | source)
XLA Modules:
  0.0 63.5 jit_solution(12929373910838094023)
XLA Ops:
  0.6 3.0 %collective-permute-start.1 = (f32[1,192]{1,0:T(1,128)}, f32[1,192]{1,0:T(1,128)S(1)}, u32[]{:S(2)}, u32[]{:S(2)}) collective-permute-start(f32[1,192]{1,0:T(1,128)} %bitcast.13), channel_id=1, source_target_pairs={{0,16},{8,24},{16,0},{24,8},{1,17},{9,25},{17,1},{25,9},{2,18},{10... | collective-permute-start | bytes 2312 | tf_op jit(solution)/shard_map/ppermute | solution.py:62
  3.6 0.1 collective-permute-start
  3.7 1.0 %load.1 = (bf16[64,768]{1,0:T(8,128)(2,1)S(1)}, f32[1,192]{1,0:T(1,128)S(1)}, f32[1,192]{1,0:T(1,128)S(1)}, f32[48,256]{1,0:T(8,128)S(1)}) custom-call(f32[64,768]{1,0:T(8,128)} %refs_0_.2, f32[1,192]{1,0:T(1,128)} %bitcast.14, f32[1,192]{1,0:T(1,128)} %bitcast.12, s32[16,256]{1,0:T(8,128)} %refs_3_.1, s32[16,256]{1,0:T(8,128)} %refs_4_.1, s32[16,256]{1,0:T(8,128)} %refs_5_.1), custom_call_target="tpu_custom_call" | custom-call | flops 99999997952 | tf_op jit(solution)/shard_map/load/pallas_call | solution.py:48
  4.8 0.6 %collective-permute-done.1.refs_1_ = f32[1,192]{1,0:T(1,128)S(1)} collective-permute-done((f32[1,192]{1,0:T(1,128)}, f32[1,192]{1,0:T(1,128)S(1)}, u32[]{:S(2)}, u32[]{:S(2)}) %collective-permute-start.1) | collective-permute-done | bytes 800 | tf_op jit(solution)/shard_map/ppermute | solution.py:62
  5.4 0.0 collective-permute-start.2
  5.4 1.7 %weight_low.1.refs_3_.refs_0_ = bf16[768,768]{1,0:T(8,128)(2,1)S(1)} custom-call(f32[768,768]{1,0:T(8,128)} %refs_0_.3, bf16[64,768]{1,0:T(8,128)(2,1)S(1)} %get-tuple-element.45.refs_1_.refs_0_), custom_call_target="tpu_custom_call" | custom-call | tf_op jit(solution)/shard_map/weight_low/pallas_call | solution.py:48
  7.1 0.7 %scorer.1 = (bf16[16,768]{1,0:T(8,128)(2,1)S(1)}, f32[48,768]{1,0:T(8,128)S(1)}) custom-call(f32[2,192]{1,0:T(2,128)S(1)} %score.1.refs_0_, f32[2,192]{1,0:T(2,128)S(1)} %collective-permute-done.2.refs_1_, f32[1,192]{1,0:T(1,128)S(1)} %get-tuple-element.47.refs_2_, bf16[768,768]{1,0:T(8,128)(2,1)S(1)} %weight_low.1.refs_3_.refs_0_), custom_call_target="tpu_custom_call" | custom-call | tf_op jit(solution)/shard_map/scorer/pallas_call | solution.py:48
  7.8 2.4 %collective-permute-done.refs_1_ = f32[64,768]{1,0:T(8,128)S(1)} collective-permute-done((f32[64,768]{1,0:T(8,128)}, f32[64,768]{1,0:T(8,128)S(1)}, u32[]{:S(2)}, u32[]{:S(2)}) %collective-permute-start) | collective-permute-done | bytes 196640 | tf_op jit(solution)/shard_map/ppermute | solution.py:62
  10.2 0.1 collective-permute-start.3
  10.3 0.4 collective-permute-start.6
  10.7 1.0 %collective-permute-done.3.second = bf16[128,768]{1,0:T(8,128)(2,1)S(1)} collective-permute-done((bf16[128,768]{1,0:T(8,128)(2,1)S(1)}, bf16[128,768]{1,0:T(8,128)(2,1)S(1)}, u32[]{:S(2)}, u32[]{:S(2)}) %collective-permute-start.3) | collective-permute-done | bytes 196640 | tf_op jit(solution)/shard_map/ppermute | solution.py:62
  11.8 0.5 products.1
  12.3 0.7 %collective-permute-start.4 = (bf16[256,768]{1,0:T(8,128)(2,1)S(1)}, bf16[256,768]{1,0:T(8,128)(2,1)S(1)}, u32[]{:S(2)}, u32[]{:S(2)}) collective-permute-start(bf16[256,768]{1,0:T(8,128)(2,1)S(1)} %get-tuple-element.49.refs_0_.refs_1_), channel_id=1, source_target_pairs={{0,16},{8,24},{16,0},{24,8},{1,17},{9,25},{17,1},{25,9},{2,18},{10... | collective-permute-start | bytes 1179656 | tf_op jit(solution)/shard_map/ppermute | solution.py:62
  13.0 3.4 %collective-permute-start.8 = (f32[48,256]{1,0:T(8,128)S(1)}, f32[48,256]{1,0:T(8,128)S(1)}, u32[]{:S(2)}, u32[]{:S(2)}) collective-permute-start(f32[48,256]{1,0:T(8,128)S(1)} %tail.1), channel_id=1, source_target_pairs={{0,1},{1,2},{2,3},{3,4},{4,5},{5,6},{6,7},{8,9},{9,10},{10,11},{11... | collective-permute-start | bytes 147464 | tf_op jit(solution)/shard_map/ppermute | solution.py:809
  16.4 0.6 collective-permute-done.6.second
  17.0 0.0 collective-permute-start.7
  17.0 0.7 %planes.1 = (f32[48,1024]{1,0:T(8,128)S(1)}, bf16[256,4096]{1,0:T(8,128)(2,1)S(1)}) custom-call(f32[48,256]{1,0:T(8,128)S(1)} %get-tuple-element.50.refs_0_, bf16[256,768]{1,0:T(8,128)(2,1)S(1)} %get-tuple-element.49.refs_0_.refs_1_), custom_call_target="tpu_custom_call" | custom-call | tf_op jit(solution)/shard_map/planes/pallas_call | solution.py:48
  17.7 0.4 collective-permute-done.8.before
  18.2 0.2 halo.1.refs_3_
  18.4 1.8 %far.1 = (bf16[128,768]{1,0:T(8,128)(2,1)S(1)}, bf16[128,768]{1,0:T(8,128)(2,1)S(1)}, f32[57,16,128]{2,1,0:T(8,128)S(1)}, bf16[16,768]{1,0:T(8,128)(2,1)S(1)}) custom-call(f32[16,768]{1,0:T(8,128)S(1)} %scored.1.refs_0_.refs_7_, f32[16,768]{1,0:T(8,128)S(1)} %collective-permute-done.7.refs_1_.refs_8_, bf16[256,768]{1,0:T(8,128)(2,1)S(1)} %table.1.table_low.refs_2_, ...), custom_call_target="tpu_custom_call" | custom-call | tf_op jit(solution)/shard_map/far/pallas_call | solution.py:48
  20.2 0.1 collective-permute-start.9
  20.3 0.4 collective-permute-start.10
  20.8 1.0 %far_own.1.mine = f32[256,768]{1,0:T(8,128)S(1)} custom-call(f32[57,16,128]{2,1,0:T(8,128)S(1)} %get-tuple-element.53.plan.refs_0_.refs_2_, bf16[2048,768]{1,0:T(8,128)(2,1)S(1)} %bitcast.7), custom_call_target="tpu_custom_call" | custom-call | tf_op jit(solution)/shard_map/far_own/pallas_call | solution.py:48
  21.8 0.0 collective-permute-done.9.one
  21.8 0.2 collective-permute-done.10.two
  22.0 0.1 far_sum.1
  22.1 1.4 %collective-permute-start.13 = (bf16[128,768]{1,0:T(8,128)(2,1)S(1)}, bf16[128,768]{1,0:T(8,128)(2,1)S(1)}, u32[]{:S(2)}, u32[]{:S(2)}) collective-permute-start(bf16[128,768]{1,0:T(8,128)(2,1)S(1)} %get-tuple-element.64), channel_id=1, source_target_pairs={{0,16},{8,24},{16,0},{24,8},{1,17},{9,25},{17,1},{25,9},{2,18},{10... | collective-permute-start | bytes 589832 | tf_op jit(solution)/shard_map/ppermute | solution.py:62
  23.6 0.7 %collective-permute-start.12 = (bf16[128,768]{1,0:T(8,128)(2,1)S(1)}, bf16[128,768]{1,0:T(8,128)(2,1)S(1)}, u32[]{:S(2)}, u32[]{:S(2)}) collective-permute-start(bf16[128,768]{1,0:T(8,128)(2,1)S(1)} %get-tuple-element.57.refs_3_), channel_id=1, source_target_pairs={{0,16},{8,24},{16,0},{24,8},{1,17},{9,25},{17,1},{25,9},{2,18},{10... | collective-permute-start | bytes 589832 | tf_op jit(solution)/shard_map/ppermute | solution.py:62
  24.2 0.8 %collective-permute-done.4.refs_1_.refs_2_ = bf16[256,768]{1,0:T(8,128)(2,1)S(1)} collective-permute-done((bf16[256,768]{1,0:T(8,128)(2,1)S(1)}, bf16[256,768]{1,0:T(8,128)(2,1)S(1)}, u32[]{:S(2)}, u32[]{:S(2)}) %collective-permute-start.4) | collective-permute-done | bytes 393248 | tf_op jit(solution)/shard_map/ppermute | solution.py:62
  25.0 0.1 passed.1.products.refs_0_.refs_9_
  25.1 0.1 collective-permute-start.5
  25.1 2.0 %near.1 = (f32[256,768]{1,0:T(8,128)S(1)}, bf16[256,768]{1,0:T(8,128)(2,1)S(1)}, f32[8,768]{1,0:T(8,128)S(1)}) custom-call(f32[57,16,128]{2,1,0:T(8,128)S(1)} %get-tuple-element.53.plan.refs_0_.refs_2_, bf16[2048,768]{1,0:T(8,128)(2,1)S(1)} %bitcast.8, bf16[256,768]{1,0:T(8,128)(2,1)S(1)} %collective-permute-done.4.refs_1_.refs_2_, ...), custom_call_target="tpu_custom_call" | custom-call | tf_op jit(solution)/shard_map/near/pallas_call | solution.py:48
  27.1 0.6 collective-permute-start.11
  27.7 2.2 %inner_near.1.refs_0_ = f32[5,16,128]{2,1,0:T(8,128)S(1)} custom-call(bf16[512,768]{1,0:T(8,128)(2,1)S(1)} %passed.1.products.refs_0_.refs_9_, f32[57,16,128]{2,1,0:T(8,128)S(1)} %get-tuple-element.53.plan.refs_0_.refs_2_, bf16[16,768]{1,0:T(8,128)(2,1)S(1)} %get-tuple-element.54.vectors.refs_3_.refs_5_, bf16[2048,768]{1,0:T(8,128)(2,1)S(1)} %bitcast.9), custom_call_target="tpu_custom_call" | custom-call | flops 99999997952 | tf_op jit(solution)/shard_map/inner_near/pallas_call | solution.py:48
  29.9 0.0 collective-permute-done.11.other
  29.9 0.1 near_sum.1.near
  30.0 2.1 %inner_far.1.inner_ref = f32[5,16,128]{2,1,0:T(8,128)S(1)} custom-call(bf16[512,768]{1,0:T(8,128)(2,1)S(1)} %collective-permute-done.5.products.refs_1_.refs_10_, f32[57,16,128]{2,1,0:T(8,128)S(1)} %get-tuple-element.53.plan.refs_0_.refs_2_, bf16[16,768]{1,0:T(8,128)(2,1)S(1)} %get-tuple-element.54.vectors.refs_3_.refs_5_, bf16[2048,768]{1,0:T(8,128)(2,1)S(1)} %bitcast.10, ...), custom_call_target="tpu_custom_call" | custom-call | tf_op jit(solution)/shard_map/inner_far/pallas_call | solution.py:48
  32.1 0.9 %scores.1.sums = f32[4,768]{1,0:T(4,128)S(1)} custom-call(f32[5,16,128]{2,1,0:T(8,128)S(1)} %inner_far.1.inner_ref, f32[57,16,128]{2,1,0:T(8,128)S(1)} %get-tuple-element.53.plan.refs_0_.refs_2_, bf16[16,768]{1,0:T(8,128)(2,1)S(1)} %get-tuple-element.54.vectors.refs_3_.refs_5_, bf16[256,4096]{1,0:T(8,128)(2,1)S(1)} %get-tuple-element.60.hot), custom_call_target="tpu_custom_call" | custom-call | tf_op jit(solution)/shard_map/scores/pallas_call | solution.py:48
  33.0 0.1 merge.1
  33.1 1.6 %collective-permute-start.14 = (bf16[72,768]{1,0:T(8,128)(2,1)S(1)}, bf16[72,768]{1,0:T(8,128)(2,1)S(1)}, u32[]{:S(2)}, u32[]{:S(2)}) collective-permute-start(bf16[72,768]{1,0:T(8,128)(2,1)S(1)} %get-tuple-element.66), channel_id=1, source_target_pairs={{0,1},{1,0},{2,3},{3,2},{4,5},{5,4},{6,7},{7,6},{8,9},{9,8},{10,11... | collective-permute-start | bytes 331784 | tf_op jit(solution)/shard_map/ppermute | solution.py:62
  34.7 2.4 %collective-permute-start.16 = (bf16[72,768]{1,0:T(8,128)(2,1)S(1)}, bf16[72,768]{1,0:T(8,128)(2,1)S(1)}, u32[]{:S(2)}, u32[]{:S(2)}) collective-permute-start(bf16[72,768]{1,0:T(8,128)(2,1)S(1)} %get-tuple-element.65.refs_1_), channel_id=1, source_target_pairs={{0,3},{1,2},{2,1},{3,0},{4,7},{5,6},{6,5},{7,4},{8,11},{9,10},{10,... | collective-permute-start | bytes 331784 | tf_op jit(solution)/shard_map/ppermute | solution.py:62
  37.2 0.1 rest.1
  37.2 0.1 collective-permute-start.15
  37.3 3.3 %output.2 = (bf16[2048,768]{1,0:T(8,128)(2,1)}, f32[8,128]{1,0:T(8,128)S(1)}) custom-call(bf16[512,768]{1,0:T(8,128)(2,1)S(1)} %passed.1.products.refs_0_.refs_9_, bf16[512,768]{1,0:T(8,128)(2,1)S(1)} %collective-permute-done.5.products.refs_1_.refs_10_, f32[57,16,128]{2,1,0:T(8,128)S(1)} %get-tuple-element.53.plan.refs_0_.refs_2_, ...), custom_call_target="tpu_custom_call" | custom-call | tf_op jit(solution)/shard_map/output/pallas_call | solution.py:547
  40.7 0.7 %collective-permute-done.16.refs_4_ = bf16[72,768]{1,0:T(8,128)(2,1)S(1)} collective-permute-done((bf16[72,768]{1,0:T(8,128)(2,1)S(1)}, bf16[72,768]{1,0:T(8,128)(2,1)S(1)}, u32[]{:S(2)}, u32[]{:S(2)}) %collective-permute-start.16) | collective-permute-done | bytes 110624 | tf_op jit(solution)/shard_map/ppermute | solution.py:62
  41.4 0.7 %collective-permute-done.15.refs_3_ = bf16[72,768]{1,0:T(8,128)(2,1)S(1)} collective-permute-done((bf16[72,768]{1,0:T(8,128)(2,1)S(1)}, bf16[72,768]{1,0:T(8,128)(2,1)S(1)}, u32[]{:S(2)}, u32[]{:S(2)}) %collective-permute-start.15) | collective-permute-done | bytes 110624 | tf_op jit(solution)/shard_map/ppermute | solution.py:62
  42.0 0.1 slice.1.refs_5_.refs_0_
  42.1 3.3 %collective-permute-start.17 = (bf16[72,768]{1,0:T(8,128)(2,1)S(1)}, bf16[72,768]{1,0:T(8,128)(2,1)S(1)}, u32[]{:S(2)}, u32[]{:S(2)}) collective-permute-start(bf16[72,768]{1,0:T(8,128)(2,1)S(1)} %slice.1.refs_5_.refs_0_), channel_id=1, source_target_pairs={{0,4},{1,5},{2,6},{3,7},{4,0},{5,1},{6,2},{7,3},{8,12},{9,13},{10,... | collective-permute-start | bytes 331784 | tf_op jit(solution)/shard_map/ppermute | solution.py:62
  45.4 3.1 %output.3 = (bf16[2048,768]{1,0:T(8,128)(2,1)}, f32[8,128]{1,0:T(8,128)S(1)}) custom-call(bf16[512,768]{1,0:T(8,128)(2,1)S(1)} %passed.1.products.refs_0_.refs_9_, bf16[512,768]{1,0:T(8,128)(2,1)S(1)} %collective-permute-done.5.products.refs_1_.refs_10_, f32[57,16,128]{2,1,0:T(8,128)S(1)} %get-tuple-element.53.plan.refs_0_.refs_2_, ...), custom_call_target="tpu_custom_call", output_to_operand_aliasing={{0}: (4, {})} | custom-call | tf_op jit(solution)/shard_map/output/pallas_call | solution.py:547
  48.6 0.4 turned.1.weight_turned
  48.9 1.2 %collective-permute-done.17.refs_1_ = bf16[72,768]{1,0:T(8,128)(2,1)S(1)} collective-permute-done((bf16[72,768]{1,0:T(8,128)(2,1)S(1)}, bf16[72,768]{1,0:T(8,128)(2,1)S(1)}, u32[]{:S(2)}, u32[]{:S(2)}) %collective-permute-start.17) | collective-permute-done | bytes 110624 | tf_op jit(solution)/shard_map/ppermute | solution.py:62
  50.2 0.3 share.1
  50.5 1.4 %collective-permute-start.18 = (bf16[40,768]{1,0:T(8,128)(2,1)S(1)}, bf16[40,768]{1,0:T(8,128)(2,1)S(1)}, u32[]{:S(2)}, u32[]{:S(2)}) collective-permute-start(bf16[40,768]{1,0:T(8,128)(2,1)S(1)} %get-tuple-element.74), channel_id=1, source_target_pairs={{0,16},{8,24},{16,0},{24,8},{1,17},{9,25},{17,1},{25,9},{2,18},{10... | collective-permute-start | bytes 184328 | tf_op jit(solution)/shard_map/ppermute | solution.py:62
  51.9 0.7 %collective-permute-start.25 = (bf16[64,768]{1,0:T(8,128)(2,1)S(1)}, bf16[64,768]{1,0:T(8,128)(2,1)S(1)}, u32[]{:S(2)}, u32[]{:S(2)}) collective-permute-start(bf16[64,768]{1,0:T(8,128)(2,1)S(1)} %get-tuple-element.71.block.refs_0_), channel_id=1, source_target_pairs={{0,3},{1,2},{2,1},{3,0},{4,7},{5,6},{6,5},{7,4},{8,11},{9,10},{10,... | collective-permute-start | bytes 294920 | tf_op jit(solution)/shard_map/ppermute | solution.py:62
  52.6 1.5 %collective-permute-start.24 = (bf16[64,768]{1,0:T(8,128)(2,1)S(1)}, bf16[64,768]{1,0:T(8,128)(2,1)S(1)}, u32[]{:S(2)}, u32[]{:S(2)}) collective-permute-start(bf16[64,768]{1,0:T(8,128)(2,1)S(1)} %get-tuple-element.71.block.refs_0_), channel_id=1, source_target_pairs={{0,2},{1,3},{2,0},{3,1},{4,6},{5,7},{6,4},{7,5},{8,10},{9,11},{10,... | collective-permute-start | bytes 294920 | tf_op jit(solution)/shard_map/ppermute | solution.py:62
  54.1 1.4 %collective-permute-start.23 = (bf16[64,768]{1,0:T(8,128)(2,1)S(1)}, bf16[64,768]{1,0:T(8,128)(2,1)S(1)}, u32[]{:S(2)}, u32[]{:S(2)}) collective-permute-start(bf16[64,768]{1,0:T(8,128)(2,1)S(1)} %get-tuple-element.71.block.refs_0_), channel_id=1, source_target_pairs={{0,1},{1,0},{2,3},{3,2},{4,5},{5,4},{6,7},{7,6},{8,9},{9,8},{10,11... | collective-permute-start | bytes 294920 | tf_op jit(solution)/shard_map/ppermute | solution.py:62
  55.4 0.1 collective-permute-start.19
  55.5 1.2 %collective-permute-done.19.other = bf16[24,768]{1,0:T(8,128)(2,1)S(1)} collective-permute-done((bf16[24,768]{1,0:T(8,128)(2,1)S(1)}, bf16[24,768]{1,0:T(8,128)(2,1)S(1)}, u32[]{:S(2)}, u32[]{:S(2)}) %collective-permute-start.19) | collective-permute-done | bytes 36896 | tf_op jit(solution)/shard_map/ppermute | solution.py:62
  56.7 0.7 %collective-permute-start.22 = (bf16[16,768]{1,0:T(8,128)(2,1)S(1)}, bf16[16,768]{1,0:T(8,128)(2,1)S(1)}, u32[]{:S(2)}, u32[]{:S(2)}) collective-permute-start(bf16[16,768]{1,0:T(8,128)(2,1)S(1)} %get-tuple-element.78.refs_0_), channel_id=1, source_target_pairs={{0,3},{1,2},{2,1},{3,0},{4,7},{5,6},{6,5},{7,4},{8,11},{9,10},{10,... | collective-permute-start | bytes 73736 | tf_op jit(solution)/shard_map/ppermute | solution.py:62
  57.5 1.5 %collective-permute-start.21 = (bf16[16,768]{1,0:T(8,128)(2,1)S(1)}, bf16[16,768]{1,0:T(8,128)(2,1)S(1)}, u32[]{:S(2)}, u32[]{:S(2)}) collective-permute-start(bf16[16,768]{1,0:T(8,128)(2,1)S(1)} %get-tuple-element.78.refs_0_), channel_id=1, source_target_pairs={{0,2},{1,3},{2,0},{3,1},{4,6},{5,7},{6,4},{7,5},{8,10},{9,11},{10,... | collective-permute-start | bytes 73736 | tf_op jit(solution)/shard_map/ppermute | solution.py:62
  58.9 1.4 %collective-permute-start.20 = (bf16[16,768]{1,0:T(8,128)(2,1)S(1)}, bf16[16,768]{1,0:T(8,128)(2,1)S(1)}, u32[]{:S(2)}, u32[]{:S(2)}) collective-permute-start(bf16[16,768]{1,0:T(8,128)(2,1)S(1)} %get-tuple-element.78.refs_0_), channel_id=1, source_target_pairs={{0,1},{1,0},{2,3},{3,2},{4,5},{5,4},{6,7},{7,6},{8,9},{9,8},{10,11... | collective-permute-start | bytes 73736 | tf_op jit(solution)/shard_map/ppermute | solution.py:62
  60.3 1.8 %weights.1 = (f32[768,768]{1,0:T(8,128)}, f32[1,192]{1,0:T(1,128)}, f32[1,192]{1,0:T(1,128)}, f32[256,768]{1,0:T(8,128)S(1)}) custom-call(bf16[64,768]{1,0:T(8,128)(2,1)S(1)} %get-tuple-element.71.block.refs_0_, bf16[64,768]{1,0:T(8,128)(2,1)S(1)} %collective-permute-done.23.refs_1_, bf16[64,768]{1,0:T(8,128)(2,1)S(1)} %collective-permute-done.24.refs_2_, ...), custom_call_target="tpu_custom_call" | custom-call | tf_op jit(solution)/shard_map/weights/pallas_call | solution.py:48
  62.2 0.6 collective-permute-done.20.refs_1_
  62.8 0.7 %table_grad.1 = f32[64,768]{1,0:T(8,128)} custom-call(bf16[16,768]{1,0:T(8,128)(2,1)S(1)} %get-tuple-element.78.refs_0_, bf16[16,768]{1,0:T(8,128)(2,1)S(1)} %collective-permute-done.20.refs_1_, bf16[16,768]{1,0:T(8,128)(2,1)S(1)} %collective-permute-done.21.refs_2_, bf16[16,768]{1,0:T(8,128)(2,1)S(1)} %collective-permute-done.22.refs_3_, ...), custom_call_target="tpu_custom_call" | custom-call | tf_op jit(solution)/shard_map/table_grad/pallas_call | solution.py:48
  (22 shorter events, 0.2 us)
Async XLA Ops:
  0.6 4.8 %collective-permute-start.1 = (f32[1,192]{1,0:T(1,128)}, f32[1,192]{1,0:T(1,128)S(1)}, u32[]{:S(2)}, u32[]{:S(2)}) collective-permute-start(f32[1,192]{1,0:T(1,128)} %bitcast.13), channel_id=1, source_target_pairs={{0,16},{8,24},{16,0},{24,8},{1,17},{9,25},{17,1},{25,9},{2,18},{10... | collective-permute-start | bytes 2312 | tf_op jit(solution)/shard_map/ppermute | solution.py:62
  3.6 6.6 %collective-permute-start = (f32[64,768]{1,0:T(8,128)}, f32[64,768]{1,0:T(8,128)S(1)}, u32[]{:S(2)}, u32[]{:S(2)}) collective-permute-start(f32[64,768]{1,0:T(8,128)} %refs_0_.2), channel_id=1, source_target_pairs={{0,16},{8,24},{16,0},{24,8},{1,17},{9,25},{17,1},{25,9},{2,18},{10... | collective-permute-start | bytes 589832 | tf_op jit(solution)/shard_map/ppermute | solution.py:62
  5.4 1.7 %collective-permute-start.2 = (f32[2,192]{1,0:T(2,128)S(1)}, f32[2,192]{1,0:T(2,128)S(1)}, u32[]{:S(2)}, u32[]{:S(2)}) collective-permute-start(f32[2,192]{1,0:T(2,128)S(1)} %score.1.refs_0_), channel_id=1, source_target_pairs={{0,8},{8,0},{16,24},{24,16},{1,9},{9,1},{17,25},{25,17},{2,10},{10... | collective-permute-start | bytes 4616 | tf_op jit(solution)/shard_map/ppermute | solution.py:62
  10.2 8.2 %copy-start = (bf16[16,128,768]{2,1,0:T(8,128)(2,1)S(1)}, bf16[16,128,768]{2,1,0:T(8,128)(2,1)}, u32[]{:S(2)}) copy-start(bf16[16,128,768]{2,1,0:T(8,128)(2,1)} %param.15) | copy-start | bytes 9437188
  10.2 1.5 %collective-permute-start.3 = (bf16[128,768]{1,0:T(8,128)(2,1)S(1)}, bf16[128,768]{1,0:T(8,128)(2,1)S(1)}, u32[]{:S(2)}, u32[]{:S(2)}) collective-permute-start(bf16[128,768]{1,0:T(8,128)(2,1)S(1)} %table_pair.1.first), channel_id=1, source_target_pairs={{0,8},{8,0},{16,24},{24,16},{1,9},{9,1},{17,25},{25,17},{2,10},{10... | collective-permute-start | bytes 589832 | tf_op jit(solution)/shard_map/ppermute | solution.py:62
  10.3 6.7 %collective-permute-start.6 = (f32[48,768]{1,0:T(8,128)S(1)}, f32[48,768]{1,0:T(8,128)S(1)}, u32[]{:S(2)}, u32[]{:S(2)}) collective-permute-start(f32[48,768]{1,0:T(8,128)S(1)} %get-tuple-element.48.refs_2_.first), channel_id=1, source_target_pairs={{0,16},{8,24},{16,0},{24,8},{1,17},{9,25},{17,1},{25,9},{2,18},{10... | collective-permute-start | bytes 442376 | tf_op jit(solution)/shard_map/ppermute | solution.py:62
  12.3 12.7 %collective-permute-start.4 = (bf16[256,768]{1,0:T(8,128)(2,1)S(1)}, bf16[256,768]{1,0:T(8,128)(2,1)S(1)}, u32[]{:S(2)}, u32[]{:S(2)}) collective-permute-start(bf16[256,768]{1,0:T(8,128)(2,1)S(1)} %get-tuple-element.49.refs_0_.refs_1_), channel_id=1, source_target_pairs={{0,16},{8,24},{16,0},{24,8},{1,17},{9,25},{17,1},{25,9},{2,18},{10... | collective-permute-start | bytes 1179656 | tf_op jit(solution)/shard_map/ppermute | solution.py:62
  13.0 5.2 %collective-permute-start.8 = (f32[48,256]{1,0:T(8,128)S(1)}, f32[48,256]{1,0:T(8,128)S(1)}, u32[]{:S(2)}, u32[]{:S(2)}) collective-permute-start(f32[48,256]{1,0:T(8,128)S(1)} %tail.1), channel_id=1, source_target_pairs={{0,1},{1,2},{2,3},{3,4},{4,5},{5,6},{6,7},{8,9},{9,10},{10,11},{11... | collective-permute-start | bytes 147464 | tf_op jit(solution)/shard_map/ppermute | solution.py:809
  17.0 1.3 %collective-permute-start.7 = (f32[16,768]{1,0:T(8,128)S(1)}, f32[16,768]{1,0:T(8,128)S(1)}, u32[]{:S(2)}, u32[]{:S(2)}) collective-permute-start(f32[16,768]{1,0:T(8,128)S(1)} %scored.1.refs_0_.refs_7_), channel_id=1, source_target_pairs={{0,8},{8,0},{16,24},{24,16},{1,9},{9,1},{17,25},{25,17},{2,10},{10... | collective-permute-start | bytes 147464 | tf_op jit(solution)/shard_map/ppermute | solution.py:62
  20.2 1.6 %collective-permute-start.9 = (bf16[128,768]{1,0:T(8,128)(2,1)S(1)}, bf16[128,768]{1,0:T(8,128)(2,1)S(1)}, u32[]{:S(2)}, u32[]{:S(2)}) collective-permute-start(bf16[128,768]{1,0:T(8,128)(2,1)S(1)} %get-tuple-element.55), channel_id=1, source_target_pairs={{0,8},{8,0},{16,24},{24,16},{1,9},{9,1},{17,25},{25,17},{2,10},{10... | collective-permute-start | bytes 589832 | tf_op jit(solution)/shard_map/ppermute | solution.py:62
  20.3 1.6 %collective-permute-start.10 = (bf16[128,768]{1,0:T(8,128)(2,1)S(1)}, bf16[128,768]{1,0:T(8,128)(2,1)S(1)}, u32[]{:S(2)}, u32[]{:S(2)}) collective-permute-start(bf16[128,768]{1,0:T(8,128)(2,1)S(1)} %get-tuple-element.56), channel_id=1, source_target_pairs={{0,8},{8,0},{16,24},{24,16},{1,9},{9,1},{17,25},{25,17},{2,10},{10... | collective-permute-start | bytes 589832 | tf_op jit(solution)/shard_map/ppermute | solution.py:62
  22.1 10.9 %collective-permute-start.13 = (bf16[128,768]{1,0:T(8,128)(2,1)S(1)}, bf16[128,768]{1,0:T(8,128)(2,1)S(1)}, u32[]{:S(2)}, u32[]{:S(2)}) collective-permute-start(bf16[128,768]{1,0:T(8,128)(2,1)S(1)} %get-tuple-element.64), channel_id=1, source_target_pairs={{0,16},{8,24},{16,0},{24,8},{1,17},{9,25},{17,1},{25,9},{2,18},{10... | collective-permute-start | bytes 589832 | tf_op jit(solution)/shard_map/ppermute | solution.py:62
  23.6 13.6 %collective-permute-start.12 = (bf16[128,768]{1,0:T(8,128)(2,1)S(1)}, bf16[128,768]{1,0:T(8,128)(2,1)S(1)}, u32[]{:S(2)}, u32[]{:S(2)}) collective-permute-start(bf16[128,768]{1,0:T(8,128)(2,1)S(1)} %get-tuple-element.57.refs_3_), channel_id=1, source_target_pairs={{0,16},{8,24},{16,0},{24,8},{1,17},{9,25},{17,1},{25,9},{2,18},{10... | collective-permute-start | bytes 589832 | tf_op jit(solution)/shard_map/ppermute | solution.py:62
  25.1 4.9 %collective-permute-start.5 = (bf16[512,768]{1,0:T(8,128)(2,1)S(1)}, bf16[512,768]{1,0:T(8,128)(2,1)S(1)}, u32[]{:S(2)}, u32[]{:S(2)}) collective-permute-start(bf16[512,768]{1,0:T(8,128)(2,1)S(1)} %passed.1.products.refs_0_.refs_9_), channel_id=1, source_target_pairs={{0,8},{8,0},{16,24},{24,16},{1,9},{9,1},{17,25},{25,17},{2,10},{10... | collective-permute-start | bytes 2359304 | tf_op jit(solution)/shard_map/ppermute | solution.py:62
  27.1 2.7 %collective-permute-start.11 = (bf16[256,768]{1,0:T(8,128)(2,1)S(1)}, bf16[256,768]{1,0:T(8,128)(2,1)S(1)}, u32[]{:S(2)}, u32[]{:S(2)}) collective-permute-start(bf16[256,768]{1,0:T(8,128)(2,1)S(1)} %get-tuple-element.59), channel_id=1, source_target_pairs={{0,8},{8,0},{16,24},{24,16},{1,9},{9,1},{17,25},{25,17},{2,10},{10... | collective-permute-start | bytes 1179656 | tf_op jit(solution)/shard_map/ppermute | solution.py:62
  33.1 7.5 %collective-permute-start.14 = (bf16[72,768]{1,0:T(8,128)(2,1)S(1)}, bf16[72,768]{1,0:T(8,128)(2,1)S(1)}, u32[]{:S(2)}, u32[]{:S(2)}) collective-permute-start(bf16[72,768]{1,0:T(8,128)(2,1)S(1)} %get-tuple-element.66), channel_id=1, source_target_pairs={{0,1},{1,0},{2,3},{3,2},{4,5},{5,4},{6,7},{7,6},{8,9},{9,8},{10,11... | collective-permute-start | bytes 331784 | tf_op jit(solution)/shard_map/ppermute | solution.py:62
  34.7 6.6 %collective-permute-start.16 = (bf16[72,768]{1,0:T(8,128)(2,1)S(1)}, bf16[72,768]{1,0:T(8,128)(2,1)S(1)}, u32[]{:S(2)}, u32[]{:S(2)}) collective-permute-start(bf16[72,768]{1,0:T(8,128)(2,1)S(1)} %get-tuple-element.65.refs_1_), channel_id=1, source_target_pairs={{0,3},{1,2},{2,1},{3,0},{4,7},{5,6},{6,5},{7,4},{8,11},{9,10},{10,... | collective-permute-start | bytes 331784 | tf_op jit(solution)/shard_map/ppermute | solution.py:62
  37.2 4.8 %collective-permute-start.15 = (bf16[72,768]{1,0:T(8,128)(2,1)S(1)}, bf16[72,768]{1,0:T(8,128)(2,1)S(1)}, u32[]{:S(2)}, u32[]{:S(2)}) collective-permute-start(bf16[72,768]{1,0:T(8,128)(2,1)S(1)} %get-tuple-element.67), channel_id=1, source_target_pairs={{0,2},{1,3},{2,0},{3,1},{4,6},{5,7},{6,4},{7,5},{8,10},{9,11},{10,... | collective-permute-start | bytes 331784 | tf_op jit(solution)/shard_map/ppermute | solution.py:62
  42.1 8.0 %collective-permute-start.17 = (bf16[72,768]{1,0:T(8,128)(2,1)S(1)}, bf16[72,768]{1,0:T(8,128)(2,1)S(1)}, u32[]{:S(2)}, u32[]{:S(2)}) collective-permute-start(bf16[72,768]{1,0:T(8,128)(2,1)S(1)} %slice.1.refs_5_.refs_0_), channel_id=1, source_target_pairs={{0,4},{1,5},{2,6},{3,7},{4,0},{5,1},{6,2},{7,3},{8,12},{9,13},{10,... | collective-permute-start | bytes 331784 | tf_op jit(solution)/shard_map/ppermute | solution.py:62
  50.5 4.9 %collective-permute-start.18 = (bf16[40,768]{1,0:T(8,128)(2,1)S(1)}, bf16[40,768]{1,0:T(8,128)(2,1)S(1)}, u32[]{:S(2)}, u32[]{:S(2)}) collective-permute-start(bf16[40,768]{1,0:T(8,128)(2,1)S(1)} %get-tuple-element.74), channel_id=1, source_target_pairs={{0,16},{8,24},{16,0},{24,8},{1,17},{9,25},{17,1},{25,9},{2,18},{10... | collective-permute-start | bytes 184328 | tf_op jit(solution)/shard_map/ppermute | solution.py:62
  51.9 7.0 %collective-permute-start.25 = (bf16[64,768]{1,0:T(8,128)(2,1)S(1)}, bf16[64,768]{1,0:T(8,128)(2,1)S(1)}, u32[]{:S(2)}, u32[]{:S(2)}) collective-permute-start(bf16[64,768]{1,0:T(8,128)(2,1)S(1)} %get-tuple-element.71.block.refs_0_), channel_id=1, source_target_pairs={{0,3},{1,2},{2,1},{3,0},{4,7},{5,6},{6,5},{7,4},{8,11},{9,10},{10,... | collective-permute-start | bytes 294920 | tf_op jit(solution)/shard_map/ppermute | solution.py:62
  52.6 7.7 %collective-permute-start.24 = (bf16[64,768]{1,0:T(8,128)(2,1)S(1)}, bf16[64,768]{1,0:T(8,128)(2,1)S(1)}, u32[]{:S(2)}, u32[]{:S(2)}) collective-permute-start(bf16[64,768]{1,0:T(8,128)(2,1)S(1)} %get-tuple-element.71.block.refs_0_), channel_id=1, source_target_pairs={{0,2},{1,3},{2,0},{3,1},{4,6},{5,7},{6,4},{7,5},{8,10},{9,11},{10,... | collective-permute-start | bytes 294920 | tf_op jit(solution)/shard_map/ppermute | solution.py:62
  54.1 6.2 %collective-permute-start.23 = (bf16[64,768]{1,0:T(8,128)(2,1)S(1)}, bf16[64,768]{1,0:T(8,128)(2,1)S(1)}, u32[]{:S(2)}, u32[]{:S(2)}) collective-permute-start(bf16[64,768]{1,0:T(8,128)(2,1)S(1)} %get-tuple-element.71.block.refs_0_), channel_id=1, source_target_pairs={{0,1},{1,0},{2,3},{3,2},{4,5},{5,4},{6,7},{7,6},{8,9},{9,8},{10,11... | collective-permute-start | bytes 294920 | tf_op jit(solution)/shard_map/ppermute | solution.py:62
  55.4 1.3 %collective-permute-start.19 = (bf16[24,768]{1,0:T(8,128)(2,1)S(1)}, bf16[24,768]{1,0:T(8,128)(2,1)S(1)}, u32[]{:S(2)}, u32[]{:S(2)}) collective-permute-start(bf16[24,768]{1,0:T(8,128)(2,1)S(1)} %get-tuple-element.77), channel_id=1, source_target_pairs={{0,8},{8,0},{16,24},{24,16},{1,9},{9,1},{17,25},{25,17},{2,10},{10... | collective-permute-start | bytes 110600 | tf_op jit(solution)/shard_map/ppermute | solution.py:62
  56.7 5.4 %collective-permute-start.22 = (bf16[16,768]{1,0:T(8,128)(2,1)S(1)}, bf16[16,768]{1,0:T(8,128)(2,1)S(1)}, u32[]{:S(2)}, u32[]{:S(2)}) collective-permute-start(bf16[16,768]{1,0:T(8,128)(2,1)S(1)} %get-tuple-element.78.refs_0_), channel_id=1, source_target_pairs={{0,3},{1,2},{2,1},{3,0},{4,7},{5,6},{6,5},{7,4},{8,11},{9,10},{10,... | collective-permute-start | bytes 73736 | tf_op jit(solution)/shard_map/ppermute | solution.py:62
  57.5 4.7 %collective-permute-start.21 = (bf16[16,768]{1,0:T(8,128)(2,1)S(1)}, bf16[16,768]{1,0:T(8,128)(2,1)S(1)}, u32[]{:S(2)}, u32[]{:S(2)}) collective-permute-start(bf16[16,768]{1,0:T(8,128)(2,1)S(1)} %get-tuple-element.78.refs_0_), channel_id=1, source_target_pairs={{0,2},{1,3},{2,0},{3,1},{4,6},{5,7},{6,4},{7,5},{8,10},{9,11},{10,... | collective-permute-start | bytes 73736 | tf_op jit(solution)/shard_map/ppermute | solution.py:62
  58.9 3.8 %collective-permute-start.20 = (bf16[16,768]{1,0:T(8,128)(2,1)S(1)}, bf16[16,768]{1,0:T(8,128)(2,1)S(1)}, u32[]{:S(2)}, u32[]{:S(2)}) collective-permute-start(bf16[16,768]{1,0:T(8,128)(2,1)S(1)} %get-tuple-element.78.refs_0_), channel_id=1, source_target_pairs={{0,1},{1,0},{2,3},{3,2},{4,5},{5,4},{6,7},{7,6},{8,9},{9,8},{10,11... | collective-permute-start | bytes 73736 | tf_op jit(solution)/shard_map/ppermute | solution.py:62

commit v8 on v6

--- a/solution.py
+++ b/solution.py
@@ -66,7 +66,7 @@
     out = refs[-1]
     rows = refs[0].shape[0]
     for at, value in enumerate(refs[:-1]):
-        out[at * rows : (at + 1) * rows] = value[...]
+        out[at * rows : (at + 1) * rows] = value[...].astype(out.dtype)
 
 
 def stacked(*values, name, after=()):
@@ -786,7 +786,7 @@
     weight_low = call(
         weight_low_kernel, [(weight.shape, BF16)], (weight,),
         scratch=[pltpu.VMEM((parts, weight.shape[0] // parts, width), F32), pltpu.SemaphoreType.DMA((parts,))],
-        name="weight_low", after=[table_low],
+        name="weight_low", after=[table_low], cost=LONG,
     )[0]
     scores = gathered(stacked(score, far_score, name="score"), "rows", row_bits[1:], "score")
     scorer, scored = call(
@@ -794,7 +794,6 @@
         [((EXTRA, width), BF16), ((SENT, width), F32)], *scores, *biases, weight_low, name="scorer",
     )
     far_scored = swap(scored, "rows", group_bits[0])
-    table_low = stacked(table_low, name="table_low", after=[far_score])
     far_table = swap(table_low, "rows", row_bits[0])
     table_low = stacked(table_low, far_table, name="table_pair", after=[scored])
     table_low = call(

time: 64.3 us -> 62.8 us (0.977)
  starting transfers between devices: 31.5 us -> 27.5 us
  waiting for transfers between devices: 6.56 us -> 9.05 us
    ppermute x25, starting transfers between devices: 28.1 us -> 24.1 us  [swap(): return lax.ppermute(value, axis, [(i, i ^ bit) for i in range(count)])]
    ppermute x25, waiting for transfers between devices: 5.63 us -> 8.61 us  [swap(): return lax.ppermute(value, axis, [(i, i ^ bit) for i in range(count)])]
    pallas_call x31 -> x30, Pallas kernels: 18.6 us -> 18.6 us  [call(): pl.pallas_call(run if after else kernel, out_shape=[jax.ShapeDtypeStruct(...]
  transfers between devices with their start and end apart: 26 -> 26, of which waited for: 10 -> 12; matrix products, arithmetic and copies ran while one was open for 0% -> 0% of each run, Pallas kernels for 37% -> 38%
where the time goes in v8:
time: 62.8 us; the launch traced here: 62.6 us
  starting transfers between devices  27.5 us (44%)
  Pallas kernels  25.1 us (40%)
  waiting for transfers between devices  9.05 us (14%)
  between operations  0.92 us (1%)
    ppermute x25, starting transfers between devices, swap(): return lax.ppermute(value, axis, [(i, i ^ bit) for i in range(count)])  24.1 us
    pallas_call x30, Pallas kernels, call(): pl.pallas_call(run if after else kernel, out_shape=[jax.ShapeDtypeStruct(...  18.6 us
    ppermute x25, waiting for transfers between devices, swap(): return lax.ppermute(value, axis, [(i, i ^ bit) for i in range(count)])  8.61 us
    pallas_call x2, Pallas kernels, output_part(): pl.pallas_call(run, out_shape=[jax.ShapeDtypeStruct((rows * half, width),...  6.47 us
    ppermute x1, starting transfers between devices, body(): lax.ppermute(tail, 'tract', [(i, i + 1) for i in range(tract_count - 1)])  3.41 us
  transfers between devices with their start and end apart: 26, of which 12 were waited for; matrix products, arithmetic and copies ran while one was open for 0% of the time, Pallas kernels for 38%

profile of v8, /device:TPU:0, one launch (start us, length us, event | category | flops | bytes accessed | tf_op | source)
XLA Modules:
  0.0 62.6 jit_solution(16709401557645962115)
XLA Ops:
  0.6 3.0 %collective-permute-start.1 = (f32[1,192]{1,0:T(1,128)}, f32[1,192]{1,0:T(1,128)S(1)}, u32[]{:S(2)}, u32[]{:S(2)}) collective-permute-start(f32[1,192]{1,0:T(1,128)} %bitcast.13), channel_id=1, source_target_pairs={{0,16},{8,24},{16,0},{24,8},{1,17},{9,25},{17,1},{25,9},{2,18},{10... | collective-permute-start | bytes 2312 | tf_op jit(solution)/shard_map/ppermute | solution.py:62
  3.6 1.0 %load.1 = (bf16[64,768]{1,0:T(8,128)(2,1)S(1)}, f32[1,192]{1,0:T(1,128)S(1)}, f32[1,192]{1,0:T(1,128)S(1)}, f32[48,256]{1,0:T(8,128)S(1)}) custom-call(f32[64,768]{1,0:T(8,128)} %refs_0_.2, f32[1,192]{1,0:T(1,128)} %bitcast.14, f32[1,192]{1,0:T(1,128)} %bitcast.12, s32[16,256]{1,0:T(8,128)} %refs_3_.1, s32[16,256]{1,0:T(8,128)} %refs_4_.1, s32[16,256]{1,0:T(8,128)} %refs_5_.1), custom_call_target="tpu_custom_call" | custom-call | tf_op jit(solution)/shard_map/load/pallas_call | solution.py:48
  4.6 0.1 collective-permute-start
  4.7 0.7 %collective-permute-done.1.refs_1_ = f32[1,192]{1,0:T(1,128)S(1)} collective-permute-done((f32[1,192]{1,0:T(1,128)}, f32[1,192]{1,0:T(1,128)S(1)}, u32[]{:S(2)}, u32[]{:S(2)}) %collective-permute-start.1) | collective-permute-done | bytes 800 | tf_op jit(solution)/shard_map/ppermute | solution.py:62
  5.4 0.0 collective-permute-start.2
  5.4 1.7 %weight_low.1.refs_3_.refs_0_ = bf16[768,768]{1,0:T(8,128)(2,1)S(1)} custom-call(f32[768,768]{1,0:T(8,128)} %refs_0_.3, bf16[64,768]{1,0:T(8,128)(2,1)S(1)} %get-tuple-element.45.refs_1_.refs_0_), custom_call_target="tpu_custom_call" | custom-call | flops 99999997952 | tf_op jit(solution)/shard_map/weight_low/pallas_call | solution.py:48
  7.1 0.0 collective-permute-done.2.refs_1_
  7.1 0.7 %scorer.1 = (bf16[16,768]{1,0:T(8,128)(2,1)S(1)}, f32[48,768]{1,0:T(8,128)S(1)}) custom-call(f32[2,192]{1,0:T(2,128)S(1)} %score.1.refs_0_, f32[2,192]{1,0:T(2,128)S(1)} %collective-permute-done.2.refs_1_, f32[1,192]{1,0:T(1,128)S(1)} %get-tuple-element.47.refs_2_, bf16[768,768]{1,0:T(8,128)(2,1)S(1)} %weight_low.1.refs_3_.refs_0_), custom_call_target="tpu_custom_call" | custom-call | tf_op jit(solution)/shard_map/scorer/pallas_call | solution.py:48
  7.8 1.6 %collective-permute-done.refs_1_ = bf16[64,768]{1,0:T(8,128)(2,1)S(1)} collective-permute-done((bf16[64,768]{1,0:T(8,128)(2,1)S(1)}, bf16[64,768]{1,0:T(8,128)(2,1)S(1)}, u32[]{:S(2)}, u32[]{:S(2)}) %collective-permute-start) | collective-permute-done | bytes 98336 | tf_op jit(solution)/shard_map/ppermute | solution.py:62
  9.3 0.1 collective-permute-start.3
  9.4 1.0 %collective-permute-start.6 = (f32[48,768]{1,0:T(8,128)S(1)}, f32[48,768]{1,0:T(8,128)S(1)}, u32[]{:S(2)}, u32[]{:S(2)}) collective-permute-start(f32[48,768]{1,0:T(8,128)S(1)} %get-tuple-element.48.refs_2_.first), channel_id=1, source_target_pairs={{0,16},{8,24},{16,0},{24,8},{1,17},{9,25},{17,1},{25,9},{2,18},{10... | collective-permute-start | bytes 442376 | tf_op jit(solution)/shard_map/ppermute | solution.py:62
  10.4 0.4 collective-permute-done.3.second
  10.9 0.5 products.1
  11.4 0.7 %collective-permute-start.4 = (bf16[256,768]{1,0:T(8,128)(2,1)S(1)}, bf16[256,768]{1,0:T(8,128)(2,1)S(1)}, u32[]{:S(2)}, u32[]{:S(2)}) collective-permute-start(bf16[256,768]{1,0:T(8,128)(2,1)S(1)} %get-tuple-element.49.refs_0_.refs_1_), channel_id=1, source_target_pairs={{0,16},{8,24},{16,0},{24,8},{1,17},{9,25},{17,1},{25,9},{2,18},{10... | collective-permute-start | bytes 1179656 | tf_op jit(solution)/shard_map/ppermute | solution.py:62
  12.1 3.4 %collective-permute-start.8 = (f32[48,256]{1,0:T(8,128)S(1)}, f32[48,256]{1,0:T(8,128)S(1)}, u32[]{:S(2)}, u32[]{:S(2)}) collective-permute-start(f32[48,256]{1,0:T(8,128)S(1)} %tail.1), channel_id=1, source_target_pairs={{0,1},{1,2},{2,3},{3,4},{4,5},{5,6},{6,7},{8,9},{9,10},{10,11},{11... | collective-permute-start | bytes 147464 | tf_op jit(solution)/shard_map/ppermute | solution.py:807
  15.6 0.6 collective-permute-done.6.second
  16.1 0.0 collective-permute-start.7
  16.1 0.7 %planes.1 = (f32[48,1024]{1,0:T(8,128)S(1)}, bf16[256,4096]{1,0:T(8,128)(2,1)S(1)}) custom-call(f32[48,256]{1,0:T(8,128)S(1)} %get-tuple-element.50.refs_0_, bf16[256,768]{1,0:T(8,128)(2,1)S(1)} %get-tuple-element.49.refs_0_.refs_1_), custom_call_target="tpu_custom_call" | custom-call | tf_op jit(solution)/shard_map/planes/pallas_call | solution.py:48
  16.9 0.4 collective-permute-done.8.before
  17.3 0.2 halo.1.refs_3_
  17.5 0.0 collective-permute-done.7.refs_1_.refs_8_
  17.5 1.8 %far.1 = (bf16[128,768]{1,0:T(8,128)(2,1)S(1)}, bf16[128,768]{1,0:T(8,128)(2,1)S(1)}, f32[57,16,128]{2,1,0:T(8,128)S(1)}, bf16[16,768]{1,0:T(8,128)(2,1)S(1)}) custom-call(f32[16,768]{1,0:T(8,128)S(1)} %scored.1.refs_0_.refs_7_, f32[16,768]{1,0:T(8,128)S(1)} %collective-permute-done.7.refs_1_.refs_8_, bf16[256,768]{1,0:T(8,128)(2,1)S(1)} %table.1.table_low.refs_2_, ...), custom_call_target="tpu_custom_call" | custom-call | tf_op jit(solution)/shard_map/far/pallas_call | solution.py:48
  19.3 0.1 collective-permute-start.9
  19.5 0.4 collective-permute-start.10
  19.9 1.0 %far_own.1.mine = f32[256,768]{1,0:T(8,128)S(1)} custom-call(f32[57,16,128]{2,1,0:T(8,128)S(1)} %get-tuple-element.53.plan.refs_0_.refs_2_, bf16[2048,768]{1,0:T(8,128)(2,1)S(1)} %bitcast.7), custom_call_target="tpu_custom_call" | custom-call | tf_op jit(solution)/shard_map/far_own/pallas_call | solution.py:48
  20.9 0.2 collective-permute-done.10.two
  21.1 0.1 far_sum.1
  21.2 1.4 %collective-permute-start.13 = (bf16[128,768]{1,0:T(8,128)(2,1)S(1)}, bf16[128,768]{1,0:T(8,128)(2,1)S(1)}, u32[]{:S(2)}, u32[]{:S(2)}) collective-permute-start(bf16[128,768]{1,0:T(8,128)(2,1)S(1)} %get-tuple-element.64), channel_id=1, source_target_pairs={{0,16},{8,24},{16,0},{24,8},{1,17},{9,25},{17,1},{25,9},{2,18},{10... | collective-permute-start | bytes 589832 | tf_op jit(solution)/shard_map/ppermute | solution.py:62
  22.7 0.7 %collective-permute-start.12 = (bf16[128,768]{1,0:T(8,128)(2,1)S(1)}, bf16[128,768]{1,0:T(8,128)(2,1)S(1)}, u32[]{:S(2)}, u32[]{:S(2)}) collective-permute-start(bf16[128,768]{1,0:T(8,128)(2,1)S(1)} %get-tuple-element.57.refs_3_), channel_id=1, source_target_pairs={{0,16},{8,24},{16,0},{24,8},{1,17},{9,25},{17,1},{25,9},{2,18},{10... | collective-permute-start | bytes 589832 | tf_op jit(solution)/shard_map/ppermute | solution.py:62
  23.3 0.8 %collective-permute-done.4.refs_1_.refs_2_ = bf16[256,768]{1,0:T(8,128)(2,1)S(1)} collective-permute-done((bf16[256,768]{1,0:T(8,128)(2,1)S(1)}, bf16[256,768]{1,0:T(8,128)(2,1)S(1)}, u32[]{:S(2)}, u32[]{:S(2)}) %collective-permute-start.4) | collective-permute-done | bytes 393248 | tf_op jit(solution)/shard_map/ppermute | solution.py:62
  24.1 0.1 passed.1.products.refs_0_.refs_9_
  24.2 0.1 collective-permute-start.5
  24.2 2.0 %near.1 = (f32[256,768]{1,0:T(8,128)S(1)}, bf16[256,768]{1,0:T(8,128)(2,1)S(1)}, f32[8,768]{1,0:T(8,128)S(1)}) custom-call(f32[57,16,128]{2,1,0:T(8,128)S(1)} %get-tuple-element.53.plan.refs_0_.refs_2_, bf16[2048,768]{1,0:T(8,128)(2,1)S(1)} %bitcast.8, bf16[256,768]{1,0:T(8,128)(2,1)S(1)} %collective-permute-done.4.refs_1_.refs_2_, ...), custom_call_target="tpu_custom_call" | custom-call | tf_op jit(solution)/shard_map/near/pallas_call | solution.py:48
  26.2 0.6 collective-permute-start.11
  26.8 2.2 %inner_near.1.refs_0_ = f32[5,16,128]{2,1,0:T(8,128)S(1)} custom-call(bf16[512,768]{1,0:T(8,128)(2,1)S(1)} %passed.1.products.refs_0_.refs_9_, f32[57,16,128]{2,1,0:T(8,128)S(1)} %get-tuple-element.53.plan.refs_0_.refs_2_, bf16[16,768]{1,0:T(8,128)(2,1)S(1)} %get-tuple-element.54.vectors.refs_3_.refs_5_, bf16[2048,768]{1,0:T(8,128)(2,1)S(1)} %bitcast.9), custom_call_target="tpu_custom_call" | custom-call | flops 99999997952 | tf_op jit(solution)/shard_map/inner_near/pallas_call | solution.py:48
  29.0 0.1 near_sum.1.near
  29.1 2.1 %inner_far.1.inner_ref = f32[5,16,128]{2,1,0:T(8,128)S(1)} custom-call(bf16[512,768]{1,0:T(8,128)(2,1)S(1)} %collective-permute-done.5.products.refs_1_.refs_10_, f32[57,16,128]{2,1,0:T(8,128)S(1)} %get-tuple-element.53.plan.refs_0_.refs_2_, bf16[16,768]{1,0:T(8,128)(2,1)S(1)} %get-tuple-element.54.vectors.refs_3_.refs_5_, bf16[2048,768]{1,0:T(8,128)(2,1)S(1)} %bitcast.10, ...), custom_call_target="tpu_custom_call" | custom-call | tf_op jit(solution)/shard_map/inner_far/pallas_call | solution.py:48
  31.2 0.9 %scores.1.sums = f32[4,768]{1,0:T(4,128)S(1)} custom-call(f32[5,16,128]{2,1,0:T(8,128)S(1)} %inner_far.1.inner_ref, f32[57,16,128]{2,1,0:T(8,128)S(1)} %get-tuple-element.53.plan.refs_0_.refs_2_, bf16[16,768]{1,0:T(8,128)(2,1)S(1)} %get-tuple-element.54.vectors.refs_3_.refs_5_, bf16[256,4096]{1,0:T(8,128)(2,1)S(1)} %get-tuple-element.60.hot), custom_call_target="tpu_custom_call" | custom-call | tf_op jit(solution)/shard_map/scores/pallas_call | solution.py:48
  32.2 0.1 merge.1
  32.2 1.6 %collective-permute-start.14 = (bf16[72,768]{1,0:T(8,128)(2,1)S(1)}, bf16[72,768]{1,0:T(8,128)(2,1)S(1)}, u32[]{:S(2)}, u32[]{:S(2)}) collective-permute-start(bf16[72,768]{1,0:T(8,128)(2,1)S(1)} %get-tuple-element.66), channel_id=1, source_target_pairs={{0,1},{1,0},{2,3},{3,2},{4,5},{5,4},{6,7},{7,6},{8,9},{9,8},{10,11... | collective-permute-start | bytes 331784 | tf_op jit(solution)/shard_map/ppermute | solution.py:62
  33.8 2.4 %collective-permute-start.16 = (bf16[72,768]{1,0:T(8,128)(2,1)S(1)}, bf16[72,768]{1,0:T(8,128)(2,1)S(1)}, u32[]{:S(2)}, u32[]{:S(2)}) collective-permute-start(bf16[72,768]{1,0:T(8,128)(2,1)S(1)} %get-tuple-element.65.refs_1_), channel_id=1, source_target_pairs={{0,3},{1,2},{2,1},{3,0},{4,7},{5,6},{6,5},{7,4},{8,11},{9,10},{10,... | collective-permute-start | bytes 331784 | tf_op jit(solution)/shard_map/ppermute | solution.py:62
  36.3 0.1 rest.1
  36.3 0.1 collective-permute-start.15
  36.4 3.3 %output.2 = (bf16[2048,768]{1,0:T(8,128)(2,1)}, f32[8,128]{1,0:T(8,128)S(1)}) custom-call(bf16[512,768]{1,0:T(8,128)(2,1)S(1)} %passed.1.products.refs_0_.refs_9_, bf16[512,768]{1,0:T(8,128)(2,1)S(1)} %collective-permute-done.5.products.refs_1_.refs_10_, f32[57,16,128]{2,1,0:T(8,128)S(1)} %get-tuple-element.53.plan.refs_0_.refs_2_, ...), custom_call_target="tpu_custom_call" | custom-call | tf_op jit(solution)/shard_map/output/pallas_call | solution.py:547
  39.8 0.7 %collective-permute-done.16.refs_4_ = bf16[72,768]{1,0:T(8,128)(2,1)S(1)} collective-permute-done((bf16[72,768]{1,0:T(8,128)(2,1)S(1)}, bf16[72,768]{1,0:T(8,128)(2,1)S(1)}, u32[]{:S(2)}, u32[]{:S(2)}) %collective-permute-start.16) | collective-permute-done | bytes 110624 | tf_op jit(solution)/shard_map/ppermute | solution.py:62
  40.5 0.7 %collective-permute-done.15.refs_3_ = bf16[72,768]{1,0:T(8,128)(2,1)S(1)} collective-permute-done((bf16[72,768]{1,0:T(8,128)(2,1)S(1)}, bf16[72,768]{1,0:T(8,128)(2,1)S(1)}, u32[]{:S(2)}, u32[]{:S(2)}) %collective-permute-start.15) | collective-permute-done | bytes 110624 | tf_op jit(solution)/shard_map/ppermute | solution.py:62
  41.1 0.1 slice.1.refs_5_.refs_0_
  41.2 3.3 %collective-permute-start.17 = (bf16[72,768]{1,0:T(8,128)(2,1)S(1)}, bf16[72,768]{1,0:T(8,128)(2,1)S(1)}, u32[]{:S(2)}, u32[]{:S(2)}) collective-permute-start(bf16[72,768]{1,0:T(8,128)(2,1)S(1)} %slice.1.refs_5_.refs_0_), channel_id=1, source_target_pairs={{0,4},{1,5},{2,6},{3,7},{4,0},{5,1},{6,2},{7,3},{8,12},{9,13},{10,... | collective-permute-start | bytes 331784 | tf_op jit(solution)/shard_map/ppermute | solution.py:62
  44.5 3.1 %output.3 = (bf16[2048,768]{1,0:T(8,128)(2,1)}, f32[8,128]{1,0:T(8,128)S(1)}) custom-call(bf16[512,768]{1,0:T(8,128)(2,1)S(1)} %passed.1.products.refs_0_.refs_9_, bf16[512,768]{1,0:T(8,128)(2,1)S(1)} %collective-permute-done.5.products.refs_1_.refs_10_, f32[57,16,128]{2,1,0:T(8,128)S(1)} %get-tuple-element.53.plan.refs_0_.refs_2_, ...), custom_call_target="tpu_custom_call", output_to_operand_aliasing={{0}: (4, {})} | custom-call | tf_op jit(solution)/shard_map/output/pallas_call | solution.py:547
  47.7 0.4 turned.1.weight_turned
  48.0 1.2 %collective-permute-done.17.refs_1_ = bf16[72,768]{1,0:T(8,128)(2,1)S(1)} collective-permute-done((bf16[72,768]{1,0:T(8,128)(2,1)S(1)}, bf16[72,768]{1,0:T(8,128)(2,1)S(1)}, u32[]{:S(2)}, u32[]{:S(2)}) %collective-permute-start.17) | collective-permute-done | bytes 110624 | tf_op jit(solution)/shard_map/ppermute | solution.py:62
  49.3 0.3 share.1
  49.6 1.4 %collective-permute-start.18 = (bf16[40,768]{1,0:T(8,128)(2,1)S(1)}, bf16[40,768]{1,0:T(8,128)(2,1)S(1)}, u32[]{:S(2)}, u32[]{:S(2)}) collective-permute-start(bf16[40,768]{1,0:T(8,128)(2,1)S(1)} %get-tuple-element.74), channel_id=1, source_target_pairs={{0,16},{8,24},{16,0},{24,8},{1,17},{9,25},{17,1},{25,9},{2,18},{10... | collective-permute-start | bytes 184328 | tf_op jit(solution)/shard_map/ppermute | solution.py:62
  51.0 0.7 %collective-permute-start.25 = (bf16[64,768]{1,0:T(8,128)(2,1)S(1)}, bf16[64,768]{1,0:T(8,128)(2,1)S(1)}, u32[]{:S(2)}, u32[]{:S(2)}) collective-permute-start(bf16[64,768]{1,0:T(8,128)(2,1)S(1)} %get-tuple-element.71.block.refs_0_), channel_id=1, source_target_pairs={{0,3},{1,2},{2,1},{3,0},{4,7},{5,6},{6,5},{7,4},{8,11},{9,10},{10,... | collective-permute-start | bytes 294920 | tf_op jit(solution)/shard_map/ppermute | solution.py:62
  51.7 1.5 %collective-permute-start.24 = (bf16[64,768]{1,0:T(8,128)(2,1)S(1)}, bf16[64,768]{1,0:T(8,128)(2,1)S(1)}, u32[]{:S(2)}, u32[]{:S(2)}) collective-permute-start(bf16[64,768]{1,0:T(8,128)(2,1)S(1)} %get-tuple-element.71.block.refs_0_), channel_id=1, source_target_pairs={{0,2},{1,3},{2,0},{3,1},{4,6},{5,7},{6,4},{7,5},{8,10},{9,11},{10,... | collective-permute-start | bytes 294920 | tf_op jit(solution)/shard_map/ppermute | solution.py:62
  53.2 1.4 %collective-permute-start.23 = (bf16[64,768]{1,0:T(8,128)(2,1)S(1)}, bf16[64,768]{1,0:T(8,128)(2,1)S(1)}, u32[]{:S(2)}, u32[]{:S(2)}) collective-permute-start(bf16[64,768]{1,0:T(8,128)(2,1)S(1)} %get-tuple-element.71.block.refs_0_), channel_id=1, source_target_pairs={{0,1},{1,0},{2,3},{3,2},{4,5},{5,4},{6,7},{7,6},{8,9},{9,8},{10,11... | collective-permute-start | bytes 294920 | tf_op jit(solution)/shard_map/ppermute | solution.py:62
  54.6 0.1 collective-permute-start.19
  54.6 1.2 %collective-permute-done.19.other = bf16[24,768]{1,0:T(8,128)(2,1)S(1)} collective-permute-done((bf16[24,768]{1,0:T(8,128)(2,1)S(1)}, bf16[24,768]{1,0:T(8,128)(2,1)S(1)}, u32[]{:S(2)}, u32[]{:S(2)}) %collective-permute-start.19) | collective-permute-done | bytes 36896 | tf_op jit(solution)/shard_map/ppermute | solution.py:62
  55.8 0.7 %collective-permute-start.22 = (bf16[16,768]{1,0:T(8,128)(2,1)S(1)}, bf16[16,768]{1,0:T(8,128)(2,1)S(1)}, u32[]{:S(2)}, u32[]{:S(2)}) collective-permute-start(bf16[16,768]{1,0:T(8,128)(2,1)S(1)} %get-tuple-element.78.refs_0_), channel_id=1, source_target_pairs={{0,3},{1,2},{2,1},{3,0},{4,7},{5,6},{6,5},{7,4},{8,11},{9,10},{10,... | collective-permute-start | bytes 73736 | tf_op jit(solution)/shard_map/ppermute | solution.py:62
  56.6 1.5 %collective-permute-start.21 = (bf16[16,768]{1,0:T(8,128)(2,1)S(1)}, bf16[16,768]{1,0:T(8,128)(2,1)S(1)}, u32[]{:S(2)}, u32[]{:S(2)}) collective-permute-start(bf16[16,768]{1,0:T(8,128)(2,1)S(1)} %get-tuple-element.78.refs_0_), channel_id=1, source_target_pairs={{0,2},{1,3},{2,0},{3,1},{4,6},{5,7},{6,4},{7,5},{8,10},{9,11},{10,... | collective-permute-start | bytes 73736 | tf_op jit(solution)/shard_map/ppermute | solution.py:62
  58.0 1.4 %collective-permute-start.20 = (bf16[16,768]{1,0:T(8,128)(2,1)S(1)}, bf16[16,768]{1,0:T(8,128)(2,1)S(1)}, u32[]{:S(2)}, u32[]{:S(2)}) collective-permute-start(bf16[16,768]{1,0:T(8,128)(2,1)S(1)} %get-tuple-element.78.refs_0_), channel_id=1, source_target_pairs={{0,1},{1,0},{2,3},{3,2},{4,5},{5,4},{6,7},{7,6},{8,9},{9,8},{10,11... | collective-permute-start | bytes 73736 | tf_op jit(solution)/shard_map/ppermute | solution.py:62
  59.4 1.8 %weights.1 = (f32[768,768]{1,0:T(8,128)}, f32[1,192]{1,0:T(1,128)}, f32[1,192]{1,0:T(1,128)}, f32[256,768]{1,0:T(8,128)S(1)}) custom-call(bf16[64,768]{1,0:T(8,128)(2,1)S(1)} %get-tuple-element.71.block.refs_0_, bf16[64,768]{1,0:T(8,128)(2,1)S(1)} %collective-permute-done.23.refs_1_, bf16[64,768]{1,0:T(8,128)(2,1)S(1)} %collective-permute-done.24.refs_2_, ...), custom_call_target="tpu_custom_call" | custom-call | tf_op jit(solution)/shard_map/weights/pallas_call | solution.py:48
  61.3 0.6 collective-permute-done.20.refs_1_
  61.9 0.7 %table_grad.1 = f32[64,768]{1,0:T(8,128)} custom-call(bf16[16,768]{1,0:T(8,128)(2,1)S(1)} %get-tuple-element.78.refs_0_, bf16[16,768]{1,0:T(8,128)(2,1)S(1)} %collective-permute-done.20.refs_1_, bf16[16,768]{1,0:T(8,128)(2,1)S(1)} %collective-permute-done.21.refs_2_, bf16[16,768]{1,0:T(8,128)(2,1)S(1)} %collective-permute-done.22.refs_3_, ...), custom_call_target="tpu_custom_call" | custom-call | tf_op jit(solution)/shard_map/table_grad/pallas_call | solution.py:48
  (22 shorter events, 0.2 us)
Async XLA Ops:
  0.6 4.8 %collective-permute-start.1 = (f32[1,192]{1,0:T(1,128)}, f32[1,192]{1,0:T(1,128)S(1)}, u32[]{:S(2)}, u32[]{:S(2)}) collective-permute-start(f32[1,192]{1,0:T(1,128)} %bitcast.13), channel_id=1, source_target_pairs={{0,16},{8,24},{16,0},{24,8},{1,17},{9,25},{17,1},{25,9},{2,18},{10... | collective-permute-start | bytes 2312 | tf_op jit(solution)/shard_map/ppermute | solution.py:62
  4.6 4.7 %collective-permute-start = (bf16[64,768]{1,0:T(8,128)(2,1)S(1)}, bf16[64,768]{1,0:T(8,128)(2,1)S(1)}, u32[]{:S(2)}, u32[]{:S(2)}) collective-permute-start(bf16[64,768]{1,0:T(8,128)(2,1)S(1)} %get-tuple-element.45.refs_1_.refs_0_), channel_id=1, source_target_pairs={{0,16},{8,24},{16,0},{24,8},{1,17},{9,25},{17,1},{25,9},{2,18},{10... | collective-permute-start | bytes 294920 | tf_op jit(solution)/shard_map/ppermute | solution.py:62
  5.4 1.7 %collective-permute-start.2 = (f32[2,192]{1,0:T(2,128)S(1)}, f32[2,192]{1,0:T(2,128)S(1)}, u32[]{:S(2)}, u32[]{:S(2)}) collective-permute-start(f32[2,192]{1,0:T(2,128)S(1)} %score.1.refs_0_), channel_id=1, source_target_pairs={{0,8},{8,0},{16,24},{24,16},{1,9},{9,1},{17,25},{25,17},{2,10},{10... | collective-permute-start | bytes 4616 | tf_op jit(solution)/shard_map/ppermute | solution.py:62
  7.8 9.7 %copy-start = (bf16[16,128,768]{2,1,0:T(8,128)(2,1)S(1)}, bf16[16,128,768]{2,1,0:T(8,128)(2,1)}, u32[]{:S(2)}) copy-start(bf16[16,128,768]{2,1,0:T(8,128)(2,1)} %param.15) | copy-start | bytes 9437188
  9.3 1.5 %collective-permute-start.3 = (bf16[128,768]{1,0:T(8,128)(2,1)S(1)}, bf16[128,768]{1,0:T(8,128)(2,1)S(1)}, u32[]{:S(2)}, u32[]{:S(2)}) collective-permute-start(bf16[128,768]{1,0:T(8,128)(2,1)S(1)} %table_pair.1.first), channel_id=1, source_target_pairs={{0,8},{8,0},{16,24},{24,16},{1,9},{9,1},{17,25},{25,17},{2,10},{10... | collective-permute-start | bytes 589832 | tf_op jit(solution)/shard_map/ppermute | solution.py:62
  9.4 6.7 %collective-permute-start.6 = (f32[48,768]{1,0:T(8,128)S(1)}, f32[48,768]{1,0:T(8,128)S(1)}, u32[]{:S(2)}, u32[]{:S(2)}) collective-permute-start(f32[48,768]{1,0:T(8,128)S(1)} %get-tuple-element.48.refs_2_.first), channel_id=1, source_target_pairs={{0,16},{8,24},{16,0},{24,8},{1,17},{9,25},{17,1},{25,9},{2,18},{10... | collective-permute-start | bytes 442376 | tf_op jit(solution)/shard_map/ppermute | solution.py:62
  11.4 12.7 %collective-permute-start.4 = (bf16[256,768]{1,0:T(8,128)(2,1)S(1)}, bf16[256,768]{1,0:T(8,128)(2,1)S(1)}, u32[]{:S(2)}, u32[]{:S(2)}) collective-permute-start(bf16[256,768]{1,0:T(8,128)(2,1)S(1)} %get-tuple-element.49.refs_0_.refs_1_), channel_id=1, source_target_pairs={{0,16},{8,24},{16,0},{24,8},{1,17},{9,25},{17,1},{25,9},{2,18},{10... | collective-permute-start | bytes 1179656 | tf_op jit(solution)/shard_map/ppermute | solution.py:62
  12.1 5.2 %collective-permute-start.8 = (f32[48,256]{1,0:T(8,128)S(1)}, f32[48,256]{1,0:T(8,128)S(1)}, u32[]{:S(2)}, u32[]{:S(2)}) collective-permute-start(f32[48,256]{1,0:T(8,128)S(1)} %tail.1), channel_id=1, source_target_pairs={{0,1},{1,2},{2,3},{3,4},{4,5},{5,6},{6,7},{8,9},{9,10},{10,11},{11... | collective-permute-start | bytes 147464 | tf_op jit(solution)/shard_map/ppermute | solution.py:807
  16.1 1.3 %collective-permute-start.7 = (f32[16,768]{1,0:T(8,128)S(1)}, f32[16,768]{1,0:T(8,128)S(1)}, u32[]{:S(2)}, u32[]{:S(2)}) collective-permute-start(f32[16,768]{1,0:T(8,128)S(1)} %scored.1.refs_0_.refs_7_), channel_id=1, source_target_pairs={{0,8},{8,0},{16,24},{24,16},{1,9},{9,1},{17,25},{25,17},{2,10},{10... | collective-permute-start | bytes 147464 | tf_op jit(solution)/shard_map/ppermute | solution.py:62
  19.3 1.6 %collective-permute-start.9 = (bf16[128,768]{1,0:T(8,128)(2,1)S(1)}, bf16[128,768]{1,0:T(8,128)(2,1)S(1)}, u32[]{:S(2)}, u32[]{:S(2)}) collective-permute-start(bf16[128,768]{1,0:T(8,128)(2,1)S(1)} %get-tuple-element.55), channel_id=1, source_target_pairs={{0,8},{8,0},{16,24},{24,16},{1,9},{9,1},{17,25},{25,17},{2,10},{10... | collective-permute-start | bytes 589832 | tf_op jit(solution)/shard_map/ppermute | solution.py:62
  19.5 1.6 %collective-permute-start.10 = (bf16[128,768]{1,0:T(8,128)(2,1)S(1)}, bf16[128,768]{1,0:T(8,128)(2,1)S(1)}, u32[]{:S(2)}, u32[]{:S(2)}) collective-permute-start(bf16[128,768]{1,0:T(8,128)(2,1)S(1)} %get-tuple-element.56), channel_id=1, source_target_pairs={{0,8},{8,0},{16,24},{24,16},{1,9},{9,1},{17,25},{25,17},{2,10},{10... | collective-permute-start | bytes 589832 | tf_op jit(solution)/shard_map/ppermute | solution.py:62
  21.2 10.9 %collective-permute-start.13 = (bf16[128,768]{1,0:T(8,128)(2,1)S(1)}, bf16[128,768]{1,0:T(8,128)(2,1)S(1)}, u32[]{:S(2)}, u32[]{:S(2)}) collective-permute-start(bf16[128,768]{1,0:T(8,128)(2,1)S(1)} %get-tuple-element.64), channel_id=1, source_target_pairs={{0,16},{8,24},{16,0},{24,8},{1,17},{9,25},{17,1},{25,9},{2,18},{10... | collective-permute-start | bytes 589832 | tf_op jit(solution)/shard_map/ppermute | solution.py:62
  22.7 13.6 %collective-permute-start.12 = (bf16[128,768]{1,0:T(8,128)(2,1)S(1)}, bf16[128,768]{1,0:T(8,128)(2,1)S(1)}, u32[]{:S(2)}, u32[]{:S(2)}) collective-permute-start(bf16[128,768]{1,0:T(8,128)(2,1)S(1)} %get-tuple-element.57.refs_3_), channel_id=1, source_target_pairs={{0,16},{8,24},{16,0},{24,8},{1,17},{9,25},{17,1},{25,9},{2,18},{10... | collective-permute-start | bytes 589832 | tf_op jit(solution)/shard_map/ppermute | solution.py:62
  24.2 4.9 %collective-permute-start.5 = (bf16[512,768]{1,0:T(8,128)(2,1)S(1)}, bf16[512,768]{1,0:T(8,128)(2,1)S(1)}, u32[]{:S(2)}, u32[]{:S(2)}) collective-permute-start(bf16[512,768]{1,0:T(8,128)(2,1)S(1)} %passed.1.products.refs_0_.refs_9_), channel_id=1, source_target_pairs={{0,8},{8,0},{16,24},{24,16},{1,9},{9,1},{17,25},{25,17},{2,10},{10... | collective-permute-start | bytes 2359304 | tf_op jit(solution)/shard_map/ppermute | solution.py:62
  26.2 2.7 %collective-permute-start.11 = (bf16[256,768]{1,0:T(8,128)(2,1)S(1)}, bf16[256,768]{1,0:T(8,128)(2,1)S(1)}, u32[]{:S(2)}, u32[]{:S(2)}) collective-permute-start(bf16[256,768]{1,0:T(8,128)(2,1)S(1)} %get-tuple-element.59), channel_id=1, source_target_pairs={{0,8},{8,0},{16,24},{24,16},{1,9},{9,1},{17,25},{25,17},{2,10},{10... | collective-permute-start | bytes 1179656 | tf_op jit(solution)/shard_map/ppermute | solution.py:62
  32.2 7.5 %collective-permute-start.14 = (bf16[72,768]{1,0:T(8,128)(2,1)S(1)}, bf16[72,768]{1,0:T(8,128)(2,1)S(1)}, u32[]{:S(2)}, u32[]{:S(2)}) collective-permute-start(bf16[72,768]{1,0:T(8,128)(2,1)S(1)} %get-tuple-element.66), channel_id=1, source_target_pairs={{0,1},{1,0},{2,3},{3,2},{4,5},{5,4},{6,7},{7,6},{8,9},{9,8},{10,11... | collective-permute-start | bytes 331784 | tf_op jit(solution)/shard_map/ppermute | solution.py:62
  33.8 6.6 %collective-permute-start.16 = (bf16[72,768]{1,0:T(8,128)(2,1)S(1)}, bf16[72,768]{1,0:T(8,128)(2,1)S(1)}, u32[]{:S(2)}, u32[]{:S(2)}) collective-permute-start(bf16[72,768]{1,0:T(8,128)(2,1)S(1)} %get-tuple-element.65.refs_1_), channel_id=1, source_target_pairs={{0,3},{1,2},{2,1},{3,0},{4,7},{5,6},{6,5},{7,4},{8,11},{9,10},{10,... | collective-permute-start | bytes 331784 | tf_op jit(solution)/shard_map/ppermute | solution.py:62
  36.3 4.8 %collective-permute-start.15 = (bf16[72,768]{1,0:T(8,128)(2,1)S(1)}, bf16[72,768]{1,0:T(8,128)(2,1)S(1)}, u32[]{:S(2)}, u32[]{:S(2)}) collective-permute-start(bf16[72,768]{1,0:T(8,128)(2,1)S(1)} %get-tuple-element.67), channel_id=1, source_target_pairs={{0,2},{1,3},{2,0},{3,1},{4,6},{5,7},{6,4},{7,5},{8,10},{9,11},{10,... | collective-permute-start | bytes 331784 | tf_op jit(solution)/shard_map/ppermute | solution.py:62
  41.2 8.0 %collective-permute-start.17 = (bf16[72,768]{1,0:T(8,128)(2,1)S(1)}, bf16[72,768]{1,0:T(8,128)(2,1)S(1)}, u32[]{:S(2)}, u32[]{:S(2)}) collective-permute-start(bf16[72,768]{1,0:T(8,128)(2,1)S(1)} %slice.1.refs_5_.refs_0_), channel_id=1, source_target_pairs={{0,4},{1,5},{2,6},{3,7},{4,0},{5,1},{6,2},{7,3},{8,12},{9,13},{10,... | collective-permute-start | bytes 331784 | tf_op jit(solution)/shard_map/ppermute | solution.py:62
  49.6 4.9 %collective-permute-start.18 = (bf16[40,768]{1,0:T(8,128)(2,1)S(1)}, bf16[40,768]{1,0:T(8,128)(2,1)S(1)}, u32[]{:S(2)}, u32[]{:S(2)}) collective-permute-start(bf16[40,768]{1,0:T(8,128)(2,1)S(1)} %get-tuple-element.74), channel_id=1, source_target_pairs={{0,16},{8,24},{16,0},{24,8},{1,17},{9,25},{17,1},{25,9},{2,18},{10... | collective-permute-start | bytes 184328 | tf_op jit(solution)/shard_map/ppermute | solution.py:62
  51.0 7.0 %collective-permute-start.25 = (bf16[64,768]{1,0:T(8,128)(2,1)S(1)}, bf16[64,768]{1,0:T(8,128)(2,1)S(1)}, u32[]{:S(2)}, u32[]{:S(2)}) collective-permute-start(bf16[64,768]{1,0:T(8,128)(2,1)S(1)} %get-tuple-element.71.block.refs_0_), channel_id=1, source_target_pairs={{0,3},{1,2},{2,1},{3,0},{4,7},{5,6},{6,5},{7,4},{8,11},{9,10},{10,... | collective-permute-start | bytes 294920 | tf_op jit(solution)/shard_map/ppermute | solution.py:62
  51.7 7.7 %collective-permute-start.24 = (bf16[64,768]{1,0:T(8,128)(2,1)S(1)}, bf16[64,768]{1,0:T(8,128)(2,1)S(1)}, u32[]{:S(2)}, u32[]{:S(2)}) collective-permute-start(bf16[64,768]{1,0:T(8,128)(2,1)S(1)} %get-tuple-element.71.block.refs_0_), channel_id=1, source_target_pairs={{0,2},{1,3},{2,0},{3,1},{4,6},{5,7},{6,4},{7,5},{8,10},{9,11},{10,... | collective-permute-start | bytes 294920 | tf_op jit(solution)/shard_map/ppermute | solution.py:62
  53.2 6.2 %collective-permute-start.23 = (bf16[64,768]{1,0:T(8,128)(2,1)S(1)}, bf16[64,768]{1,0:T(8,128)(2,1)S(1)}, u32[]{:S(2)}, u32[]{:S(2)}) collective-permute-start(bf16[64,768]{1,0:T(8,128)(2,1)S(1)} %get-tuple-element.71.block.refs_0_), channel_id=1, source_target_pairs={{0,1},{1,0},{2,3},{3,2},{4,5},{5,4},{6,7},{7,6},{8,9},{9,8},{10,11... | collective-permute-start | bytes 294920 | tf_op jit(solution)/shard_map/ppermute | solution.py:62
  54.6 1.3 %collective-permute-start.19 = (bf16[24,768]{1,0:T(8,128)(2,1)S(1)}, bf16[24,768]{1,0:T(8,128)(2,1)S(1)}, u32[]{:S(2)}, u32[]{:S(2)}) collective-permute-start(bf16[24,768]{1,0:T(8,128)(2,1)S(1)} %get-tuple-element.77), channel_id=1, source_target_pairs={{0,8},{8,0},{16,24},{24,16},{1,9},{9,1},{17,25},{25,17},{2,10},{10... | collective-permute-start | bytes 110600 | tf_op jit(solution)/shard_map/ppermute | solution.py:62
  55.8 5.4 %collective-permute-start.22 = (bf16[16,768]{1,0:T(8,128)(2,1)S(1)}, bf16[16,768]{1,0:T(8,128)(2,1)S(1)}, u32[]{:S(2)}, u32[]{:S(2)}) collective-permute-start(bf16[16,768]{1,0:T(8,128)(2,1)S(1)} %get-tuple-element.78.refs_0_), channel_id=1, source_target_pairs={{0,3},{1,2},{2,1},{3,0},{4,7},{5,6},{6,5},{7,4},{8,11},{9,10},{10,... | collective-permute-start | bytes 73736 | tf_op jit(solution)/shard_map/ppermute | solution.py:62
  56.6 4.7 %collective-permute-start.21 = (bf16[16,768]{1,0:T(8,128)(2,1)S(1)}, bf16[16,768]{1,0:T(8,128)(2,1)S(1)}, u32[]{:S(2)}, u32[]{:S(2)}) collective-permute-start(bf16[16,768]{1,0:T(8,128)(2,1)S(1)} %get-tuple-element.78.refs_0_), channel_id=1, source_target_pairs={{0,2},{1,3},{2,0},{3,1},{4,6},{5,7},{6,4},{7,5},{8,10},{9,11},{10,... | collective-permute-start | bytes 73736 | tf_op jit(solution)/shard_map/ppermute | solution.py:62
  58.0 3.8 %collective-permute-start.20 = (bf16[16,768]{1,0:T(8,128)(2,1)S(1)}, bf16[16,768]{1,0:T(8,128)(2,1)S(1)}, u32[]{:S(2)}, u32[]{:S(2)}) collective-permute-start(bf16[16,768]{1,0:T(8,128)(2,1)S(1)} %get-tuple-element.78.refs_0_), channel_id=1, source_target_pairs={{0,1},{1,0},{2,3},{3,2},{4,5},{5,4},{6,7},{7,6},{8,9},{9,8},{10,11... | collective-permute-start | bytes 73736 | tf_op jit(solution)/shard_map/ppermute | solution.py:62
